TPU v7x, 256 devices: a whole 4x4x8 slice. The times are simulated.
256 devices in a mesh: slot: 32 (over z_hi, y, core), tp: 8 (over z_lo, x).
Axes of the slice: x: 4, y: 4, z: 8 (z_hi: 4, z_lo: 2; z = z_hi * 2 + z_lo), core: 2. Of those that a mesh axis runs over, the one named last changes fastest.
Arguments:
- hidden: bfloat16 [14336, 6144], P('slot', 'tp'), may hold values from -4 to 4
- queries: bfloat16 [14336, 3072], P('slot', 'tp'), may hold values from -22 to 22
- key_rows: bfloat16 [14336, 3072], P('slot', 'tp'), may hold values from -6 to 6
- values: bfloat16 [14336, 3072], P('slot', 'tp'), may hold values from -6 to 6
- out_weight: bfloat16 [3072, 6144], P('tp'), may hold values from -0.109375 to 0.109375
- level_table: float32 [64, 6144], P(None, 'tp'), may hold values from 0.3 to 3
- noise_level: int32 [32], P('slot'), may hold values from 0 to 63
- group_live: int32 [32], replicated, may hold values 0 or 1
Outputs:
- refined: bfloat16 [14336, 6144], P('slot', 'tp')
All inputs are finite; a program needn't handle non-finite values.
Results may differ from a plain program's by a relative error of at most 0.014.
Values may be sent and summed in bfloat16 or wider, within the bound.
No kernel may reach another device: no remote copies, remote signals or barrier semaphores. Data moves between devices by JAX's collectives and lax.ppermute only.
A program may use at most 128 MiB of HBM per device.

v0:
```python
import functools
import math

import jax
import jax.numpy as jnp
import numpy as np
from jax import lax
from jax.experimental import pallas as pl
from jax.experimental.pallas import tpu as pltpu
from jax.sharding import Mesh
from jax.sharding import PartitionSpec as P

HD = 128
ROWS = 448
HEADS_HERE = 3
WIDTH = HEADS_HERE * HD
STAT = 32
LOWEST = -(2.0**100)
EXP2_SCALE = HD**-0.5 * math.log2(math.e)
Y_STEPS = (0, -1, 1, 2)
SLOT = ("z", "y", "c")
ATTEND_VMEM = 32 * 1024 * 1024
SMALL_VMEM = 16 * 1024 * 1024


def score(query, key):
    return lax.dot_general(
        query, key, (((1,), (1,)), ((), ())), preferred_element_type=jnp.float32
    )


def attend_kernel(ids, live, level, *refs):
    query_in, pair_in, out = refs[0:4], refs[4:12], refs[12:16]
    raw, scaled, pairs, held, acc, top, done, raw_sem, pair_sem, out_sem = refs[16:]
    here, y, core = ids[0], ids[1], ids[2]
    first = here * 8
    mine = first + y * 2 + core
    groups = []
    for other in (0, 1):
        for step in Y_STEPS:
            core_there = core if other == 0 else 1 - core
            groups.append(first + lax.rem(y + step + 4, 4) * 2 + core_there)
    alive = [live[first + k] for k in range(8)]

    def live_before(group):
        count = jnp.int32(0)
        for k in range(8):
            count = count + jnp.where(first + k < group, alive[k], 0)
        return count

    n_all, n_own = live_before(first + 8), live_before(mine)
    last = here == 3
    own_place = jnp.where((live[mine] == 1) | last, n_own, n_all)

    def raw_copy(d):
        return pltpu.make_async_copy(query_in[d], raw.at[d], raw_sem.at[d])

    def place_copy(p, place):
        at = pl.ds(pl.multiple_of(place * ROWS, 64), ROWS)
        return pltpu.make_async_copy(pair_in[p], pairs.at[at], pair_sem.at[place])

    def wait_place(place):
        place_copy(0, place).wait()

    raw_copy(0).start()
    place_copy(0, own_place).start()
    for p in range(1, 8):

        @pl.when((live[groups[p]] == 1) & ((groups[p] < mine) | jnp.logical_not(last)))
        def _():
            place_copy(p, live_before(groups[p])).start()

    for d in range(1, 4):

        @pl.when(here + d <= 3)
        def _():
            raw_copy(d).start()

    raw_copy(0).wait()
    wait_place(own_place)
    for k in range(8):

        @pl.when(k < n_own)
        def _():
            wait_place(k)

    def source(d, unused):
        @pl.when(d == 1)
        def _():
            for k in range(8):

                @pl.when((k >= n_own) & (k < n_all) & (k != own_place))
                def _():
                    wait_place(k)

            for e in range(1, 4):

                @pl.when(here + e <= 3)
                def _():
                    raw_copy(e).wait()

        count = jnp.where(d == 0, n_own + 1, n_all)
        chunks = (count + 1) // 2

        def place(i):
            i = jnp.maximum(jnp.minimum(i, count - 1), 0)
            return jnp.where((d == 0) & (i == n_own), own_place, i)

        def at(i):
            return pl.ds(pl.multiple_of(place(i) * ROWS, 64), ROWS)

        for head in range(HEADS_HERE):
            exact = raw[d, :, head * HD : (head + 1) * HD].astype(jnp.float32) * EXP2_SCALE
            high = exact.astype(jnp.bfloat16)
            scaled[head, :, :HD] = high
            scaled[head, :, HD:] = (exact - high.astype(jnp.float32)).astype(jnp.bfloat16)
        top[...] = jnp.full(top.shape, LOWEST, jnp.float32)
        acc[...] = jnp.zeros(acc.shape, jnp.float32)

        def scores_of(t, head):
            cols = slice(head * HD, (head + 1) * HD)
            key = jnp.concatenate([pairs[at(2 * t), cols], pairs[at(2 * t + 1), cols]], axis=0)
            return score(scaled[head], jnp.concatenate([key, key], axis=1))

        def absorb(t, head, scores):
            old = top[head]
            new = jnp.maximum(old, jnp.max(scores, axis=1, keepdims=True))
            weights = jnp.exp2(scores - jnp.concatenate([new] * (2 * ROWS // HD), axis=1))
            cols = slice(WIDTH + head * HD, WIDTH + (head + 1) * HD)
            there = jnp.where(2 * t + 1 < count, 1.0, 0.0).astype(jnp.bfloat16)
            ones = jnp.ones((ROWS, HD), jnp.bfloat16)
            value = jnp.concatenate(
                [
                    jnp.concatenate([pairs[at(2 * t), cols], ones], axis=1),
                    jnp.concatenate([pairs[at(2 * t + 1), cols], ones], axis=1) * there,
                ],
                axis=0,
            )
            weighted = jnp.dot(
                weights.astype(jnp.bfloat16), value, preferred_element_type=jnp.float32
            )
            shrink = jnp.exp2(old - new)
            acc[head] = acc[head] * jnp.concatenate([shrink, shrink], axis=1) + weighted
            top[head] = new

        held[...] = scores_of(0, 0)

        def chunk(t, unused_too):
            scores = held[...]
            following = scores_of(t, 1)
            absorb(t, 0, scores)
            scores = scores_of(t, 2)
            absorb(t, 1, following)
            held[...] = scores_of(t + 1, 0)
            absorb(t, 2, scores)
            return 0

        lax.fori_loop(0, chunks, chunk, 0)

        lane = lax.broadcasted_iota(jnp.int32, (ROWS, HD), 1)
        stats = jnp.where(lane == 3 * HEADS_HERE, level[0].astype(jnp.float32), 0.0)
        for head in range(HEADS_HERE):
            exact = top[head]
            sent = exact.astype(jnp.bfloat16).astype(jnp.float32)
            factor = jnp.exp2(exact - sent)
            both = acc[head]
            done[d, 0:ROWS, head * HD : (head + 1) * HD] = (both[:, :HD] * factor).astype(
                jnp.bfloat16
            )
            total = both[:, HD:] * factor
            high = total.astype(jnp.bfloat16).astype(jnp.float32)
            stats = jnp.where(lane == head, sent, stats)
            stats = jnp.where(lane == HEADS_HERE + head, high, stats)
            stats = jnp.where(lane == 2 * HEADS_HERE + head, total - high, stats)
        flat = jnp.transpose(stats)[:16].astype(jnp.bfloat16)
        done[d, ROWS : ROWS + 16, :] = flat[:, :WIDTH]
        pad = jnp.zeros((16, 2 * WIDTH - ROWS), jnp.bfloat16)
        done[d, ROWS + 16 : ROWS + 32, :] = jnp.concatenate([flat[:, WIDTH:], pad], axis=1)
        for k in range(4):

            @pl.when(d == k)
            def _():
                pltpu.make_async_copy(done.at[k], out[k], out_sem.at[k]).start()

        return 0

    lax.fori_loop(0, 4 - here, source, 0)
    for k in range(4):

        @pl.when(here + k <= 3)
        def _():
            pltpu.make_async_copy(done.at[k], out[k], out_sem.at[k]).wait()


def attend(ids, live, level, queries, pairs):
    smem = pl.BlockSpec(memory_space=pltpu.SMEM)
    anywhere = pl.BlockSpec(memory_space=pl.ANY)
    bf16, f32 = jnp.bfloat16, jnp.float32
    return pl.pallas_call(
        attend_kernel,
        out_shape=[jax.ShapeDtypeStruct((ROWS + STAT, WIDTH), bf16)] * 4,
        in_specs=[smem] * 3 + [anywhere] * 12,
        out_specs=[anywhere] * 4,
        scratch_shapes=[
            pltpu.VMEM((4, ROWS, WIDTH), bf16),
            pltpu.VMEM((HEADS_HERE, ROWS, 2 * HD), bf16),
            pltpu.VMEM((8 * ROWS, 2 * WIDTH), bf16),
            pltpu.VMEM((ROWS, 2 * ROWS), f32),
            pltpu.VMEM((HEADS_HERE, ROWS, 2 * HD), f32),
            pltpu.VMEM((HEADS_HERE, ROWS, HD), f32),
            pltpu.VMEM((4, ROWS + STAT, WIDTH), bf16),
            pltpu.SemaphoreType.DMA((4,)),
            pltpu.SemaphoreType.DMA((8,)),
            pltpu.SemaphoreType.DMA((4,)),
        ],
        compiler_params=pltpu.CompilerParams(vmem_limit_bytes=ATTEND_VMEM),
        cost_estimate=pl.CostEstimate(
            flops=32 * HEADS_HERE * ROWS * ROWS * HD * 8, bytes_accessed=8000000, transcendentals=0
        ),
        name="attend",
    )(ids, live, level, *queries, *pairs)


def combine_kernel(ids, table, *refs):
    parts, out, gate = refs[0:4], refs[4], refs[5]
    home = ids[3]
    maxima, sums = [], []
    for d in range(4):
        tail = parts[d][ROWS : ROWS + STAT, :].astype(jnp.float32)
        flat = jnp.concatenate([tail[0:16], tail[16:32, : ROWS - WIDTH]], axis=1)
        if d == 0:
            noise = flat[3 * HEADS_HERE : 3 * HEADS_HERE + 1, 0:1]
        stats = jnp.transpose(jnp.concatenate([flat, jnp.zeros((HD - 16, ROWS), jnp.float32)]))
        present = d <= home
        row_max, row_sum = [], []
        for head in range(HEADS_HERE):
            total = (
                stats[:, HEADS_HERE + head : HEADS_HERE + head + 1]
                + stats[:, 2 * HEADS_HERE + head : 2 * HEADS_HERE + head + 1]
            )
            row_max.append(jnp.where(present, stats[:, head : head + 1], LOWEST))
            row_sum.append(jnp.where(present, total, 0.0))
        maxima.append(row_max)
        sums.append(row_sum)
    for head in range(HEADS_HERE):
        at = slice(head * HD, (head + 1) * HD)
        highest = maxima[0][head]
        for d in range(1, 4):
            highest = jnp.maximum(highest, maxima[d][head])
        numerator = jnp.zeros((ROWS, HD), jnp.float32)
        denominator = jnp.zeros((ROWS, 1), jnp.float32)
        for d in range(4):
            factor = jnp.exp2(maxima[d][head] - highest)
            share = jnp.where(d <= home, parts[d][0:ROWS, at].astype(jnp.float32), 0.0)
            numerator = numerator + share * factor
            denominator = denominator + sums[d][head] * factor
        out[:, at] = (numerator / denominator).astype(jnp.bfloat16)
    index = lax.broadcasted_iota(jnp.int32, table.shape, 0).astype(jnp.float32)
    gate[...] = jnp.sum(jnp.where(index == noise, table[...], 0.0), axis=0, keepdims=True)


def combine(ids, table, parts):
    vmem = pl.BlockSpec(memory_space=pltpu.VMEM)
    return pl.pallas_call(
        combine_kernel,
        out_shape=[
            jax.ShapeDtypeStruct((ROWS, WIDTH), jnp.bfloat16),
            jax.ShapeDtypeStruct((1, table.shape[1]), jnp.float32),
        ],
        in_specs=[pl.BlockSpec(memory_space=pltpu.SMEM)] + [vmem] * 5,
        out_specs=[vmem] * 2,
        compiler_params=pltpu.CompilerParams(vmem_limit_bytes=SMALL_VMEM),
        name="combine",
    )(ids, table, *parts)


def project_kernel(far, ids, *refs):
    rows, own, fetched, swapped, out, held, sem = refs[0:4], refs[4], refs[5], refs[6], refs[7], refs[8], refs[9]
    mine = ids[2] == (1 if far else 0)

    @pl.when(mine)
    def _():
        pltpu.make_async_copy(fetched, held, sem).start()

    @pl.when(jnp.logical_not(mine))
    def _():
        pltpu.make_async_copy(swapped, held, sem).start()

    pltpu.make_async_copy(fetched, held, sem).wait()
    block = out.shape[1] // 3

    def columns(n, unused):
        at = pl.ds(pl.multiple_of(n * block, block), block)
        total = jnp.dot(rows[0][...], own[:, at], preferred_element_type=jnp.float32)
        for k in range(3):
            total = total + jnp.dot(
                rows[k + 1][...], held[k, :, at], preferred_element_type=jnp.float32
            )
        out[:, at] = total.astype(out.dtype)
        return 0

    lax.fori_loop(0, 3, columns, 0)


def project(far, ids, rows, own, fetched, swapped):
    vmem = pl.BlockSpec(memory_space=pltpu.VMEM)
    anywhere = pl.BlockSpec(memory_space=pl.ANY)
    part = own.shape[1]
    return pl.pallas_call(
        functools.partial(project_kernel, far),
        out_shape=jax.ShapeDtypeStruct((ROWS, part), jnp.bfloat16 if far else jnp.float32),
        in_specs=[pl.BlockSpec(memory_space=pltpu.SMEM)] + [vmem] * 5 + [anywhere] * 2,
        out_specs=vmem,
        scratch_shapes=[pltpu.VMEM((3, WIDTH, part), jnp.bfloat16), pltpu.SemaphoreType.DMA],
        compiler_params=pltpu.CompilerParams(vmem_limit_bytes=SMALL_VMEM),
        cost_estimate=pl.CostEstimate(
            flops=8 * ROWS * WIDTH * part, bytes_accessed=5000000, transcendentals=0
        ),
        name="project",
    )(ids, *rows, own, fetched, swapped)


def around(value, axis, steps):
    count = lax.axis_size(axis)
    return lax.ppermute(value, axis, [(i, (i + steps) % count) for i in range(count)])


def together(*values):
    return lax.optimization_barrier(values)


def per_device(hidden, queries, key_rows, values, out_weight, level_table, noise_level, group_live):
    z, y, core = lax.axis_index("z"), lax.axis_index("y"), lax.axis_index("c")
    w, x = lax.axis_index("w"), lax.axis_index("x")
    slot = z * 8 + y * 2 + core
    home = lax.rem(slot + 1, 32) // 8
    ids = jnp.stack([z, y, core, home]).astype(jnp.int32)

    def to_level(value, d):
        return lax.ppermute(value, "z", [(i, i - d) for i in range(d, 4)])

    part = out_weight.shape[1] // 8

    def columns(owner):
        return lax.dynamic_slice_in_dim(out_weight, owner * part, part, 1)

    block = jnp.where(core == 0, w, 1 - w) * 4

    def fetch(step):
        return around(columns(block + lax.rem(x + step, 4)), "x", step)

    pair = jnp.concatenate([key_rows, values], axis=1)
    next_one, next_three, below, above, piece_one, pair, queries, hidden, out_weight = together(
        to_level(queries, 1),
        to_level(queries, 3),
        around(pair, "y", 1),
        around(pair, "y", -1),
        fetch(1),
        pair,
        queries,
        hidden,
        out_weight,
    )
    next_two, across, pair_there, piece_two, below, above, hidden, out_weight = together(
        to_level(queries, 2),
        around(pair, "y", 2),
        around(pair, "c", 1),
        fetch(2),
        below,
        above,
        hidden,
        out_weight,
    )
    below_there, above_there, across_there, hidden, out_weight = together(
        around(below, "c", 1),
        around(above, "c", 1),
        around(across, "c", 1),
        hidden,
        out_weight,
    )
    pairs = [pair, below, above, across, pair_there, below_there, above_there, across_there]
    weight_near, weight_far = columns(w * 4 + x), columns((1 - w) * 4 + x)
    piece_three = fetch(3)
    hidden_next = around(hidden, SLOT, -1)

    def back(share, d):
        pairs_back = [
            (8 * (i - d) + j, (8 * i + j - 1) % 32) for i in range(d, 4) for j in range(8)
        ]
        return lax.ppermute(share, SLOT, pairs_back)

    shares = attend(
        ids, group_live, noise_level, [queries, next_one, next_two, next_three], pairs
    )
    *shares, hidden_next, piece_three, weight_near, weight_far = together(
        *shares, hidden_next, piece_three, weight_near, weight_far
    )
    fetched = jnp.stack([piece_one, piece_two, piece_three])
    swapped = around(fetched, "c", 1)
    returned = [back(shares[d], d) for d in range(4)]
    attended, gate_row = combine(ids, level_table, returned)

    rows = [attended] + [around(attended, "x", step) for step in (1, 2, 3)]
    far_sum = project(True, ids, rows, weight_far, fetched, swapped)
    arrived = around(far_sum, "w", 1)
    near_sum = project(False, ids, rows, weight_near, fetched, swapped)
    projected = near_sum + arrived.astype(jnp.float32)
    return (hidden_next.astype(jnp.float32) + gate_row * projected).astype(jnp.bfloat16)


def solution(mesh):
    fine = Mesh(np.asarray(mesh.devices).reshape(4, 4, 2, 2, 4), ("z", "y", "c", "w", "x"))
    tp = ("w", "x")
    block = P(SLOT, tp)
    in_specs = (block, block, block, block, P(tp, None), P(None, tp), P(SLOT), P())
    return jax.shard_map(
        per_device, mesh=fine, in_specs=in_specs, out_specs=block, check_vma=False
    )
```

profile of v0, /device:TPU:208, one launch (start us, length us, event | category | flops | bytes accessed | tf_op | source)
XLA Modules:
  0.0 172.4 jit_solution(6290146520431798849)
XLA Ops:
  0.0 1.1 constant_dynamic-update-slice_fusion.1
  1.1 1.0 constant_dynamic-update-slice_fusion.refs_4_
  2.1 0.5 collective-permute-start.3
  2.6 1.6 collective-permute-start.2
  4.2 1.9 %constant_dynamic-slice_fusion.4 = bf16[384,768]{1,0:T(8,128)(2,1)} fusion(bf16[384,6144]{1,0:T(8,128)(2,1)} %param.12, s32[]{:T(128)S(6)} %select_n.25), kind=kLoop, calls=%fused_computation.8 | loop fusion | bytes 1179652 | tf_op jit(solution)/shard_map/dynamic_slice | solution.py:345
  6.1 1.5 collective-permute-start.4
  7.6 3.4 %collective-permute-start = (bf16[448,384]{1,0:T(8,128)(2,1)S(1)}, bf16[448,384]{1,0:T(8,128)(2,1)S(1)}, u32[]{:S(2)}, u32[]{:S(2)}) collective-permute-start(bf16[448,384]{1,0:T(8,128)(2,1)S(1)} %copy-done.10), channel_id=1, source_target_pairs={{64,0},{128,64},{192,128},{65,1},{129,65},{193,129},{66,2},{130,66... | collective-permute-start | bytes 1032200 | tf_op jit(solution)/shard_map/ppermute | solution.py:340
  11.0 1.3 collective-permute-start.1
  12.3 12.5 %collective-permute-done.refs_1_ = bf16[448,384]{1,0:T(8,128)(2,1)S(1)} collective-permute-done((bf16[448,384]{1,0:T(8,128)(2,1)S(1)}, bf16[448,384]{1,0:T(8,128)(2,1)S(1)}, u32[]{:S(2)}, u32[]{:S(2)}) %collective-permute-start) | collective-permute-done | bytes 344096 | tf_op jit(solution)/shard_map/ppermute | solution.py:340
  24.8 0.7 copy-done.12
  25.5 0.7 copy-done.14
  26.4 1.7 collective-permute-start.6
  28.1 1.1 constant_dynamic-slice_fusion.3
  29.2 2.8 %collective-permute-start.8 = (bf16[384,768]{1,0:T(8,128)(2,1)S(1)}, bf16[384,768]{1,0:T(8,128)(2,1)S(1)}, u32[]{:S(2)}, u32[]{:S(2)}) collective-permute-start(bf16[384,768]{1,0:T(8,128)(2,1)S(1)} %constant_dynamic-slice_fusion.3), channel_id=1, source_target_pairs={{0,2},{1,3},{2,0},{3,1},{4,6},{5,7},{6,4},{7,5},{8,10},{9,11},{10,... | collective-permute-start | bytes 1769480 | tf_op jit(solution)/shard_map/ppermute | solution.py:325
  32.0 6.2 %collective-permute-start.5 = (bf16[448,384]{1,0:T(8,128)(2,1)}, bf16[448,384]{1,0:T(8,128)(2,1)S(1)}, u32[]{:S(2)}, u32[]{:S(2)}) collective-permute-start(bf16[448,384]{1,0:T(8,128)(2,1)} %refs_0_), channel_id=1, source_target_pairs={{128,0},{192,64},{129,1},{193,65},{130,2},{194,66},{131,3},{195,67... | collective-permute-start | bytes 1032200 | tf_op jit(solution)/shard_map/ppermute | solution.py:340
  38.2 13.2 %collective-permute-done.5.refs_2_ = bf16[448,384]{1,0:T(8,128)(2,1)S(1)} collective-permute-done((bf16[448,384]{1,0:T(8,128)(2,1)}, bf16[448,384]{1,0:T(8,128)(2,1)S(1)}, u32[]{:S(2)}, u32[]{:S(2)}) %collective-permute-start.5) | collective-permute-done | bytes 344096 | tf_op jit(solution)/shard_map/ppermute | solution.py:340
  51.4 0.7 copy-done.16
  52.3 0.7 copy-done.21
  53.0 0.5 collective-permute-start.11
  54.5 1.0 collective-permute-done.10.refs_10_
  55.5 1.0 collective-permute-done.11.refs_11_
  56.5 2.1 %collective-permute-start.12 = (bf16[448,768]{1,0:T(8,128)(2,1)}, bf16[448,768]{1,0:T(8,128)(2,1)S(1)}, u32[]{:S(2)}, u32[]{:S(2)}) collective-permute-start(bf16[448,768]{1,0:T(8,128)(2,1)} %param.8), channel_id=1, source_target_pairs={{0,248},{8,0},{16,8},{24,16},{32,24},{40,32},{48,40},{56,48},{64,5... | collective-permute-start | bytes 2064392 | tf_op jit(solution)/shard_map/ppermute | solution.py:325
  58.6 2.4 %constant_dynamic-slice_fusion = (bf16[384,768]{1,0:T(8,128)(2,1)S(1)}, bf16[384,768]{1,0:T(8,128)(2,1)}, bf16[384,768]{1,0:T(8,128)(2,1)S(1)}) fusion(bf16[384,6144]{1,0:T(8,128)(2,1)} %param.12, s32[]{:T(128)S(6)} %select_n.29, s32[]{:T(128)S(6)} %select_n.28, s32[]{:T(128)S(6)} %select_n.27), kind=kLoop, calls=%fused_computation.4 | loop fusion | bytes 3538956 | tf_op jit(solution)/shard_map/dynamic_slice | solution.py:345
  60.9 1.4 collective-permute-start.13
  62.4 7.5 %attend.1 = (bf16[480,384]{1,0:T(8,128)(2,1)S(1)}, bf16[480,384]{1,0:T(8,128)(2,1)S(1)}, bf16[480,384]{1,0:T(8,128)(2,1)S(1)}, bf16[480,384]{1,0:T(8,128)(2,1)S(1)}) custom-call(s32[4]{0:T(128)S(1)} %pad_add_fusion.ids, s32[32]{0:T(128)S(1)} %copy-done.18, s32[1]{0:T(128)S(6)} %copy.10.level, bf16[448,384]{1,0:T(8,128)(2,1)S(1)} %copy-done.11, ...), custom_call_target="tpu_custom_call" | custom-call | flops 19730006016 | bytes 8000000 | tf_op jit(solution)/shard_map/attend/pallas_call | solution.py:199
  69.9 4.7 %collective-permute-done.13 = bf16[384,768]{1,0:T(8,128)(2,1)S(1)} collective-permute-done((bf16[384,768]{1,0:T(8,128)(2,1)S(1)}, bf16[384,768]{1,0:T(8,128)(2,1)S(1)}, u32[]{:S(2)}, u32[]{:S(2)}) %collective-permute-start.13) | collective-permute-done | bytes 589856 | tf_op jit(solution)/shard_map/ppermute | solution.py:325
  74.6 1.5 pad_maximum_fusion.refs_5_
  76.3 2.5 %collective-permute-start.14 = (bf16[480,384]{1,0:T(8,128)(2,1)S(1)}, bf16[480,384]{1,0:T(8,128)(2,1)S(1)}, u32[]{:S(2)}, u32[]{:S(2)}) collective-permute-start(bf16[480,384]{1,0:T(8,128)(2,1)S(1)} %get-tuple-element.66), channel_id=1, source_target_pairs={{0,248},{8,0},{16,8},{24,16},{32,24},{40,32},{48,40},{56,48},{64,5... | collective-permute-start | bytes 1105928 | tf_op jit(solution)/shard_map/ppermute | solution.py:390
  78.7 1.3 collective-permute-start.15
  80.0 1.3 collective-permute-start.16
  81.3 1.3 collective-permute-start.17
  82.6 1.1 collective-permute-done.14.refs_0_
  83.7 16.2 %collective-permute-done.15.refs_1_ = bf16[480,384]{1,0:T(8,128)(2,1)S(1)} collective-permute-done((bf16[480,384]{1,0:T(8,128)(2,1)S(1)}, bf16[480,384]{1,0:T(8,128)(2,1)S(1)}, u32[]{:S(2)}, u32[]{:S(2)}) %collective-permute-start.15) | collective-permute-done | bytes 368672 | tf_op jit(solution)/shard_map/ppermute | solution.py:390
  100.0 26.4 %collective-permute-done.16.refs_2_ = bf16[480,384]{1,0:T(8,128)(2,1)S(1)} collective-permute-done((bf16[480,384]{1,0:T(8,128)(2,1)S(1)}, bf16[480,384]{1,0:T(8,128)(2,1)S(1)}, u32[]{:S(2)}, u32[]{:S(2)}) %collective-permute-start.16) | collective-permute-done | bytes 368672 | tf_op jit(solution)/shard_map/ppermute | solution.py:390
  126.4 2.3 %combine.1 = (bf16[448,384]{1,0:T(8,128)(2,1)S(1)}, f32[1,768]{1,0:T(1,128)S(1)}) custom-call(s32[4]{0:T(128)S(1)} %pad_add_fusion.ids, f32[64,768]{1,0:T(8,128)S(1)} %copy-done.9, bf16[480,384]{1,0:T(8,128)(2,1)S(1)} %collective-permute-done.14.refs_0_, bf16[480,384]{1,0:T(8,128)(2,1)S(1)} %collective-permute-done.15.refs_1_, ...), custom_call_target="tpu_custom_call" | custom-call | tf_op jit(solution)/shard_map/combine/pallas_call | solution.py:264
  128.9 2.6 %collective-permute-start.19 = (bf16[448,384]{1,0:T(8,128)(2,1)S(1)}, bf16[448,384]{1,0:T(8,128)(2,1)S(1)}, u32[]{:S(2)}, u32[]{:S(2)}) collective-permute-start(bf16[448,384]{1,0:T(8,128)(2,1)S(1)} %get-tuple-element.71.refs_0_), channel_id=1, source_target_pairs={{0,2},{1,3},{2,0},{3,1},{4,6},{5,7},{6,4},{7,5},{8,10},{9,11},{10,... | collective-permute-start | bytes 1032200 | tf_op jit(solution)/shard_map/ppermute | solution.py:325
  131.4 8.2 %collective-permute-done.20.refs_3_ = bf16[448,384]{1,0:T(8,128)(2,1)S(1)} collective-permute-done((bf16[448,384]{1,0:T(8,128)(2,1)S(1)}, bf16[448,384]{1,0:T(8,128)(2,1)S(1)}, u32[]{:S(2)}, u32[]{:S(2)}) %collective-permute-start.20) | collective-permute-done | bytes 344096 | tf_op jit(solution)/shard_map/ppermute | solution.py:325
  139.7 1.7 collective-permute-done.19.refs_2_
  141.4 7.3 %collective-permute-done.18.refs_1_ = bf16[448,384]{1,0:T(8,128)(2,1)S(1)} collective-permute-done((bf16[448,384]{1,0:T(8,128)(2,1)S(1)}, bf16[448,384]{1,0:T(8,128)(2,1)S(1)}, u32[]{:S(2)}, u32[]{:S(2)}) %collective-permute-start.18) | collective-permute-done | bytes 344096 | tf_op jit(solution)/shard_map/ppermute | solution.py:325
  148.7 3.7 %project.3 = bf16[448,768]{1,0:T(8,128)(2,1)} custom-call(s32[4]{0:T(128)S(1)} %pad_add_fusion.ids, bf16[448,384]{1,0:T(8,128)(2,1)S(1)} %get-tuple-element.71.refs_0_, bf16[448,384]{1,0:T(8,128)(2,1)S(1)} %collective-permute-done.18.refs_1_, bf16[448,384]{1,0:T(8,128)(2,1)S(1)} %collective-permute-done.19.refs_2_, ...), custom_call_target="tpu_custom_call" | custom-call | flops 1056964608 | bytes 5000000 | tf_op jit(solution)/shard_map/project/pallas_call | solution.py:309
  152.5 1.1 copy-done
  153.6 1.0 copy-done.2
  154.6 1.0 copy-done.4
  155.6 1.0 copy-done.6
  156.5 1.0 copy-done.8
  157.5 2.8 %project.2 = f32[448,768]{1,0:T(8,128)S(1)} custom-call(s32[4]{0:T(128)S(1)} %pad_add_fusion.ids, bf16[448,384]{1,0:T(8,128)(2,1)S(1)} %copy-done.2, bf16[448,384]{1,0:T(8,128)(2,1)S(1)} %copy-done.8, bf16[448,384]{1,0:T(8,128)(2,1)S(1)} %copy-done.6, bf16[448,384]{1,0:T(8,128)(2,1)S(1)} %copy-done.4, bf16[384,768]{1,0:T(8,128)(2,1)S(1)} %copy-done, ...), custom_call_target="tpu_custom_call" | custom-call | flops 1056964608 | bytes 5000000 | tf_op jit(solution)/shard_map/project/pallas_call | solution.py:309
  160.3 9.9 %collective-permute-done.22 = bf16[448,768]{1,0:T(8,128)(2,1)} collective-permute-done((bf16[448,768]{1,0:T(8,128)(2,1)}, bf16[448,768]{1,0:T(8,128)(2,1)}, u32[]{:S(2)}, u32[]{:S(2)}) %collective-permute-start.22) | collective-permute-done | bytes 688160 | tf_op jit(solution)/shard_map/ppermute | solution.py:325
  170.2 2.2 %add_convert_fusion = bf16[448,768]{1,0:T(8,128)(2,1)} fusion(f32[448,768]{1,0:T(8,128)S(1)} %project.2, bf16[448,768]{1,0:T(8,128)(2,1)} %collective-permute-done.22, bf16[448,768]{1,0:T(8,128)(2,1)S(1)} %copy-done.20, f32[768]{0:T(1024)S(1)} %reduce), kind=kLoop, calls=%fused_computation.1 | loop fusion | flops 2064384 | bytes 3443712 | tf_op jit(solution)/shard_map/convert_element_type | solution.py:408
  (57 shorter events, 1.0 us)
Async XLA Ops:
  0.0 7.6 %copy-start.10 = (bf16[448,384]{1,0:T(8,128)(2,1)S(1)}, bf16[448,384]{1,0:T(8,128)(2,1)}, u32[]{:S(2)}) copy-start(bf16[448,384]{1,0:T(8,128)(2,1)} %refs_0_) | copy-start | bytes 1032196
  2.1 24.2 %collective-permute-start.3 = (bf16[448,768]{1,0:T(8,128)(2,1)S(1)}, bf16[448,768]{1,0:T(8,128)(2,1)S(1)}, u32[]{:S(2)}, u32[]{:S(2)}) collective-permute-start(bf16[448,768]{1,0:T(8,128)(2,1)S(1)} %constant_dynamic-update-slice_fusion.refs_4_), channel_id=1, source_target_pairs={{0,48},{16,0},{32,16},{48,32},{1,49},{17,1},{33,17},{49,33},{2,50}... | collective-permute-start | bytes 2064392 | tf_op jit(solution)/shard_map/ppermute | solution.py:325
  2.6 23.6 %collective-permute-start.2 = (bf16[448,768]{1,0:T(8,128)(2,1)S(1)}, bf16[448,768]{1,0:T(8,128)(2,1)S(1)}, u32[]{:S(2)}, u32[]{:S(2)}) collective-permute-start(bf16[448,768]{1,0:T(8,128)(2,1)S(1)} %constant_dynamic-update-slice_fusion.refs_4_), channel_id=1, source_target_pairs={{0,16},{16,32},{32,48},{48,0},{1,17},{17,33},{33,49},{49,1},{2,18}... | collective-permute-start | bytes 2064392 | tf_op jit(solution)/shard_map/ppermute | solution.py:325
  6.1 20.1 %collective-permute-start.4 = (bf16[384,768]{1,0:T(8,128)(2,1)}, bf16[384,768]{1,0:T(8,128)(2,1)}, u32[]{:S(2)}, u32[]{:S(2)}) collective-permute-start(bf16[384,768]{1,0:T(8,128)(2,1)} %constant_dynamic-slice_fusion.4), channel_id=1, source_target_pairs={{0,1},{1,2},{2,3},{3,0},{4,5},{5,6},{6,7},{7,4},{8,9},{9,10},{10,1... | collective-permute-start | bytes 1769480 | tf_op jit(solution)/shard_map/ppermute | solution.py:325
  7.6 17.2 %collective-permute-start = (bf16[448,384]{1,0:T(8,128)(2,1)S(1)}, bf16[448,384]{1,0:T(8,128)(2,1)S(1)}, u32[]{:S(2)}, u32[]{:S(2)}) collective-permute-start(bf16[448,384]{1,0:T(8,128)(2,1)S(1)} %copy-done.10), channel_id=1, source_target_pairs={{64,0},{128,64},{192,128},{65,1},{129,65},{193,129},{66,2},{130,66... | collective-permute-start | bytes 1032200 | tf_op jit(solution)/shard_map/ppermute | solution.py:340
  11.0 14.5 %collective-permute-start.1 = (bf16[448,384]{1,0:T(8,128)(2,1)S(1)}, bf16[448,384]{1,0:T(8,128)(2,1)S(1)}, u32[]{:S(2)}, u32[]{:S(2)}) collective-permute-start(bf16[448,384]{1,0:T(8,128)(2,1)S(1)} %copy-done.10), channel_id=1, source_target_pairs={{192,0},{193,1},{194,2},{195,3},{196,4},{197,5},{198,6},{199,7},{2... | collective-permute-start | bytes 1032200 | tf_op jit(solution)/shard_map/ppermute | solution.py:340
  24.8 0.7 copy-start.12
  25.5 0.7 copy-start.14
  26.3 25.9 %collective-permute-start.7 = (bf16[448,768]{1,0:T(8,128)(2,1)S(1)}, bf16[448,768]{1,0:T(8,128)(2,1)S(1)}, u32[]{:S(2)}, u32[]{:S(2)}) collective-permute-start(bf16[448,768]{1,0:T(8,128)(2,1)S(1)} %constant_dynamic-update-slice_fusion.refs_4_), channel_id=1, source_target_pairs={{0,8},{8,0},{1,9},{9,1},{2,10},{10,2},{3,11},{11,3},{4,12},{12,4},... | collective-permute-start | bytes 2064392 | tf_op jit(solution)/shard_map/ppermute | solution.py:325
  26.4 25.8 %collective-permute-start.6 = (bf16[448,768]{1,0:T(8,128)(2,1)S(1)}, bf16[448,768]{1,0:T(8,128)(2,1)S(1)}, u32[]{:S(2)}, u32[]{:S(2)}) collective-permute-start(bf16[448,768]{1,0:T(8,128)(2,1)S(1)} %constant_dynamic-update-slice_fusion.refs_4_), channel_id=1, source_target_pairs={{0,32},{16,48},{32,0},{48,16},{1,33},{17,49},{33,1},{49,17},{2,34}... | collective-permute-start | bytes 2064392 | tf_op jit(solution)/shard_map/ppermute | solution.py:325
  29.2 23.0 %collective-permute-start.8 = (bf16[384,768]{1,0:T(8,128)(2,1)S(1)}, bf16[384,768]{1,0:T(8,128)(2,1)S(1)}, u32[]{:S(2)}, u32[]{:S(2)}) collective-permute-start(bf16[384,768]{1,0:T(8,128)(2,1)S(1)} %constant_dynamic-slice_fusion.3), channel_id=1, source_target_pairs={{0,2},{1,3},{2,0},{3,1},{4,6},{5,7},{6,4},{7,5},{8,10},{9,11},{10,... | collective-permute-start | bytes 1769480 | tf_op jit(solution)/shard_map/ppermute | solution.py:325
  32.0 19.4 %collective-permute-start.5 = (bf16[448,384]{1,0:T(8,128)(2,1)}, bf16[448,384]{1,0:T(8,128)(2,1)S(1)}, u32[]{:S(2)}, u32[]{:S(2)}) collective-permute-start(bf16[448,384]{1,0:T(8,128)(2,1)} %refs_0_), channel_id=1, source_target_pairs={{128,0},{192,64},{129,1},{193,65},{130,2},{194,66},{131,3},{195,67... | collective-permute-start | bytes 1032200 | tf_op jit(solution)/shard_map/ppermute | solution.py:340
  51.4 0.7 copy-start.16
  52.2 0.8 copy-start.21
  52.2 2.4 %collective-permute-start.9 = (bf16[448,768]{1,0:T(8,128)(2,1)S(1)}, bf16[448,768]{1,0:T(8,128)(2,1)}, u32[]{:S(2)}, u32[]{:S(2)}) collective-permute-start(bf16[448,768]{1,0:T(8,128)(2,1)S(1)} %collective-permute-done.2.refs_5_), channel_id=1, source_target_pairs={{0,8},{8,0},{1,9},{9,1},{2,10},{10,2},{3,11},{11,3},{4,12},{12,4},... | collective-permute-start | bytes 2064392 | tf_op jit(solution)/shard_map/ppermute | solution.py:325
  53.0 2.5 %collective-permute-start.10 = (bf16[448,768]{1,0:T(8,128)(2,1)S(1)}, bf16[448,768]{1,0:T(8,128)(2,1)}, u32[]{:S(2)}, u32[]{:S(2)}) collective-permute-start(bf16[448,768]{1,0:T(8,128)(2,1)S(1)} %collective-permute-done.3.refs_6_), channel_id=1, source_target_pairs={{0,8},{8,0},{1,9},{9,1},{2,10},{10,2},{3,11},{11,3},{4,12},{12,4},... | collective-permute-start | bytes 2064392 | tf_op jit(solution)/shard_map/ppermute | solution.py:325
  53.0 3.5 %collective-permute-start.11 = (bf16[448,768]{1,0:T(8,128)(2,1)S(1)}, bf16[448,768]{1,0:T(8,128)(2,1)}, u32[]{:S(2)}, u32[]{:S(2)}) collective-permute-start(bf16[448,768]{1,0:T(8,128)(2,1)S(1)} %collective-permute-done.6.refs_7_), channel_id=1, source_target_pairs={{0,8},{8,0},{1,9},{9,1},{2,10},{10,2},{3,11},{11,3},{4,12},{12,4},... | collective-permute-start | bytes 2064392 | tf_op jit(solution)/shard_map/ppermute | solution.py:325
  54.2 8.2 %copy-start.11 = (bf16[448,384]{1,0:T(8,128)(2,1)S(1)}, bf16[448,384]{1,0:T(8,128)(2,1)}, u32[]{:S(2)}) copy-start(bf16[448,384]{1,0:T(8,128)(2,1)} %refs_0_) | copy-start | bytes 1032196
  54.2 8.2 %copy-start.13 = (bf16[448,384]{1,0:T(8,128)(2,1)S(1)}, bf16[448,384]{1,0:T(8,128)(2,1)}, u32[]{:S(2)}) copy-start(bf16[448,384]{1,0:T(8,128)(2,1)} %copy-done.12) | copy-start | bytes 1032196
  54.2 8.2 %copy-start.15 = (bf16[448,384]{1,0:T(8,128)(2,1)S(1)}, bf16[448,384]{1,0:T(8,128)(2,1)}, u32[]{:S(2)}) copy-start(bf16[448,384]{1,0:T(8,128)(2,1)} %copy-done.14) | copy-start | bytes 1032196
  54.2 8.2 %copy-start.17 = (bf16[448,384]{1,0:T(8,128)(2,1)S(1)}, bf16[448,384]{1,0:T(8,128)(2,1)}, u32[]{:S(2)}) copy-start(bf16[448,384]{1,0:T(8,128)(2,1)} %copy-done.16) | copy-start | bytes 1032196
  54.2 8.2 %copy-start.18 = (s32[32]{0:T(128)S(1)}, s32[32]{0:T(128)}, u32[]{:S(2)}) copy-start(s32[32]{0:T(128)} %live.1) | copy-start | bytes 388
  56.5 18.1 %collective-permute-start.12 = (bf16[448,768]{1,0:T(8,128)(2,1)}, bf16[448,768]{1,0:T(8,128)(2,1)S(1)}, u32[]{:S(2)}, u32[]{:S(2)}) collective-permute-start(bf16[448,768]{1,0:T(8,128)(2,1)} %param.8), channel_id=1, source_target_pairs={{0,248},{8,0},{16,8},{24,16},{32,24},{40,32},{48,40},{56,48},{64,5... | collective-permute-start | bytes 2064392 | tf_op jit(solution)/shard_map/ppermute | solution.py:325
  60.9 13.7 %copy-start.22 = (bf16[384,768]{1,0:T(8,128)(2,1)S(1)}, bf16[384,768]{1,0:T(8,128)(2,1)}, u32[]{:S(2)}) copy-start(bf16[384,768]{1,0:T(8,128)(2,1)} %copy-done.21) | copy-start | bytes 1769476
  60.9 13.7 %collective-permute-start.13 = (bf16[384,768]{1,0:T(8,128)(2,1)S(1)}, bf16[384,768]{1,0:T(8,128)(2,1)S(1)}, u32[]{:S(2)}, u32[]{:S(2)}) collective-permute-start(bf16[384,768]{1,0:T(8,128)(2,1)S(1)} %get-tuple-element.79), channel_id=1, source_target_pairs={{0,3},{1,0},{2,1},{3,2},{4,7},{5,4},{6,5},{7,6},{8,11},{9,8},{10,9... | collective-permute-start | bytes 1769480 | tf_op jit(solution)/shard_map/ppermute | solution.py:325
  74.6 1.6 copy-start.19
  74.6 51.8 %copy-start.9 = (f32[64,768]{1,0:T(8,128)S(1)}, f32[64,768]{1,0:T(8,128)}, u32[]{:S(2)}) copy-start(f32[64,768]{1,0:T(8,128)} %table.1) | copy-start | bytes 589828
  76.2 72.5 %collective-permute-start.21 = (bf16[3,384,768]{2,1,0:T(8,128)(2,1)S(1)}, bf16[3,384,768]{2,1,0:T(8,128)(2,1)S(1)}, u32[]{:S(2)}, u32[]{:S(2)}) collective-permute-start(bf16[3,384,768]{2,1,0:T(8,128)(2,1)S(1)} %pad_maximum_fusion.refs_5_), channel_id=1, source_target_pairs={{0,8},{8,0},{1,9},{9,1},{2,10},{10,2},{3,11},{11,3},{4,12},{12,4},... | collective-permute-start | bytes 5308424 | tf_op jit(solution)/shard_map/ppermute | solution.py:325
  76.3 7.5 %collective-permute-start.14 = (bf16[480,384]{1,0:T(8,128)(2,1)S(1)}, bf16[480,384]{1,0:T(8,128)(2,1)S(1)}, u32[]{:S(2)}, u32[]{:S(2)}) collective-permute-start(bf16[480,384]{1,0:T(8,128)(2,1)S(1)} %get-tuple-element.66), channel_id=1, source_target_pairs={{0,248},{8,0},{16,8},{24,16},{32,24},{40,32},{48,40},{56,48},{64,5... | collective-permute-start | bytes 1105928 | tf_op jit(solution)/shard_map/ppermute | solution.py:390
  78.7 21.3 %collective-permute-start.15 = (bf16[480,384]{1,0:T(8,128)(2,1)S(1)}, bf16[480,384]{1,0:T(8,128)(2,1)S(1)}, u32[]{:S(2)}, u32[]{:S(2)}) collective-permute-start(bf16[480,384]{1,0:T(8,128)(2,1)S(1)} %get-tuple-element.67), channel_id=1, source_target_pairs={{0,56},{8,64},{16,72},{24,80},{32,88},{40,96},{48,104},{56,112},{6... | collective-permute-start | bytes 1105928 | tf_op jit(solution)/shard_map/ppermute | solution.py:390
  80.0 46.4 %collective-permute-start.16 = (bf16[480,384]{1,0:T(8,128)(2,1)S(1)}, bf16[480,384]{1,0:T(8,128)(2,1)S(1)}, u32[]{:S(2)}, u32[]{:S(2)}) collective-permute-start(bf16[480,384]{1,0:T(8,128)(2,1)S(1)} %get-tuple-element.68), channel_id=1, source_target_pairs={{0,120},{8,128},{16,136},{24,144},{32,152},{40,160},{48,168},{56,1... | collective-permute-start | bytes 1105928 | tf_op jit(solution)/shard_map/ppermute | solution.py:390
  81.3 45.1 %collective-permute-start.17 = (bf16[480,384]{1,0:T(8,128)(2,1)S(1)}, bf16[480,384]{1,0:T(8,128)(2,1)S(1)}, u32[]{:S(2)}, u32[]{:S(2)}) collective-permute-start(bf16[480,384]{1,0:T(8,128)(2,1)S(1)} %get-tuple-element.69), channel_id=1, source_target_pairs={{0,184},{8,192},{16,200},{24,208},{32,216},{40,224},{48,232},{56,2... | collective-permute-start | bytes 1105928 | tf_op jit(solution)/shard_map/ppermute | solution.py:390
  128.7 23.7 %copy-start.1 = (bf16[448,384]{1,0:T(8,128)(2,1)}, bf16[448,384]{1,0:T(8,128)(2,1)S(1)}, u32[]{:S(2)}) copy-start(bf16[448,384]{1,0:T(8,128)(2,1)S(1)} %get-tuple-element.71.refs_0_) | copy-start | bytes 1032196
  128.7 11.0 %collective-permute-start.20 = (bf16[448,384]{1,0:T(8,128)(2,1)S(1)}, bf16[448,384]{1,0:T(8,128)(2,1)S(1)}, u32[]{:S(2)}, u32[]{:S(2)}) collective-permute-start(bf16[448,384]{1,0:T(8,128)(2,1)S(1)} %get-tuple-element.71.refs_0_), channel_id=1, source_target_pairs={{0,3},{1,0},{2,1},{3,2},{4,7},{5,4},{6,5},{7,6},{8,11},{9,8},{10,9... | collective-permute-start | bytes 1032200 | tf_op jit(solution)/shard_map/ppermute | solution.py:325
  128.9 12.5 %collective-permute-start.19 = (bf16[448,384]{1,0:T(8,128)(2,1)S(1)}, bf16[448,384]{1,0:T(8,128)(2,1)S(1)}, u32[]{:S(2)}, u32[]{:S(2)}) collective-permute-start(bf16[448,384]{1,0:T(8,128)(2,1)S(1)} %get-tuple-element.71.refs_0_), channel_id=1, source_target_pairs={{0,2},{1,3},{2,0},{3,1},{4,6},{5,7},{6,4},{7,5},{8,10},{9,11},{10,... | collective-permute-start | bytes 1032200 | tf_op jit(solution)/shard_map/ppermute | solution.py:325
  131.4 17.3 %collective-permute-start.18 = (bf16[448,384]{1,0:T(8,128)(2,1)S(1)}, bf16[448,384]{1,0:T(8,128)(2,1)S(1)}, u32[]{:S(2)}, u32[]{:S(2)}) collective-permute-start(bf16[448,384]{1,0:T(8,128)(2,1)S(1)} %get-tuple-element.71.refs_0_), channel_id=1, source_target_pairs={{0,1},{1,2},{2,3},{3,0},{4,5},{5,6},{6,7},{7,4},{8,9},{9,10},{10,1... | collective-permute-start | bytes 1032200 | tf_op jit(solution)/shard_map/ppermute | solution.py:325
  139.7 12.7 %copy-start.3 = (bf16[448,384]{1,0:T(8,128)(2,1)}, bf16[448,384]{1,0:T(8,128)(2,1)S(1)}, u32[]{:S(2)}) copy-start(bf16[448,384]{1,0:T(8,128)(2,1)S(1)} %collective-permute-done.20.refs_3_) | copy-start | bytes 1032196
  141.4 11.0 %copy-start.5 = (bf16[448,384]{1,0:T(8,128)(2,1)}, bf16[448,384]{1,0:T(8,128)(2,1)S(1)}, u32[]{:S(2)}) copy-start(bf16[448,384]{1,0:T(8,128)(2,1)S(1)} %collective-permute-done.19.refs_2_) | copy-start | bytes 1032196
  148.7 3.7 %copy-start.7 = (bf16[448,384]{1,0:T(8,128)(2,1)}, bf16[448,384]{1,0:T(8,128)(2,1)S(1)}, u32[]{:S(2)}) copy-start(bf16[448,384]{1,0:T(8,128)(2,1)S(1)} %collective-permute-done.18.refs_1_) | copy-start | bytes 1032196
  152.4 17.8 %collective-permute-start.22 = (bf16[448,768]{1,0:T(8,128)(2,1)}, bf16[448,768]{1,0:T(8,128)(2,1)}, u32[]{:S(2)}, u32[]{:S(2)}) collective-permute-start(bf16[448,768]{1,0:T(8,128)(2,1)} %project.3), channel_id=1, source_target_pairs={{0,4},{4,0},{1,5},{5,1},{2,6},{6,2},{3,7},{7,3},{8,12},{12,8},{9,1... | collective-permute-start | bytes 2064392 | tf_op jit(solution)/shard_map/ppermute | solution.py:325
  152.5 1.1 copy-start
  153.6 1.0 copy-start.2
  154.6 1.0 copy-start.4
  155.5 1.0 copy-start.6
  156.5 1.0 copy-start.8
  157.5 12.7 %copy-start.20 = (bf16[448,768]{1,0:T(8,128)(2,1)S(1)}, bf16[448,768]{1,0:T(8,128)(2,1)}, u32[]{:S(2)}) copy-start(bf16[448,768]{1,0:T(8,128)(2,1)} %copy-done.19) | copy-start | bytes 2064388
where the time goes:
time: 175 us; the launch traced here: 172 us
  waiting for transfers between devices  104 us (59%)
  starting transfers between devices  32.5 us (19%)
  Pallas kernels  16.2 us (9%)
  local copies, waits for them, and re-layouts  15.4 us (9%)
  other arithmetic  3.85 us (2%)
    ppermute x4, waiting for transfers between devices, back(): return lax.ppermute(share, SLOT, pairs_back)  43.8 us
    ppermute x16, waiting for transfers between devices, around(): lax.ppermute(value, axis, [(i, (i + steps) % count) for i in range(count)])  34.1 us
    ppermute x3, waiting for transfers between devices, to_level(): return lax.ppermute(value, 'z', [(i, i - d) for i in range(d, 4)])  25.7 us
    ppermute x16, starting transfers between devices, around(): lax.ppermute(value, axis, [(i, (i + steps) % count) for i in range(count)])  15.3 us
    ppermute x3, starting transfers between devices, to_level(): return lax.ppermute(value, 'z', [(i, i - d) for i in range(d, 4)])  10.9 us
    unnamed x47, local copies, waits for them, and re-layouts  8.97 us
    pallas_call x1, Pallas kernels, attend(): pl.pallas_call(attend_kernel, out_shape=[jax.ShapeDtypeStruct((ROWS + STA...  7.51 us
    pallas_call x2, Pallas kernels, project(): pl.pallas_call(functools.partial(project_kernel, far), out_shape=jax.Shap...  6.46 us
  transfers between devices with their start and end apart: 23, of which 13 were waited for; matrix products, arithmetic and copies ran while one was open for 3% of the time, Pallas kernels for 7%

commit v1 on v0

--- a/solution.py
+++ b/solution.py
@@ -29,93 +29,180 @@
     )
 
 
-def attend_kernel(ids, live, level, *refs):
-    query_in, pair_in, out = refs[0:4], refs[4:12], refs[12:16]
-    raw, scaled, pairs, held, acc, top, done, raw_sem, pair_sem, out_sem = refs[16:]
+CALLS = {"early": (1, 3, 0), "middle": (2, 1), "late": (3, 0)}
+EARLY, LATER = (0, 1, 2, 4), (3, 5, 6, 7)
+
+
+def attend_kernel(call, ids, live, level, *refs):
+    steps = CALLS[call]
+    many = len(steps)
+    early, middle = call == "early", call == "middle"
+    members = EARLY if early else EARLY + LATER if middle else LATER
+    resumed = () if early else (1,) if middle else (0, 1)
+    kept = many if early else len(resumed)
+    refs = list(refs)
+
+    def take(count):
+        taken = refs[:count]
+        del refs[:count]
+        return taken
+
+    query_in, pair_in = take(many), take(len(members))
+    state_in = [] if early else take(2 * kept)
+    out = take(2 * many if early else many)
+    raw, scaled, pairs, held, acc, top, done, raw_sem, pair_sem, state_sem, out_sem = refs
     here, y, core = ids[0], ids[1], ids[2]
     first = here * 8
     mine = first + y * 2 + core
-    groups = []
-    for other in (0, 1):
-        for step in Y_STEPS:
-            core_there = core if other == 0 else 1 - core
-            groups.append(first + lax.rem(y + step + 4, 4) * 2 + core_there)
-    alive = [live[first + k] for k in range(8)]
-
-    def live_before(group):
+    groups = {}
+    for p in members:
+        core_there = core if p < 4 else 1 - core
+        groups[p] = first + lax.rem(y + Y_STEPS[p % 4] + 4, 4) * 2 + core_there
+
+    def live_before(group, part):
         count = jnp.int32(0)
+        for p in part:
+            if p in groups:
+                count = count + jnp.where(groups[p] < group, live[groups[p]], 0)
+        return count
+
+    everything = first + 8
+    n_early, n_later = live_before(everything, EARLY), live_before(everything, LATER)
+    n_own = live_before(mine, EARLY if early else LATER)
+    own_place = jnp.where(live[mine] == 1, n_own, n_early)
+
+    def raw_copy(i):
+        return pltpu.make_async_copy(query_in[i], raw.at[i], raw_sem.at[i])
+
+    def place_copy(j, place):
+        at = pl.ds(pl.multiple_of(place * ROWS, 64), ROWS)
+        return pltpu.make_async_copy(pair_in[j], pairs.at[at], pair_sem.at[place])
+
+    def state_copies(k):
+        i = resumed[k]
+        return (
+            pltpu.make_async_copy(state_in[2 * k], acc.at[i], state_sem.at[2 * k]),
+            pltpu.make_async_copy(state_in[2 * k + 1], top.at[i], state_sem.at[2 * k + 1]),
+        )
+
+    def out_copies(i):
+        if early:
+            return (
+                pltpu.make_async_copy(acc.at[i], out[2 * i], out_sem.at[2 * i]),
+                pltpu.make_async_copy(top.at[i], out[2 * i + 1], out_sem.at[2 * i + 1]),
+            )
+        return (pltpu.make_async_copy(done.at[i], out[i], out_sem.at[i]),)
+
+    def active(i):
+        return here + steps[i] <= 3
+
+    def step_of(i):
+        step = jnp.int32(steps[-1])
+        for k in range(many - 1):
+            step = jnp.where(i == k, steps[k], step)
+        return step
+
+    def run():
+        for j, p in enumerate(members):
+            part = EARLY if p in EARLY else LATER
+            base = 0 if p in EARLY else 4
+            if early and p == 0:
+                place_copy(j, own_place).start()
+            else:
+
+                @pl.when(live[groups[p]] == 1)
+                def _():
+                    place_copy(j, base + live_before(groups[p], part)).start()
+
+        for i in range(many):
+
+            @pl.when(active(i))
+            def _():
+                raw_copy(i).start()
+
+        for k in range(len(resumed)):
+
+            @pl.when(active(resumed[k]))
+            def _():
+                for copy in state_copies(k):
+                    copy.start()
+
+        if early:
+            place_copy(0, own_place).wait()
         for k in range(8):
-            count = count + jnp.where(first + k < group, alive[k], 0)
-        return count
-
-    n_all, n_own = live_before(first + 8), live_before(mine)
-    last = here == 3
-    own_place = jnp.where((live[mine] == 1) | last, n_own, n_all)
-
-    def raw_copy(d):
-        return pltpu.make_async_copy(query_in[d], raw.at[d], raw_sem.at[d])
-
-    def place_copy(p, place):
-        at = pl.ds(pl.multiple_of(place * ROWS, 64), ROWS)
-        return pltpu.make_async_copy(pair_in[p], pairs.at[at], pair_sem.at[place])
-
-    def wait_place(place):
-        place_copy(0, place).wait()
-
-    raw_copy(0).start()
-    place_copy(0, own_place).start()
-    for p in range(1, 8):
-
-        @pl.when((live[groups[p]] == 1) & ((groups[p] < mine) | jnp.logical_not(last)))
-        def _():
-            place_copy(p, live_before(groups[p])).start()
-
-    for d in range(1, 4):
-
-        @pl.when(here + d <= 3)
-        def _():
-            raw_copy(d).start()
-
-    raw_copy(0).wait()
-    wait_place(own_place)
-    for k in range(8):
-
-        @pl.when(k < n_own)
-        def _():
-            wait_place(k)
-
-    def source(d, unused):
-        @pl.when(d == 1)
-        def _():
-            for k in range(8):
-
-                @pl.when((k >= n_own) & (k < n_all) & (k != own_place))
-                def _():
-                    wait_place(k)
-
-            for e in range(1, 4):
-
-                @pl.when(here + e <= 3)
-                def _():
-                    raw_copy(e).wait()
-
-        count = jnp.where(d == 0, n_own + 1, n_all)
+            if k < 4 and call != "late":
+                there = k < n_early
+                if early:
+                    there = there & (k != own_place)
+            elif k >= 4 and not early:
+                there = k - 4 < n_later
+            else:
+                continue
+
+            @pl.when(there)
+            def _():
+                place_copy(0, k).wait()
+
+        for i in range(many):
+
+            @pl.when(active(i))
+            def _():
+                raw_copy(i).wait()
+
+        for k in range(len(resumed)):
+
+            @pl.when(active(resumed[k]))
+            def _():
+                for copy in state_copies(k):
+                    copy.wait()
+
+        def one(i, unused):
+            @pl.when(here + step_of(i) <= 3)
+            def _():
+                source(i)
+
+            return 0
+
+        lax.fori_loop(0, many, one, 0)
+        for i in range(many):
+
+            @pl.when(active(i))
+            def _():
+                for copy in out_copies(i):
+                    copy.wait()
+
+    def source(i):
+        own = step_of(i) == 0
+        if early:
+            count = jnp.where(own, n_own + 1, n_early)
+            split, base = jnp.where(own, n_own, n_early), own_place
+        elif middle:
+            count = jnp.where(i == 0, n_early + n_later, n_later)
+            split, base = jnp.where(i == 0, n_early, 0), 4
+        else:
+            count = jnp.where(own, n_own, n_later)
+            split, base = jnp.int32(0), 4
         chunks = (count + 1) // 2
 
-        def place(i):
-            i = jnp.maximum(jnp.minimum(i, count - 1), 0)
-            return jnp.where((d == 0) & (i == n_own), own_place, i)
-
-        def at(i):
-            return pl.ds(pl.multiple_of(place(i) * ROWS, 64), ROWS)
+        def at(k):
+            k = jnp.maximum(jnp.minimum(k, count - 1), 0)
+            place = jnp.where(k < split, k, base + k - split)
+            return pl.ds(pl.multiple_of(place * ROWS, 64), ROWS)
 
         for head in range(HEADS_HERE):
-            exact = raw[d, :, head * HD : (head + 1) * HD].astype(jnp.float32) * EXP2_SCALE
+            exact = raw[i, :, head * HD : (head + 1) * HD].astype(jnp.float32) * EXP2_SCALE
             high = exact.astype(jnp.bfloat16)
             scaled[head, :, :HD] = high
             scaled[head, :, HD:] = (exact - high.astype(jnp.float32)).astype(jnp.bfloat16)
-        top[...] = jnp.full(top.shape, LOWEST, jnp.float32)
-        acc[...] = jnp.zeros(acc.shape, jnp.float32)
+
+        def fresh():
+            top[i] = jnp.full(top.shape[1:], LOWEST, jnp.float32)
+            acc[i] = jnp.zeros(acc.shape[1:], jnp.float32)
+
+        if early:
+            fresh()
+        elif middle:
+            pl.when(i == 0)(fresh)
 
         def scores_of(t, head):
             cols = slice(head * HD, (head + 1) * HD)
@@ -123,7 +210,7 @@
             return score(scaled[head], jnp.concatenate([key, key], axis=1))
 
         def absorb(t, head, scores):
-            old = top[head]
+            old = top[i, head]
             new = jnp.maximum(old, jnp.max(scores, axis=1, keepdims=True))
             weights = jnp.exp2(scores - jnp.concatenate([new] * (2 * ROWS // HD), axis=1))
             cols = slice(WIDTH + head * HD, WIDTH + (head + 1) * HD)
@@ -140,12 +227,14 @@
                 weights.astype(jnp.bfloat16), value, preferred_element_type=jnp.float32
             )
             shrink = jnp.exp2(old - new)
-            acc[head] = acc[head] * jnp.concatenate([shrink, shrink], axis=1) + weighted
-            top[head] = new
-
-        held[...] = scores_of(0, 0)
-
-        def chunk(t, unused_too):
+            acc[i, head] = acc[i, head] * jnp.concatenate([shrink, shrink], axis=1) + weighted
+            top[i, head] = new
+
+        @pl.when(chunks > 0)
+        def _():
+            held[...] = scores_of(0, 0)
+
+        def chunk(t, unused):
             scores = held[...]
             following = scores_of(t, 1)
             absorb(t, 0, scores)
@@ -156,15 +245,24 @@
             return 0
 
         lax.fori_loop(0, chunks, chunk, 0)
-
+        if not early:
+            finish(i)
+        for k in range(many):
+
+            @pl.when(i == k)
+            def _():
+                for copy in out_copies(k):
+                    copy.start()
+
+    def finish(i):
         lane = lax.broadcasted_iota(jnp.int32, (ROWS, HD), 1)
         stats = jnp.where(lane == 3 * HEADS_HERE, level[0].astype(jnp.float32), 0.0)
         for head in range(HEADS_HERE):
-            exact = top[head]
+            exact = top[i, head]
             sent = exact.astype(jnp.bfloat16).astype(jnp.float32)
             factor = jnp.exp2(exact - sent)
-            both = acc[head]
-            done[d, 0:ROWS, head * HD : (head + 1) * HD] = (both[:, :HD] * factor).astype(
+            both = acc[i, head]
+            done[i, 0:ROWS, head * HD : (head + 1) * HD] = (both[:, :HD] * factor).astype(
                 jnp.bfloat16
             )
             total = both[:, HD:] * factor
@@ -173,52 +271,53 @@
             stats = jnp.where(lane == HEADS_HERE + head, high, stats)
             stats = jnp.where(lane == 2 * HEADS_HERE + head, total - high, stats)
         flat = jnp.transpose(stats)[:16].astype(jnp.bfloat16)
-        done[d, ROWS : ROWS + 16, :] = flat[:, :WIDTH]
+        done[i, ROWS : ROWS + 16, :] = flat[:, :WIDTH]
         pad = jnp.zeros((16, 2 * WIDTH - ROWS), jnp.bfloat16)
-        done[d, ROWS + 16 : ROWS + 32, :] = jnp.concatenate([flat[:, WIDTH:], pad], axis=1)
-        for k in range(4):
-
-            @pl.when(d == k)
-            def _():
-                pltpu.make_async_copy(done.at[k], out[k], out_sem.at[k]).start()
-
-        return 0
-
-    lax.fori_loop(0, 4 - here, source, 0)
-    for k in range(4):
-
-        @pl.when(here + k <= 3)
-        def _():
-            pltpu.make_async_copy(done.at[k], out[k], out_sem.at[k]).wait()
-
-
-def attend(ids, live, level, queries, pairs):
+        done[i, ROWS + 16 : ROWS + 32, :] = jnp.concatenate([flat[:, WIDTH:], pad], axis=1)
+
+    if middle:
+        pl.when(active(1))(run)
+    else:
+        run()
+
+
+def attend(call, ids, live, level, queries, pairs, states=()):
     smem = pl.BlockSpec(memory_space=pltpu.SMEM)
     anywhere = pl.BlockSpec(memory_space=pl.ANY)
     bf16, f32 = jnp.bfloat16, jnp.float32
+    many = len(CALLS[call])
+    early = call == "early"
+    members = EARLY if early else EARLY + LATER if call == "middle" else LATER
+    state = [(HEADS_HERE, ROWS, 2 * HD), (HEADS_HERE, ROWS, HD)]
+    if early:
+        out_shape = [jax.ShapeDtypeStruct(shape, f32) for shape in state * many]
+    else:
+        out_shape = [jax.ShapeDtypeStruct((ROWS + STAT, WIDTH), bf16)] * many
+    operands = [*queries, *[pairs[p] for p in members], *states]
     return pl.pallas_call(
-        attend_kernel,
-        out_shape=[jax.ShapeDtypeStruct((ROWS + STAT, WIDTH), bf16)] * 4,
-        in_specs=[smem] * 3 + [anywhere] * 12,
-        out_specs=[anywhere] * 4,
+        functools.partial(attend_kernel, call),
+        out_shape=out_shape,
+        in_specs=[smem] * 3 + [anywhere] * len(operands),
+        out_specs=[anywhere] * len(out_shape),
         scratch_shapes=[
-            pltpu.VMEM((4, ROWS, WIDTH), bf16),
+            pltpu.VMEM((many, ROWS, WIDTH), bf16),
             pltpu.VMEM((HEADS_HERE, ROWS, 2 * HD), bf16),
             pltpu.VMEM((8 * ROWS, 2 * WIDTH), bf16),
             pltpu.VMEM((ROWS, 2 * ROWS), f32),
-            pltpu.VMEM((HEADS_HERE, ROWS, 2 * HD), f32),
-            pltpu.VMEM((HEADS_HERE, ROWS, HD), f32),
-            pltpu.VMEM((4, ROWS + STAT, WIDTH), bf16),
-            pltpu.SemaphoreType.DMA((4,)),
+            pltpu.VMEM((many, *state[0]), f32),
+            pltpu.VMEM((many, *state[1]), f32),
+            pltpu.VMEM((many, ROWS + STAT, WIDTH), bf16),
+            pltpu.SemaphoreType.DMA((many,)),
             pltpu.SemaphoreType.DMA((8,)),
             pltpu.SemaphoreType.DMA((4,)),
+            pltpu.SemaphoreType.DMA((2 * many,)),
         ],
         compiler_params=pltpu.CompilerParams(vmem_limit_bytes=ATTEND_VMEM),
         cost_estimate=pl.CostEstimate(
-            flops=32 * HEADS_HERE * ROWS * ROWS * HD * 8, bytes_accessed=8000000, transcendentals=0
+            flops=12 * HEADS_HERE * ROWS * ROWS * HD * 12, bytes_accessed=8000000, transcendentals=0
         ),
-        name="attend",
-    )(ids, live, level, *queries, *pairs)
+        name="attend_" + call,
+    )(ids, live, level, *operands)
 
 
 def combine_kernel(ids, table, *refs):
@@ -350,37 +449,33 @@
         return around(columns(block + lax.rem(x + step, 4)), "x", step)
 
     pair = jnp.concatenate([key_rows, values], axis=1)
-    next_one, next_three, below, above, piece_one, pair, queries, hidden, out_weight = together(
+    next_one, next_three, below, above, pair_there, pair, queries, hidden, out_weight = together(
         to_level(queries, 1),
         to_level(queries, 3),
         around(pair, "y", 1),
         around(pair, "y", -1),
-        fetch(1),
+        around(pair, "c", 1),
         pair,
         queries,
         hidden,
         out_weight,
     )
-    next_two, across, pair_there, piece_two, below, above, hidden, out_weight = together(
+    pairs = [pair, below, above, None, pair_there, None, None, None]
+    states = attend(
+        "early", ids, group_live, noise_level, [next_one, next_three, queries], pairs
+    )
+    next_two, across, below_there, above_there, piece_one, hidden, out_weight, *states = together(
         to_level(queries, 2),
         around(pair, "y", 2),
-        around(pair, "c", 1),
-        fetch(2),
-        below,
-        above,
+        around(below, "c", 1),
+        around(above, "c", 1),
+        fetch(1),
         hidden,
         out_weight,
-    )
-    below_there, above_there, across_there, hidden, out_weight = together(
-        around(below, "c", 1),
-        around(above, "c", 1),
-        around(across, "c", 1),
-        hidden,
-        out_weight,
-    )
-    pairs = [pair, below, above, across, pair_there, below_there, above_there, across_there]
-    weight_near, weight_far = columns(w * 4 + x), columns((1 - w) * 4 + x)
-    piece_three = fetch(3)
+        *states,
+    )
+    pairs = [pair, below, above, across, pair_there, below_there, above_there, around(across, "c", 1)]
+    piece_two, piece_three = fetch(2), fetch(3)
     hidden_next = around(hidden, SLOT, -1)
 
     def back(share, d):
@@ -389,16 +484,23 @@
         ]
         return lax.ppermute(share, SLOT, pairs_back)
 
-    shares = attend(
-        ids, group_live, noise_level, [queries, next_one, next_two, next_three], pairs
-    )
-    *shares, hidden_next, piece_three, weight_near, weight_far = together(
-        *shares, hidden_next, piece_three, weight_near, weight_far
-    )
+    state_one, state_three, state_own = states[0:2], states[2:4], states[4:6]
+    two, one = attend(
+        "middle", ids, group_live, noise_level, [next_two, next_one], pairs, state_one
+    )
+    back_two, back_one = back(two, 2), back(one, 1)
+    live_later, one = together(group_live, one)
+    three, zero = attend(
+        "late", ids, live_later, noise_level, [next_three, queries], pairs, state_three + state_own
+    )
+    three, zero, hidden_next, piece_two, piece_three, out_weight = together(
+        three, zero, hidden_next, piece_two, piece_three, out_weight
+    )
+    back_three, back_zero = back(three, 3), back(zero, 0)
     fetched = jnp.stack([piece_one, piece_two, piece_three])
     swapped = around(fetched, "c", 1)
-    returned = [back(shares[d], d) for d in range(4)]
-    attended, gate_row = combine(ids, level_table, returned)
+    weight_near, weight_far = columns(w * 4 + x), columns((1 - w) * 4 + x)
+    attended, gate_row = combine(ids, level_table, [back_zero, back_one, back_two, back_three])
 
     rows = [attended] + [around(attended, "x", step) for step in (1, 2, 3)]
     far_sum = project(True, ids, rows, weight_far, fetched, swapped)

time: 175 us -> 179 us (1.023)
  the two profiles are of different devices: /device:TPU:208 before, /device:TPU:25 now
where the time goes in v1:
time: 179 us; the launch traced here: 177 us
  waiting for transfers between devices  71.1 us (40%)
  Pallas kernels  56.2 us (31%)
  starting transfers between devices  23.3 us (13%)
  local copies, waits for them, and re-layouts  22.5 us (13%)
  other arithmetic  2.51 us (1%)
    pallas_call x3, Pallas kernels, attend(): pl.pallas_call(functools.partial(attend_kernel, call), out_shape=out_shap...  45.2 us
    ppermute x4, waiting for transfers between devices, back(): return lax.ppermute(share, SLOT, pairs_back)  29.9 us
    ppermute x16, waiting for transfers between devices, around(): lax.ppermute(value, axis, [(i, (i + steps) % count) for i in range(count)])  23.6 us
    ppermute x3, waiting for transfers between devices, to_level(): return lax.ppermute(value, 'z', [(i, i - d) for i in range(d, 4)])  17.5 us
    unnamed x67, local copies, waits for them, and re-layouts  16.5 us
    ppermute x16, starting transfers between devices, around(): lax.ppermute(value, axis, [(i, (i + steps) % count) for i in range(count)])  14.8 us
    pallas_call x2, Pallas kernels, project(): pl.pallas_call(functools.partial(project_kernel, far), out_shape=jax.Shap...  8.04 us
    dynamic_slice x3, local copies, waits for them, and re-layouts, columns(): return lax.dynamic_slice_in_dim(out_weight, owner * part, part, 1)  4.96 us
  transfers between devices with their start and end apart: 23, of which 7 were waited for; matrix products, arithmetic and copies ran while one was open for 2% of the time, Pallas kernels for 29%

profile of v1, /device:TPU:25, one launch (start us, length us, event | category | flops | bytes accessed | tf_op | source)
XLA Modules:
  0.0 176.7 jit_solution(17219007528758734777)
XLA Ops:
  0.0 1.0 constant_dynamic-update-slice_fusion.1
  1.0 1.0 constant_dynamic-update-slice_fusion.refs_3_.refs_2_
  2.2 1.5 collective-permute-start.3
  3.6 1.2 collective-permute-start.4
  4.9 1.3 collective-permute-start
  6.1 1.3 collective-permute-start.1
  8.2 17.5 %collective-permute-done.refs_0_.refs_1_ = bf16[448,384]{1,0:T(8,128)(2,1)S(1)} collective-permute-done((bf16[448,384]{1,0:T(8,128)(2,1)}, bf16[448,384]{1,0:T(8,128)(2,1)S(1)}, u32[]{:S(2)}, u32[]{:S(2)}) %collective-permute-start) | collective-permute-done | bytes 344096 | tf_op jit(solution)/shard_map/ppermute | solution.py:439
  25.8 1.3 constant_dynamic-slice_fusion.4
  27.1 1.3 collective-permute-start.9
  28.4 1.0 collective-permute-start.6
  29.4 1.1 collective-permute-start.7
  30.5 1.3 collective-permute-start.5
  31.8 1.0 copy-done.6
  32.8 1.0 copy-done.9
  33.8 1.0 copy-done.12
  34.8 16.5 %attend_early.1 = (f32[3,448,256]{2,1,0:T(8,128)S(1)}, f32[3,448,128]{2,1,0:T(8,128)S(1)}, f32[3,448,256]{2,1,0:T(8,128)S(1)}, f32[3,448,128]{2,1,0:T(8,128)S(1)...) custom-call(s32[4]{0:T(128)S(1)} %pad_add_fusion.ids, s32[32]{0:T(128)S(1)} %copy-done.16, s32[1]{0:T(128)S(6)} %copy.10.level, ...), custom_call_target="tpu_custom_call" | custom-call | flops 11098128384 | bytes 8000000 | tf_op jit(solution)/shard_map/attend_early/pallas_call | solution.py:297
  51.3 1.1 copy-done.17
  52.3 1.1 copy-done.19
  53.5 1.1 copy-done.21
  54.6 0.8 copy-done.23
  55.4 0.9 copy-done.25
  56.3 0.9 copy-done.27
  57.9 0.9 copy-done.2
  58.8 0.9 copy-done.4
  60.2 1.5 constant_dynamic-slice_fusion.2
  61.7 2.5 %collective-permute-start.12 = (bf16[384,768]{1,0:T(8,128)(2,1)S(1)}, bf16[384,768]{1,0:T(8,128)(2,1)S(1)}, u32[]{:S(2)}, u32[]{:S(2)}) collective-permute-start(bf16[384,768]{1,0:T(8,128)(2,1)S(1)} %get-tuple-element.90), channel_id=1, source_target_pairs={{0,2},{1,3},{2,0},{3,1},{4,6},{5,7},{6,4},{7,5},{8,10},{9,11},{10,... | collective-permute-start | bytes 1769480 | tf_op jit(solution)/shard_map/ppermute | solution.py:424
  64.2 1.2 collective-permute-start.13
  66.0 1.3 copy-done.18
  67.3 1.1 copy-done.24
  68.4 16.8 %attend_middle.1 = (bf16[480,384]{1,0:T(8,128)(2,1)S(1)}, bf16[480,384]{1,0:T(8,128)(2,1)S(1)}) custom-call(s32[4]{0:T(128)S(1)} %pad_add_fusion.ids, s32[32]{0:T(128)S(1)} %copy-done.16, s32[1]{0:T(128)S(6)} %copy.10.level, bf16[448,384]{1,0:T(8,128)(2,1)S(1)} %copy-done.15, bf16[448,384]{1,0:T(8,128)(2,1)S(1)} %copy-done.13, ...), custom_call_target="tpu_custom_call" | custom-call | flops 11098128384 | bytes 8000000 | tf_op jit(solution)/shard_map/attend_middle/pallas_call | solution.py:297
  85.3 11.9 %attend_late.1 = (bf16[480,384]{1,0:T(8,128)(2,1)S(1)}, bf16[480,384]{1,0:T(8,128)(2,1)S(1)}) custom-call(s32[4]{0:T(128)S(1)} %pad_add_fusion.ids, s32[32]{0:T(128)S(1)} %copy-done.16, s32[1]{0:T(128)S(6)} %copy.10.level, bf16[448,384]{1,0:T(8,128)(2,1)S(1)} %copy-done.10, bf16[448,384]{1,0:T(8,128)(2,1)S(1)} %copy-done.7, ...), custom_call_target="tpu_custom_call" | custom-call | flops 11098128384 | bytes 8000000 | tf_op jit(solution)/shard_map/attend_late/pallas_call | solution.py:297
  98.3 1.9 %collective-permute-start.15 = (bf16[480,384]{1,0:T(8,128)(2,1)S(1)}, bf16[480,384]{1,0:T(8,128)(2,1)S(1)}, u32[]{:S(2)}, u32[]{:S(2)}) collective-permute-start(bf16[480,384]{1,0:T(8,128)(2,1)S(1)} %get-tuple-element.67), channel_id=1, source_target_pairs={{0,56},{8,64},{16,72},{24,80},{32,88},{40,96},{48,104},{56,112},{6... | collective-permute-start | bytes 1105928 | tf_op jit(solution)/shard_map/ppermute | solution.py:485
  100.3 1.3 collective-permute-start.17
  101.6 1.3 collective-permute-start.16
  102.9 15.4 %collective-permute-done.14.refs_0_ = bf16[480,384]{1,0:T(8,128)(2,1)S(1)} collective-permute-done((bf16[480,384]{1,0:T(8,128)(2,1)S(1)}, bf16[480,384]{1,0:T(8,128)(2,1)S(1)}, u32[]{:S(2)}, u32[]{:S(2)}) %collective-permute-start.14) | collective-permute-done | bytes 368672 | tf_op jit(solution)/shard_map/ppermute | solution.py:485
  118.3 14.5 %collective-permute-done.17.refs_3_ = bf16[480,384]{1,0:T(8,128)(2,1)S(1)} collective-permute-done((bf16[480,384]{1,0:T(8,128)(2,1)S(1)}, bf16[480,384]{1,0:T(8,128)(2,1)S(1)}, u32[]{:S(2)}, u32[]{:S(2)}) %collective-permute-start.17) | collective-permute-done | bytes 368672 | tf_op jit(solution)/shard_map/ppermute | solution.py:485
  132.8 3.0 %combine.1 = (bf16[448,384]{1,0:T(8,128)(2,1)}, f32[1,768]{1,0:T(1,128)S(1)}) custom-call(s32[4]{0:T(128)S(1)} %pad_add_fusion.ids, f32[64,768]{1,0:T(8,128)S(1)} %copy-done.1, bf16[480,384]{1,0:T(8,128)(2,1)S(1)} %collective-permute-done.14.refs_0_, bf16[480,384]{1,0:T(8,128)(2,1)S(1)} %collective-permute-done.15.refs_1_, ...), custom_call_target="tpu_custom_call" | custom-call | tf_op jit(solution)/shard_map/combine/pallas_call | solution.py:363
  136.1 1.3 collective-permute-start.19
  137.4 2.1 %collective-permute-start.20 = (bf16[448,384]{1,0:T(8,128)(2,1)}, bf16[448,384]{1,0:T(8,128)(2,1)}, u32[]{:S(2)}, u32[]{:S(2)}) collective-permute-start(bf16[448,384]{1,0:T(8,128)(2,1)} %get-tuple-element.82.refs_0_), channel_id=1, source_target_pairs={{0,3},{1,0},{2,1},{3,2},{4,7},{5,4},{6,5},{7,6},{8,11},{9,8},{10,9... | collective-permute-start | bytes 1032200 | tf_op jit(solution)/shard_map/ppermute | solution.py:424
  139.5 2.1 %constant_dynamic-slice_fusion = (bf16[384,768]{1,0:T(8,128)(2,1)S(1)}, bf16[384,768]{1,0:T(8,128)(2,1)}) fusion(bf16[384,6144]{1,0:T(8,128)(2,1)} %param.12, s32[]{:T(128)S(6)} %select_n.29, s32[]{:T(128)S(6)} %select_n.28), kind=kLoop, calls=%fused_computation.4 | loop fusion | bytes 2359304 | tf_op jit(solution)/shard_map/dynamic_slice | solution.py:444
  141.6 4.7 %collective-permute-done.18.refs_1_ = bf16[448,384]{1,0:T(8,128)(2,1)} collective-permute-done((bf16[448,384]{1,0:T(8,128)(2,1)}, bf16[448,384]{1,0:T(8,128)(2,1)}, u32[]{:S(2)}, u32[]{:S(2)}) %collective-permute-start.18) | collective-permute-done | bytes 344096 | tf_op jit(solution)/shard_map/ppermute | solution.py:424
  146.3 6.1 %collective-permute-done.19.refs_2_ = bf16[448,384]{1,0:T(8,128)(2,1)} collective-permute-done((bf16[448,384]{1,0:T(8,128)(2,1)}, bf16[448,384]{1,0:T(8,128)(2,1)}, u32[]{:S(2)}, u32[]{:S(2)}) %collective-permute-start.19) | collective-permute-done | bytes 344096 | tf_op jit(solution)/shard_map/ppermute | solution.py:424
  152.4 1.8 %collective-permute-done.20.refs_3_ = bf16[448,384]{1,0:T(8,128)(2,1)} collective-permute-done((bf16[448,384]{1,0:T(8,128)(2,1)}, bf16[448,384]{1,0:T(8,128)(2,1)}, u32[]{:S(2)}, u32[]{:S(2)}) %collective-permute-start.20) | collective-permute-done | bytes 344096 | tf_op jit(solution)/shard_map/ppermute | solution.py:424
  154.3 4.4 %project.3 = bf16[448,768]{1,0:T(8,128)(2,1)} custom-call(s32[4]{0:T(128)S(1)} %pad_add_fusion.ids, bf16[448,384]{1,0:T(8,128)(2,1)} %get-tuple-element.82.refs_0_, bf16[448,384]{1,0:T(8,128)(2,1)} %collective-permute-done.18.refs_1_, bf16[448,384]{1,0:T(8,128)(2,1)} %collective-permute-done.19.refs_2_, bf16[448,384]{1,0:T(8,128)(2,1)} %collective-permute-done.20.refs_3_, ...), custom_call_target="tpu_custom_call" | custom-call | flops 1056964608 | bytes 5000000 | tf_op jit(solution)/shard_map/project/pallas_call | solution.py:408
  158.8 1.1 copy-done
  159.9 3.6 %project.2 = f32[448,768]{1,0:T(8,128)S(1)} custom-call(s32[4]{0:T(128)S(1)} %pad_add_fusion.ids, bf16[448,384]{1,0:T(8,128)(2,1)} %get-tuple-element.82.refs_0_, bf16[448,384]{1,0:T(8,128)(2,1)} %collective-permute-done.18.refs_1_, bf16[448,384]{1,0:T(8,128)(2,1)} %collective-permute-done.19.refs_2_, bf16[448,384]{1,0:T(8,128)(2,1)} %collective-permute-done.20.refs_3_, ...), custom_call_target="tpu_custom_call" | custom-call | flops 1056964608 | bytes 5000000 | tf_op jit(solution)/shard_map/project/pallas_call | solution.py:408
  163.5 10.9 %collective-permute-done.22 = bf16[448,768]{1,0:T(8,128)(2,1)} collective-permute-done((bf16[448,768]{1,0:T(8,128)(2,1)}, bf16[448,768]{1,0:T(8,128)(2,1)}, u32[]{:S(2)}, u32[]{:S(2)}) %collective-permute-start.22) | collective-permute-done | bytes 688160 | tf_op jit(solution)/shard_map/ppermute | solution.py:424
  174.5 2.2 %add_convert_fusion = bf16[448,768]{1,0:T(8,128)(2,1)} fusion(f32[448,768]{1,0:T(8,128)S(1)} %project.2, bf16[448,768]{1,0:T(8,128)(2,1)} %collective-permute-done.22, bf16[448,768]{1,0:T(8,128)(2,1)S(1)} %copy-done.30, f32[768]{0:T(1024)S(1)} %reduce), kind=kLoop, calls=%fused_computation.1 | loop fusion | flops 2064384 | bytes 3443712 | tf_op jit(solution)/shard_map/convert_element_type | solution.py:510
  (79 shorter events, 3.5 us)
Async XLA Ops:
  0.0 31.8 %copy-start.16 = (s32[32]{0:T(128)S(1)}, s32[32]{0:T(128)}, u32[]{:S(2)}) copy-start(s32[32]{0:T(128)} %live.4) | copy-start | bytes 388
  2.1 23.7 %collective-permute-start.2 = (bf16[448,768]{1,0:T(8,128)(2,1)S(1)}, bf16[448,768]{1,0:T(8,128)(2,1)S(1)}, u32[]{:S(2)}, u32[]{:S(2)}) collective-permute-start(bf16[448,768]{1,0:T(8,128)(2,1)S(1)} %constant_dynamic-update-slice_fusion.refs_3_.refs_2_), channel_id=1, source_target_pairs={{0,16},{16,32},{32,48},{48,0},{1,17},{17,33},{33,49},{49,1},{2,18}... | collective-permute-start | bytes 2064392 | tf_op jit(solution)/shard_map/ppermute | solution.py:424
  2.2 23.6 %collective-permute-start.3 = (bf16[448,768]{1,0:T(8,128)(2,1)S(1)}, bf16[448,768]{1,0:T(8,128)(2,1)S(1)}, u32[]{:S(2)}, u32[]{:S(2)}) collective-permute-start(bf16[448,768]{1,0:T(8,128)(2,1)S(1)} %constant_dynamic-update-slice_fusion.refs_3_.refs_2_), channel_id=1, source_target_pairs={{0,48},{16,0},{32,16},{48,32},{1,49},{17,1},{33,17},{49,33},{2,50}... | collective-permute-start | bytes 2064392 | tf_op jit(solution)/shard_map/ppermute | solution.py:424
  3.6 22.2 %collective-permute-start.4 = (bf16[448,768]{1,0:T(8,128)(2,1)S(1)}, bf16[448,768]{1,0:T(8,128)(2,1)S(1)}, u32[]{:S(2)}, u32[]{:S(2)}) collective-permute-start(bf16[448,768]{1,0:T(8,128)(2,1)S(1)} %constant_dynamic-update-slice_fusion.refs_3_.refs_2_), channel_id=1, source_target_pairs={{0,8},{8,0},{1,9},{9,1},{2,10},{10,2},{3,11},{11,3},{4,12},{12,4},... | collective-permute-start | bytes 2064392 | tf_op jit(solution)/shard_map/ppermute | solution.py:424
  4.9 20.9 %collective-permute-start = (bf16[448,384]{1,0:T(8,128)(2,1)}, bf16[448,384]{1,0:T(8,128)(2,1)S(1)}, u32[]{:S(2)}, u32[]{:S(2)}) collective-permute-start(bf16[448,384]{1,0:T(8,128)(2,1)} %refs_1_), channel_id=1, source_target_pairs={{64,0},{128,64},{192,128},{65,1},{129,65},{193,129},{66,2},{130,66... | collective-permute-start | bytes 1032200 | tf_op jit(solution)/shard_map/ppermute | solution.py:439
  6.1 19.6 %collective-permute-start.1 = (bf16[448,384]{1,0:T(8,128)(2,1)}, bf16[448,384]{1,0:T(8,128)(2,1)S(1)}, u32[]{:S(2)}, u32[]{:S(2)}) collective-permute-start(bf16[448,384]{1,0:T(8,128)(2,1)} %refs_1_), channel_id=1, source_target_pairs={{192,0},{193,1},{194,2},{195,3},{196,4},{197,5},{198,6},{199,7},{2... | collective-permute-start | bytes 1032200 | tf_op jit(solution)/shard_map/ppermute | solution.py:439
  25.8 1.4 copy-start.11
  25.8 1.4 copy-start.8
  27.1 30.7 %collective-permute-start.9 = (bf16[384,768]{1,0:T(8,128)(2,1)S(1)}, bf16[384,768]{1,0:T(8,128)(2,1)S(1)}, u32[]{:S(2)}, u32[]{:S(2)}) collective-permute-start(bf16[384,768]{1,0:T(8,128)(2,1)S(1)} %constant_dynamic-slice_fusion.4), channel_id=1, source_target_pairs={{0,1},{1,2},{2,3},{3,0},{4,5},{5,6},{6,7},{7,4},{8,9},{9,10},{10,1... | collective-permute-start | bytes 1769480 | tf_op jit(solution)/shard_map/ppermute | solution.py:424
  28.4 29.4 %collective-permute-start.6 = (bf16[448,768]{1,0:T(8,128)(2,1)S(1)}, bf16[448,768]{1,0:T(8,128)(2,1)S(1)}, u32[]{:S(2)}, u32[]{:S(2)}) collective-permute-start(bf16[448,768]{1,0:T(8,128)(2,1)S(1)} %constant_dynamic-update-slice_fusion.refs_3_.refs_2_), channel_id=1, source_target_pairs={{0,32},{16,48},{32,0},{48,16},{1,33},{17,49},{33,1},{49,17},{2,34}... | collective-permute-start | bytes 2064392 | tf_op jit(solution)/shard_map/ppermute | solution.py:424
  29.4 28.5 %collective-permute-start.7 = (bf16[448,768]{1,0:T(8,128)(2,1)S(1)}, bf16[448,768]{1,0:T(8,128)(2,1)S(1)}, u32[]{:S(2)}, u32[]{:S(2)}) collective-permute-start(bf16[448,768]{1,0:T(8,128)(2,1)S(1)} %collective-permute-done.2.refs_4_.refs_3_), channel_id=1, source_target_pairs={{0,8},{8,0},{1,9},{9,1},{2,10},{10,2},{3,11},{11,3},{4,12},{12,4},... | collective-permute-start | bytes 2064392 | tf_op jit(solution)/shard_map/ppermute | solution.py:424
  30.5 28.2 %collective-permute-start.8 = (bf16[448,768]{1,0:T(8,128)(2,1)S(1)}, bf16[448,768]{1,0:T(8,128)(2,1)S(1)}, u32[]{:S(2)}, u32[]{:S(2)}) collective-permute-start(bf16[448,768]{1,0:T(8,128)(2,1)S(1)} %collective-permute-done.3.refs_5_.refs_4_), channel_id=1, source_target_pairs={{0,8},{8,0},{1,9},{9,1},{2,10},{10,2},{3,11},{11,3},{4,12},{12,4},... | collective-permute-start | bytes 2064392 | tf_op jit(solution)/shard_map/ppermute | solution.py:424
  30.5 26.6 %collective-permute-start.5 = (bf16[448,384]{1,0:T(8,128)(2,1)}, bf16[448,384]{1,0:T(8,128)(2,1)S(1)}, u32[]{:S(2)}, u32[]{:S(2)}) collective-permute-start(bf16[448,384]{1,0:T(8,128)(2,1)} %refs_1_), channel_id=1, source_target_pairs={{128,0},{192,64},{129,1},{193,65},{130,2},{194,66},{131,3},{195,67... | collective-permute-start | bytes 1032200 | tf_op jit(solution)/shard_map/ppermute | solution.py:439
  31.8 1.0 copy-start.6
  32.8 1.0 copy-start.9
  51.2 1.1 copy-start.17
  52.3 1.1 copy-start.19
  53.5 1.1 copy-start.21
  57.9 1.8 %copy-start.31 = (bf16[384,768]{1,0:T(8,128)(2,1)}, bf16[384,768]{1,0:T(8,128)(2,1)S(1)}, u32[]{:S(2)}) copy-start(bf16[384,768]{1,0:T(8,128)(2,1)S(1)} %collective-permute-done.9) | copy-start | bytes 1769476
  59.7 6.3 %collective-permute-start.10 = (bf16[448,768]{1,0:T(8,128)(2,1)S(1)}, bf16[448,768]{1,0:T(8,128)(2,1)}, u32[]{:S(2)}, u32[]{:S(2)}) collective-permute-start(bf16[448,768]{1,0:T(8,128)(2,1)S(1)} %collective-permute-done.6.refs_6_.refs_2_), channel_id=1, source_target_pairs={{0,8},{8,0},{1,9},{9,1},{2,10},{10,2},{3,11},{11,3},{4,12},{12,4},... | collective-permute-start | bytes 2064392 | tf_op jit(solution)/shard_map/ppermute | solution.py:424
  60.2 5.8 %copy-start.3 = (bf16[448,768]{1,0:T(8,128)(2,1)S(1)}, bf16[448,768]{1,0:T(8,128)(2,1)}, u32[]{:S(2)}) copy-start(bf16[448,768]{1,0:T(8,128)(2,1)} %copy-done.2) | copy-start | bytes 2064388
  60.2 5.8 %copy-start.5 = (bf16[448,768]{1,0:T(8,128)(2,1)S(1)}, bf16[448,768]{1,0:T(8,128)(2,1)}, u32[]{:S(2)}) copy-start(bf16[448,768]{1,0:T(8,128)(2,1)} %copy-done.4) | copy-start | bytes 2064388
  60.2 5.8 %copy-start.13 = (bf16[448,384]{1,0:T(8,128)(2,1)S(1)}, bf16[448,384]{1,0:T(8,128)(2,1)}, u32[]{:S(2)}) copy-start(bf16[448,384]{1,0:T(8,128)(2,1)} %copy-done.11) | copy-start | bytes 1032196
  60.2 5.8 %copy-start.15 = (bf16[448,384]{1,0:T(8,128)(2,1)S(1)}, bf16[448,384]{1,0:T(8,128)(2,1)}, u32[]{:S(2)}) copy-start(bf16[448,384]{1,0:T(8,128)(2,1)} %copy-done.14) | copy-start | bytes 1032196
  61.7 35.6 %collective-permute-start.12 = (bf16[384,768]{1,0:T(8,128)(2,1)S(1)}, bf16[384,768]{1,0:T(8,128)(2,1)S(1)}, u32[]{:S(2)}, u32[]{:S(2)}) collective-permute-start(bf16[384,768]{1,0:T(8,128)(2,1)S(1)} %get-tuple-element.90), channel_id=1, source_target_pairs={{0,2},{1,3},{2,0},{3,1},{4,6},{5,7},{6,4},{7,5},{8,10},{9,11},{10,... | collective-permute-start | bytes 1769480 | tf_op jit(solution)/shard_map/ppermute | solution.py:424
  64.2 21.1 %copy-start.7 = (bf16[448,384]{1,0:T(8,128)(2,1)S(1)}, bf16[448,384]{1,0:T(8,128)(2,1)}, u32[]{:S(2)}) copy-start(bf16[448,384]{1,0:T(8,128)(2,1)} %refs_1_) | copy-start | bytes 1032196
  64.2 21.1 %copy-start.10 = (bf16[448,384]{1,0:T(8,128)(2,1)S(1)}, bf16[448,384]{1,0:T(8,128)(2,1)}, u32[]{:S(2)}) copy-start(bf16[448,384]{1,0:T(8,128)(2,1)} %copy-done.8) | copy-start | bytes 1032196
  64.2 33.1 %collective-permute-start.13 = (bf16[384,768]{1,0:T(8,128)(2,1)S(1)}, bf16[384,768]{1,0:T(8,128)(2,1)S(1)}, u32[]{:S(2)}, u32[]{:S(2)}) collective-permute-start(bf16[384,768]{1,0:T(8,128)(2,1)S(1)} %get-tuple-element.89), channel_id=1, source_target_pairs={{0,3},{1,0},{2,1},{3,2},{4,7},{5,4},{6,5},{7,6},{8,11},{9,8},{10,9... | collective-permute-start | bytes 1769480 | tf_op jit(solution)/shard_map/ppermute | solution.py:424
  65.4 31.9 %collective-permute-start.11 = (bf16[448,768]{1,0:T(8,128)(2,1)}, bf16[448,768]{1,0:T(8,128)(2,1)S(1)}, u32[]{:S(2)}, u32[]{:S(2)}) collective-permute-start(bf16[448,768]{1,0:T(8,128)(2,1)} %param.8), channel_id=1, source_target_pairs={{0,248},{8,0},{16,8},{24,16},{32,24},{40,32},{48,40},{56,48},{64,5... | collective-permute-start | bytes 2064392 | tf_op jit(solution)/shard_map/ppermute | solution.py:424
  66.0 1.3 copy-start.18
  67.3 1.1 copy-start.24
  68.4 16.9 %copy-start.20 = (f32[3,448,256]{2,1,0:T(8,128)S(1)}, f32[3,448,256]{2,1,0:T(8,128)}, u32[]{:S(2)}) copy-start(f32[3,448,256]{2,1,0:T(8,128)} %copy-done.19) | copy-start | bytes 4128772
  68.4 16.9 %copy-start.22 = (f32[3,448,256]{2,1,0:T(8,128)S(1)}, f32[3,448,256]{2,1,0:T(8,128)}, u32[]{:S(2)}) copy-start(f32[3,448,256]{2,1,0:T(8,128)} %copy-done.21) | copy-start | bytes 4128772
  68.4 16.9 %copy-start.26 = (f32[3,448,128]{2,1,0:T(8,128)S(1)}, f32[3,448,128]{2,1,0:T(8,128)}, u32[]{:S(2)}) copy-start(f32[3,448,128]{2,1,0:T(8,128)} %copy-done.25) | copy-start | bytes 2064388
  68.4 16.9 %copy-start.28 = (f32[3,448,128]{2,1,0:T(8,128)S(1)}, f32[3,448,128]{2,1,0:T(8,128)}, u32[]{:S(2)}) copy-start(f32[3,448,128]{2,1,0:T(8,128)} %copy-done.27) | copy-start | bytes 2064388
  85.3 12.0 %copy-start.32 = (bf16[384,768]{1,0:T(8,128)(2,1)S(1)}, bf16[384,768]{1,0:T(8,128)(2,1)}, u32[]{:S(2)}) copy-start(bf16[384,768]{1,0:T(8,128)(2,1)} %copy-done.31) | copy-start | bytes 1769476
  97.3 35.5 %copy-start.1 = (f32[64,768]{1,0:T(8,128)S(1)}, f32[64,768]{1,0:T(8,128)}, u32[]{:S(2)}) copy-start(f32[64,768]{1,0:T(8,128)} %table.1) | copy-start | bytes 589828
  98.2 56.1 %collective-permute-start.21 = (bf16[3,384,768]{2,1,0:T(8,128)(2,1)S(1)}, bf16[3,384,768]{2,1,0:T(8,128)(2,1)S(1)}, u32[]{:S(2)}, u32[]{:S(2)}) collective-permute-start(bf16[3,384,768]{2,1,0:T(8,128)(2,1)S(1)} %pad_maximum_fusion.refs_5_), channel_id=1, source_target_pairs={{0,8},{8,0},{1,9},{9,1},{2,10},{10,2},{3,11},{11,3},{4,12},{12,4},... | collective-permute-start | bytes 5308424 | tf_op jit(solution)/shard_map/ppermute | solution.py:424
  98.3 34.6 %collective-permute-start.15 = (bf16[480,384]{1,0:T(8,128)(2,1)S(1)}, bf16[480,384]{1,0:T(8,128)(2,1)S(1)}, u32[]{:S(2)}, u32[]{:S(2)}) collective-permute-start(bf16[480,384]{1,0:T(8,128)(2,1)S(1)} %get-tuple-element.67), channel_id=1, source_target_pairs={{0,56},{8,64},{16,72},{24,80},{32,88},{40,96},{48,104},{56,112},{6... | collective-permute-start | bytes 1105928 | tf_op jit(solution)/shard_map/ppermute | solution.py:485
  100.2 18.1 %collective-permute-start.14 = (bf16[480,384]{1,0:T(8,128)(2,1)S(1)}, bf16[480,384]{1,0:T(8,128)(2,1)S(1)}, u32[]{:S(2)}, u32[]{:S(2)}) collective-permute-start(bf16[480,384]{1,0:T(8,128)(2,1)S(1)} %get-tuple-element.78), channel_id=1, source_target_pairs={{0,248},{8,0},{16,8},{24,16},{32,24},{40,32},{48,40},{56,48},{64,5... | collective-permute-start | bytes 1105928 | tf_op jit(solution)/shard_map/ppermute | solution.py:485
  100.3 32.5 %collective-permute-start.17 = (bf16[480,384]{1,0:T(8,128)(2,1)S(1)}, bf16[480,384]{1,0:T(8,128)(2,1)S(1)}, u32[]{:S(2)}, u32[]{:S(2)}) collective-permute-start(bf16[480,384]{1,0:T(8,128)(2,1)S(1)} %get-tuple-element.80), channel_id=1, source_target_pairs={{0,184},{8,192},{16,200},{24,208},{32,216},{40,224},{48,232},{56,2... | collective-permute-start | bytes 1105928 | tf_op jit(solution)/shard_map/ppermute | solution.py:485
  101.6 31.2 %collective-permute-start.16 = (bf16[480,384]{1,0:T(8,128)(2,1)S(1)}, bf16[480,384]{1,0:T(8,128)(2,1)S(1)}, u32[]{:S(2)}, u32[]{:S(2)}) collective-permute-start(bf16[480,384]{1,0:T(8,128)(2,1)S(1)} %get-tuple-element.79), channel_id=1, source_target_pairs={{0,120},{8,128},{16,136},{24,144},{32,152},{40,160},{48,168},{56,1... | collective-permute-start | bytes 1105928 | tf_op jit(solution)/shard_map/ppermute | solution.py:485
  135.8 10.5 %collective-permute-start.18 = (bf16[448,384]{1,0:T(8,128)(2,1)}, bf16[448,384]{1,0:T(8,128)(2,1)}, u32[]{:S(2)}, u32[]{:S(2)}) collective-permute-start(bf16[448,384]{1,0:T(8,128)(2,1)} %get-tuple-element.82.refs_0_), channel_id=1, source_target_pairs={{0,1},{1,2},{2,3},{3,0},{4,5},{5,6},{6,7},{7,4},{8,9},{9,10},{10,1... | collective-permute-start | bytes 1032200 | tf_op jit(solution)/shard_map/ppermute | solution.py:424
  136.1 16.3 %collective-permute-start.19 = (bf16[448,384]{1,0:T(8,128)(2,1)}, bf16[448,384]{1,0:T(8,128)(2,1)}, u32[]{:S(2)}, u32[]{:S(2)}) collective-permute-start(bf16[448,384]{1,0:T(8,128)(2,1)} %get-tuple-element.82.refs_0_), channel_id=1, source_target_pairs={{0,2},{1,3},{2,0},{3,1},{4,6},{5,7},{6,4},{7,5},{8,10},{9,11},{10,... | collective-permute-start | bytes 1032200 | tf_op jit(solution)/shard_map/ppermute | solution.py:424
  137.4 16.8 %collective-permute-start.20 = (bf16[448,384]{1,0:T(8,128)(2,1)}, bf16[448,384]{1,0:T(8,128)(2,1)}, u32[]{:S(2)}, u32[]{:S(2)}) collective-permute-start(bf16[448,384]{1,0:T(8,128)(2,1)} %get-tuple-element.82.refs_0_), channel_id=1, source_target_pairs={{0,3},{1,0},{2,1},{3,2},{4,7},{5,4},{6,5},{7,6},{8,11},{9,8},{10,9... | collective-permute-start | bytes 1032200 | tf_op jit(solution)/shard_map/ppermute | solution.py:424
  158.7 15.8 %collective-permute-start.22 = (bf16[448,768]{1,0:T(8,128)(2,1)}, bf16[448,768]{1,0:T(8,128)(2,1)}, u32[]{:S(2)}, u32[]{:S(2)}) collective-permute-start(bf16[448,768]{1,0:T(8,128)(2,1)} %project.3), channel_id=1, source_target_pairs={{0,4},{4,0},{1,5},{5,1},{2,6},{6,2},{3,7},{7,3},{8,12},{12,8},{9,1... | collective-permute-start | bytes 2064392 | tf_op jit(solution)/shard_map/ppermute | solution.py:424
  158.8 1.1 copy-start
  159.9 14.6 %copy-start.30 = (bf16[448,768]{1,0:T(8,128)(2,1)S(1)}, bf16[448,768]{1,0:T(8,128)(2,1)}, u32[]{:S(2)}) copy-start(bf16[448,768]{1,0:T(8,128)(2,1)} %copy-done.29) | copy-start | bytes 2064388
  (8 other events, 6.9 us)

commit v2 on v1

--- a/solution.py
+++ b/solution.py
@@ -19,8 +19,9 @@
 EXP2_SCALE = HD**-0.5 * math.log2(math.e)
 Y_STEPS = (0, -1, 1, 2)
 SLOT = ("z", "y", "c")
-ATTEND_VMEM = 32 * 1024 * 1024
-SMALL_VMEM = 16 * 1024 * 1024
+ATTEND_VMEM = 22 * 1024 * 1024
+SMALL_VMEM = 8 * 1024 * 1024
+WHOLE_VMEM = 60 * 1024 * 1024
 
 
 def score(query, key):
@@ -30,7 +31,7 @@
 
 
 CALLS = {"early": (1, 3, 0), "middle": (2, 1), "late": (3, 0)}
-EARLY, LATER = (0, 1, 2, 4), (3, 5, 6, 7)
+EARLY, LATER = (0, 1, 2), (3, 4, 5, 6, 7)
 
 
 def attend_kernel(call, ids, live, level, *refs):
@@ -105,7 +106,7 @@
     def run():
         for j, p in enumerate(members):
             part = EARLY if p in EARLY else LATER
-            base = 0 if p in EARLY else 4
+            base = 0 if p in EARLY else 3
             if early and p == 0:
                 place_copy(j, own_place).start()
             else:
@@ -130,12 +131,12 @@
         if early:
             place_copy(0, own_place).wait()
         for k in range(8):
-            if k < 4 and call != "late":
+            if k < 3 and call != "late":
                 there = k < n_early
                 if early:
                     there = there & (k != own_place)
-            elif k >= 4 and not early:
-                there = k - 4 < n_later
+            elif k >= 3 and not early:
+                there = k - 3 < n_later
             else:
                 continue
 
@@ -178,10 +179,10 @@
             split, base = jnp.where(own, n_own, n_early), own_place
         elif middle:
             count = jnp.where(i == 0, n_early + n_later, n_later)
-            split, base = jnp.where(i == 0, n_early, 0), 4
+            split, base = jnp.where(i == 0, n_early, 0), 3
         else:
             count = jnp.where(own, n_own, n_later)
-            split, base = jnp.int32(0), 4
+            split, base = jnp.int32(0), 3
         chunks = (count + 1) // 2
 
         def at(k):
@@ -320,45 +321,99 @@
     )(ids, live, level, *operands)
 
 
-def combine_kernel(ids, table, *refs):
-    parts, out, gate = refs[0:4], refs[4], refs[5]
+def stats_of(tail):
+    tail = tail.astype(jnp.float32)
+    flat = jnp.concatenate([tail[0:16], tail[16:32, : ROWS - WIDTH]], axis=1)
+    noise = flat[3 * HEADS_HERE : 3 * HEADS_HERE + 1, 0:1]
+    padded = jnp.concatenate([flat, jnp.zeros((HD - 16, ROWS), jnp.float32)])
+    return jnp.transpose(padded), noise
+
+
+def merged(parts):
+    highest = parts[0][1]
+    for part in parts[1:]:
+        highest = jnp.maximum(highest, part[1])
+    values = total = None
+    for value, row_max, row_sum in parts:
+        factor = jnp.exp2(row_max - highest)
+        values = value * factor if values is None else values + value * factor
+        total = row_sum * factor if total is None else total + row_sum * factor
+    return values, highest, total
+
+
+def share_of(ref, stats, head, present):
+    value = ref[0:ROWS, head * HD : (head + 1) * HD].astype(jnp.float32)
+    row_max = stats[:, head : head + 1]
+    row_sum = (
+        stats[:, HEADS_HERE + head : HEADS_HERE + head + 1]
+        + stats[:, 2 * HEADS_HERE + head : 2 * HEADS_HERE + head + 1]
+    )
+    return (
+        jnp.where(present, value, 0.0),
+        jnp.where(present, row_max, LOWEST),
+        jnp.where(present, row_sum, 0.0),
+    )
+
+
+def combine_two_kernel(ids, one, two, values, sides):
     home = ids[3]
-    maxima, sums = [], []
-    for d in range(4):
-        tail = parts[d][ROWS : ROWS + STAT, :].astype(jnp.float32)
-        flat = jnp.concatenate([tail[0:16], tail[16:32, : ROWS - WIDTH]], axis=1)
-        if d == 0:
-            noise = flat[3 * HEADS_HERE : 3 * HEADS_HERE + 1, 0:1]
-        stats = jnp.transpose(jnp.concatenate([flat, jnp.zeros((HD - 16, ROWS), jnp.float32)]))
-        present = d <= home
-        row_max, row_sum = [], []
-        for head in range(HEADS_HERE):
-            total = (
-                stats[:, HEADS_HERE + head : HEADS_HERE + head + 1]
-                + stats[:, 2 * HEADS_HERE + head : 2 * HEADS_HERE + head + 1]
-            )
-            row_max.append(jnp.where(present, stats[:, head : head + 1], LOWEST))
-            row_sum.append(jnp.where(present, total, 0.0))
-        maxima.append(row_max)
-        sums.append(row_sum)
+    stats = [stats_of(ref[ROWS : ROWS + STAT, :])[0] for ref in (one, two)]
+    lane = lax.broadcasted_iota(jnp.int32, (ROWS, HD), 1)
+    side = jnp.zeros((ROWS, HD), jnp.float32)
+    for head in range(HEADS_HERE):
+        value, row_max, row_sum = merged(
+            [
+                share_of(one, stats[0], head, home >= 1),
+                share_of(two, stats[1], head, home >= 2),
+            ]
+        )
+        values[:, head * HD : (head + 1) * HD] = value
+        side = jnp.where(lane == head, row_max, side)
+        side = jnp.where(lane == HEADS_HERE + head, row_sum, side)
+    sides[...] = side
+
+
+def combine_two(ids, one, two):
+    vmem = pl.BlockSpec(memory_space=pltpu.VMEM)
+    return pl.pallas_call(
+        combine_two_kernel,
+        out_shape=[
+            jax.ShapeDtypeStruct((ROWS, WIDTH), jnp.float32),
+            jax.ShapeDtypeStruct((ROWS, HD), jnp.float32),
+        ],
+        in_specs=[pl.BlockSpec(memory_space=pltpu.SMEM)] + [vmem] * 2,
+        out_specs=[vmem] * 2,
+        compiler_params=pltpu.CompilerParams(vmem_limit_bytes=SMALL_VMEM),
+        cost_estimate=pl.CostEstimate(
+            flops=10**11, bytes_accessed=2 * 10**8, transcendentals=0
+        ),
+        name="combine_two",
+    )(ids, one, two)
+
+
+def combine_kernel(ids, table, zero, three, values, sides, out, gate):
+    home = ids[3]
+    own, noise = stats_of(zero[ROWS : ROWS + STAT, :])
+    far = stats_of(three[ROWS : ROWS + STAT, :])[0]
     for head in range(HEADS_HERE):
         at = slice(head * HD, (head + 1) * HD)
-        highest = maxima[0][head]
-        for d in range(1, 4):
-            highest = jnp.maximum(highest, maxima[d][head])
-        numerator = jnp.zeros((ROWS, HD), jnp.float32)
-        denominator = jnp.zeros((ROWS, 1), jnp.float32)
-        for d in range(4):
-            factor = jnp.exp2(maxima[d][head] - highest)
-            share = jnp.where(d <= home, parts[d][0:ROWS, at].astype(jnp.float32), 0.0)
-            numerator = numerator + share * factor
-            denominator = denominator + sums[d][head] * factor
-        out[:, at] = (numerator / denominator).astype(jnp.bfloat16)
+        value, unused, row_sum = merged(
+            [
+                share_of(zero, own, head, home >= 0),
+                share_of(three, far, head, home >= 3),
+                (
+                    values[:, at],
+                    sides[:, head : head + 1],
+                    sides[:, HEADS_HERE + head : HEADS_HERE + head + 1],
+                ),
+            ]
+        )
+        out[:, at] = (value / row_sum).astype(jnp.bfloat16)
     index = lax.broadcasted_iota(jnp.int32, table.shape, 0).astype(jnp.float32)
     gate[...] = jnp.sum(jnp.where(index == noise, table[...], 0.0), axis=0, keepdims=True)
 
 
-def combine(ids, table, parts):
+def combine(ids, table, zero, three, values, sides):
     vmem = pl.BlockSpec(memory_space=pltpu.VMEM)
     return pl.pallas_call(
         combine_kernel,
@@ -370,7 +425,58 @@
         out_specs=[vmem] * 2,
         compiler_params=pltpu.CompilerParams(vmem_limit_bytes=SMALL_VMEM),
         name="combine",
-    )(ids, table, *parts)
+    )(ids, table, zero, three, values, sides)
+
+
+def finish_kernel(hidden, near, arrived, gate, out):
+    projected = near[...] + arrived[...].astype(jnp.float32)
+    out[...] = (hidden[...].astype(jnp.float32) + gate[...] * projected).astype(jnp.bfloat16)
+
+
+def finish(hidden, near, arrived, gate):
+    part = hidden.shape[1]
+    rows = pl.BlockSpec((ROWS // 4, part), lambda i: (i, 0))
+    return pl.pallas_call(
+        finish_kernel,
+        grid=(4,),
+        out_shape=jax.ShapeDtypeStruct(hidden.shape, jnp.bfloat16),
+        in_specs=[rows, rows, rows, pl.BlockSpec((1, part), lambda i: (0, 0))],
+        out_specs=rows,
+        compiler_params=pltpu.CompilerParams(vmem_limit_bytes=SMALL_VMEM),
+        name="finish",
+    )(hidden, near, arrived, gate)
+
+
+def copies_kernel(plan, ids, *refs):
+    inputs, outs, sem = refs[: plan[0]], refs[plan[0] : -1], refs[-1]
+    copies = []
+    for n, (kind, source, target, number) in enumerate(plan[1]):
+        src, dst = inputs[source], outs[target]
+        if kind == "beside":
+            dst = dst.at[:, pl.ds(number * src.shape[1], src.shape[1])]
+        elif kind == "columns":
+            width = dst.shape[1]
+            src = src.at[:, pl.ds(pl.multiple_of(ids[number] * width, width), width)]
+        else:
+            dst = dst.at[number]
+        copies.append(pltpu.make_async_copy(src, dst, sem.at[n]))
+    for copy in copies:
+        copy.start()
+    for copy in copies:
+        copy.wait()
+
+
+def copied(name, ids, inputs, shapes, plan, vmem):
+    anywhere = pl.BlockSpec(memory_space=pl.ANY)
+    return pl.pallas_call(
+        functools.partial(copies_kernel, (len(inputs), plan)),
+        out_shape=[jax.ShapeDtypeStruct(shape, jnp.bfloat16) for shape in shapes],
+        in_specs=[pl.BlockSpec(memory_space=pltpu.SMEM)] + [anywhere] * len(inputs),
+        out_specs=[anywhere] * len(shapes),
+        scratch_shapes=[pltpu.SemaphoreType.DMA((len(plan),))],
+        compiler_params=pltpu.CompilerParams(vmem_limit_bytes=vmem),
+        name=name,
+    )(ids, *inputs)
 
 
 def project_kernel(far, ids, *refs):
@@ -413,7 +519,7 @@
         scratch_shapes=[pltpu.VMEM((3, WIDTH, part), jnp.bfloat16), pltpu.SemaphoreType.DMA],
         compiler_params=pltpu.CompilerParams(vmem_limit_bytes=SMALL_VMEM),
         cost_estimate=pl.CostEstimate(
-            flops=8 * ROWS * WIDTH * part, bytes_accessed=5000000, transcendentals=0
+            flops=8 * ROWS * WIDTH * part, bytes_accessed=5 * 10**6, transcendentals=0
         ),
         name="project",
     )(ids, *rows, own, fetched, swapped)
@@ -433,49 +539,89 @@
     w, x = lax.axis_index("w"), lax.axis_index("x")
     slot = z * 8 + y * 2 + core
     home = lax.rem(slot + 1, 32) // 8
-    ids = jnp.stack([z, y, core, home]).astype(jnp.int32)
+    block = jnp.where(core == 0, w, 1 - w) * 4
+    owners = [block + lax.rem(x + step, 4) for step in (1, 2, 3)] + [w * 4 + x, (1 - w) * 4 + x]
+    ids = jnp.stack([z, y, core, home, *owners]).astype(jnp.int32)
+    column_block = (out_weight.shape[0], out_weight.shape[1] // 8)
 
     def to_level(value, d):
         return lax.ppermute(value, "z", [(i, i - d) for i in range(d, 4)])
 
-    part = out_weight.shape[1] // 8
-
-    def columns(owner):
-        return lax.dynamic_slice_in_dim(out_weight, owner * part, part, 1)
-
-    block = jnp.where(core == 0, w, 1 - w) * 4
-
-    def fetch(step):
-        return around(columns(block + lax.rem(x + step, 4)), "x", step)
-
-    pair = jnp.concatenate([key_rows, values], axis=1)
-    next_one, next_three, below, above, pair_there, pair, queries, hidden, out_weight = together(
+    pair, piece_one = copied(
+        "pack",
+        ids,
+        [key_rows, values, out_weight],
+        [(ROWS, 2 * WIDTH), column_block],
+        (("beside", 0, 0, 0), ("beside", 1, 0, 1), ("columns", 2, 1, 4)),
+        WHOLE_VMEM,
+    )
+    piece_two, piece_three, weight_near, weight_far = copied(
+        "columns",
+        ids,
+        [out_weight],
+        [column_block] * 4,
+        tuple(("columns", 0, k, 5 + k) for k in range(4)),
+        SMALL_VMEM,
+    )
+    (
+        next_one,
+        next_three,
+        below,
+        above,
+        piece_one,
+        pair,
+        queries,
+        hidden,
+        piece_two,
+        piece_three,
+        weight_near,
+        weight_far,
+    ) = together(
         to_level(queries, 1),
         to_level(queries, 3),
         around(pair, "y", 1),
         around(pair, "y", -1),
-        around(pair, "c", 1),
+        around(piece_one, "x", 1),
         pair,
         queries,
         hidden,
-        out_weight,
-    )
-    pairs = [pair, below, above, None, pair_there, None, None, None]
+        piece_two,
+        piece_three,
+        weight_near,
+        weight_far,
+    )
     states = attend(
-        "early", ids, group_live, noise_level, [next_one, next_three, queries], pairs
-    )
-    next_two, across, below_there, above_there, piece_one, hidden, out_weight, *states = together(
+        "early",
+        ids,
+        group_live,
+        noise_level,
+        [next_one, next_three, queries],
+        [pair, below, above],
+    )
+    (
+        next_two,
+        across,
+        piece_three,
+        below_there,
+        above_there,
+        hidden,
+        piece_two,
+        pair,
+        *states,
+    ) = together(
         to_level(queries, 2),
         around(pair, "y", 2),
+        around(piece_three, "x", 3),
         around(below, "c", 1),
         around(above, "c", 1),
-        fetch(1),
         hidden,
-        out_weight,
+        piece_two,
+        pair,
         *states,
     )
-    pairs = [pair, below, above, across, pair_there, below_there, above_there, around(across, "c", 1)]
-    piece_two, piece_three = fetch(2), fetch(3)
+    across_there, pair_there = around(across, "c", 1), around(pair, "c", 1)
+    pairs = [pair, below, above, across, pair_there, below_there, above_there, across_there]
+    piece_two = around(piece_two, "x", 2)
     hidden_next = around(hidden, SLOT, -1)
 
     def back(share, d):
@@ -488,26 +634,30 @@
     two, one = attend(
         "middle", ids, group_live, noise_level, [next_two, next_one], pairs, state_one
     )
-    back_two, back_one = back(two, 2), back(one, 1)
+    values_two, sides_two = combine_two(ids, back(one, 1), back(two, 2))
     live_later, one = together(group_live, one)
     three, zero = attend(
         "late", ids, live_later, noise_level, [next_three, queries], pairs, state_three + state_own
     )
-    three, zero, hidden_next, piece_two, piece_three, out_weight = together(
-        three, zero, hidden_next, piece_two, piece_three, out_weight
-    )
-    back_three, back_zero = back(three, 3), back(zero, 0)
-    fetched = jnp.stack([piece_one, piece_two, piece_three])
+    three, zero, hidden_next, piece_two = together(three, zero, hidden_next, piece_two)
+    (fetched,) = copied(
+        "stack",
+        ids,
+        [piece_one, piece_two, piece_three],
+        [(3, *column_block)],
+        tuple(("stack", k, 0, k) for k in range(3)),
+        SMALL_VMEM,
+    )
     swapped = around(fetched, "c", 1)
-    weight_near, weight_far = columns(w * 4 + x), columns((1 - w) * 4 + x)
-    attended, gate_row = combine(ids, level_table, [back_zero, back_one, back_two, back_three])
+    attended, gate_row = combine(
+        ids, level_table, back(zero, 0), back(three, 3), values_two, sides_two
+    )
 
     rows = [attended] + [around(attended, "x", step) for step in (1, 2, 3)]
     far_sum = project(True, ids, rows, weight_far, fetched, swapped)
     arrived = around(far_sum, "w", 1)
     near_sum = project(False, ids, rows, weight_near, fetched, swapped)
-    projected = near_sum + arrived.astype(jnp.float32)
-    return (hidden_next.astype(jnp.float32) + gate_row * projected).astype(jnp.bfloat16)
+    return finish(hidden_next, near_sum, arrived, gate_row)
 
 
 def solution(mesh):

time: 179 us -> 192 us (1.073)
  the two profiles are of different devices: /device:TPU:25 before, /device:TPU:6 now
where the time goes in v2:
time: 192 us; the launch traced here: 191 us
  Pallas kernels  86.9 us (45%)
  waiting for transfers between devices  65.2 us (34%)
  starting transfers between devices  35.2 us (18%)
  local copies, waits for them, and re-layouts  2.98 us (2%)
    pallas_call x3, Pallas kernels, copied(): pl.pallas_call(functools.partial(copies_kernel, (len(inputs), plan)), out...  42.4 us
    pallas_call x3, Pallas kernels, attend(): pl.pallas_call(functools.partial(attend_kernel, call), out_shape=out_shap...  33.5 us
    ppermute x16, waiting for transfers between devices, around(): lax.ppermute(value, axis, [(i, (i + steps) % count) for i in range(count)])  32.2 us
    ppermute x16, starting transfers between devices, around(): lax.ppermute(value, axis, [(i, (i + steps) % count) for i in range(count)])  21.8 us
    ppermute x4, waiting for transfers between devices, back(): return lax.ppermute(share, SLOT, pairs_back)  17.7 us
    ppermute x3, waiting for transfers between devices, to_level(): return lax.ppermute(value, 'z', [(i, i - d) for i in range(d, 4)])  15.3 us
    ppermute x4, starting transfers between devices, back(): return lax.ppermute(share, SLOT, pairs_back)  9.55 us
    pallas_call x2, Pallas kernels, project(): pl.pallas_call(functools.partial(project_kernel, far), out_shape=jax.Shap...  5.62 us
  transfers between devices with their start and end apart: 23, of which 6 were waited for; matrix products, arithmetic and copies ran while one was open for 0% of the time, Pallas kernels for 22%

profile of v2, /device:TPU:6, one launch (start us, length us, event | category | flops | bytes accessed | tf_op | source)
XLA Modules:
  0.0 191.2 jit_solution(2596001104887901461)
XLA Ops:
  0.0 0.6 stack.40.ids
  0.6 40.6 %pack.1 = (bf16[448,768]{1,0:T(8,128)(2,1)}, bf16[384,768]{1,0:T(8,128)(2,1)}) custom-call(s32[9]{0:T(128)} %stack.40.ids, bf16[448,384]{1,0:T(8,128)(2,1)} %refs_0_.2, bf16[448,384]{1,0:T(8,128)(2,1)} %refs_1_.1, bf16[384,6144]{1,0:T(8,128)(2,1)} %refs_0_.3), custom_call_target="tpu_custom_call" | custom-call | tf_op jit(solution)/shard_map/pack/pallas_call | solution.py:471
  41.3 1.7 collective-permute-start.2
  42.9 1.7 collective-permute-start.3
  44.6 2.2 %collective-permute-start.4 = (bf16[384,768]{1,0:T(8,128)(2,1)}, bf16[384,768]{1,0:T(8,128)(2,1)S(1)}, u32[]{:S(2)}, u32[]{:S(2)}) collective-permute-start(bf16[384,768]{1,0:T(8,128)(2,1)} %get-tuple-element.57), channel_id=1, source_target_pairs={{0,1},{1,2},{2,3},{3,0},{4,5},{5,6},{6,7},{7,4},{8,9},{9,10},{10,1... | collective-permute-start | bytes 1769480 | tf_op jit(solution)/shard_map/ppermute | solution.py:530
  46.8 1.3 collective-permute-start
  48.1 1.3 collective-permute-start.1
  49.4 0.0 copy-start
  49.4 2.3 %copy-done = bf16[384,6144]{1,0:T(8,128)(2,1)S(1)} copy-done((bf16[384,6144]{1,0:T(8,128)(2,1)S(1)}, bf16[384,6144]{1,0:T(8,128)(2,1)}, u32[]{:S(2)}) %copy-start) | copy-done | bytes 4718616
  51.7 0.8 columns.1
  53.2 11.7 %collective-permute-done.refs_0_.refs_1_ = bf16[448,384]{1,0:T(8,128)(2,1)S(1)} collective-permute-done((bf16[448,384]{1,0:T(8,128)(2,1)S(1)}, bf16[448,384]{1,0:T(8,128)(2,1)S(1)}, u32[]{:S(2)}, u32[]{:S(2)}) %collective-permute-start) | collective-permute-done | bytes 344096 | tf_op jit(solution)/shard_map/ppermute | solution.py:548
  65.0 0.0 collective-permute-done.3.refs_5_.refs_4_
  65.0 0.0 copy-start.6
  65.0 1.9 %collective-permute-start.6 = (bf16[448,768]{1,0:T(8,128)(2,1)S(1)}, bf16[448,768]{1,0:T(8,128)(2,1)S(1)}, u32[]{:S(2)}, u32[]{:S(2)}) collective-permute-start(bf16[448,768]{1,0:T(8,128)(2,1)S(1)} %copy-done.3), channel_id=1, source_target_pairs={{0,32},{16,48},{32,0},{48,16},{1,33},{17,49},{33,1},{49,17},{2,34}... | collective-permute-start | bytes 2064392 | tf_op jit(solution)/shard_map/ppermute | solution.py:530
  66.9 0.0 collective-permute-start.8
  66.9 0.5 collective-permute-start.9
  67.4 1.5 collective-permute-start.7
  69.0 1.3 collective-permute-start.5
  70.3 11.0 %attend_early.1 = (f32[3,448,256]{2,1,0:T(8,128)S(1)}, f32[3,448,128]{2,1,0:T(8,128)S(1)}, f32[3,448,256]{2,1,0:T(8,128)S(1)}, f32[3,448,128]{2,1,0:T(8,128)S(1)...) custom-call(s32[9]{0:T(128)S(1)} %copy-done.2, s32[32]{0:T(128)S(1)} %copy-done.5, s32[1]{0:T(128)S(6)} %copy.9.level, ...), custom_call_target="tpu_custom_call" | custom-call | flops 11098128384 | bytes 8000000 | tf_op jit(solution)/shard_map/attend_early/pallas_call | solution.py:298
  81.3 3.6 %collective-permute-done.5.refs_0_ = bf16[448,384]{1,0:T(8,128)(2,1)S(1)} collective-permute-done((bf16[448,384]{1,0:T(8,128)(2,1)S(1)}, bf16[448,384]{1,0:T(8,128)(2,1)S(1)}, u32[]{:S(2)}, u32[]{:S(2)}) %collective-permute-start.5) | collective-permute-done | bytes 344096 | tf_op jit(solution)/shard_map/ppermute | solution.py:548
  84.9 0.0 collective-permute-done.9.refs_8_.refs_5_
  84.9 0.1 collective-permute-start.10
  85.0 0.5 collective-permute-start.11
  85.5 7.0 %collective-permute-start.12 = (bf16[448,768]{1,0:T(8,128)(2,1)S(1)}, bf16[448,768]{1,0:T(8,128)(2,1)S(1)}, u32[]{:S(2)}, u32[]{:S(2)}) collective-permute-start(bf16[448,768]{1,0:T(8,128)(2,1)S(1)} %copy-done.6), channel_id=1, source_target_pairs={{0,248},{8,0},{16,8},{24,16},{32,24},{40,32},{48,40},{56,48},{64,5... | collective-permute-start | bytes 2064392 | tf_op jit(solution)/shard_map/ppermute | solution.py:530
  92.5 1.4 collective-permute-start.13
  93.9 14.5 %attend_middle.1 = (bf16[480,384]{1,0:T(8,128)(2,1)S(1)}, bf16[480,384]{1,0:T(8,128)(2,1)S(1)}) custom-call(s32[9]{0:T(128)S(1)} %copy-done.2, s32[32]{0:T(128)S(1)} %copy-done.5, s32[1]{0:T(128)S(6)} %copy.9.level, bf16[448,384]{1,0:T(8,128)(2,1)S(1)} %collective-permute-done.5.refs_0_, bf16[448,384]{1,0:T(8,128)(2,1)S(1)} %collective-permute-done.refs_0_.refs_1_, ...), custom_call_target="tpu_custom_call" | custom-call | flops 11098128384 | bytes 8000000 | tf_op jit(solution)/shard_map/attend_middle/pallas_call | solution.py:298
  108.4 1.3 collective-permute-start.16
  109.7 6.8 %collective-permute-start.17 = (bf16[480,384]{1,0:T(8,128)(2,1)S(1)}, bf16[480,384]{1,0:T(8,128)(2,1)S(1)}, u32[]{:S(2)}, u32[]{:S(2)}) collective-permute-start(bf16[480,384]{1,0:T(8,128)(2,1)S(1)} %get-tuple-element.97), channel_id=1, source_target_pairs={{0,120},{8,128},{16,136},{24,144},{32,152},{40,160},{48,168},{56,1... | collective-permute-start | bytes 1105928 | tf_op jit(solution)/shard_map/ppermute | solution.py:631
  116.5 8.1 %attend_late.1 = (bf16[480,384]{1,0:T(8,128)(2,1)S(1)}, bf16[480,384]{1,0:T(8,128)(2,1)S(1)}) custom-call(s32[9]{0:T(128)S(1)} %copy-done.2, s32[32]{0:T(128)S(1)} %copy-done.5, s32[1]{0:T(128)S(6)} %copy.9.level, bf16[448,384]{1,0:T(8,128)(2,1)S(1)} %collective-permute-done.1.refs_1_.refs_0_, bf16[448,384]{1,0:T(8,128)(2,1)S(1)} %copy-done.4, ...), custom_call_target="tpu_custom_call" | custom-call | flops 11098128384 | bytes 8000000 | tf_op jit(solution)/shard_map/attend_late/pallas_call | solution.py:298
  124.7 0.0 collective-permute-done.13.refs_1_
  124.7 0.0 collective-permute-done.12.hidden
  124.7 0.9 stack.41.refs_5_
  125.6 0.0 copy-start.1
  125.6 0.1 collective-permute-start.21
  125.7 0.1 collective-permute-start.14
  125.8 1.3 collective-permute-start.15
  127.2 1.5 combine_two.1
  128.7 17.6 %collective-permute-done.14.zero = bf16[480,384]{1,0:T(8,128)(2,1)S(1)} collective-permute-done((bf16[480,384]{1,0:T(8,128)(2,1)S(1)}, bf16[480,384]{1,0:T(8,128)(2,1)S(1)}, u32[]{:S(2)}, u32[]{:S(2)}) %collective-permute-start.14) | collective-permute-done | bytes 368672 | tf_op jit(solution)/shard_map/ppermute | solution.py:631
  146.4 2.2 %combine.1 = (bf16[448,384]{1,0:T(8,128)(2,1)S(1)}, f32[1,768]{1,0:T(1,128)S(1)}) custom-call(s32[9]{0:T(128)S(1)} %copy-done.2, f32[64,768]{1,0:T(8,128)S(1)} %copy-done.1, bf16[480,384]{1,0:T(8,128)(2,1)S(1)} %collective-permute-done.14.zero, bf16[480,384]{1,0:T(8,128)(2,1)S(1)} %collective-permute-done.15.three, f32[448,384]{1,0:T(8,128)S(1)} %get-tuple-element.98.values, ...), custom_call_target="tpu_custom_call" | custom-call | tf_op jit(solution)/shard_map/combine/pallas_call | solution.py:418
  148.6 1.8 collective-permute-start.18
  150.4 1.3 collective-permute-start.19
  151.7 14.0 %collective-permute-done.18.refs_1_ = bf16[448,384]{1,0:T(8,128)(2,1)S(1)} collective-permute-done((bf16[448,384]{1,0:T(8,128)(2,1)S(1)}, bf16[448,384]{1,0:T(8,128)(2,1)S(1)}, u32[]{:S(2)}, u32[]{:S(2)}) %collective-permute-start.18) | collective-permute-done | bytes 344096 | tf_op jit(solution)/shard_map/ppermute | solution.py:530
  165.7 3.7 %collective-permute-done.20.refs_3_ = bf16[448,384]{1,0:T(8,128)(2,1)S(1)} collective-permute-done((bf16[448,384]{1,0:T(8,128)(2,1)S(1)}, bf16[448,384]{1,0:T(8,128)(2,1)S(1)}, u32[]{:S(2)}, u32[]{:S(2)}) %collective-permute-start.20) | collective-permute-done | bytes 344096 | tf_op jit(solution)/shard_map/ppermute | solution.py:530
  169.4 2.8 %project.3 = bf16[448,768]{1,0:T(8,128)(2,1)S(1)} custom-call(s32[9]{0:T(128)S(1)} %copy-done.2, bf16[448,384]{1,0:T(8,128)(2,1)S(1)} %get-tuple-element.100.refs_0_, bf16[448,384]{1,0:T(8,128)(2,1)S(1)} %collective-permute-done.18.refs_1_, bf16[448,384]{1,0:T(8,128)(2,1)S(1)} %collective-permute-done.19.refs_2_, ...), custom_call_target="tpu_custom_call" | custom-call | flops 1056964608 | bytes 5000000 | tf_op jit(solution)/shard_map/project/pallas_call | solution.py:514
  172.2 0.1 collective-permute-start.22
  172.3 2.8 %project.2.near = f32[448,768]{1,0:T(8,128)S(1)} custom-call(s32[9]{0:T(128)S(1)} %copy-done.2, bf16[448,384]{1,0:T(8,128)(2,1)S(1)} %get-tuple-element.100.refs_0_, bf16[448,384]{1,0:T(8,128)(2,1)S(1)} %collective-permute-done.18.refs_1_, bf16[448,384]{1,0:T(8,128)(2,1)S(1)} %collective-permute-done.19.refs_2_, ...), custom_call_target="tpu_custom_call" | custom-call | flops 1056964608 | bytes 5000000 | tf_op jit(solution)/shard_map/project/pallas_call | solution.py:514
  175.1 14.5 %collective-permute-done.22.arrived = bf16[448,768]{1,0:T(8,128)(2,1)S(1)} collective-permute-done((bf16[448,768]{1,0:T(8,128)(2,1)S(1)}, bf16[448,768]{1,0:T(8,128)(2,1)S(1)}, u32[]{:S(2)}, u32[]{:S(2)}) %collective-permute-start.22) | collective-permute-done | bytes 688160 | tf_op jit(solution)/shard_map/ppermute | solution.py:530
  189.6 1.6 finish.1
  (24 shorter events, 0.1 us)
Async XLA Ops:
  0.6 46.2 %copy-start.4 = (bf16[448,384]{1,0:T(8,128)(2,1)S(1)}, bf16[448,384]{1,0:T(8,128)(2,1)}, u32[]{:S(2)}) copy-start(bf16[448,384]{1,0:T(8,128)(2,1)} %refs_1_.2) | copy-start | bytes 1032196
  0.6 48.8 %copy-start.2 = (s32[9]{0:T(128)S(1)}, s32[9]{0:T(128)}, u32[]{:S(2)}) copy-start(s32[9]{0:T(128)} %stack.40.ids) | copy-start | bytes 112
  41.3 23.7 %collective-permute-start.2 = (bf16[448,768]{1,0:T(8,128)(2,1)}, bf16[448,768]{1,0:T(8,128)(2,1)S(1)}, u32[]{:S(2)}, u32[]{:S(2)}) collective-permute-start(bf16[448,768]{1,0:T(8,128)(2,1)} %get-tuple-element.78.refs_3_.refs_2_), channel_id=1, source_target_pairs={{0,16},{16,32},{32,48},{48,0},{1,17},{17,33},{33,49},{49,1},{2,18}... | collective-permute-start | bytes 2064392 | tf_op jit(solution)/shard_map/ppermute | solution.py:530
  42.9 22.1 %collective-permute-start.3 = (bf16[448,768]{1,0:T(8,128)(2,1)}, bf16[448,768]{1,0:T(8,128)(2,1)S(1)}, u32[]{:S(2)}, u32[]{:S(2)}) collective-permute-start(bf16[448,768]{1,0:T(8,128)(2,1)} %get-tuple-element.78.refs_3_.refs_2_), channel_id=1, source_target_pairs={{0,48},{16,0},{32,16},{48,32},{1,49},{17,1},{33,17},{49,33},{2,50}... | collective-permute-start | bytes 2064392 | tf_op jit(solution)/shard_map/ppermute | solution.py:530
  44.6 25.7 %copy-start.5 = (s32[32]{0:T(128)S(1)}, s32[32]{0:T(128)}, u32[]{:S(2)}) copy-start(s32[32]{0:T(128)} %live.4) | copy-start | bytes 388
  44.6 20.4 %collective-permute-start.4 = (bf16[384,768]{1,0:T(8,128)(2,1)}, bf16[384,768]{1,0:T(8,128)(2,1)S(1)}, u32[]{:S(2)}, u32[]{:S(2)}) collective-permute-start(bf16[384,768]{1,0:T(8,128)(2,1)} %get-tuple-element.57), channel_id=1, source_target_pairs={{0,1},{1,2},{2,3},{3,0},{4,5},{5,6},{6,7},{7,4},{8,9},{9,10},{10,1... | collective-permute-start | bytes 1769480 | tf_op jit(solution)/shard_map/ppermute | solution.py:530
  46.8 18.2 %collective-permute-start = (bf16[448,384]{1,0:T(8,128)(2,1)S(1)}, bf16[448,384]{1,0:T(8,128)(2,1)S(1)}, u32[]{:S(2)}, u32[]{:S(2)}) collective-permute-start(bf16[448,384]{1,0:T(8,128)(2,1)S(1)} %copy-done.4), channel_id=1, source_target_pairs={{64,0},{128,64},{192,128},{65,1},{129,65},{193,129},{66,2},{130,66... | collective-permute-start | bytes 1032200 | tf_op jit(solution)/shard_map/ppermute | solution.py:548
  48.1 16.9 %collective-permute-start.1 = (bf16[448,384]{1,0:T(8,128)(2,1)S(1)}, bf16[448,384]{1,0:T(8,128)(2,1)S(1)}, u32[]{:S(2)}, u32[]{:S(2)}) collective-permute-start(bf16[448,384]{1,0:T(8,128)(2,1)S(1)} %copy-done.4), channel_id=1, source_target_pairs={{192,0},{193,1},{194,2},{195,3},{196,4},{197,5},{198,6},{199,7},{2... | collective-permute-start | bytes 1032200 | tf_op jit(solution)/shard_map/ppermute | solution.py:548
  49.4 2.3 %copy-start = (bf16[384,6144]{1,0:T(8,128)(2,1)S(1)}, bf16[384,6144]{1,0:T(8,128)(2,1)}, u32[]{:S(2)}) copy-start(bf16[384,6144]{1,0:T(8,128)(2,1)} %refs_0_.3) | copy-start | bytes 14155780
  51.7 13.3 %copy-start.3 = (bf16[448,768]{1,0:T(8,128)(2,1)S(1)}, bf16[448,768]{1,0:T(8,128)(2,1)}, u32[]{:S(2)}) copy-start(bf16[448,768]{1,0:T(8,128)(2,1)} %get-tuple-element.78.refs_3_.refs_2_) | copy-start | bytes 2064388
  65.0 20.5 %copy-start.6 = (bf16[448,768]{1,0:T(8,128)(2,1)S(1)}, bf16[448,768]{1,0:T(8,128)(2,1)}, u32[]{:S(2)}) copy-start(bf16[448,768]{1,0:T(8,128)(2,1)} %param.8) | copy-start | bytes 2064388
  65.0 19.9 %collective-permute-start.6 = (bf16[448,768]{1,0:T(8,128)(2,1)S(1)}, bf16[448,768]{1,0:T(8,128)(2,1)S(1)}, u32[]{:S(2)}, u32[]{:S(2)}) collective-permute-start(bf16[448,768]{1,0:T(8,128)(2,1)S(1)} %copy-done.3), channel_id=1, source_target_pairs={{0,32},{16,48},{32,0},{48,16},{1,33},{17,49},{33,1},{49,17},{2,34}... | collective-permute-start | bytes 2064392 | tf_op jit(solution)/shard_map/ppermute | solution.py:530
  66.9 17.9 %collective-permute-start.8 = (bf16[448,768]{1,0:T(8,128)(2,1)S(1)}, bf16[448,768]{1,0:T(8,128)(2,1)S(1)}, u32[]{:S(2)}, u32[]{:S(2)}) collective-permute-start(bf16[448,768]{1,0:T(8,128)(2,1)S(1)} %collective-permute-done.2.refs_4_.refs_3_), channel_id=1, source_target_pairs={{0,8},{8,0},{1,9},{9,1},{2,10},{10,2},{3,11},{11,3},{4,12},{12,4},... | collective-permute-start | bytes 2064392 | tf_op jit(solution)/shard_map/ppermute | solution.py:530
  66.9 17.9 %collective-permute-start.9 = (bf16[448,768]{1,0:T(8,128)(2,1)S(1)}, bf16[448,768]{1,0:T(8,128)(2,1)S(1)}, u32[]{:S(2)}, u32[]{:S(2)}) collective-permute-start(bf16[448,768]{1,0:T(8,128)(2,1)S(1)} %collective-permute-done.3.refs_5_.refs_4_), channel_id=1, source_target_pairs={{0,8},{8,0},{1,9},{9,1},{2,10},{10,2},{3,11},{11,3},{4,12},{12,4},... | collective-permute-start | bytes 2064392 | tf_op jit(solution)/shard_map/ppermute | solution.py:530
  67.4 17.4 %collective-permute-start.7 = (bf16[384,768]{1,0:T(8,128)(2,1)S(1)}, bf16[384,768]{1,0:T(8,128)(2,1)S(1)}, u32[]{:S(2)}, u32[]{:S(2)}) collective-permute-start(bf16[384,768]{1,0:T(8,128)(2,1)S(1)} %get-tuple-element.64), channel_id=1, source_target_pairs={{0,3},{1,0},{2,1},{3,2},{4,7},{5,4},{6,5},{7,6},{8,11},{9,8},{10,9... | collective-permute-start | bytes 1769480 | tf_op jit(solution)/shard_map/ppermute | solution.py:530
  69.0 15.9 %collective-permute-start.5 = (bf16[448,384]{1,0:T(8,128)(2,1)S(1)}, bf16[448,384]{1,0:T(8,128)(2,1)S(1)}, u32[]{:S(2)}, u32[]{:S(2)}) collective-permute-start(bf16[448,384]{1,0:T(8,128)(2,1)S(1)} %copy-done.4), channel_id=1, source_target_pairs={{128,0},{192,64},{129,1},{193,65},{130,2},{194,66},{131,3},{195,67... | collective-permute-start | bytes 1032200 | tf_op jit(solution)/shard_map/ppermute | solution.py:548
  84.9 9.0 %collective-permute-start.10 = (bf16[448,768]{1,0:T(8,128)(2,1)S(1)}, bf16[448,768]{1,0:T(8,128)(2,1)S(1)}, u32[]{:S(2)}, u32[]{:S(2)}) collective-permute-start(bf16[448,768]{1,0:T(8,128)(2,1)S(1)} %copy-done.3), channel_id=1, source_target_pairs={{0,8},{8,0},{1,9},{9,1},{2,10},{10,2},{3,11},{11,3},{4,12},{12,4},... | collective-permute-start | bytes 2064392 | tf_op jit(solution)/shard_map/ppermute | solution.py:530
  85.0 8.9 %collective-permute-start.11 = (bf16[448,768]{1,0:T(8,128)(2,1)S(1)}, bf16[448,768]{1,0:T(8,128)(2,1)S(1)}, u32[]{:S(2)}, u32[]{:S(2)}) collective-permute-start(bf16[448,768]{1,0:T(8,128)(2,1)S(1)} %collective-permute-done.6.refs_5_.refs_2_), channel_id=1, source_target_pairs={{0,8},{8,0},{1,9},{9,1},{2,10},{10,2},{3,11},{11,3},{4,12},{12,4},... | collective-permute-start | bytes 2064392 | tf_op jit(solution)/shard_map/ppermute | solution.py:530
  85.5 39.2 %collective-permute-start.12 = (bf16[448,768]{1,0:T(8,128)(2,1)S(1)}, bf16[448,768]{1,0:T(8,128)(2,1)S(1)}, u32[]{:S(2)}, u32[]{:S(2)}) collective-permute-start(bf16[448,768]{1,0:T(8,128)(2,1)S(1)} %copy-done.6), channel_id=1, source_target_pairs={{0,248},{8,0},{16,8},{24,16},{32,24},{40,32},{48,40},{56,48},{64,5... | collective-permute-start | bytes 2064392 | tf_op jit(solution)/shard_map/ppermute | solution.py:530
  92.5 32.2 %collective-permute-start.13 = (bf16[384,768]{1,0:T(8,128)(2,1)S(1)}, bf16[384,768]{1,0:T(8,128)(2,1)S(1)}, u32[]{:S(2)}, u32[]{:S(2)}) collective-permute-start(bf16[384,768]{1,0:T(8,128)(2,1)S(1)} %get-tuple-element.93), channel_id=1, source_target_pairs={{0,2},{1,3},{2,0},{3,1},{4,6},{5,7},{6,4},{7,5},{8,10},{9,11},{10,... | collective-permute-start | bytes 1769480 | tf_op jit(solution)/shard_map/ppermute | solution.py:530
  108.4 18.8 %collective-permute-start.16 = (bf16[480,384]{1,0:T(8,128)(2,1)S(1)}, bf16[480,384]{1,0:T(8,128)(2,1)S(1)}, u32[]{:S(2)}, u32[]{:S(2)}) collective-permute-start(bf16[480,384]{1,0:T(8,128)(2,1)S(1)} %get-tuple-element.84), channel_id=1, source_target_pairs={{0,56},{8,64},{16,72},{24,80},{32,88},{40,96},{48,104},{56,112},{6... | collective-permute-start | bytes 1105928 | tf_op jit(solution)/shard_map/ppermute | solution.py:631
  109.7 17.5 %collective-permute-start.17 = (bf16[480,384]{1,0:T(8,128)(2,1)S(1)}, bf16[480,384]{1,0:T(8,128)(2,1)S(1)}, u32[]{:S(2)}, u32[]{:S(2)}) collective-permute-start(bf16[480,384]{1,0:T(8,128)(2,1)S(1)} %get-tuple-element.97), channel_id=1, source_target_pairs={{0,120},{8,128},{16,136},{24,144},{32,152},{40,160},{48,168},{56,1... | collective-permute-start | bytes 1105928 | tf_op jit(solution)/shard_map/ppermute | solution.py:631
  125.6 20.7 %copy-start.1 = (f32[64,768]{1,0:T(8,128)S(1)}, f32[64,768]{1,0:T(8,128)}, u32[]{:S(2)}) copy-start(f32[64,768]{1,0:T(8,128)} %table.1) | copy-start | bytes 589828
  125.6 43.7 %collective-permute-start.21 = (bf16[3,384,768]{2,1,0:T(8,128)(2,1)S(1)}, bf16[3,384,768]{2,1,0:T(8,128)(2,1)S(1)}, u32[]{:S(2)}, u32[]{:S(2)}) collective-permute-start(bf16[3,384,768]{2,1,0:T(8,128)(2,1)S(1)} %stack.41.refs_5_), channel_id=1, source_target_pairs={{0,8},{8,0},{1,9},{9,1},{2,10},{10,2},{3,11},{11,3},{4,12},{12,4},... | collective-permute-start | bytes 5308424 | tf_op jit(solution)/shard_map/ppermute | solution.py:530
  125.7 20.6 %collective-permute-start.14 = (bf16[480,384]{1,0:T(8,128)(2,1)S(1)}, bf16[480,384]{1,0:T(8,128)(2,1)S(1)}, u32[]{:S(2)}, u32[]{:S(2)}) collective-permute-start(bf16[480,384]{1,0:T(8,128)(2,1)S(1)} %get-tuple-element.95), channel_id=1, source_target_pairs={{0,248},{8,0},{16,8},{24,16},{32,24},{40,32},{48,40},{56,48},{64,5... | collective-permute-start | bytes 1105928 | tf_op jit(solution)/shard_map/ppermute | solution.py:631
  125.8 20.5 %collective-permute-start.15 = (bf16[480,384]{1,0:T(8,128)(2,1)S(1)}, bf16[480,384]{1,0:T(8,128)(2,1)S(1)}, u32[]{:S(2)}, u32[]{:S(2)}) collective-permute-start(bf16[480,384]{1,0:T(8,128)(2,1)S(1)} %get-tuple-element.96), channel_id=1, source_target_pairs={{0,184},{8,192},{16,200},{24,208},{32,216},{40,224},{48,232},{56,2... | collective-permute-start | bytes 1105928 | tf_op jit(solution)/shard_map/ppermute | solution.py:631
  148.6 17.1 %collective-permute-start.18 = (bf16[448,384]{1,0:T(8,128)(2,1)S(1)}, bf16[448,384]{1,0:T(8,128)(2,1)S(1)}, u32[]{:S(2)}, u32[]{:S(2)}) collective-permute-start(bf16[448,384]{1,0:T(8,128)(2,1)S(1)} %get-tuple-element.100.refs_0_), channel_id=1, source_target_pairs={{0,1},{1,2},{2,3},{3,0},{4,5},{5,6},{6,7},{7,4},{8,9},{9,10},{10,1... | collective-permute-start | bytes 1032200 | tf_op jit(solution)/shard_map/ppermute | solution.py:530
  150.4 15.3 %collective-permute-start.19 = (bf16[448,384]{1,0:T(8,128)(2,1)S(1)}, bf16[448,384]{1,0:T(8,128)(2,1)S(1)}, u32[]{:S(2)}, u32[]{:S(2)}) collective-permute-start(bf16[448,384]{1,0:T(8,128)(2,1)S(1)} %get-tuple-element.100.refs_0_), channel_id=1, source_target_pairs={{0,2},{1,3},{2,0},{3,1},{4,6},{5,7},{6,4},{7,5},{8,10},{9,11},{10,... | collective-permute-start | bytes 1032200 | tf_op jit(solution)/shard_map/ppermute | solution.py:530
  151.7 17.7 %collective-permute-start.20 = (bf16[448,384]{1,0:T(8,128)(2,1)S(1)}, bf16[448,384]{1,0:T(8,128)(2,1)S(1)}, u32[]{:S(2)}, u32[]{:S(2)}) collective-permute-start(bf16[448,384]{1,0:T(8,128)(2,1)S(1)} %get-tuple-element.100.refs_0_), channel_id=1, source_target_pairs={{0,3},{1,0},{2,1},{3,2},{4,7},{5,4},{6,5},{7,6},{8,11},{9,8},{10,9... | collective-permute-start | bytes 1032200 | tf_op jit(solution)/shard_map/ppermute | solution.py:530
  172.2 17.4 %collective-permute-start.22 = (bf16[448,768]{1,0:T(8,128)(2,1)S(1)}, bf16[448,768]{1,0:T(8,128)(2,1)S(1)}, u32[]{:S(2)}, u32[]{:S(2)}) collective-permute-start(bf16[448,768]{1,0:T(8,128)(2,1)S(1)} %project.3), channel_id=1, source_target_pairs={{0,4},{4,0},{1,5},{5,1},{2,6},{6,2},{3,7},{7,3},{8,12},{12,8},{9,1... | collective-permute-start | bytes 2064392 | tf_op jit(solution)/shard_map/ppermute | solution.py:530

commit v3 on v2

--- a/solution.py
+++ b/solution.py
@@ -111,7 +111,13 @@
                 place_copy(j, own_place).start()
             else:
 
-                @pl.when(live[groups[p]] == 1)
+                wanted = live[groups[p]] == 1
+                if middle and p in EARLY:
+                    wanted = wanted & active(0)
+                if call == "late":
+                    wanted = wanted & (active(0) | (groups[p] < mine))
+
+                @pl.when(wanted)
                 def _():
                     place_copy(j, base + live_before(groups[p], part)).start()
 
@@ -130,32 +136,17 @@
 
         if early:
             place_copy(0, own_place).wait()
-        for k in range(8):
-            if k < 3 and call != "late":
-                there = k < n_early
-                if early:
-                    there = there & (k != own_place)
-            elif k >= 3 and not early:
-                there = k - 3 < n_later
-            else:
-                continue
-
-            @pl.when(there)
-            def _():
-                place_copy(0, k).wait()
+            for k in range(len(EARLY)):
+
+                @pl.when((k < n_early) & (k != own_place))
+                def _():
+                    place_copy(0, k).wait()
 
         for i in range(many):
 
             @pl.when(active(i))
             def _():
                 raw_copy(i).wait()
-
-        for k in range(len(resumed)):
-
-            @pl.when(active(resumed[k]))
-            def _():
-                for copy in state_copies(k):
-                    copy.wait()
 
         def one(i, unused):
             @pl.when(here + step_of(i) <= 3)
@@ -185,9 +176,21 @@
             split, base = jnp.int32(0), 3
         chunks = (count + 1) // 2
 
+        waits = (i == 0) | jnp.logical_not(active(0))
+
+        def place_of(k):
+            return jnp.where(k < split, k, base + k - split)
+
+        def arrive(t):
+            if not early:
+                for k in (2 * t, 2 * t + 1):
+
+                    @pl.when(waits & (k < count))
+                    def _():
+                        place_copy(0, place_of(k)).wait()
+
         def at(k):
-            k = jnp.maximum(jnp.minimum(k, count - 1), 0)
-            place = jnp.where(k < split, k, base + k - split)
+            place = place_of(jnp.maximum(jnp.minimum(k, count - 1), 0))
             return pl.ds(pl.multiple_of(place * ROWS, 64), ROWS)
 
         for head in range(HEADS_HERE):
@@ -231,9 +234,18 @@
             acc[i, head] = acc[i, head] * jnp.concatenate([shrink, shrink], axis=1) + weighted
             top[i, head] = new
 
+        arrive(0)
+
         @pl.when(chunks > 0)
         def _():
             held[...] = scores_of(0, 0)
+
+        for k in range(len(resumed)):
+
+            @pl.when(i == resumed[k])
+            def _():
+                for copy in state_copies(k):
+                    copy.wait()
 
         def chunk(t, unused):
             scores = held[...]
@@ -241,6 +253,7 @@
             absorb(t, 0, scores)
             scores = scores_of(t, 2)
             absorb(t, 1, following)
+            arrive(t + 1)
             held[...] = scores_of(t + 1, 0)
             absorb(t, 2, scores)
             return 0
@@ -447,14 +460,43 @@
     )(hidden, near, arrived, gate)
 
 
+def pack_kernel(ids, keys, values, weight, pair, piece, sem):
+    width = piece.shape[1]
+    at = pl.ds(pl.multiple_of(ids[4] * width, width), width)
+    copy = pltpu.make_async_copy(weight.at[:, at], piece, sem)
+    copy.start()
+    pair[:, :WIDTH] = keys[...]
+    pair[:, WIDTH:] = values[...]
+    copy.wait()
+
+
+def pack(ids, keys, values, weight):
+    vmem = pl.BlockSpec(memory_space=pltpu.VMEM)
+    return pl.pallas_call(
+        pack_kernel,
+        out_shape=[
+            jax.ShapeDtypeStruct((ROWS, 2 * WIDTH), jnp.bfloat16),
+            jax.ShapeDtypeStruct((weight.shape[0], weight.shape[1] // 8), jnp.bfloat16),
+        ],
+        in_specs=[
+            pl.BlockSpec(memory_space=pltpu.SMEM),
+            vmem,
+            vmem,
+            pl.BlockSpec(memory_space=pl.ANY),
+        ],
+        out_specs=[vmem] * 2,
+        scratch_shapes=[pltpu.SemaphoreType.DMA],
+        compiler_params=pltpu.CompilerParams(vmem_limit_bytes=WHOLE_VMEM),
+        name="pack",
+    )(ids, keys, values, weight)
+
+
 def copies_kernel(plan, ids, *refs):
     inputs, outs, sem = refs[: plan[0]], refs[plan[0] : -1], refs[-1]
     copies = []
     for n, (kind, source, target, number) in enumerate(plan[1]):
         src, dst = inputs[source], outs[target]
-        if kind == "beside":
-            dst = dst.at[:, pl.ds(number * src.shape[1], src.shape[1])]
-        elif kind == "columns":
+        if kind == "columns":
             width = dst.shape[1]
             src = src.at[:, pl.ds(pl.multiple_of(ids[number] * width, width), width)]
         else:
@@ -466,7 +508,7 @@
         copy.wait()
 
 
-def copied(name, ids, inputs, shapes, plan, vmem):
+def copied(name, ids, inputs, shapes, plan):
     anywhere = pl.BlockSpec(memory_space=pl.ANY)
     return pl.pallas_call(
         functools.partial(copies_kernel, (len(inputs), plan)),
@@ -474,7 +516,7 @@
         in_specs=[pl.BlockSpec(memory_space=pltpu.SMEM)] + [anywhere] * len(inputs),
         out_specs=[anywhere] * len(shapes),
         scratch_shapes=[pltpu.SemaphoreType.DMA((len(plan),))],
-        compiler_params=pltpu.CompilerParams(vmem_limit_bytes=vmem),
+        compiler_params=pltpu.CompilerParams(vmem_limit_bytes=SMALL_VMEM),
         name=name,
     )(ids, *inputs)
 
@@ -547,21 +589,13 @@
     def to_level(value, d):
         return lax.ppermute(value, "z", [(i, i - d) for i in range(d, 4)])
 
-    pair, piece_one = copied(
-        "pack",
-        ids,
-        [key_rows, values, out_weight],
-        [(ROWS, 2 * WIDTH), column_block],
-        (("beside", 0, 0, 0), ("beside", 1, 0, 1), ("columns", 2, 1, 4)),
-        WHOLE_VMEM,
-    )
+    pair, piece_one = pack(ids, key_rows, values, out_weight)
     piece_two, piece_three, weight_near, weight_far = copied(
         "columns",
         ids,
         [out_weight],
         [column_block] * 4,
         tuple(("columns", 0, k, 5 + k) for k in range(4)),
-        SMALL_VMEM,
     )
     (
         next_one,
@@ -622,7 +656,6 @@
     across_there, pair_there = around(across, "c", 1), around(pair, "c", 1)
     pairs = [pair, below, above, across, pair_there, below_there, above_there, across_there]
     piece_two = around(piece_two, "x", 2)
-    hidden_next = around(hidden, SLOT, -1)
 
     def back(share, d):
         pairs_back = [
@@ -639,20 +672,21 @@
     three, zero = attend(
         "late", ids, live_later, noise_level, [next_three, queries], pairs, state_three + state_own
     )
-    three, zero, hidden_next, piece_two = together(three, zero, hidden_next, piece_two)
+    three, zero, piece_two = together(three, zero, piece_two)
     (fetched,) = copied(
         "stack",
         ids,
         [piece_one, piece_two, piece_three],
         [(3, *column_block)],
         tuple(("stack", k, 0, k) for k in range(3)),
-        SMALL_VMEM,
     )
     swapped = around(fetched, "c", 1)
     attended, gate_row = combine(
         ids, level_table, back(zero, 0), back(three, 3), values_two, sides_two
     )
 
+    attended, hidden = together(attended, hidden)
+    hidden_next = around(hidden, SLOT, -1)
     rows = [attended] + [around(attended, "x", step) for step in (1, 2, 3)]
     far_sum = project(True, ids, rows, weight_far, fetched, swapped)
     arrived = around(far_sum, "w", 1)

time: 192 us -> 153 us (0.80)
  the two profiles are of different devices: /device:TPU:6 before, /device:TPU:25 now
where the time goes in v3:
time: 153 us; the launch traced here: 150 us
  Pallas kernels  57.7 us (38%)
  waiting for transfers between devices  55.4 us (36%)
  starting transfers between devices  33.3 us (22%)
  local copies, waits for them, and re-layouts  2.98 us (2%)
    pallas_call x3, Pallas kernels, attend(): pl.pallas_call(functools.partial(attend_kernel, call), out_shape=out_shap...  41.7 us
    ppermute x16, waiting for transfers between devices, around(): lax.ppermute(value, axis, [(i, (i + steps) % count) for i in range(count)])  31.2 us
    ppermute x16, starting transfers between devices, around(): lax.ppermute(value, axis, [(i, (i + steps) % count) for i in range(count)])  19.6 us
    ppermute x3, waiting for transfers between devices, to_level(): return lax.ppermute(value, 'z', [(i, i - d) for i in range(d, 4)])  12.9 us
    ppermute x4, waiting for transfers between devices, back(): return lax.ppermute(share, SLOT, pairs_back)  11.3 us
    ppermute x4, starting transfers between devices, back(): return lax.ppermute(share, SLOT, pairs_back)  9.77 us
    pallas_call x2, Pallas kernels, project(): pl.pallas_call(functools.partial(project_kernel, far), out_shape=jax.Shap...  5.62 us
    ppermute x3, starting transfers between devices, to_level(): return lax.ppermute(value, 'z', [(i, i - d) for i in range(d, 4)])  3.86 us
  transfers between devices with their start and end apart: 23, of which 10 were waited for; matrix products, arithmetic and copies ran while one was open for 0% of the time, Pallas kernels for 35%

profile of v3, /device:TPU:25, one launch (start us, length us, event | category | flops | bytes accessed | tf_op | source)
XLA Modules:
  0.0 150.2 jit_solution(18388528395628630233)
XLA Ops:
  0.0 0.6 stack.40.ids
  0.6 3.3 %pack.1 = (bf16[448,768]{1,0:T(8,128)(2,1)}, bf16[384,768]{1,0:T(8,128)(2,1)}) custom-call(s32[9]{0:T(128)} %stack.40.ids, bf16[448,384]{1,0:T(8,128)(2,1)} %keys.1, bf16[448,384]{1,0:T(8,128)(2,1)} %values.1, bf16[384,6144]{1,0:T(8,128)(2,1)} %refs_0_.1), custom_call_target="tpu_custom_call" | custom-call | tf_op jit(solution)/shard_map/pack/pallas_call | solution.py:475
  3.9 0.5 collective-permute-start.3
  4.4 2.2 %collective-permute-start.2 = (bf16[448,768]{1,0:T(8,128)(2,1)}, bf16[448,768]{1,0:T(8,128)(2,1)S(1)}, u32[]{:S(2)}, u32[]{:S(2)}) collective-permute-start(bf16[448,768]{1,0:T(8,128)(2,1)} %get-tuple-element.79.refs_3_.refs_2_), channel_id=1, source_target_pairs={{0,16},{16,32},{32,48},{48,0},{1,17},{17,33},{33,49},{49,1},{2,18}... | collective-permute-start | bytes 2064392 | tf_op jit(solution)/shard_map/ppermute | solution.py:572
  6.6 1.2 collective-permute-start.4
  7.9 1.3 collective-permute-start
  9.2 1.3 collective-permute-start.1
  10.5 0.0 copy-start
  10.5 2.3 %copy-done = bf16[384,6144]{1,0:T(8,128)(2,1)S(1)} copy-done((bf16[384,6144]{1,0:T(8,128)(2,1)S(1)}, bf16[384,6144]{1,0:T(8,128)(2,1)}, u32[]{:S(2)}) %copy-start) | copy-done | bytes 4718616
  12.8 0.8 columns.1
  14.3 12.9 %collective-permute-done.refs_0_.refs_1_ = bf16[448,384]{1,0:T(8,128)(2,1)S(1)} collective-permute-done((bf16[448,384]{1,0:T(8,128)(2,1)S(1)}, bf16[448,384]{1,0:T(8,128)(2,1)S(1)}, u32[]{:S(2)}, u32[]{:S(2)}) %collective-permute-start) | collective-permute-done | bytes 344096 | tf_op jit(solution)/shard_map/ppermute | solution.py:590
  27.2 1.3 collective-permute-start.5
  28.5 1.5 %collective-permute-start.7 = (bf16[384,768]{1,0:T(8,128)(2,1)S(1)}, bf16[384,768]{1,0:T(8,128)(2,1)S(1)}, u32[]{:S(2)}, u32[]{:S(2)}) collective-permute-start(bf16[384,768]{1,0:T(8,128)(2,1)S(1)} %get-tuple-element.65), channel_id=1, source_target_pairs={{0,3},{1,0},{2,1},{3,2},{4,7},{5,4},{6,5},{7,6},{8,11},{9,8},{10,9... | collective-permute-start | bytes 1769480 | tf_op jit(solution)/shard_map/ppermute | solution.py:572
  30.1 2.2 %collective-permute-start.8 = (bf16[448,768]{1,0:T(8,128)(2,1)S(1)}, bf16[448,768]{1,0:T(8,128)(2,1)S(1)}, u32[]{:S(2)}, u32[]{:S(2)}) collective-permute-start(bf16[448,768]{1,0:T(8,128)(2,1)S(1)} %collective-permute-done.2.refs_4_.refs_3_), channel_id=1, source_target_pairs={{0,8},{8,0},{1,9},{9,1},{2,10},{10,2},{3,11},{11,3},{4,12},{12,4},... | collective-permute-start | bytes 2064392 | tf_op jit(solution)/shard_map/ppermute | solution.py:572
  32.3 0.1 collective-permute-start.9
  32.4 12.7 %attend_early.1 = (f32[3,448,256]{2,1,0:T(8,128)S(1)}, f32[3,448,128]{2,1,0:T(8,128)S(1)}, f32[3,448,256]{2,1,0:T(8,128)S(1)}, f32[3,448,128]{2,1,0:T(8,128)S(1)...) custom-call(s32[9]{0:T(128)S(1)} %copy-done.2, s32[32]{0:T(128)S(1)} %copy-done.5, s32[1]{0:T(128)S(6)} %copy.9.level, ...), custom_call_target="tpu_custom_call" | custom-call | flops 11098128384 | bytes 8000000 | tf_op jit(solution)/shard_map/attend_early/pallas_call | solution.py:311
  45.1 1.2 collective-permute-done.6.refs_5_.refs_2_
  46.3 3.1 %collective-permute-start.10 = (bf16[448,768]{1,0:T(8,128)(2,1)S(1)}, bf16[448,768]{1,0:T(8,128)(2,1)S(1)}, u32[]{:S(2)}, u32[]{:S(2)}) collective-permute-start(bf16[448,768]{1,0:T(8,128)(2,1)S(1)} %copy-done.3), channel_id=1, source_target_pairs={{0,8},{8,0},{1,9},{9,1},{2,10},{10,2},{3,11},{11,3},{4,12},{12,4},... | collective-permute-start | bytes 2064392 | tf_op jit(solution)/shard_map/ppermute | solution.py:572
  49.5 0.1 collective-permute-start.11
  49.5 1.5 %collective-permute-start.12 = (bf16[384,768]{1,0:T(8,128)(2,1)S(1)}, bf16[384,768]{1,0:T(8,128)(2,1)S(1)}, u32[]{:S(2)}, u32[]{:S(2)}) collective-permute-start(bf16[384,768]{1,0:T(8,128)(2,1)S(1)} %get-tuple-element.93), channel_id=1, source_target_pairs={{0,2},{1,3},{2,0},{3,1},{4,6},{5,7},{6,4},{7,5},{8,10},{9,11},{10,... | collective-permute-start | bytes 1769480 | tf_op jit(solution)/shard_map/ppermute | solution.py:572
  51.1 0.1 collective-permute-done.10.refs_6_.refs_3_
  51.2 1.0 collective-permute-done.11.refs_9_.refs_6_
  52.2 15.9 %attend_middle.1 = (bf16[480,384]{1,0:T(8,128)(2,1)S(1)}, bf16[480,384]{1,0:T(8,128)(2,1)S(1)}) custom-call(s32[9]{0:T(128)S(1)} %copy-done.2, s32[32]{0:T(128)S(1)} %copy-done.5, s32[1]{0:T(128)S(6)} %copy.9.level, bf16[448,384]{1,0:T(8,128)(2,1)S(1)} %collective-permute-done.5.refs_0_, bf16[448,384]{1,0:T(8,128)(2,1)S(1)} %collective-permute-done.refs_0_.refs_1_, ...), custom_call_target="tpu_custom_call" | custom-call | flops 11098128384 | bytes 8000000 | tf_op jit(solution)/shard_map/attend_middle/pallas_call | solution.py:311
  68.1 7.1 %collective-permute-start.15 = (bf16[480,384]{1,0:T(8,128)(2,1)S(1)}, bf16[480,384]{1,0:T(8,128)(2,1)S(1)}, u32[]{:S(2)}, u32[]{:S(2)}) collective-permute-start(bf16[480,384]{1,0:T(8,128)(2,1)S(1)} %get-tuple-element.85), channel_id=1, source_target_pairs={{0,56},{8,64},{16,72},{24,80},{32,88},{40,96},{48,104},{56,112},{6... | collective-permute-start | bytes 1105928 | tf_op jit(solution)/shard_map/ppermute | solution.py:664
  75.2 1.3 collective-permute-start.16
  76.5 13.2 %attend_late.1 = (bf16[480,384]{1,0:T(8,128)(2,1)S(1)}, bf16[480,384]{1,0:T(8,128)(2,1)S(1)}) custom-call(s32[9]{0:T(128)S(1)} %copy-done.2, s32[32]{0:T(128)S(1)} %copy-done.5, s32[1]{0:T(128)S(6)} %copy.9.level, bf16[448,384]{1,0:T(8,128)(2,1)S(1)} %collective-permute-done.1.refs_1_.refs_0_, bf16[448,384]{1,0:T(8,128)(2,1)S(1)} %copy-done.4, ...), custom_call_target="tpu_custom_call" | custom-call | flops 11098128384 | bytes 8000000 | tf_op jit(solution)/shard_map/attend_late/pallas_call | solution.py:311
  89.6 0.1 collective-permute-start.13
  89.7 1.3 collective-permute-start.14
  91.1 0.9 stack.41.refs_5_
  92.0 0.0 copy-start.1
  92.0 2.0 %collective-permute-start.21 = (bf16[3,384,768]{2,1,0:T(8,128)(2,1)S(1)}, bf16[3,384,768]{2,1,0:T(8,128)(2,1)S(1)}, u32[]{:S(2)}, u32[]{:S(2)}) collective-permute-start(bf16[3,384,768]{2,1,0:T(8,128)(2,1)S(1)} %stack.41.refs_5_), channel_id=1, source_target_pairs={{0,8},{8,0},{1,9},{9,1},{2,10},{10,2},{3,11},{11,3},{4,12},{12,4},... | collective-permute-start | bytes 5308424 | tf_op jit(solution)/shard_map/ppermute | solution.py:572
  94.0 1.5 %combine_two.1 = (f32[448,384]{1,0:T(8,128)S(1)}, f32[448,128]{1,0:T(8,128)S(1)}) custom-call(s32[9]{0:T(128)S(1)} %copy-done.2, bf16[480,384]{1,0:T(8,128)(2,1)S(1)} %collective-permute-done.15.one, bf16[480,384]{1,0:T(8,128)(2,1)S(1)} %collective-permute-done.16.two), custom_call_target="tpu_custom_call" | custom-call | flops 99999997952 | bytes 200000000 | tf_op jit(solution)/shard_map/combine_two/pallas_call | solution.py:391
  95.5 0.0 copy-start.6
  95.5 8.2 %collective-permute-done.13.zero = bf16[480,384]{1,0:T(8,128)(2,1)S(1)} collective-permute-done((bf16[480,384]{1,0:T(8,128)(2,1)S(1)}, bf16[480,384]{1,0:T(8,128)(2,1)S(1)}, u32[]{:S(2)}, u32[]{:S(2)}) %collective-permute-start.13) | collective-permute-done | bytes 368672 | tf_op jit(solution)/shard_map/ppermute | solution.py:664
  103.8 3.0 %collective-permute-done.14.three = bf16[480,384]{1,0:T(8,128)(2,1)S(1)} collective-permute-done((bf16[480,384]{1,0:T(8,128)(2,1)S(1)}, bf16[480,384]{1,0:T(8,128)(2,1)S(1)}, u32[]{:S(2)}, u32[]{:S(2)}) %collective-permute-start.14) | collective-permute-done | bytes 368672 | tf_op jit(solution)/shard_map/ppermute | solution.py:664
  106.8 2.2 %combine.1 = (bf16[448,384]{1,0:T(8,128)(2,1)S(1)}, f32[1,768]{1,0:T(1,128)S(1)}) custom-call(s32[9]{0:T(128)S(1)} %copy-done.2, f32[64,768]{1,0:T(8,128)S(1)} %copy-done.1, bf16[480,384]{1,0:T(8,128)(2,1)S(1)} %collective-permute-done.13.zero, bf16[480,384]{1,0:T(8,128)(2,1)S(1)} %collective-permute-done.14.three, f32[448,384]{1,0:T(8,128)S(1)} %get-tuple-element.97.values, ...), custom_call_target="tpu_custom_call" | custom-call | tf_op jit(solution)/shard_map/combine/pallas_call | solution.py:431
  109.0 1.3 collective-permute-start.20
  110.4 1.4 collective-permute-start.19
  111.7 0.0 collective-permute-start.18
  111.8 2.3 %collective-permute-start.17 = (bf16[448,768]{1,0:T(8,128)(2,1)S(1)}, bf16[448,768]{1,0:T(8,128)(2,1)S(1)}, u32[]{:S(2)}, u32[]{:S(2)}) collective-permute-start(bf16[448,768]{1,0:T(8,128)(2,1)S(1)} %copy-done.6), channel_id=1, source_target_pairs={{0,248},{8,0},{16,8},{24,16},{32,24},{40,32},{48,40},{56,48},{64,5... | collective-permute-start | bytes 2064392 | tf_op jit(solution)/shard_map/ppermute | solution.py:572
  114.1 3.0 %collective-permute-done.20.refs_3_ = bf16[448,384]{1,0:T(8,128)(2,1)S(1)} collective-permute-done((bf16[448,384]{1,0:T(8,128)(2,1)S(1)}, bf16[448,384]{1,0:T(8,128)(2,1)S(1)}, u32[]{:S(2)}, u32[]{:S(2)}) %collective-permute-start.20) | collective-permute-done | bytes 344096 | tf_op jit(solution)/shard_map/ppermute | solution.py:572
  117.1 2.5 %collective-permute-done.19.refs_2_ = bf16[448,384]{1,0:T(8,128)(2,1)S(1)} collective-permute-done((bf16[448,384]{1,0:T(8,128)(2,1)S(1)}, bf16[448,384]{1,0:T(8,128)(2,1)S(1)}, u32[]{:S(2)}, u32[]{:S(2)}) %collective-permute-start.19) | collective-permute-done | bytes 344096 | tf_op jit(solution)/shard_map/ppermute | solution.py:572
  119.6 9.6 %collective-permute-done.18.refs_1_ = bf16[448,384]{1,0:T(8,128)(2,1)S(1)} collective-permute-done((bf16[448,384]{1,0:T(8,128)(2,1)S(1)}, bf16[448,384]{1,0:T(8,128)(2,1)S(1)}, u32[]{:S(2)}, u32[]{:S(2)}) %collective-permute-start.18) | collective-permute-done | bytes 344096 | tf_op jit(solution)/shard_map/ppermute | solution.py:572
  129.2 2.8 %project.3 = bf16[448,768]{1,0:T(8,128)(2,1)S(1)} custom-call(s32[9]{0:T(128)S(1)} %copy-done.2, bf16[448,384]{1,0:T(8,128)(2,1)S(1)} %get-tuple-element.102.refs_0_, bf16[448,384]{1,0:T(8,128)(2,1)S(1)} %collective-permute-done.18.refs_1_, bf16[448,384]{1,0:T(8,128)(2,1)S(1)} %collective-permute-done.19.refs_2_, ...), custom_call_target="tpu_custom_call" | custom-call | flops 1056964608 | bytes 5000000 | tf_op jit(solution)/shard_map/project/pallas_call | solution.py:556
  132.1 0.1 collective-permute-start.22
  132.2 2.8 %project.2.near = f32[448,768]{1,0:T(8,128)S(1)} custom-call(s32[9]{0:T(128)S(1)} %copy-done.2, bf16[448,384]{1,0:T(8,128)(2,1)S(1)} %get-tuple-element.102.refs_0_, bf16[448,384]{1,0:T(8,128)(2,1)S(1)} %collective-permute-done.18.refs_1_, bf16[448,384]{1,0:T(8,128)(2,1)S(1)} %collective-permute-done.19.refs_2_, ...), custom_call_target="tpu_custom_call" | custom-call | flops 1056964608 | bytes 5000000 | tf_op jit(solution)/shard_map/project/pallas_call | solution.py:556
  135.0 13.7 %collective-permute-done.22.arrived = bf16[448,768]{1,0:T(8,128)(2,1)S(1)} collective-permute-done((bf16[448,768]{1,0:T(8,128)(2,1)S(1)}, bf16[448,768]{1,0:T(8,128)(2,1)S(1)}, u32[]{:S(2)}, u32[]{:S(2)}) %collective-permute-start.22) | collective-permute-done | bytes 688160 | tf_op jit(solution)/shard_map/ppermute | solution.py:572
  148.7 1.6 %finish.1 = bf16[448,768]{1,0:T(8,128)(2,1)} custom-call(bf16[448,768]{1,0:T(8,128)(2,1)S(1)} %collective-permute-done.17.hidden, f32[448,768]{1,0:T(8,128)S(1)} %project.2.near, bf16[448,768]{1,0:T(8,128)(2,1)S(1)} %collective-permute-done.22.arrived, f32[1,768]{1,0:T(1,128)S(1)} %get-tuple-element.108.gate), custom_call_target="tpu_custom_call" | custom-call | tf_op jit(solution)/shard_map/finish/pallas_call | solution.py:452
  (24 shorter events, 0.1 us)
Async XLA Ops:
  0.6 7.2 %copy-start.4 = (bf16[448,384]{1,0:T(8,128)(2,1)S(1)}, bf16[448,384]{1,0:T(8,128)(2,1)}, u32[]{:S(2)}) copy-start(bf16[448,384]{1,0:T(8,128)(2,1)} %refs_1_) | copy-start | bytes 1032196
  0.6 9.8 %copy-start.2 = (s32[9]{0:T(128)S(1)}, s32[9]{0:T(128)}, u32[]{:S(2)}) copy-start(s32[9]{0:T(128)} %stack.40.ids) | copy-start | bytes 112
  3.9 23.3 %collective-permute-start.3 = (bf16[448,768]{1,0:T(8,128)(2,1)}, bf16[448,768]{1,0:T(8,128)(2,1)S(1)}, u32[]{:S(2)}, u32[]{:S(2)}) collective-permute-start(bf16[448,768]{1,0:T(8,128)(2,1)} %get-tuple-element.79.refs_3_.refs_2_), channel_id=1, source_target_pairs={{0,48},{16,0},{32,16},{48,32},{1,49},{17,1},{33,17},{49,33},{2,50}... | collective-permute-start | bytes 2064392 | tf_op jit(solution)/shard_map/ppermute | solution.py:572
  4.4 22.8 %collective-permute-start.2 = (bf16[448,768]{1,0:T(8,128)(2,1)}, bf16[448,768]{1,0:T(8,128)(2,1)S(1)}, u32[]{:S(2)}, u32[]{:S(2)}) collective-permute-start(bf16[448,768]{1,0:T(8,128)(2,1)} %get-tuple-element.79.refs_3_.refs_2_), channel_id=1, source_target_pairs={{0,16},{16,32},{32,48},{48,0},{1,17},{17,33},{33,49},{49,1},{2,18}... | collective-permute-start | bytes 2064392 | tf_op jit(solution)/shard_map/ppermute | solution.py:572
  6.6 25.7 %copy-start.5 = (s32[32]{0:T(128)S(1)}, s32[32]{0:T(128)}, u32[]{:S(2)}) copy-start(s32[32]{0:T(128)} %live.4) | copy-start | bytes 388
  6.6 20.6 %collective-permute-start.4 = (bf16[384,768]{1,0:T(8,128)(2,1)}, bf16[384,768]{1,0:T(8,128)(2,1)S(1)}, u32[]{:S(2)}, u32[]{:S(2)}) collective-permute-start(bf16[384,768]{1,0:T(8,128)(2,1)} %get-tuple-element.58), channel_id=1, source_target_pairs={{0,1},{1,2},{2,3},{3,0},{4,5},{5,6},{6,7},{7,4},{8,9},{9,10},{10,1... | collective-permute-start | bytes 1769480 | tf_op jit(solution)/shard_map/ppermute | solution.py:572
  7.9 19.4 %collective-permute-start = (bf16[448,384]{1,0:T(8,128)(2,1)S(1)}, bf16[448,384]{1,0:T(8,128)(2,1)S(1)}, u32[]{:S(2)}, u32[]{:S(2)}) collective-permute-start(bf16[448,384]{1,0:T(8,128)(2,1)S(1)} %copy-done.4), channel_id=1, source_target_pairs={{64,0},{128,64},{192,128},{65,1},{129,65},{193,129},{66,2},{130,66... | collective-permute-start | bytes 1032200 | tf_op jit(solution)/shard_map/ppermute | solution.py:590
  9.2 18.1 %collective-permute-start.1 = (bf16[448,384]{1,0:T(8,128)(2,1)S(1)}, bf16[448,384]{1,0:T(8,128)(2,1)S(1)}, u32[]{:S(2)}, u32[]{:S(2)}) collective-permute-start(bf16[448,384]{1,0:T(8,128)(2,1)S(1)} %copy-done.4), channel_id=1, source_target_pairs={{192,0},{193,1},{194,2},{195,3},{196,4},{197,5},{198,6},{199,7},{2... | collective-permute-start | bytes 1032200 | tf_op jit(solution)/shard_map/ppermute | solution.py:590
  10.5 2.3 %copy-start = (bf16[384,6144]{1,0:T(8,128)(2,1)S(1)}, bf16[384,6144]{1,0:T(8,128)(2,1)}, u32[]{:S(2)}) copy-start(bf16[384,6144]{1,0:T(8,128)(2,1)} %refs_0_.1) | copy-start | bytes 14155780
  12.8 17.3 %copy-start.3 = (bf16[448,768]{1,0:T(8,128)(2,1)S(1)}, bf16[448,768]{1,0:T(8,128)(2,1)}, u32[]{:S(2)}) copy-start(bf16[448,768]{1,0:T(8,128)(2,1)} %get-tuple-element.79.refs_3_.refs_2_) | copy-start | bytes 2064388
  27.2 17.9 %collective-permute-start.5 = (bf16[448,384]{1,0:T(8,128)(2,1)S(1)}, bf16[448,384]{1,0:T(8,128)(2,1)S(1)}, u32[]{:S(2)}, u32[]{:S(2)}) collective-permute-start(bf16[448,384]{1,0:T(8,128)(2,1)S(1)} %copy-done.4), channel_id=1, source_target_pairs={{128,0},{192,64},{129,1},{193,65},{130,2},{194,66},{131,3},{195,67... | collective-permute-start | bytes 1032200 | tf_op jit(solution)/shard_map/ppermute | solution.py:590
  28.5 16.6 %collective-permute-start.7 = (bf16[384,768]{1,0:T(8,128)(2,1)S(1)}, bf16[384,768]{1,0:T(8,128)(2,1)S(1)}, u32[]{:S(2)}, u32[]{:S(2)}) collective-permute-start(bf16[384,768]{1,0:T(8,128)(2,1)S(1)} %get-tuple-element.65), channel_id=1, source_target_pairs={{0,3},{1,0},{2,1},{3,2},{4,7},{5,4},{6,5},{7,6},{8,11},{9,8},{10,9... | collective-permute-start | bytes 1769480 | tf_op jit(solution)/shard_map/ppermute | solution.py:572
  30.1 16.2 %collective-permute-start.6 = (bf16[448,768]{1,0:T(8,128)(2,1)S(1)}, bf16[448,768]{1,0:T(8,128)(2,1)S(1)}, u32[]{:S(2)}, u32[]{:S(2)}) collective-permute-start(bf16[448,768]{1,0:T(8,128)(2,1)S(1)} %copy-done.3), channel_id=1, source_target_pairs={{0,32},{16,48},{32,0},{48,16},{1,33},{17,49},{33,1},{49,17},{2,34}... | collective-permute-start | bytes 2064392 | tf_op jit(solution)/shard_map/ppermute | solution.py:572
  30.1 16.2 %collective-permute-start.8 = (bf16[448,768]{1,0:T(8,128)(2,1)S(1)}, bf16[448,768]{1,0:T(8,128)(2,1)S(1)}, u32[]{:S(2)}, u32[]{:S(2)}) collective-permute-start(bf16[448,768]{1,0:T(8,128)(2,1)S(1)} %collective-permute-done.2.refs_4_.refs_3_), channel_id=1, source_target_pairs={{0,8},{8,0},{1,9},{9,1},{2,10},{10,2},{3,11},{11,3},{4,12},{12,4},... | collective-permute-start | bytes 2064392 | tf_op jit(solution)/shard_map/ppermute | solution.py:572
  32.3 14.0 %collective-permute-start.9 = (bf16[448,768]{1,0:T(8,128)(2,1)S(1)}, bf16[448,768]{1,0:T(8,128)(2,1)S(1)}, u32[]{:S(2)}, u32[]{:S(2)}) collective-permute-start(bf16[448,768]{1,0:T(8,128)(2,1)S(1)} %collective-permute-done.3.refs_5_.refs_4_), channel_id=1, source_target_pairs={{0,8},{8,0},{1,9},{9,1},{2,10},{10,2},{3,11},{11,3},{4,12},{12,4},... | collective-permute-start | bytes 2064392 | tf_op jit(solution)/shard_map/ppermute | solution.py:572
  46.3 4.9 %collective-permute-start.10 = (bf16[448,768]{1,0:T(8,128)(2,1)S(1)}, bf16[448,768]{1,0:T(8,128)(2,1)S(1)}, u32[]{:S(2)}, u32[]{:S(2)}) collective-permute-start(bf16[448,768]{1,0:T(8,128)(2,1)S(1)} %copy-done.3), channel_id=1, source_target_pairs={{0,8},{8,0},{1,9},{9,1},{2,10},{10,2},{3,11},{11,3},{4,12},{12,4},... | collective-permute-start | bytes 2064392 | tf_op jit(solution)/shard_map/ppermute | solution.py:572
  49.5 2.8 %collective-permute-start.11 = (bf16[448,768]{1,0:T(8,128)(2,1)S(1)}, bf16[448,768]{1,0:T(8,128)(2,1)S(1)}, u32[]{:S(2)}, u32[]{:S(2)}) collective-permute-start(bf16[448,768]{1,0:T(8,128)(2,1)S(1)} %collective-permute-done.6.refs_5_.refs_2_), channel_id=1, source_target_pairs={{0,8},{8,0},{1,9},{9,1},{2,10},{10,2},{3,11},{11,3},{4,12},{12,4},... | collective-permute-start | bytes 2064392 | tf_op jit(solution)/shard_map/ppermute | solution.py:572
  49.5 40.1 %collective-permute-start.12 = (bf16[384,768]{1,0:T(8,128)(2,1)S(1)}, bf16[384,768]{1,0:T(8,128)(2,1)S(1)}, u32[]{:S(2)}, u32[]{:S(2)}) collective-permute-start(bf16[384,768]{1,0:T(8,128)(2,1)S(1)} %get-tuple-element.93), channel_id=1, source_target_pairs={{0,2},{1,3},{2,0},{3,1},{4,6},{5,7},{6,4},{7,5},{8,10},{9,11},{10,... | collective-permute-start | bytes 1769480 | tf_op jit(solution)/shard_map/ppermute | solution.py:572
  68.1 25.9 %collective-permute-start.15 = (bf16[480,384]{1,0:T(8,128)(2,1)S(1)}, bf16[480,384]{1,0:T(8,128)(2,1)S(1)}, u32[]{:S(2)}, u32[]{:S(2)}) collective-permute-start(bf16[480,384]{1,0:T(8,128)(2,1)S(1)} %get-tuple-element.85), channel_id=1, source_target_pairs={{0,56},{8,64},{16,72},{24,80},{32,88},{40,96},{48,104},{56,112},{6... | collective-permute-start | bytes 1105928 | tf_op jit(solution)/shard_map/ppermute | solution.py:664
  75.2 18.8 %collective-permute-start.16 = (bf16[480,384]{1,0:T(8,128)(2,1)S(1)}, bf16[480,384]{1,0:T(8,128)(2,1)S(1)}, u32[]{:S(2)}, u32[]{:S(2)}) collective-permute-start(bf16[480,384]{1,0:T(8,128)(2,1)S(1)} %get-tuple-element.96), channel_id=1, source_target_pairs={{0,120},{8,128},{16,136},{24,144},{32,152},{40,160},{48,168},{56,1... | collective-permute-start | bytes 1105928 | tf_op jit(solution)/shard_map/ppermute | solution.py:664
  89.6 14.1 %collective-permute-start.13 = (bf16[480,384]{1,0:T(8,128)(2,1)S(1)}, bf16[480,384]{1,0:T(8,128)(2,1)S(1)}, u32[]{:S(2)}, u32[]{:S(2)}) collective-permute-start(bf16[480,384]{1,0:T(8,128)(2,1)S(1)} %get-tuple-element.94), channel_id=1, source_target_pairs={{0,248},{8,0},{16,8},{24,16},{32,24},{40,32},{48,40},{56,48},{64,5... | collective-permute-start | bytes 1105928 | tf_op jit(solution)/shard_map/ppermute | solution.py:664
  89.7 17.1 %collective-permute-start.14 = (bf16[480,384]{1,0:T(8,128)(2,1)S(1)}, bf16[480,384]{1,0:T(8,128)(2,1)S(1)}, u32[]{:S(2)}, u32[]{:S(2)}) collective-permute-start(bf16[480,384]{1,0:T(8,128)(2,1)S(1)} %get-tuple-element.95), channel_id=1, source_target_pairs={{0,184},{8,192},{16,200},{24,208},{32,216},{40,224},{48,232},{56,2... | collective-permute-start | bytes 1105928 | tf_op jit(solution)/shard_map/ppermute | solution.py:664
  92.0 14.8 %copy-start.1 = (f32[64,768]{1,0:T(8,128)S(1)}, f32[64,768]{1,0:T(8,128)}, u32[]{:S(2)}) copy-start(f32[64,768]{1,0:T(8,128)} %table.1) | copy-start | bytes 589828
  92.0 37.2 %collective-permute-start.21 = (bf16[3,384,768]{2,1,0:T(8,128)(2,1)S(1)}, bf16[3,384,768]{2,1,0:T(8,128)(2,1)S(1)}, u32[]{:S(2)}, u32[]{:S(2)}) collective-permute-start(bf16[3,384,768]{2,1,0:T(8,128)(2,1)S(1)} %stack.41.refs_5_), channel_id=1, source_target_pairs={{0,8},{8,0},{1,9},{9,1},{2,10},{10,2},{3,11},{11,3},{4,12},{12,4},... | collective-permute-start | bytes 5308424 | tf_op jit(solution)/shard_map/ppermute | solution.py:572
  95.5 16.2 %copy-start.6 = (bf16[448,768]{1,0:T(8,128)(2,1)S(1)}, bf16[448,768]{1,0:T(8,128)(2,1)}, u32[]{:S(2)}) copy-start(bf16[448,768]{1,0:T(8,128)(2,1)} %param.8) | copy-start | bytes 2064388
  109.0 8.1 %collective-permute-start.20 = (bf16[448,384]{1,0:T(8,128)(2,1)S(1)}, bf16[448,384]{1,0:T(8,128)(2,1)S(1)}, u32[]{:S(2)}, u32[]{:S(2)}) collective-permute-start(bf16[448,384]{1,0:T(8,128)(2,1)S(1)} %get-tuple-element.102.refs_0_), channel_id=1, source_target_pairs={{0,3},{1,0},{2,1},{3,2},{4,7},{5,4},{6,5},{7,6},{8,11},{9,8},{10,9... | collective-permute-start | bytes 1032200 | tf_op jit(solution)/shard_map/ppermute | solution.py:572
  110.4 9.3 %collective-permute-start.19 = (bf16[448,384]{1,0:T(8,128)(2,1)S(1)}, bf16[448,384]{1,0:T(8,128)(2,1)S(1)}, u32[]{:S(2)}, u32[]{:S(2)}) collective-permute-start(bf16[448,384]{1,0:T(8,128)(2,1)S(1)} %get-tuple-element.102.refs_0_), channel_id=1, source_target_pairs={{0,2},{1,3},{2,0},{3,1},{4,6},{5,7},{6,4},{7,5},{8,10},{9,11},{10,... | collective-permute-start | bytes 1032200 | tf_op jit(solution)/shard_map/ppermute | solution.py:572
  111.7 17.5 %collective-permute-start.18 = (bf16[448,384]{1,0:T(8,128)(2,1)S(1)}, bf16[448,384]{1,0:T(8,128)(2,1)S(1)}, u32[]{:S(2)}, u32[]{:S(2)}) collective-permute-start(bf16[448,384]{1,0:T(8,128)(2,1)S(1)} %get-tuple-element.102.refs_0_), channel_id=1, source_target_pairs={{0,1},{1,2},{2,3},{3,0},{4,5},{5,6},{6,7},{7,4},{8,9},{9,10},{10,1... | collective-permute-start | bytes 1032200 | tf_op jit(solution)/shard_map/ppermute | solution.py:572
  111.8 23.2 %collective-permute-start.17 = (bf16[448,768]{1,0:T(8,128)(2,1)S(1)}, bf16[448,768]{1,0:T(8,128)(2,1)S(1)}, u32[]{:S(2)}, u32[]{:S(2)}) collective-permute-start(bf16[448,768]{1,0:T(8,128)(2,1)S(1)} %copy-done.6), channel_id=1, source_target_pairs={{0,248},{8,0},{16,8},{24,16},{32,24},{40,32},{48,40},{56,48},{64,5... | collective-permute-start | bytes 2064392 | tf_op jit(solution)/shard_map/ppermute | solution.py:572
  132.1 16.6 %collective-permute-start.22 = (bf16[448,768]{1,0:T(8,128)(2,1)S(1)}, bf16[448,768]{1,0:T(8,128)(2,1)S(1)}, u32[]{:S(2)}, u32[]{:S(2)}) collective-permute-start(bf16[448,768]{1,0:T(8,128)(2,1)S(1)} %project.3), channel_id=1, source_target_pairs={{0,4},{4,0},{1,5},{5,1},{2,6},{6,2},{3,7},{7,3},{8,12},{12,8},{9,1... | collective-permute-start | bytes 2064392 | tf_op jit(solution)/shard_map/ppermute | solution.py:572

commit v4 on v3

--- a/solution.py
+++ b/solution.py
@@ -30,16 +30,16 @@
     )
 
 
-CALLS = {"early": (1, 3, 0), "middle": (2, 1), "late": (3, 0)}
-EARLY, LATER = (0, 1, 2), (3, 4, 5, 6, 7)
+CALLS = {"early": (1, 3), "middle": (2, 1, 3), "late": (0,)}
+EARLY, LATER = (0, 1, 2, 4), (3, 5, 6, 7)
 
 
 def attend_kernel(call, ids, live, level, *refs):
     steps = CALLS[call]
     many = len(steps)
-    early, middle = call == "early", call == "middle"
-    members = EARLY if early else EARLY + LATER if middle else LATER
-    resumed = () if early else (1,) if middle else (0, 1)
+    early, middle, late = call == "early", call == "middle", call == "late"
+    members = EARLY if early else tuple(range(8))
+    resumed = (1, 2) if middle else ()
     kept = many if early else len(resumed)
     refs = list(refs)
 
@@ -68,9 +68,10 @@
         return count
 
     everything = first + 8
-    n_early, n_later = live_before(everything, EARLY), live_before(everything, LATER)
-    n_own = live_before(mine, EARLY if early else LATER)
-    own_place = jnp.where(live[mine] == 1, n_own, n_early)
+    if late:
+        n_own = live_before(mine, members)
+    else:
+        n_early, n_later = live_before(everything, EARLY), live_before(everything, LATER)
 
     def raw_copy(i):
         return pltpu.make_async_copy(query_in[i], raw.at[i], raw_sem.at[i])
@@ -105,21 +106,22 @@
 
     def run():
         for j, p in enumerate(members):
-            part = EARLY if p in EARLY else LATER
-            base = 0 if p in EARLY else 3
-            if early and p == 0:
-                place_copy(j, own_place).start()
+            if late and p == 0:
+                place_copy(j, n_own).start()
+                continue
+            wanted = live[groups[p]] == 1
+            if late:
+                wanted = wanted & (groups[p] < mine)
+                place = live_before(groups[p], members)
+            elif p in EARLY:
+                wanted = wanted & active(0) if middle else wanted
+                place = live_before(groups[p], EARLY)
             else:
-
-                wanted = live[groups[p]] == 1
-                if middle and p in EARLY:
-                    wanted = wanted & active(0)
-                if call == "late":
-                    wanted = wanted & (active(0) | (groups[p] < mine))
-
-                @pl.when(wanted)
-                def _():
-                    place_copy(j, base + live_before(groups[p], part)).start()
+                place = 4 + live_before(groups[p], LATER)
+
+            @pl.when(wanted)
+            def _():
+                place_copy(j, place).start()
 
         for i in range(many):
 
@@ -134,14 +136,6 @@
                 for copy in state_copies(k):
                     copy.start()
 
-        if early:
-            place_copy(0, own_place).wait()
-            for k in range(len(EARLY)):
-
-                @pl.when((k < n_early) & (k != own_place))
-                def _():
-                    place_copy(0, k).wait()
-
         for i in range(many):
 
             @pl.when(active(i))
@@ -164,16 +158,14 @@
                     copy.wait()
 
     def source(i):
-        own = step_of(i) == 0
         if early:
-            count = jnp.where(own, n_own + 1, n_early)
-            split, base = jnp.where(own, n_own, n_early), own_place
+            count, split, base = n_early, n_early, 4
         elif middle:
             count = jnp.where(i == 0, n_early + n_later, n_later)
-            split, base = jnp.where(i == 0, n_early, 0), 3
+            split, base = jnp.where(i == 0, n_early, 0), 4
         else:
-            count = jnp.where(own, n_own, n_later)
-            split, base = jnp.int32(0), 3
+            count = n_own + 1
+            split, base = count, 4
         chunks = (count + 1) // 2
 
         waits = (i == 0) | jnp.logical_not(active(0))
@@ -182,12 +174,11 @@
             return jnp.where(k < split, k, base + k - split)
 
         def arrive(t):
-            if not early:
-                for k in (2 * t, 2 * t + 1):
-
-                    @pl.when(waits & (k < count))
-                    def _():
-                        place_copy(0, place_of(k)).wait()
+            for k in (2 * t, 2 * t + 1):
+
+                @pl.when(waits & (k < count))
+                def _():
+                    place_copy(0, place_of(k)).wait()
 
         def at(k):
             place = place_of(jnp.maximum(jnp.minimum(k, count - 1), 0))
@@ -203,10 +194,10 @@
             top[i] = jnp.full(top.shape[1:], LOWEST, jnp.float32)
             acc[i] = jnp.zeros(acc.shape[1:], jnp.float32)
 
-        if early:
+        if middle:
+            pl.when(i == 0)(fresh)
+        else:
             fresh()
-        elif middle:
-            pl.when(i == 0)(fresh)
 
         def scores_of(t, head):
             cols = slice(head * HD, (head + 1) * HD)
@@ -289,10 +280,10 @@
         pad = jnp.zeros((16, 2 * WIDTH - ROWS), jnp.bfloat16)
         done[i, ROWS + 16 : ROWS + 32, :] = jnp.concatenate([flat[:, WIDTH:], pad], axis=1)
 
-    if middle:
-        pl.when(active(1))(run)
+    if late:
+        run()
     else:
-        run()
+        pl.when(active(steps.index(1)))(run)
 
 
 def attend(call, ids, live, level, queries, pairs, states=()):
@@ -301,7 +292,7 @@
     bf16, f32 = jnp.bfloat16, jnp.float32
     many = len(CALLS[call])
     early = call == "early"
-    members = EARLY if early else EARLY + LATER if call == "middle" else LATER
+    members = EARLY if early else tuple(range(8))
     state = [(HEADS_HERE, ROWS, 2 * HD), (HEADS_HERE, ROWS, HD)]
     if early:
         out_shape = [jax.ShapeDtypeStruct(shape, f32) for shape in state * many]
@@ -368,9 +359,9 @@
     )
 
 
-def combine_two_kernel(ids, one, two, values, sides):
+def combine_later_kernel(ids, one, two, three, values, sides):
     home = ids[3]
-    stats = [stats_of(ref[ROWS : ROWS + STAT, :])[0] for ref in (one, two)]
+    stats = [stats_of(ref[ROWS : ROWS + STAT, :])[0] for ref in (one, two, three)]
     lane = lax.broadcasted_iota(jnp.int32, (ROWS, HD), 1)
     side = jnp.zeros((ROWS, HD), jnp.float32)
     for head in range(HEADS_HERE):
@@ -378,6 +369,7 @@
             [
                 share_of(one, stats[0], head, home >= 1),
                 share_of(two, stats[1], head, home >= 2),
+                share_of(three, stats[2], head, home >= 3),
             ]
         )
         values[:, head * HD : (head + 1) * HD] = value
@@ -386,34 +378,31 @@
     sides[...] = side
 
 
-def combine_two(ids, one, two):
+def combine_later(ids, one, two, three):
     vmem = pl.BlockSpec(memory_space=pltpu.VMEM)
     return pl.pallas_call(
-        combine_two_kernel,
+        combine_later_kernel,
         out_shape=[
             jax.ShapeDtypeStruct((ROWS, WIDTH), jnp.float32),
             jax.ShapeDtypeStruct((ROWS, HD), jnp.float32),
         ],
-        in_specs=[pl.BlockSpec(memory_space=pltpu.SMEM)] + [vmem] * 2,
+        in_specs=[pl.BlockSpec(memory_space=pltpu.SMEM)] + [vmem] * 3,
         out_specs=[vmem] * 2,
         compiler_params=pltpu.CompilerParams(vmem_limit_bytes=SMALL_VMEM),
         cost_estimate=pl.CostEstimate(
             flops=10**11, bytes_accessed=2 * 10**8, transcendentals=0
         ),
-        name="combine_two",
-    )(ids, one, two)
-
-
-def combine_kernel(ids, table, zero, three, values, sides, out, gate):
-    home = ids[3]
+        name="combine_later",
+    )(ids, one, two, three)
+
+
+def combine_kernel(table, zero, values, sides, out, gate):
     own, noise = stats_of(zero[ROWS : ROWS + STAT, :])
-    far = stats_of(three[ROWS : ROWS + STAT, :])[0]
     for head in range(HEADS_HERE):
         at = slice(head * HD, (head + 1) * HD)
         value, unused, row_sum = merged(
             [
-                share_of(zero, own, head, home >= 0),
-                share_of(three, far, head, home >= 3),
+                share_of(zero, own, head, True),
                 (
                     values[:, at],
                     sides[:, head : head + 1],
@@ -426,7 +415,7 @@
     gate[...] = jnp.sum(jnp.where(index == noise, table[...], 0.0), axis=0, keepdims=True)
 
 
-def combine(ids, table, zero, three, values, sides):
+def combine(table, zero, values, sides):
     vmem = pl.BlockSpec(memory_space=pltpu.VMEM)
     return pl.pallas_call(
         combine_kernel,
@@ -434,11 +423,11 @@
             jax.ShapeDtypeStruct((ROWS, WIDTH), jnp.bfloat16),
             jax.ShapeDtypeStruct((1, table.shape[1]), jnp.float32),
         ],
-        in_specs=[pl.BlockSpec(memory_space=pltpu.SMEM)] + [vmem] * 5,
+        in_specs=[vmem] * 4,
         out_specs=[vmem] * 2,
         compiler_params=pltpu.CompilerParams(vmem_limit_bytes=SMALL_VMEM),
         name="combine",
-    )(ids, table, zero, three, values, sides)
+    )(table, zero, values, sides)
 
 
 def finish_kernel(hidden, near, arrived, gate, out):
@@ -460,35 +449,21 @@
     )(hidden, near, arrived, gate)
 
 
-def pack_kernel(ids, keys, values, weight, pair, piece, sem):
-    width = piece.shape[1]
-    at = pl.ds(pl.multiple_of(ids[4] * width, width), width)
-    copy = pltpu.make_async_copy(weight.at[:, at], piece, sem)
-    copy.start()
+def pack_kernel(keys, values, pair):
     pair[:, :WIDTH] = keys[...]
     pair[:, WIDTH:] = values[...]
-    copy.wait()
-
-
-def pack(ids, keys, values, weight):
+
+
+def pack(keys, values):
     vmem = pl.BlockSpec(memory_space=pltpu.VMEM)
     return pl.pallas_call(
         pack_kernel,
-        out_shape=[
-            jax.ShapeDtypeStruct((ROWS, 2 * WIDTH), jnp.bfloat16),
-            jax.ShapeDtypeStruct((weight.shape[0], weight.shape[1] // 8), jnp.bfloat16),
-        ],
-        in_specs=[
-            pl.BlockSpec(memory_space=pltpu.SMEM),
-            vmem,
-            vmem,
-            pl.BlockSpec(memory_space=pl.ANY),
-        ],
-        out_specs=[vmem] * 2,
-        scratch_shapes=[pltpu.SemaphoreType.DMA],
+        out_shape=jax.ShapeDtypeStruct((ROWS, 2 * WIDTH), jnp.bfloat16),
+        in_specs=[vmem] * 2,
+        out_specs=vmem,
         compiler_params=pltpu.CompilerParams(vmem_limit_bytes=WHOLE_VMEM),
         name="pack",
-    )(ids, keys, values, weight)
+    )(keys, values)
 
 
 def copies_kernel(plan, ids, *refs):
@@ -589,73 +564,46 @@
     def to_level(value, d):
         return lax.ppermute(value, "z", [(i, i - d) for i in range(d, 4)])
 
-    pair, piece_one = pack(ids, key_rows, values, out_weight)
-    piece_two, piece_three, weight_near, weight_far = copied(
+    pair = pack(key_rows, values)
+    *pieces, weight_near, weight_far = copied(
         "columns",
         ids,
         [out_weight],
-        [column_block] * 4,
-        tuple(("columns", 0, k, 5 + k) for k in range(4)),
-    )
-    (
-        next_one,
-        next_three,
-        below,
-        above,
-        piece_one,
-        pair,
-        queries,
-        hidden,
-        piece_two,
-        piece_three,
-        weight_near,
-        weight_far,
-    ) = together(
+        [column_block] * 5,
+        tuple(("columns", 0, k, 4 + k) for k in range(5)),
+    )
+    next_one, next_three, below, above, pair_there, pair, queries, hidden, *pieces = together(
         to_level(queries, 1),
         to_level(queries, 3),
         around(pair, "y", 1),
         around(pair, "y", -1),
-        around(piece_one, "x", 1),
+        around(pair, "c", 1),
         pair,
         queries,
         hidden,
-        piece_two,
-        piece_three,
-        weight_near,
-        weight_far,
+        *pieces,
     )
     states = attend(
         "early",
         ids,
         group_live,
         noise_level,
-        [next_one, next_three, queries],
-        [pair, below, above],
-    )
-    (
-        next_two,
-        across,
-        piece_three,
-        below_there,
-        above_there,
-        hidden,
-        piece_two,
-        pair,
-        *states,
-    ) = together(
+        [next_one, next_three],
+        [pair, below, above, None, pair_there],
+    )
+    next_two, across, piece_three, below_there, above_there, piece_one, piece_two, *states = together(
         to_level(queries, 2),
         around(pair, "y", 2),
-        around(piece_three, "x", 3),
+        around(pieces[2], "x", 3),
         around(below, "c", 1),
         around(above, "c", 1),
-        hidden,
-        piece_two,
-        pair,
+        pieces[0],
+        pieces[1],
         *states,
     )
-    across_there, pair_there = around(across, "c", 1), around(pair, "c", 1)
+    across_there = around(across, "c", 1)
     pairs = [pair, below, above, across, pair_there, below_there, above_there, across_there]
-    piece_two = around(piece_two, "x", 2)
+    piece_one, piece_two = around(piece_one, "x", 1), around(piece_two, "x", 2)
 
     def back(share, d):
         pairs_back = [
@@ -663,16 +611,13 @@
         ]
         return lax.ppermute(share, SLOT, pairs_back)
 
-    state_one, state_three, state_own = states[0:2], states[2:4], states[4:6]
-    two, one = attend(
-        "middle", ids, group_live, noise_level, [next_two, next_one], pairs, state_one
-    )
-    values_two, sides_two = combine_two(ids, back(one, 1), back(two, 2))
+    two, one, three = attend(
+        "middle", ids, group_live, noise_level, [next_two, next_one, next_three], pairs, states
+    )
+    values_later, sides_later = combine_later(ids, back(one, 1), back(two, 2), back(three, 3))
     live_later, one = together(group_live, one)
-    three, zero = attend(
-        "late", ids, live_later, noise_level, [next_three, queries], pairs, state_three + state_own
-    )
-    three, zero, piece_two = together(three, zero, piece_two)
+    (zero,) = attend("late", ids, live_later, noise_level, [queries], pairs)
+    zero, piece_one, piece_two = together(zero, piece_one, piece_two)
     (fetched,) = copied(
         "stack",
         ids,
@@ -681,9 +626,7 @@
         tuple(("stack", k, 0, k) for k in range(3)),
     )
     swapped = around(fetched, "c", 1)
-    attended, gate_row = combine(
-        ids, level_table, back(zero, 0), back(three, 3), values_two, sides_two
-    )
+    attended, gate_row = combine(level_table, back(zero, 0), values_later, sides_later)
 
     attended, hidden = together(attended, hidden)
     hidden_next = around(hidden, SLOT, -1)

time: 153 us -> 151 us (0.987); the launches traced: 150 us -> 150 us
  waiting for transfers between devices: 55.4 us -> 64.7 us
  starting transfers between devices: 33.3 us -> 28.4 us
  Pallas kernels: 57.7 us -> 53.2 us
    ppermute x4, waiting for transfers between devices: 11.3 us -> 18.3 us  [back(): return lax.ppermute(share, SLOT, pairs_back)]
    ppermute x16, starting transfers between devices: 19.6 us -> 16 us  [around(): lax.ppermute(value, axis, [(i, (i + steps) % count) for i in range(count)])]
    pallas_call x3, Pallas kernels: 41.7 us -> 39.2 us  [attend(): pl.pallas_call(functools.partial(attend_kernel, call), out_shape=out_shap...]
  transfers between devices with their start and end apart: 23 -> 23, of which waited for: 10 -> 8; matrix products, arithmetic and copies ran while one was open for 0% -> 0% of each run, Pallas kernels for 35% -> 33%
where the time goes in v4:
time: 151 us; the launch traced here: 150 us
  waiting for transfers between devices  64.7 us (43%)
  Pallas kernels  53.2 us (35%)
  starting transfers between devices  28.4 us (19%)
  local copies, waits for them, and re-layouts  2.45 us (2%)
    pallas_call x3, Pallas kernels, attend(): pl.pallas_call(functools.partial(attend_kernel, call), out_shape=out_shap...  39.2 us
    ppermute x16, waiting for transfers between devices, around(): lax.ppermute(value, axis, [(i, (i + steps) % count) for i in range(count)])  32.7 us
    ppermute x4, waiting for transfers between devices, back(): return lax.ppermute(share, SLOT, pairs_back)  18.3 us
    ppermute x16, starting transfers between devices, around(): lax.ppermute(value, axis, [(i, (i + steps) % count) for i in range(count)])  16 us
    ppermute x3, waiting for transfers between devices, to_level(): return lax.ppermute(value, 'z', [(i, i - d) for i in range(d, 4)])  13.8 us
    ppermute x4, starting transfers between devices, back(): return lax.ppermute(share, SLOT, pairs_back)  8.6 us
    pallas_call x2, Pallas kernels, project(): pl.pallas_call(functools.partial(project_kernel, far), out_shape=jax.Shap...  5.61 us
    ppermute x3, starting transfers between devices, to_level(): return lax.ppermute(value, 'z', [(i, i - d) for i in range(d, 4)])  3.86 us
  transfers between devices with their start and end apart: 23, of which 8 were waited for; matrix products, arithmetic and copies ran while one was open for 0% of the time, Pallas kernels for 33%

profile of v4, /device:TPU:25, one launch (start us, length us, event | category | flops | bytes accessed | tf_op | source)
XLA Modules:
  0.0 149.8 jit_solution(3523023110756723181)
XLA Ops:
  0.0 2.0 %pack.1.refs_2_.refs_3_.refs_1_ = bf16[448,768]{1,0:T(8,128)(2,1)} custom-call(bf16[448,384]{1,0:T(8,128)(2,1)} %keys.1, bf16[448,384]{1,0:T(8,128)(2,1)} %values.1), custom_call_target="tpu_custom_call" | custom-call | tf_op jit(solution)/shard_map/pack/pallas_call | solution.py:459
  2.0 0.7 collective-permute-start.4
  2.7 0.5 collective-permute-start.3
  3.1 2.2 %collective-permute-start.2 = (bf16[448,768]{1,0:T(8,128)(2,1)}, bf16[448,768]{1,0:T(8,128)(2,1)S(1)}, u32[]{:S(2)}, u32[]{:S(2)}) collective-permute-start(bf16[448,768]{1,0:T(8,128)(2,1)} %pack.1.refs_2_.refs_3_.refs_1_), channel_id=1, source_target_pairs={{0,16},{16,32},{32,48},{48,0},{1,17},{17,33},{33,49},{49,1},{2,18}... | collective-permute-start | bytes 2064392 | tf_op jit(solution)/shard_map/ppermute | solution.py:547
  5.3 1.3 collective-permute-start
  6.6 1.3 collective-permute-start.1
  8.6 0.1 stack.40.ids
  8.7 2.3 %copy-done = bf16[384,6144]{1,0:T(8,128)(2,1)S(1)} copy-done((bf16[384,6144]{1,0:T(8,128)(2,1)S(1)}, bf16[384,6144]{1,0:T(8,128)(2,1)}, u32[]{:S(2)}) %copy-start) | copy-done | bytes 4718616
  11.1 0.9 columns.1
  12.0 13.8 %collective-permute-done.refs_0_.refs_1_ = bf16[448,384]{1,0:T(8,128)(2,1)S(1)} collective-permute-done((bf16[448,384]{1,0:T(8,128)(2,1)}, bf16[448,384]{1,0:T(8,128)(2,1)S(1)}, u32[]{:S(2)}, u32[]{:S(2)}) %collective-permute-start) | collective-permute-done | bytes 344096 | tf_op jit(solution)/shard_map/ppermute | solution.py:565
  25.7 0.0 collective-permute-done.4.refs_5_.refs_7_
  25.7 0.0 collective-permute-done.3.refs_4_.refs_5_.refs_3_
  25.7 0.0 collective-permute-done.2.refs_3_.refs_4_.refs_2_
  25.8 1.3 collective-permute-start.5
  27.1 2.6 %collective-permute-start.7 = (bf16[384,768]{1,0:T(8,128)(2,1)S(1)}, bf16[384,768]{1,0:T(8,128)(2,1)S(1)}, u32[]{:S(2)}, u32[]{:S(2)}) collective-permute-start(bf16[384,768]{1,0:T(8,128)(2,1)S(1)} %get-tuple-element.54), channel_id=1, source_target_pairs={{0,3},{1,0},{2,1},{3,2},{4,7},{5,4},{6,5},{7,6},{8,11},{9,8},{10,9... | collective-permute-start | bytes 1769480 | tf_op jit(solution)/shard_map/ppermute | solution.py:547
  29.6 1.4 collective-permute-start.8
  31.0 0.1 collective-permute-start.9
  31.1 12.1 %attend_early.1 = (f32[3,448,256]{2,1,0:T(8,128)S(1)}, f32[3,448,128]{2,1,0:T(8,128)S(1)}, f32[3,448,256]{2,1,0:T(8,128)S(1)}, f32[3,448,128]{2,1,0:T(8,128)S(1)}) custom-call(s32[9]{0:T(128)S(1)} %stack.40.ids, s32[32]{0:T(128)S(1)} %copy-done.4, s32[1]{0:T(128)S(6)} %copy.9.level, bf16[448,384]{1,0:T(8,128)(2,1)S(1)} %collective-permute-done.refs_0_.refs_1_, ...), custom_call_target="tpu_custom_call" | custom-call | flops 11098128384 | bytes 8000000 | tf_op jit(solution)/shard_map/attend_early/pallas_call | solution.py:302
  43.3 3.4 %collective-permute-done.6.refs_6_.refs_4_ = bf16[448,768]{1,0:T(8,128)(2,1)S(1)} collective-permute-done((bf16[448,768]{1,0:T(8,128)(2,1)S(1)}, bf16[448,768]{1,0:T(8,128)(2,1)S(1)}, u32[]{:S(2)}, u32[]{:S(2)}) %collective-permute-start.6) | collective-permute-done | bytes 688160 | tf_op jit(solution)/shard_map/ppermute | solution.py:547
  46.7 0.0 collective-permute-done.8.refs_8_.refs_6_
  46.7 2.3 %collective-permute-start.10 = (bf16[448,768]{1,0:T(8,128)(2,1)S(1)}, bf16[448,768]{1,0:T(8,128)(2,1)S(1)}, u32[]{:S(2)}, u32[]{:S(2)}) collective-permute-start(bf16[448,768]{1,0:T(8,128)(2,1)S(1)} %collective-permute-done.6.refs_6_.refs_4_), channel_id=1, source_target_pairs={{0,8},{8,0},{1,9},{9,1},{2,10},{10,2},{3,11},{11,3},{4,12},{12,4},... | collective-permute-start | bytes 2064392 | tf_op jit(solution)/shard_map/ppermute | solution.py:547
  49.0 1.7 %collective-permute-start.12 = (bf16[384,768]{1,0:T(8,128)(2,1)S(1)}, bf16[384,768]{1,0:T(8,128)(2,1)S(1)}, u32[]{:S(2)}, u32[]{:S(2)}) collective-permute-start(bf16[384,768]{1,0:T(8,128)(2,1)S(1)} %get-tuple-element.77), channel_id=1, source_target_pairs={{0,2},{1,3},{2,0},{3,1},{4,6},{5,7},{6,4},{7,5},{8,10},{9,11},{10,... | collective-permute-start | bytes 1769480 | tf_op jit(solution)/shard_map/ppermute | solution.py:547
  50.7 0.0 collective-permute-done.10.refs_10_.refs_8_
  50.7 17.4 %attend_middle.1 = (bf16[480,384]{1,0:T(8,128)(2,1)S(1)}, bf16[480,384]{1,0:T(8,128)(2,1)S(1)}, bf16[480,384]{1,0:T(8,128)(2,1)S(1)}) custom-call(s32[9]{0:T(128)S(1)} %stack.40.ids, s32[32]{0:T(128)S(1)} %copy-done.4, s32[1]{0:T(128)S(6)} %copy.9.level, bf16[448,384]{1,0:T(8,128)(2,1)S(1)} %collective-permute-done.5.refs_0_, ...), custom_call_target="tpu_custom_call" | custom-call | flops 11098128384 | bytes 8000000 | tf_op jit(solution)/shard_map/attend_middle/pallas_call | solution.py:302
  68.1 5.9 %collective-permute-start.14 = (bf16[480,384]{1,0:T(8,128)(2,1)S(1)}, bf16[480,384]{1,0:T(8,128)(2,1)S(1)}, u32[]{:S(2)}, u32[]{:S(2)}) collective-permute-start(bf16[480,384]{1,0:T(8,128)(2,1)S(1)} %get-tuple-element.74), channel_id=1, source_target_pairs={{0,56},{8,64},{16,72},{24,80},{32,88},{40,96},{48,104},{56,112},{6... | collective-permute-start | bytes 1105928 | tf_op jit(solution)/shard_map/ppermute | solution.py:612
  74.0 1.3 collective-permute-start.15
  75.4 1.3 collective-permute-start.16
  76.7 9.7 %attend_late.1 = bf16[480,384]{1,0:T(8,128)(2,1)S(1)} custom-call(s32[9]{0:T(128)S(1)} %stack.40.ids, s32[32]{0:T(128)S(1)} %copy-done.4, s32[1]{0:T(128)S(6)} %copy.9.level, bf16[448,384]{1,0:T(8,128)(2,1)S(1)} %copy-done.3, bf16[448,768]{1,0:T(8,128)(2,1)S(1)} %copy-done.1, bf16[448,768]{1,0:T(8,128)(2,1)S(1)} %collective-permute-done.2.refs_3_.refs_4_.refs_2_, ...), custom_call_target="tpu_custom_call" | custom-call | flops 11098128384 | bytes 8000000 | tf_op jit(solution)/shard_map/attend_late/pallas_call | solution.py:302
  86.4 0.1 collective-permute-start.13
  86.5 0.9 stack.41.refs_5_
  87.4 0.0 copy-start.2
  87.4 0.0 copy-start.5
  87.4 0.1 collective-permute-start.21
  87.5 2.7 %collective-permute-done.15.two = bf16[480,384]{1,0:T(8,128)(2,1)S(1)} collective-permute-done((bf16[480,384]{1,0:T(8,128)(2,1)S(1)}, bf16[480,384]{1,0:T(8,128)(2,1)S(1)}, u32[]{:S(2)}, u32[]{:S(2)}) %collective-permute-start.15) | collective-permute-done | bytes 368672 | tf_op jit(solution)/shard_map/ppermute | solution.py:612
  90.3 15.5 %collective-permute-done.16.three = bf16[480,384]{1,0:T(8,128)(2,1)S(1)} collective-permute-done((bf16[480,384]{1,0:T(8,128)(2,1)S(1)}, bf16[480,384]{1,0:T(8,128)(2,1)S(1)}, u32[]{:S(2)}, u32[]{:S(2)}) %collective-permute-start.16) | collective-permute-done | bytes 368672 | tf_op jit(solution)/shard_map/ppermute | solution.py:612
  105.8 1.9 %combine_later.1 = (f32[448,384]{1,0:T(8,128)S(1)}, f32[448,128]{1,0:T(8,128)S(1)}) custom-call(s32[9]{0:T(128)S(1)} %stack.40.ids, bf16[480,384]{1,0:T(8,128)(2,1)S(1)} %collective-permute-done.14.one, bf16[480,384]{1,0:T(8,128)(2,1)S(1)} %collective-permute-done.15.two, bf16[480,384]{1,0:T(8,128)(2,1)S(1)} %collective-permute-done.16.three), custom_call_target="tpu_custom_call" | custom-call | flops 99999997952 | bytes 200000000 | tf_op jit(solution)/shard_map/combine_later/pallas_call | solution.py:383
  107.7 1.2 combine.1
  108.9 1.0 collective-permute-start.20
  109.9 2.3 %collective-permute-start.19 = (bf16[448,384]{1,0:T(8,128)(2,1)S(1)}, bf16[448,384]{1,0:T(8,128)(2,1)S(1)}, u32[]{:S(2)}, u32[]{:S(2)}) collective-permute-start(bf16[448,384]{1,0:T(8,128)(2,1)S(1)} %get-tuple-element.86.refs_0_), channel_id=1, source_target_pairs={{0,2},{1,3},{2,0},{3,1},{4,6},{5,7},{6,4},{7,5},{8,10},{9,11},{10,... | collective-permute-start | bytes 1032200 | tf_op jit(solution)/shard_map/ppermute | solution.py:547
  112.2 1.0 collective-permute-start.17
  113.3 5.0 %collective-permute-done.20.refs_3_ = bf16[448,384]{1,0:T(8,128)(2,1)S(1)} collective-permute-done((bf16[448,384]{1,0:T(8,128)(2,1)S(1)}, bf16[448,384]{1,0:T(8,128)(2,1)S(1)}, u32[]{:S(2)}, u32[]{:S(2)}) %collective-permute-start.20) | collective-permute-done | bytes 344096 | tf_op jit(solution)/shard_map/ppermute | solution.py:547
  118.2 2.2 %collective-permute-done.19.refs_2_ = bf16[448,384]{1,0:T(8,128)(2,1)S(1)} collective-permute-done((bf16[448,384]{1,0:T(8,128)(2,1)S(1)}, bf16[448,384]{1,0:T(8,128)(2,1)S(1)}, u32[]{:S(2)}, u32[]{:S(2)}) %collective-permute-start.19) | collective-permute-done | bytes 344096 | tf_op jit(solution)/shard_map/ppermute | solution.py:547
  120.4 8.4 %collective-permute-done.18.refs_1_ = bf16[448,384]{1,0:T(8,128)(2,1)S(1)} collective-permute-done((bf16[448,384]{1,0:T(8,128)(2,1)S(1)}, bf16[448,384]{1,0:T(8,128)(2,1)S(1)}, u32[]{:S(2)}, u32[]{:S(2)}) %collective-permute-start.18) | collective-permute-done | bytes 344096 | tf_op jit(solution)/shard_map/ppermute | solution.py:547
  128.8 2.8 %project.3 = bf16[448,768]{1,0:T(8,128)(2,1)S(1)} custom-call(s32[9]{0:T(128)S(1)} %stack.40.ids, bf16[448,384]{1,0:T(8,128)(2,1)S(1)} %get-tuple-element.86.refs_0_, bf16[448,384]{1,0:T(8,128)(2,1)S(1)} %collective-permute-done.18.refs_1_, bf16[448,384]{1,0:T(8,128)(2,1)S(1)} %collective-permute-done.19.refs_2_, ...), custom_call_target="tpu_custom_call" | custom-call | flops 1056964608 | bytes 5000000 | tf_op jit(solution)/shard_map/project/pallas_call | solution.py:531
  131.6 0.1 collective-permute-start.22
  131.7 2.8 %project.2.near = f32[448,768]{1,0:T(8,128)S(1)} custom-call(s32[9]{0:T(128)S(1)} %stack.40.ids, bf16[448,384]{1,0:T(8,128)(2,1)S(1)} %get-tuple-element.86.refs_0_, bf16[448,384]{1,0:T(8,128)(2,1)S(1)} %collective-permute-done.18.refs_1_, bf16[448,384]{1,0:T(8,128)(2,1)S(1)} %collective-permute-done.19.refs_2_, ...), custom_call_target="tpu_custom_call" | custom-call | flops 1056964608 | bytes 5000000 | tf_op jit(solution)/shard_map/project/pallas_call | solution.py:531
  134.5 13.7 %collective-permute-done.22.arrived = bf16[448,768]{1,0:T(8,128)(2,1)S(1)} collective-permute-done((bf16[448,768]{1,0:T(8,128)(2,1)S(1)}, bf16[448,768]{1,0:T(8,128)(2,1)S(1)}, u32[]{:S(2)}, u32[]{:S(2)}) %collective-permute-start.22) | collective-permute-done | bytes 688160 | tf_op jit(solution)/shard_map/ppermute | solution.py:547
  148.2 1.6 %finish.1 = bf16[448,768]{1,0:T(8,128)(2,1)} custom-call(bf16[448,768]{1,0:T(8,128)(2,1)S(1)} %collective-permute-done.17.hidden, f32[448,768]{1,0:T(8,128)S(1)} %project.2.near, bf16[448,768]{1,0:T(8,128)(2,1)S(1)} %collective-permute-done.22.arrived, f32[1,768]{1,0:T(1,128)S(1)} %get-tuple-element.92.gate), custom_call_target="tpu_custom_call" | custom-call | tf_op jit(solution)/shard_map/finish/pallas_call | solution.py:441
  (22 shorter events, 0.1 us)
Async XLA Ops:
  2.0 23.7 %collective-permute-start.4 = (bf16[448,768]{1,0:T(8,128)(2,1)}, bf16[448,768]{1,0:T(8,128)(2,1)S(1)}, u32[]{:S(2)}, u32[]{:S(2)}) collective-permute-start(bf16[448,768]{1,0:T(8,128)(2,1)} %pack.1.refs_2_.refs_3_.refs_1_), channel_id=1, source_target_pairs={{0,8},{8,0},{1,9},{9,1},{2,10},{10,2},{3,11},{11,3},{4,12},{12,4},... | collective-permute-start | bytes 2064392 | tf_op jit(solution)/shard_map/ppermute | solution.py:547
  2.7 23.1 %collective-permute-start.3 = (bf16[448,768]{1,0:T(8,128)(2,1)}, bf16[448,768]{1,0:T(8,128)(2,1)S(1)}, u32[]{:S(2)}, u32[]{:S(2)}) collective-permute-start(bf16[448,768]{1,0:T(8,128)(2,1)} %pack.1.refs_2_.refs_3_.refs_1_), channel_id=1, source_target_pairs={{0,48},{16,0},{32,16},{48,32},{1,49},{17,1},{33,17},{49,33},{2,50}... | collective-permute-start | bytes 2064392 | tf_op jit(solution)/shard_map/ppermute | solution.py:547
  3.1 22.6 %collective-permute-start.2 = (bf16[448,768]{1,0:T(8,128)(2,1)}, bf16[448,768]{1,0:T(8,128)(2,1)S(1)}, u32[]{:S(2)}, u32[]{:S(2)}) collective-permute-start(bf16[448,768]{1,0:T(8,128)(2,1)} %pack.1.refs_2_.refs_3_.refs_1_), channel_id=1, source_target_pairs={{0,16},{16,32},{32,48},{48,0},{1,17},{17,33},{33,49},{49,1},{2,18}... | collective-permute-start | bytes 2064392 | tf_op jit(solution)/shard_map/ppermute | solution.py:547
  5.3 20.4 %collective-permute-start = (bf16[448,384]{1,0:T(8,128)(2,1)}, bf16[448,384]{1,0:T(8,128)(2,1)S(1)}, u32[]{:S(2)}, u32[]{:S(2)}) collective-permute-start(bf16[448,384]{1,0:T(8,128)(2,1)} %refs_0_.2), channel_id=1, source_target_pairs={{64,0},{128,64},{192,128},{65,1},{129,65},{193,129},{66,2},{130,66... | collective-permute-start | bytes 1032200 | tf_op jit(solution)/shard_map/ppermute | solution.py:565
  6.6 19.1 %collective-permute-start.1 = (bf16[448,384]{1,0:T(8,128)(2,1)}, bf16[448,384]{1,0:T(8,128)(2,1)S(1)}, u32[]{:S(2)}, u32[]{:S(2)}) collective-permute-start(bf16[448,384]{1,0:T(8,128)(2,1)} %refs_0_.2), channel_id=1, source_target_pairs={{192,0},{193,1},{194,2},{195,3},{196,4},{197,5},{198,6},{199,7},{2... | collective-permute-start | bytes 1032200 | tf_op jit(solution)/shard_map/ppermute | solution.py:565
  8.7 2.3 %copy-start = (bf16[384,6144]{1,0:T(8,128)(2,1)S(1)}, bf16[384,6144]{1,0:T(8,128)(2,1)}, u32[]{:S(2)}) copy-start(bf16[384,6144]{1,0:T(8,128)(2,1)} %refs_0_.1) | copy-start | bytes 14155780
  11.0 14.7 %copy-start.3 = (bf16[448,384]{1,0:T(8,128)(2,1)S(1)}, bf16[448,384]{1,0:T(8,128)(2,1)}, u32[]{:S(2)}) copy-start(bf16[448,384]{1,0:T(8,128)(2,1)} %refs_0_.2) | copy-start | bytes 1032196
  11.1 18.6 %copy-start.1 = (bf16[448,768]{1,0:T(8,128)(2,1)S(1)}, bf16[448,768]{1,0:T(8,128)(2,1)}, u32[]{:S(2)}) copy-start(bf16[448,768]{1,0:T(8,128)(2,1)} %pack.1.refs_2_.refs_3_.refs_1_) | copy-start | bytes 2064388
  11.1 20.0 %copy-start.4 = (s32[32]{0:T(128)S(1)}, s32[32]{0:T(128)}, u32[]{:S(2)}) copy-start(s32[32]{0:T(128)} %live.4) | copy-start | bytes 388
  25.8 17.5 %collective-permute-start.5 = (bf16[448,384]{1,0:T(8,128)(2,1)S(1)}, bf16[448,384]{1,0:T(8,128)(2,1)S(1)}, u32[]{:S(2)}, u32[]{:S(2)}) collective-permute-start(bf16[448,384]{1,0:T(8,128)(2,1)S(1)} %copy-done.3), channel_id=1, source_target_pairs={{128,0},{192,64},{129,1},{193,65},{130,2},{194,66},{131,3},{195,67... | collective-permute-start | bytes 1032200 | tf_op jit(solution)/shard_map/ppermute | solution.py:565
  27.1 16.2 %collective-permute-start.7 = (bf16[384,768]{1,0:T(8,128)(2,1)S(1)}, bf16[384,768]{1,0:T(8,128)(2,1)S(1)}, u32[]{:S(2)}, u32[]{:S(2)}) collective-permute-start(bf16[384,768]{1,0:T(8,128)(2,1)S(1)} %get-tuple-element.54), channel_id=1, source_target_pairs={{0,3},{1,0},{2,1},{3,2},{4,7},{5,4},{6,5},{7,6},{8,11},{9,8},{10,9... | collective-permute-start | bytes 1769480 | tf_op jit(solution)/shard_map/ppermute | solution.py:547
  29.6 17.1 %collective-permute-start.6 = (bf16[448,768]{1,0:T(8,128)(2,1)S(1)}, bf16[448,768]{1,0:T(8,128)(2,1)S(1)}, u32[]{:S(2)}, u32[]{:S(2)}) collective-permute-start(bf16[448,768]{1,0:T(8,128)(2,1)S(1)} %copy-done.1), channel_id=1, source_target_pairs={{0,32},{16,48},{32,0},{48,16},{1,33},{17,49},{33,1},{49,17},{2,34}... | collective-permute-start | bytes 2064392 | tf_op jit(solution)/shard_map/ppermute | solution.py:547
  29.6 17.1 %collective-permute-start.8 = (bf16[448,768]{1,0:T(8,128)(2,1)S(1)}, bf16[448,768]{1,0:T(8,128)(2,1)S(1)}, u32[]{:S(2)}, u32[]{:S(2)}) collective-permute-start(bf16[448,768]{1,0:T(8,128)(2,1)S(1)} %collective-permute-done.2.refs_3_.refs_4_.refs_2_), channel_id=1, source_target_pairs={{0,8},{8,0},{1,9},{9,1},{2,10},{10,2},{3,11},{11,3},{4,12},{12,4},... | collective-permute-start | bytes 2064392 | tf_op jit(solution)/shard_map/ppermute | solution.py:547
  31.0 15.6 %collective-permute-start.9 = (bf16[448,768]{1,0:T(8,128)(2,1)S(1)}, bf16[448,768]{1,0:T(8,128)(2,1)S(1)}, u32[]{:S(2)}, u32[]{:S(2)}) collective-permute-start(bf16[448,768]{1,0:T(8,128)(2,1)S(1)} %collective-permute-done.3.refs_4_.refs_5_.refs_3_), channel_id=1, source_target_pairs={{0,8},{8,0},{1,9},{9,1},{2,10},{10,2},{3,11},{11,3},{4,12},{12,4},... | collective-permute-start | bytes 2064392 | tf_op jit(solution)/shard_map/ppermute | solution.py:547
  46.7 4.1 %collective-permute-start.10 = (bf16[448,768]{1,0:T(8,128)(2,1)S(1)}, bf16[448,768]{1,0:T(8,128)(2,1)S(1)}, u32[]{:S(2)}, u32[]{:S(2)}) collective-permute-start(bf16[448,768]{1,0:T(8,128)(2,1)S(1)} %collective-permute-done.6.refs_6_.refs_4_), channel_id=1, source_target_pairs={{0,8},{8,0},{1,9},{9,1},{2,10},{10,2},{3,11},{11,3},{4,12},{12,4},... | collective-permute-start | bytes 2064392 | tf_op jit(solution)/shard_map/ppermute | solution.py:547
  49.0 37.4 %collective-permute-start.11 = (bf16[384,768]{1,0:T(8,128)(2,1)S(1)}, bf16[384,768]{1,0:T(8,128)(2,1)S(1)}, u32[]{:S(2)}, u32[]{:S(2)}) collective-permute-start(bf16[384,768]{1,0:T(8,128)(2,1)S(1)} %get-tuple-element.76), channel_id=1, source_target_pairs={{0,1},{1,2},{2,3},{3,0},{4,5},{5,6},{6,7},{7,4},{8,9},{9,10},{10,1... | collective-permute-start | bytes 1769480 | tf_op jit(solution)/shard_map/ppermute | solution.py:547
  49.0 37.4 %collective-permute-start.12 = (bf16[384,768]{1,0:T(8,128)(2,1)S(1)}, bf16[384,768]{1,0:T(8,128)(2,1)S(1)}, u32[]{:S(2)}, u32[]{:S(2)}) collective-permute-start(bf16[384,768]{1,0:T(8,128)(2,1)S(1)} %get-tuple-element.77), channel_id=1, source_target_pairs={{0,2},{1,3},{2,0},{3,1},{4,6},{5,7},{6,4},{7,5},{8,10},{9,11},{10,... | collective-permute-start | bytes 1769480 | tf_op jit(solution)/shard_map/ppermute | solution.py:547
  68.1 37.7 %collective-permute-start.14 = (bf16[480,384]{1,0:T(8,128)(2,1)S(1)}, bf16[480,384]{1,0:T(8,128)(2,1)S(1)}, u32[]{:S(2)}, u32[]{:S(2)}) collective-permute-start(bf16[480,384]{1,0:T(8,128)(2,1)S(1)} %get-tuple-element.74), channel_id=1, source_target_pairs={{0,56},{8,64},{16,72},{24,80},{32,88},{40,96},{48,104},{56,112},{6... | collective-permute-start | bytes 1105928 | tf_op jit(solution)/shard_map/ppermute | solution.py:612
  74.0 16.2 %collective-permute-start.15 = (bf16[480,384]{1,0:T(8,128)(2,1)S(1)}, bf16[480,384]{1,0:T(8,128)(2,1)S(1)}, u32[]{:S(2)}, u32[]{:S(2)}) collective-permute-start(bf16[480,384]{1,0:T(8,128)(2,1)S(1)} %get-tuple-element.79), channel_id=1, source_target_pairs={{0,120},{8,128},{16,136},{24,144},{32,152},{40,160},{48,168},{56,1... | collective-permute-start | bytes 1105928 | tf_op jit(solution)/shard_map/ppermute | solution.py:612
  75.4 30.5 %collective-permute-start.16 = (bf16[480,384]{1,0:T(8,128)(2,1)S(1)}, bf16[480,384]{1,0:T(8,128)(2,1)S(1)}, u32[]{:S(2)}, u32[]{:S(2)}) collective-permute-start(bf16[480,384]{1,0:T(8,128)(2,1)S(1)} %get-tuple-element.80), channel_id=1, source_target_pairs={{0,184},{8,192},{16,200},{24,208},{32,216},{40,224},{48,232},{56,2... | collective-permute-start | bytes 1105928 | tf_op jit(solution)/shard_map/ppermute | solution.py:612
  86.4 21.3 %collective-permute-start.13 = (bf16[480,384]{1,0:T(8,128)(2,1)S(1)}, bf16[480,384]{1,0:T(8,128)(2,1)S(1)}, u32[]{:S(2)}, u32[]{:S(2)}) collective-permute-start(bf16[480,384]{1,0:T(8,128)(2,1)S(1)} %attend_late.1), channel_id=1, source_target_pairs={{0,248},{8,0},{16,8},{24,16},{32,24},{40,32},{48,40},{56,48},{64,5... | collective-permute-start | bytes 1105928 | tf_op jit(solution)/shard_map/ppermute | solution.py:612
  87.4 20.3 %copy-start.2 = (f32[64,768]{1,0:T(8,128)S(1)}, f32[64,768]{1,0:T(8,128)}, u32[]{:S(2)}) copy-start(f32[64,768]{1,0:T(8,128)} %table.1) | copy-start | bytes 589828
  87.4 24.8 %copy-start.5 = (bf16[448,768]{1,0:T(8,128)(2,1)S(1)}, bf16[448,768]{1,0:T(8,128)(2,1)}, u32[]{:S(2)}) copy-start(bf16[448,768]{1,0:T(8,128)(2,1)} %param.8) | copy-start | bytes 2064388
  87.4 41.4 %collective-permute-start.21 = (bf16[3,384,768]{2,1,0:T(8,128)(2,1)S(1)}, bf16[3,384,768]{2,1,0:T(8,128)(2,1)S(1)}, u32[]{:S(2)}, u32[]{:S(2)}) collective-permute-start(bf16[3,384,768]{2,1,0:T(8,128)(2,1)S(1)} %stack.41.refs_5_), channel_id=1, source_target_pairs={{0,8},{8,0},{1,9},{9,1},{2,10},{10,2},{3,11},{11,3},{4,12},{12,4},... | collective-permute-start | bytes 5308424 | tf_op jit(solution)/shard_map/ppermute | solution.py:547
  108.9 9.3 %collective-permute-start.20 = (bf16[448,384]{1,0:T(8,128)(2,1)S(1)}, bf16[448,384]{1,0:T(8,128)(2,1)S(1)}, u32[]{:S(2)}, u32[]{:S(2)}) collective-permute-start(bf16[448,384]{1,0:T(8,128)(2,1)S(1)} %get-tuple-element.86.refs_0_), channel_id=1, source_target_pairs={{0,3},{1,0},{2,1},{3,2},{4,7},{5,4},{6,5},{7,6},{8,11},{9,8},{10,9... | collective-permute-start | bytes 1032200 | tf_op jit(solution)/shard_map/ppermute | solution.py:547
  109.9 10.5 %collective-permute-start.19 = (bf16[448,384]{1,0:T(8,128)(2,1)S(1)}, bf16[448,384]{1,0:T(8,128)(2,1)S(1)}, u32[]{:S(2)}, u32[]{:S(2)}) collective-permute-start(bf16[448,384]{1,0:T(8,128)(2,1)S(1)} %get-tuple-element.86.refs_0_), channel_id=1, source_target_pairs={{0,2},{1,3},{2,0},{3,1},{4,6},{5,7},{6,4},{7,5},{8,10},{9,11},{10,... | collective-permute-start | bytes 1032200 | tf_op jit(solution)/shard_map/ppermute | solution.py:547
  112.2 16.6 %collective-permute-start.18 = (bf16[448,384]{1,0:T(8,128)(2,1)S(1)}, bf16[448,384]{1,0:T(8,128)(2,1)S(1)}, u32[]{:S(2)}, u32[]{:S(2)}) collective-permute-start(bf16[448,384]{1,0:T(8,128)(2,1)S(1)} %get-tuple-element.86.refs_0_), channel_id=1, source_target_pairs={{0,1},{1,2},{2,3},{3,0},{4,5},{5,6},{6,7},{7,4},{8,9},{9,10},{10,1... | collective-permute-start | bytes 1032200 | tf_op jit(solution)/shard_map/ppermute | solution.py:547
  112.2 22.3 %collective-permute-start.17 = (bf16[448,768]{1,0:T(8,128)(2,1)S(1)}, bf16[448,768]{1,0:T(8,128)(2,1)S(1)}, u32[]{:S(2)}, u32[]{:S(2)}) collective-permute-start(bf16[448,768]{1,0:T(8,128)(2,1)S(1)} %copy-done.5), channel_id=1, source_target_pairs={{0,248},{8,0},{16,8},{24,16},{32,24},{40,32},{48,40},{56,48},{64,5... | collective-permute-start | bytes 2064392 | tf_op jit(solution)/shard_map/ppermute | solution.py:547
  131.6 16.6 %collective-permute-start.22 = (bf16[448,768]{1,0:T(8,128)(2,1)S(1)}, bf16[448,768]{1,0:T(8,128)(2,1)S(1)}, u32[]{:S(2)}, u32[]{:S(2)}) collective-permute-start(bf16[448,768]{1,0:T(8,128)(2,1)S(1)} %project.3), channel_id=1, source_target_pairs={{0,4},{4,0},{1,5},{5,1},{2,6},{6,2},{3,7},{7,3},{8,12},{12,8},{9,1... | collective-permute-start | bytes 2064392 | tf_op jit(solution)/shard_map/ppermute | solution.py:547

commit v5 on v4

--- a/solution.py
+++ b/solution.py
@@ -359,17 +359,25 @@
     )
 
 
-def combine_later_kernel(ids, one, two, three, values, sides):
+def combine_later_kernel(ids, one_first, one_later, two_first, two_later, three, values, sides):
     home = ids[3]
-    stats = [stats_of(ref[ROWS : ROWS + STAT, :])[0] for ref in (one, two, three)]
     lane = lax.broadcasted_iota(jnp.int32, (ROWS, HD), 1)
+
+    def picked(first, later, is_first):
+        return jnp.where(is_first, first[...], later[...])
+
+    shares = (
+        (picked(one_first, one_later, home == 1), home >= 1),
+        (picked(two_first, two_later, home == 2), home >= 2),
+        (three[...], home >= 3),
+    )
+    stats = [stats_of(share[ROWS : ROWS + STAT, :])[0] for share, unused in shares]
     side = jnp.zeros((ROWS, HD), jnp.float32)
     for head in range(HEADS_HERE):
         value, row_max, row_sum = merged(
             [
-                share_of(one, stats[0], head, home >= 1),
-                share_of(two, stats[1], head, home >= 2),
-                share_of(three, stats[2], head, home >= 3),
+                share_of(share, stat, head, present)
+                for (share, present), stat in zip(shares, stats)
             ]
         )
         values[:, head * HD : (head + 1) * HD] = value
@@ -378,7 +386,7 @@
     sides[...] = side
 
 
-def combine_later(ids, one, two, three):
+def combine_later(ids, ones, twos, three):
     vmem = pl.BlockSpec(memory_space=pltpu.VMEM)
     return pl.pallas_call(
         combine_later_kernel,
@@ -386,14 +394,14 @@
             jax.ShapeDtypeStruct((ROWS, WIDTH), jnp.float32),
             jax.ShapeDtypeStruct((ROWS, HD), jnp.float32),
         ],
-        in_specs=[pl.BlockSpec(memory_space=pltpu.SMEM)] + [vmem] * 3,
+        in_specs=[pl.BlockSpec(memory_space=pltpu.SMEM)] + [vmem] * 5,
         out_specs=[vmem] * 2,
         compiler_params=pltpu.CompilerParams(vmem_limit_bytes=SMALL_VMEM),
         cost_estimate=pl.CostEstimate(
             flops=10**11, bytes_accessed=2 * 10**8, transcendentals=0
         ),
         name="combine_later",
-    )(ids, one, two, three)
+    )(ids, *ones, *twos, three)
 
 
 def combine_kernel(table, zero, values, sides, out, gate):
@@ -591,33 +599,38 @@
         [next_one, next_three],
         [pair, below, above, None, pair_there],
     )
-    next_two, across, piece_three, below_there, above_there, piece_one, piece_two, *states = together(
+    next_two, across, piece_one, piece_three, below_there, piece_two, above, *states = together(
         to_level(queries, 2),
         around(pair, "y", 2),
+        around(pieces[0], "x", 1),
         around(pieces[2], "x", 3),
         around(below, "c", 1),
-        around(above, "c", 1),
-        pieces[0],
         pieces[1],
+        above,
         *states,
     )
-    across_there = around(across, "c", 1)
+    above_there, across_there = around(above, "c", 1), around(across, "c", 1)
     pairs = [pair, below, above, across, pair_there, below_there, above_there, across_there]
-    piece_one, piece_two = around(piece_one, "x", 1), around(piece_two, "x", 2)
-
-    def back(share, d):
-        pairs_back = [
-            (8 * (i - d) + j, (8 * i + j - 1) % 32) for i in range(d, 4) for j in range(8)
-        ]
+    piece_two = around(piece_two, "x", 2)
+
+    def back(share, d, levels):
+        pairs_back = [(8 * i + j, (8 * (i + d) + j - 1) % 32) for i in levels for j in range(8)]
         return lax.ppermute(share, SLOT, pairs_back)
 
     two, one, three = attend(
         "middle", ids, group_live, noise_level, [next_two, next_one, next_three], pairs, states
     )
-    values_later, sides_later = combine_later(ids, back(one, 1), back(two, 2), back(three, 3))
+    one_later, two_later = back(one, 1, (1, 2)), back(two, 2, (1,))
+    one_first, two_first, three_first, piece_two = together(one, two, three, piece_two)
+    values_later, sides_later = combine_later(
+        ids,
+        [back(one_first, 1, (0,)), one_later],
+        [back(two_first, 2, (0,)), two_later],
+        back(three_first, 3, (0,)),
+    )
     live_later, one = together(group_live, one)
     (zero,) = attend("late", ids, live_later, noise_level, [queries], pairs)
-    zero, piece_one, piece_two = together(zero, piece_one, piece_two)
+    zero, one_later, two_later = together(zero, one_later, two_later)
     (fetched,) = copied(
         "stack",
         ids,
@@ -626,7 +639,9 @@
         tuple(("stack", k, 0, k) for k in range(3)),
     )
     swapped = around(fetched, "c", 1)
-    attended, gate_row = combine(level_table, back(zero, 0), values_later, sides_later)
+    attended, gate_row = combine(
+        level_table, back(zero, 0, (0, 1, 2, 3)), values_later, sides_later
+    )
 
     attended, hidden = together(attended, hidden)
     hidden_next = around(hidden, SLOT, -1)

time: 151 us -> 157 us (1.040)
  the two profiles are of different devices: /device:TPU:25 before, /device:TPU:192 now
where the time goes in v5:
time: 157 us; the launch traced here: 156 us
  waiting for transfers between devices  84.2 us (54%)
  starting transfers between devices  48.2 us (31%)
  Pallas kernels  20.2 us (13%)
  local copies, waits for them, and re-layouts  2.45 us (2%)
    ppermute x16, waiting for transfers between devices, around(): lax.ppermute(value, axis, [(i, (i + steps) % count) for i in range(count)])  51 us
    ppermute x16, starting transfers between devices, around(): lax.ppermute(value, axis, [(i, (i + steps) % count) for i in range(count)])  32.3 us
    ppermute x3, waiting for transfers between devices, to_level(): return lax.ppermute(value, 'z', [(i, i - d) for i in range(d, 4)])  16.6 us
    ppermute x6, waiting for transfers between devices, back(): return lax.ppermute(share, SLOT, pairs_back)  16.6 us
    ppermute x3, starting transfers between devices, to_level(): return lax.ppermute(value, 'z', [(i, i - d) for i in range(d, 4)])  10.6 us
    pallas_call x3, Pallas kernels, attend(): pl.pallas_call(functools.partial(attend_kernel, call), out_shape=out_shap...  6.13 us
    pallas_call x2, Pallas kernels, project(): pl.pallas_call(functools.partial(project_kernel, far), out_shape=jax.Shap...  5.61 us
    ppermute x6, starting transfers between devices, back(): return lax.ppermute(share, SLOT, pairs_back)  5.24 us
  transfers between devices with their start and end apart: 25, of which 13 were waited for; matrix products, arithmetic and copies ran while one was open for 0% of the time, Pallas kernels for 11%

profile of v5, /device:TPU:192, one launch (start us, length us, event | category | flops | bytes accessed | tf_op | source)
XLA Modules:
  0.0 156.0 jit_solution(11274091166349176959)
XLA Ops:
  0.0 2.0 %pack.1.refs_2_.refs_3_.refs_1_ = bf16[448,768]{1,0:T(8,128)(2,1)} custom-call(bf16[448,384]{1,0:T(8,128)(2,1)} %keys.1, bf16[448,384]{1,0:T(8,128)(2,1)} %values.1), custom_call_target="tpu_custom_call" | custom-call | tf_op jit(solution)/shard_map/pack/pallas_call | solution.py:467
  2.0 3.0 %collective-permute-start.3 = (bf16[448,768]{1,0:T(8,128)(2,1)}, bf16[448,768]{1,0:T(8,128)(2,1)S(1)}, u32[]{:S(2)}, u32[]{:S(2)}) collective-permute-start(bf16[448,768]{1,0:T(8,128)(2,1)} %pack.1.refs_2_.refs_3_.refs_1_), channel_id=1, source_target_pairs={{0,48},{16,0},{32,16},{48,32},{1,49},{17,1},{33,17},{49,33},{2,50}... | collective-permute-start | bytes 2064392 | tf_op jit(solution)/shard_map/ppermute | solution.py:555
  5.0 3.4 %collective-permute-start = (bf16[448,384]{1,0:T(8,128)(2,1)}, bf16[448,384]{1,0:T(8,128)(2,1)S(1)}, u32[]{:S(2)}, u32[]{:S(2)}) collective-permute-start(bf16[448,384]{1,0:T(8,128)(2,1)} %refs_0_.2), channel_id=1, source_target_pairs={{64,0},{128,64},{192,128},{65,1},{129,65},{193,129},{66,2},{130,66... | collective-permute-start | bytes 1032200 | tf_op jit(solution)/shard_map/ppermute | solution.py:573
  8.4 1.3 collective-permute-start.1
  10.4 0.1 stack.40.ids
  10.5 2.3 %copy-done = bf16[384,6144]{1,0:T(8,128)(2,1)S(1)} copy-done((bf16[384,6144]{1,0:T(8,128)(2,1)S(1)}, bf16[384,6144]{1,0:T(8,128)(2,1)}, u32[]{:S(2)}) %copy-start) | copy-done | bytes 4718616
  12.8 0.9 columns.1
  13.7 10.0 %collective-permute-done.refs_0_.refs_1_ = bf16[448,384]{1,0:T(8,128)(2,1)S(1)} collective-permute-done((bf16[448,384]{1,0:T(8,128)(2,1)}, bf16[448,384]{1,0:T(8,128)(2,1)S(1)}, u32[]{:S(2)}, u32[]{:S(2)}) %collective-permute-start) | collective-permute-done | bytes 344096 | tf_op jit(solution)/shard_map/ppermute | solution.py:573
  23.8 0.2 collective-permute-done.2.refs_3_.refs_4_.refs_2_
  24.0 5.9 %collective-permute-start.5 = (bf16[448,384]{1,0:T(8,128)(2,1)S(1)}, bf16[448,384]{1,0:T(8,128)(2,1)S(1)}, u32[]{:S(2)}, u32[]{:S(2)}) collective-permute-start(bf16[448,384]{1,0:T(8,128)(2,1)S(1)} %copy-done.3), channel_id=1, source_target_pairs={{128,0},{192,64},{129,1},{193,65},{130,2},{194,66},{131,3},{195,67... | collective-permute-start | bytes 1032200 | tf_op jit(solution)/shard_map/ppermute | solution.py:573
  29.9 1.6 %collective-permute-start.7 = (bf16[384,768]{1,0:T(8,128)(2,1)S(1)}, bf16[384,768]{1,0:T(8,128)(2,1)S(1)}, u32[]{:S(2)}, u32[]{:S(2)}) collective-permute-start(bf16[384,768]{1,0:T(8,128)(2,1)S(1)} %get-tuple-element.56), channel_id=1, source_target_pairs={{0,1},{1,2},{2,3},{3,0},{4,5},{5,6},{6,7},{7,4},{8,9},{9,10},{10,1... | collective-permute-start | bytes 1769480 | tf_op jit(solution)/shard_map/ppermute | solution.py:555
  31.5 1.7 %collective-permute-start.8 = (bf16[384,768]{1,0:T(8,128)(2,1)S(1)}, bf16[384,768]{1,0:T(8,128)(2,1)S(1)}, u32[]{:S(2)}, u32[]{:S(2)}) collective-permute-start(bf16[384,768]{1,0:T(8,128)(2,1)S(1)} %get-tuple-element.57), channel_id=1, source_target_pairs={{0,3},{1,0},{2,1},{3,2},{4,7},{5,4},{6,5},{7,6},{8,11},{9,8},{10,9... | collective-permute-start | bytes 1769480 | tf_op jit(solution)/shard_map/ppermute | solution.py:555
  33.2 1.9 %collective-permute-start.6 = (bf16[448,768]{1,0:T(8,128)(2,1)S(1)}, bf16[448,768]{1,0:T(8,128)(2,1)S(1)}, u32[]{:S(2)}, u32[]{:S(2)}) collective-permute-start(bf16[448,768]{1,0:T(8,128)(2,1)S(1)} %copy-done.1), channel_id=1, source_target_pairs={{0,32},{16,48},{32,0},{48,16},{1,33},{17,49},{33,1},{49,17},{2,34}... | collective-permute-start | bytes 2064392 | tf_op jit(solution)/shard_map/ppermute | solution.py:555
  35.2 0.7 attend_early.1
  35.9 6.6 %collective-permute-done.5.refs_0_ = bf16[448,384]{1,0:T(8,128)(2,1)S(1)} collective-permute-done((bf16[448,384]{1,0:T(8,128)(2,1)S(1)}, bf16[448,384]{1,0:T(8,128)(2,1)S(1)}, u32[]{:S(2)}, u32[]{:S(2)}) %collective-permute-start.5) | collective-permute-done | bytes 344096 | tf_op jit(solution)/shard_map/ppermute | solution.py:573
  42.5 3.4 %collective-permute-done.7.refs_0_ = bf16[384,768]{1,0:T(8,128)(2,1)S(1)} collective-permute-done((bf16[384,768]{1,0:T(8,128)(2,1)S(1)}, bf16[384,768]{1,0:T(8,128)(2,1)S(1)}, u32[]{:S(2)}, u32[]{:S(2)}) %collective-permute-start.7) | collective-permute-done | bytes 589856 | tf_op jit(solution)/shard_map/ppermute | solution.py:555
  45.9 5.1 %collective-permute-done.6.refs_6_.refs_4_ = bf16[448,768]{1,0:T(8,128)(2,1)S(1)} collective-permute-done((bf16[448,768]{1,0:T(8,128)(2,1)S(1)}, bf16[448,768]{1,0:T(8,128)(2,1)S(1)}, u32[]{:S(2)}, u32[]{:S(2)}) %collective-permute-start.6) | collective-permute-done | bytes 688160 | tf_op jit(solution)/shard_map/ppermute | solution.py:555
  51.0 0.5 collective-permute-start.11
  51.5 1.8 %collective-permute-start.15 = (bf16[384,768]{1,0:T(8,128)(2,1)S(1)}, bf16[384,768]{1,0:T(8,128)(2,1)S(1)}, u32[]{:S(2)}, u32[]{:S(2)}) collective-permute-start(bf16[384,768]{1,0:T(8,128)(2,1)S(1)} %get-tuple-element.81), channel_id=1, source_target_pairs={{0,2},{1,3},{2,0},{3,1},{4,6},{5,7},{6,4},{7,5},{8,10},{9,11},{10,... | collective-permute-start | bytes 1769480 | tf_op jit(solution)/shard_map/ppermute | solution.py:555
  53.3 0.8 collective-permute-done.11.refs_10_.refs_8_
  54.1 1.0 attend_middle.1
  55.1 1.3 collective-permute-start.12
  56.4 1.3 collective-permute-start.13
  57.7 10.5 %collective-permute-done.15.refs_1_ = bf16[384,768]{1,0:T(8,128)(2,1)S(1)} collective-permute-done((bf16[384,768]{1,0:T(8,128)(2,1)S(1)}, bf16[384,768]{1,0:T(8,128)(2,1)S(1)}, u32[]{:S(2)}, u32[]{:S(2)}) %collective-permute-start.15) | collective-permute-done | bytes 589856 | tf_op jit(solution)/shard_map/ppermute | solution.py:555
  68.2 0.7 collective-permute-start.16
  68.9 0.7 collective-permute-start.17
  69.6 1.3 collective-permute-start.18
  70.9 4.4 %attend_late.1 = bf16[480,384]{1,0:T(8,128)(2,1)S(1)} custom-call(s32[9]{0:T(128)S(1)} %stack.40.ids, s32[32]{0:T(128)S(1)} %copy-done.4, s32[1]{0:T(128)S(6)} %copy.9.level, bf16[448,384]{1,0:T(8,128)(2,1)S(1)} %copy-done.3, bf16[448,768]{1,0:T(8,128)(2,1)S(1)} %copy-done.1, bf16[448,768]{1,0:T(8,128)(2,1)S(1)} %collective-permute-done.2.refs_3_.refs_4_.refs_2_, ...), custom_call_target="tpu_custom_call" | custom-call | flops 11098128384 | bytes 8000000 | tf_op jit(solution)/shard_map/attend_late/pallas_call | solution.py:302
  75.3 0.9 stack.41.refs_5_
  76.3 0.0 copy-start.2
  76.3 0.0 copy-start.5
  76.3 9.5 %collective-permute-done.13.two_later = bf16[480,384]{1,0:T(8,128)(2,1)S(1)} collective-permute-done((bf16[480,384]{1,0:T(8,128)(2,1)S(1)}, bf16[480,384]{1,0:T(8,128)(2,1)S(1)}, u32[]{:S(2)}, u32[]{:S(2)}) %collective-permute-start.13) | collective-permute-done | bytes 368672 | tf_op jit(solution)/shard_map/ppermute | solution.py:618
  85.8 14.3 %collective-permute-start.23 = (bf16[3,384,768]{2,1,0:T(8,128)(2,1)S(1)}, bf16[3,384,768]{2,1,0:T(8,128)(2,1)S(1)}, u32[]{:S(2)}, u32[]{:S(2)}) collective-permute-start(bf16[3,384,768]{2,1,0:T(8,128)(2,1)S(1)} %stack.41.refs_5_), channel_id=1, source_target_pairs={{0,8},{8,0},{1,9},{9,1},{2,10},{10,2},{3,11},{11,3},{4,12},{12,4},... | collective-permute-start | bytes 5308424 | tf_op jit(solution)/shard_map/ppermute | solution.py:555
  100.1 1.9 %combine_later.1 = (f32[448,384]{1,0:T(8,128)S(1)}, f32[448,128]{1,0:T(8,128)S(1)}) custom-call(s32[9]{0:T(128)S(1)} %stack.40.ids, bf16[480,384]{1,0:T(8,128)(2,1)S(1)} %collective-permute-done.16.one_first, bf16[480,384]{1,0:T(8,128)(2,1)S(1)} %collective-permute-done.12.one_later, bf16[480,384]{1,0:T(8,128)(2,1)S(1)} %collective-permute-done.17.two_first, ...), custom_call_target="tpu_custom_call" | custom-call | flops 99999997952 | bytes 200000000 | tf_op jit(solution)/shard_map/combine_later/pallas_call | solution.py:391
  102.0 7.1 %collective-permute-done.14.zero = bf16[480,384]{1,0:T(8,128)(2,1)S(1)} collective-permute-done((bf16[480,384]{1,0:T(8,128)(2,1)S(1)}, bf16[480,384]{1,0:T(8,128)(2,1)S(1)}, u32[]{:S(2)}, u32[]{:S(2)}) %collective-permute-start.14) | collective-permute-done | bytes 368672 | tf_op jit(solution)/shard_map/ppermute | solution.py:618
  109.1 1.2 combine.1
  110.3 1.6 %collective-permute-start.22 = (bf16[448,384]{1,0:T(8,128)(2,1)S(1)}, bf16[448,384]{1,0:T(8,128)(2,1)S(1)}, u32[]{:S(2)}, u32[]{:S(2)}) collective-permute-start(bf16[448,384]{1,0:T(8,128)(2,1)S(1)} %get-tuple-element.90.refs_0_), channel_id=1, source_target_pairs={{0,3},{1,0},{2,1},{3,2},{4,7},{5,4},{6,5},{7,6},{8,11},{9,8},{10,9... | collective-permute-start | bytes 1032200 | tf_op jit(solution)/shard_map/ppermute | solution.py:555
  111.9 0.8 collective-permute-start.21
  112.7 0.9 collective-permute-start.20
  113.6 4.1 %collective-permute-start.19 = (bf16[448,768]{1,0:T(8,128)(2,1)S(1)}, bf16[448,768]{1,0:T(8,128)(2,1)S(1)}, u32[]{:S(2)}, u32[]{:S(2)}) collective-permute-start(bf16[448,768]{1,0:T(8,128)(2,1)S(1)} %copy-done.5), channel_id=1, source_target_pairs={{0,248},{8,0},{16,8},{24,16},{32,24},{40,32},{48,40},{56,48},{64,5... | collective-permute-start | bytes 2064392 | tf_op jit(solution)/shard_map/ppermute | solution.py:555
  117.7 3.6 %collective-permute-done.22.refs_3_ = bf16[448,384]{1,0:T(8,128)(2,1)S(1)} collective-permute-done((bf16[448,384]{1,0:T(8,128)(2,1)S(1)}, bf16[448,384]{1,0:T(8,128)(2,1)S(1)}, u32[]{:S(2)}, u32[]{:S(2)}) %collective-permute-start.22) | collective-permute-done | bytes 344096 | tf_op jit(solution)/shard_map/ppermute | solution.py:555
  121.3 3.0 %collective-permute-done.21.refs_2_ = bf16[448,384]{1,0:T(8,128)(2,1)S(1)} collective-permute-done((bf16[448,384]{1,0:T(8,128)(2,1)S(1)}, bf16[448,384]{1,0:T(8,128)(2,1)S(1)}, u32[]{:S(2)}, u32[]{:S(2)}) %collective-permute-start.21) | collective-permute-done | bytes 344096 | tf_op jit(solution)/shard_map/ppermute | solution.py:555
  124.3 7.0 %collective-permute-done.20.refs_1_ = bf16[448,384]{1,0:T(8,128)(2,1)S(1)} collective-permute-done((bf16[448,384]{1,0:T(8,128)(2,1)S(1)}, bf16[448,384]{1,0:T(8,128)(2,1)S(1)}, u32[]{:S(2)}, u32[]{:S(2)}) %collective-permute-start.20) | collective-permute-done | bytes 344096 | tf_op jit(solution)/shard_map/ppermute | solution.py:555
  131.4 2.8 %project.3 = bf16[448,768]{1,0:T(8,128)(2,1)S(1)} custom-call(s32[9]{0:T(128)S(1)} %stack.40.ids, bf16[448,384]{1,0:T(8,128)(2,1)S(1)} %get-tuple-element.90.refs_0_, bf16[448,384]{1,0:T(8,128)(2,1)S(1)} %collective-permute-done.20.refs_1_, bf16[448,384]{1,0:T(8,128)(2,1)S(1)} %collective-permute-done.21.refs_2_, ...), custom_call_target="tpu_custom_call" | custom-call | flops 1056964608 | bytes 5000000 | tf_op jit(solution)/shard_map/project/pallas_call | solution.py:539
  134.2 0.1 collective-permute-start.24
  134.3 2.8 %project.2.near = f32[448,768]{1,0:T(8,128)S(1)} custom-call(s32[9]{0:T(128)S(1)} %stack.40.ids, bf16[448,384]{1,0:T(8,128)(2,1)S(1)} %get-tuple-element.90.refs_0_, bf16[448,384]{1,0:T(8,128)(2,1)S(1)} %collective-permute-done.20.refs_1_, bf16[448,384]{1,0:T(8,128)(2,1)S(1)} %collective-permute-done.21.refs_2_, ...), custom_call_target="tpu_custom_call" | custom-call | flops 1056964608 | bytes 5000000 | tf_op jit(solution)/shard_map/project/pallas_call | solution.py:539
  137.1 17.3 %collective-permute-done.24.arrived = bf16[448,768]{1,0:T(8,128)(2,1)S(1)} collective-permute-done((bf16[448,768]{1,0:T(8,128)(2,1)S(1)}, bf16[448,768]{1,0:T(8,128)(2,1)S(1)}, u32[]{:S(2)}, u32[]{:S(2)}) %collective-permute-start.24) | collective-permute-done | bytes 688160 | tf_op jit(solution)/shard_map/ppermute | solution.py:555
  154.4 1.6 %finish.1 = bf16[448,768]{1,0:T(8,128)(2,1)} custom-call(bf16[448,768]{1,0:T(8,128)(2,1)S(1)} %collective-permute-done.19.hidden, f32[448,768]{1,0:T(8,128)S(1)} %project.2.near, bf16[448,768]{1,0:T(8,128)(2,1)S(1)} %collective-permute-done.24.arrived, f32[1,768]{1,0:T(1,128)S(1)} %get-tuple-element.96.gate), custom_call_target="tpu_custom_call" | custom-call | tf_op jit(solution)/shard_map/finish/pallas_call | solution.py:449
  (26 shorter events, 0.1 us)
Async XLA Ops:
  2.0 21.8 %collective-permute-start.4 = (bf16[448,768]{1,0:T(8,128)(2,1)}, bf16[448,768]{1,0:T(8,128)(2,1)S(1)}, u32[]{:S(2)}, u32[]{:S(2)}) collective-permute-start(bf16[448,768]{1,0:T(8,128)(2,1)} %pack.1.refs_2_.refs_3_.refs_1_), channel_id=1, source_target_pairs={{0,8},{8,0},{1,9},{9,1},{2,10},{10,2},{3,11},{11,3},{4,12},{12,4},... | collective-permute-start | bytes 2064392 | tf_op jit(solution)/shard_map/ppermute | solution.py:555
  2.0 21.8 %collective-permute-start.3 = (bf16[448,768]{1,0:T(8,128)(2,1)}, bf16[448,768]{1,0:T(8,128)(2,1)S(1)}, u32[]{:S(2)}, u32[]{:S(2)}) collective-permute-start(bf16[448,768]{1,0:T(8,128)(2,1)} %pack.1.refs_2_.refs_3_.refs_1_), channel_id=1, source_target_pairs={{0,48},{16,0},{32,16},{48,32},{1,49},{17,1},{33,17},{49,33},{2,50}... | collective-permute-start | bytes 2064392 | tf_op jit(solution)/shard_map/ppermute | solution.py:555
  5.0 19.0 %collective-permute-start.2 = (bf16[448,768]{1,0:T(8,128)(2,1)}, bf16[448,768]{1,0:T(8,128)(2,1)S(1)}, u32[]{:S(2)}, u32[]{:S(2)}) collective-permute-start(bf16[448,768]{1,0:T(8,128)(2,1)} %pack.1.refs_2_.refs_3_.refs_1_), channel_id=1, source_target_pairs={{0,16},{16,32},{32,48},{48,0},{1,17},{17,33},{33,49},{49,1},{2,18}... | collective-permute-start | bytes 2064392 | tf_op jit(solution)/shard_map/ppermute | solution.py:555
  5.0 18.7 %collective-permute-start = (bf16[448,384]{1,0:T(8,128)(2,1)}, bf16[448,384]{1,0:T(8,128)(2,1)S(1)}, u32[]{:S(2)}, u32[]{:S(2)}) collective-permute-start(bf16[448,384]{1,0:T(8,128)(2,1)} %refs_0_.2), channel_id=1, source_target_pairs={{64,0},{128,64},{192,128},{65,1},{129,65},{193,129},{66,2},{130,66... | collective-permute-start | bytes 1032200 | tf_op jit(solution)/shard_map/ppermute | solution.py:573
  8.4 15.4 %collective-permute-start.1 = (bf16[448,384]{1,0:T(8,128)(2,1)}, bf16[448,384]{1,0:T(8,128)(2,1)S(1)}, u32[]{:S(2)}, u32[]{:S(2)}) collective-permute-start(bf16[448,384]{1,0:T(8,128)(2,1)} %refs_0_.2), channel_id=1, source_target_pairs={{192,0},{193,1},{194,2},{195,3},{196,4},{197,5},{198,6},{199,7},{2... | collective-permute-start | bytes 1032200 | tf_op jit(solution)/shard_map/ppermute | solution.py:573
  10.5 2.3 %copy-start = (bf16[384,6144]{1,0:T(8,128)(2,1)S(1)}, bf16[384,6144]{1,0:T(8,128)(2,1)}, u32[]{:S(2)}) copy-start(bf16[384,6144]{1,0:T(8,128)(2,1)} %refs_0_.1) | copy-start | bytes 14155780
  12.8 11.2 %copy-start.3 = (bf16[448,384]{1,0:T(8,128)(2,1)S(1)}, bf16[448,384]{1,0:T(8,128)(2,1)}, u32[]{:S(2)}) copy-start(bf16[448,384]{1,0:T(8,128)(2,1)} %refs_0_.2) | copy-start | bytes 1032196
  12.8 20.4 %copy-start.1 = (bf16[448,768]{1,0:T(8,128)(2,1)S(1)}, bf16[448,768]{1,0:T(8,128)(2,1)}, u32[]{:S(2)}) copy-start(bf16[448,768]{1,0:T(8,128)(2,1)} %pack.1.refs_2_.refs_3_.refs_1_) | copy-start | bytes 2064388
  12.8 22.3 %copy-start.4 = (s32[32]{0:T(128)S(1)}, s32[32]{0:T(128)}, u32[]{:S(2)}) copy-start(s32[32]{0:T(128)} %live.4) | copy-start | bytes 388
  24.0 18.5 %collective-permute-start.5 = (bf16[448,384]{1,0:T(8,128)(2,1)S(1)}, bf16[448,384]{1,0:T(8,128)(2,1)S(1)}, u32[]{:S(2)}, u32[]{:S(2)}) collective-permute-start(bf16[448,384]{1,0:T(8,128)(2,1)S(1)} %copy-done.3), channel_id=1, source_target_pairs={{128,0},{192,64},{129,1},{193,65},{130,2},{194,66},{131,3},{195,67... | collective-permute-start | bytes 1032200 | tf_op jit(solution)/shard_map/ppermute | solution.py:573
  29.9 16.0 %collective-permute-start.7 = (bf16[384,768]{1,0:T(8,128)(2,1)S(1)}, bf16[384,768]{1,0:T(8,128)(2,1)S(1)}, u32[]{:S(2)}, u32[]{:S(2)}) collective-permute-start(bf16[384,768]{1,0:T(8,128)(2,1)S(1)} %get-tuple-element.56), channel_id=1, source_target_pairs={{0,1},{1,2},{2,3},{3,0},{4,5},{5,6},{6,7},{7,4},{8,9},{9,10},{10,1... | collective-permute-start | bytes 1769480 | tf_op jit(solution)/shard_map/ppermute | solution.py:555
  31.5 14.4 %collective-permute-start.8 = (bf16[384,768]{1,0:T(8,128)(2,1)S(1)}, bf16[384,768]{1,0:T(8,128)(2,1)S(1)}, u32[]{:S(2)}, u32[]{:S(2)}) collective-permute-start(bf16[384,768]{1,0:T(8,128)(2,1)S(1)} %get-tuple-element.57), channel_id=1, source_target_pairs={{0,3},{1,0},{2,1},{3,2},{4,7},{5,4},{6,5},{7,6},{8,11},{9,8},{10,9... | collective-permute-start | bytes 1769480 | tf_op jit(solution)/shard_map/ppermute | solution.py:555
  33.2 17.7 %collective-permute-start.6 = (bf16[448,768]{1,0:T(8,128)(2,1)S(1)}, bf16[448,768]{1,0:T(8,128)(2,1)S(1)}, u32[]{:S(2)}, u32[]{:S(2)}) collective-permute-start(bf16[448,768]{1,0:T(8,128)(2,1)S(1)} %copy-done.1), channel_id=1, source_target_pairs={{0,32},{16,48},{32,0},{48,16},{1,33},{17,49},{33,1},{49,17},{2,34}... | collective-permute-start | bytes 2064392 | tf_op jit(solution)/shard_map/ppermute | solution.py:555
  35.2 15.8 %collective-permute-start.9 = (bf16[448,768]{1,0:T(8,128)(2,1)S(1)}, bf16[448,768]{1,0:T(8,128)(2,1)S(1)}, u32[]{:S(2)}, u32[]{:S(2)}) collective-permute-start(bf16[448,768]{1,0:T(8,128)(2,1)S(1)} %collective-permute-done.2.refs_3_.refs_4_.refs_2_), channel_id=1, source_target_pairs={{0,8},{8,0},{1,9},{9,1},{2,10},{10,2},{3,11},{11,3},{4,12},{12,4},... | collective-permute-start | bytes 2064392 | tf_op jit(solution)/shard_map/ppermute | solution.py:555
  51.0 2.3 %collective-permute-start.10 = (bf16[448,768]{1,0:T(8,128)(2,1)S(1)}, bf16[448,768]{1,0:T(8,128)(2,1)S(1)}, u32[]{:S(2)}, u32[]{:S(2)}) collective-permute-start(bf16[448,768]{1,0:T(8,128)(2,1)S(1)} %collective-permute-done.3.refs_4_.refs_5_.refs_3_), channel_id=1, source_target_pairs={{0,8},{8,0},{1,9},{9,1},{2,10},{10,2},{3,11},{11,3},{4,12},{12,4},... | collective-permute-start | bytes 2064392 | tf_op jit(solution)/shard_map/ppermute | solution.py:555
  51.0 3.1 %collective-permute-start.11 = (bf16[448,768]{1,0:T(8,128)(2,1)S(1)}, bf16[448,768]{1,0:T(8,128)(2,1)S(1)}, u32[]{:S(2)}, u32[]{:S(2)}) collective-permute-start(bf16[448,768]{1,0:T(8,128)(2,1)S(1)} %collective-permute-done.6.refs_6_.refs_4_), channel_id=1, source_target_pairs={{0,8},{8,0},{1,9},{9,1},{2,10},{10,2},{3,11},{11,3},{4,12},{12,4},... | collective-permute-start | bytes 2064392 | tf_op jit(solution)/shard_map/ppermute | solution.py:555
  51.5 16.7 %collective-permute-start.15 = (bf16[384,768]{1,0:T(8,128)(2,1)S(1)}, bf16[384,768]{1,0:T(8,128)(2,1)S(1)}, u32[]{:S(2)}, u32[]{:S(2)}) collective-permute-start(bf16[384,768]{1,0:T(8,128)(2,1)S(1)} %get-tuple-element.81), channel_id=1, source_target_pairs={{0,2},{1,3},{2,0},{3,1},{4,6},{5,7},{6,4},{7,5},{8,10},{9,11},{10,... | collective-permute-start | bytes 1769480 | tf_op jit(solution)/shard_map/ppermute | solution.py:555
  55.1 44.9 %collective-permute-start.12 = (bf16[480,384]{1,0:T(8,128)(2,1)S(1)}, bf16[480,384]{1,0:T(8,128)(2,1)S(1)}, u32[]{:S(2)}, u32[]{:S(2)}) collective-permute-start(bf16[480,384]{1,0:T(8,128)(2,1)S(1)} %get-tuple-element.82), channel_id=1, source_target_pairs={{64,120},{72,128},{80,136},{88,144},{96,152},{104,160},{112,168},{... | collective-permute-start | bytes 1105928 | tf_op jit(solution)/shard_map/ppermute | solution.py:618
  56.4 29.4 %collective-permute-start.13 = (bf16[480,384]{1,0:T(8,128)(2,1)S(1)}, bf16[480,384]{1,0:T(8,128)(2,1)S(1)}, u32[]{:S(2)}, u32[]{:S(2)}) collective-permute-start(bf16[480,384]{1,0:T(8,128)(2,1)S(1)} %get-tuple-element.83), channel_id=1, source_target_pairs={{64,184},{72,192},{80,200},{88,208},{96,216},{104,224},{112,232},{... | collective-permute-start | bytes 1105928 | tf_op jit(solution)/shard_map/ppermute | solution.py:618
  68.2 31.8 %collective-permute-start.16 = (bf16[480,384]{1,0:T(8,128)(2,1)S(1)}, bf16[480,384]{1,0:T(8,128)(2,1)S(1)}, u32[]{:S(2)}, u32[]{:S(2)}) collective-permute-start(bf16[480,384]{1,0:T(8,128)(2,1)S(1)} %get-tuple-element.82), channel_id=1, source_target_pairs={{0,56},{8,64},{16,72},{24,80},{32,88},{40,96},{48,104},{56,112},{1... | collective-permute-start | bytes 1105928 | tf_op jit(solution)/shard_map/ppermute | solution.py:618
  68.9 31.1 %collective-permute-start.17 = (bf16[480,384]{1,0:T(8,128)(2,1)S(1)}, bf16[480,384]{1,0:T(8,128)(2,1)S(1)}, u32[]{:S(2)}, u32[]{:S(2)}) collective-permute-start(bf16[480,384]{1,0:T(8,128)(2,1)S(1)} %get-tuple-element.83), channel_id=1, source_target_pairs={{0,120},{8,128},{16,136},{24,144},{32,152},{40,160},{48,168},{56,1... | collective-permute-start | bytes 1105928 | tf_op jit(solution)/shard_map/ppermute | solution.py:618
  69.6 30.5 %collective-permute-start.18 = (bf16[480,384]{1,0:T(8,128)(2,1)S(1)}, bf16[480,384]{1,0:T(8,128)(2,1)S(1)}, u32[]{:S(2)}, u32[]{:S(2)}) collective-permute-start(bf16[480,384]{1,0:T(8,128)(2,1)S(1)} %get-tuple-element.84), channel_id=1, source_target_pairs={{0,184},{8,192},{16,200},{24,208},{32,216},{40,224},{48,232},{56,2... | collective-permute-start | bytes 1105928 | tf_op jit(solution)/shard_map/ppermute | solution.py:618
  76.3 32.8 %copy-start.2 = (f32[64,768]{1,0:T(8,128)S(1)}, f32[64,768]{1,0:T(8,128)}, u32[]{:S(2)}) copy-start(f32[64,768]{1,0:T(8,128)} %table.1) | copy-start | bytes 589828
  76.3 37.3 %copy-start.5 = (bf16[448,768]{1,0:T(8,128)(2,1)S(1)}, bf16[448,768]{1,0:T(8,128)(2,1)}, u32[]{:S(2)}) copy-start(bf16[448,768]{1,0:T(8,128)(2,1)} %param.8) | copy-start | bytes 2064388
  85.8 45.6 %collective-permute-start.23 = (bf16[3,384,768]{2,1,0:T(8,128)(2,1)S(1)}, bf16[3,384,768]{2,1,0:T(8,128)(2,1)S(1)}, u32[]{:S(2)}, u32[]{:S(2)}) collective-permute-start(bf16[3,384,768]{2,1,0:T(8,128)(2,1)S(1)} %stack.41.refs_5_), channel_id=1, source_target_pairs={{0,8},{8,0},{1,9},{9,1},{2,10},{10,2},{3,11},{11,3},{4,12},{12,4},... | collective-permute-start | bytes 5308424 | tf_op jit(solution)/shard_map/ppermute | solution.py:555
  100.0 9.0 %collective-permute-start.14 = (bf16[480,384]{1,0:T(8,128)(2,1)S(1)}, bf16[480,384]{1,0:T(8,128)(2,1)S(1)}, u32[]{:S(2)}, u32[]{:S(2)}) collective-permute-start(bf16[480,384]{1,0:T(8,128)(2,1)S(1)} %attend_late.1), channel_id=1, source_target_pairs={{0,248},{8,0},{16,8},{24,16},{32,24},{40,32},{48,40},{56,48},{64,5... | collective-permute-start | bytes 1105928 | tf_op jit(solution)/shard_map/ppermute | solution.py:618
  110.3 11.0 %collective-permute-start.22 = (bf16[448,384]{1,0:T(8,128)(2,1)S(1)}, bf16[448,384]{1,0:T(8,128)(2,1)S(1)}, u32[]{:S(2)}, u32[]{:S(2)}) collective-permute-start(bf16[448,384]{1,0:T(8,128)(2,1)S(1)} %get-tuple-element.90.refs_0_), channel_id=1, source_target_pairs={{0,3},{1,0},{2,1},{3,2},{4,7},{5,4},{6,5},{7,6},{8,11},{9,8},{10,9... | collective-permute-start | bytes 1032200 | tf_op jit(solution)/shard_map/ppermute | solution.py:555
  111.9 12.4 %collective-permute-start.21 = (bf16[448,384]{1,0:T(8,128)(2,1)S(1)}, bf16[448,384]{1,0:T(8,128)(2,1)S(1)}, u32[]{:S(2)}, u32[]{:S(2)}) collective-permute-start(bf16[448,384]{1,0:T(8,128)(2,1)S(1)} %get-tuple-element.90.refs_0_), channel_id=1, source_target_pairs={{0,2},{1,3},{2,0},{3,1},{4,6},{5,7},{6,4},{7,5},{8,10},{9,11},{10,... | collective-permute-start | bytes 1032200 | tf_op jit(solution)/shard_map/ppermute | solution.py:555
  112.7 18.6 %collective-permute-start.20 = (bf16[448,384]{1,0:T(8,128)(2,1)S(1)}, bf16[448,384]{1,0:T(8,128)(2,1)S(1)}, u32[]{:S(2)}, u32[]{:S(2)}) collective-permute-start(bf16[448,384]{1,0:T(8,128)(2,1)S(1)} %get-tuple-element.90.refs_0_), channel_id=1, source_target_pairs={{0,1},{1,2},{2,3},{3,0},{4,5},{5,6},{6,7},{7,4},{8,9},{9,10},{10,1... | collective-permute-start | bytes 1032200 | tf_op jit(solution)/shard_map/ppermute | solution.py:555
  113.6 23.5 %collective-permute-start.19 = (bf16[448,768]{1,0:T(8,128)(2,1)S(1)}, bf16[448,768]{1,0:T(8,128)(2,1)S(1)}, u32[]{:S(2)}, u32[]{:S(2)}) collective-permute-start(bf16[448,768]{1,0:T(8,128)(2,1)S(1)} %copy-done.5), channel_id=1, source_target_pairs={{0,248},{8,0},{16,8},{24,16},{32,24},{40,32},{48,40},{56,48},{64,5... | collective-permute-start | bytes 2064392 | tf_op jit(solution)/shard_map/ppermute | solution.py:555
  134.2 20.2 %collective-permute-start.24 = (bf16[448,768]{1,0:T(8,128)(2,1)S(1)}, bf16[448,768]{1,0:T(8,128)(2,1)S(1)}, u32[]{:S(2)}, u32[]{:S(2)}) collective-permute-start(bf16[448,768]{1,0:T(8,128)(2,1)S(1)} %project.3), channel_id=1, source_target_pairs={{0,4},{4,0},{1,5},{5,1},{2,6},{6,2},{3,7},{7,3},{8,12},{12,8},{9,1... | collective-permute-start | bytes 2064392 | tf_op jit(solution)/shard_map/ppermute | solution.py:555

commit v6 on v4

--- a/solution.py
+++ b/solution.py
@@ -30,16 +30,18 @@
     )
 
 
-CALLS = {"early": (1, 3), "middle": (2, 1, 3), "late": (0,)}
-EARLY, LATER = (0, 1, 2, 4), (3, 5, 6, 7)
+CALLS = {"early": (1, 3), "middle": (1, 3), "third": (2,), "late": (0,)}
+EARLY, LATER, ALL = (0, 1, 2, 4), (3, 5, 6, 7), tuple(range(8))
+COSTS = {"early": 10**10, "middle": 10**10, "third": 5 * 10**10, "late": 10**6}
+MEMBERS = {"early": EARLY, "middle": LATER, "third": ALL, "late": ALL}
 
 
 def attend_kernel(call, ids, live, level, *refs):
     steps = CALLS[call]
     many = len(steps)
     early, middle, late = call == "early", call == "middle", call == "late"
-    members = EARLY if early else tuple(range(8))
-    resumed = (1, 2) if middle else ()
+    members = MEMBERS[call]
+    resumed = (0, 1) if middle else ()
     kept = many if early else len(resumed)
     refs = list(refs)
 
@@ -60,18 +62,16 @@
         core_there = core if p < 4 else 1 - core
         groups[p] = first + lax.rem(y + Y_STEPS[p % 4] + 4, 4) * 2 + core_there
 
-    def live_before(group, part):
+    def live_before(group):
         count = jnp.int32(0)
-        for p in part:
-            if p in groups:
-                count = count + jnp.where(groups[p] < group, live[groups[p]], 0)
+        for p in members:
+            count = count + jnp.where(groups[p] < group, live[groups[p]], 0)
         return count
 
-    everything = first + 8
-    if late:
-        n_own = live_before(mine, members)
-    else:
-        n_early, n_later = live_before(everything, EARLY), live_before(everything, LATER)
+    bound = mine if late else first + 8
+    n_live = live_before(bound)
+    count = n_live + 1 if late else n_live
+    chunks = (count + 1) // 2
 
     def raw_copy(i):
         return pltpu.make_async_copy(query_in[i], raw.at[i], raw_sem.at[i])
@@ -107,21 +107,12 @@
     def run():
         for j, p in enumerate(members):
             if late and p == 0:
-                place_copy(j, n_own).start()
+                place_copy(j, n_live).start()
                 continue
-            wanted = live[groups[p]] == 1
-            if late:
-                wanted = wanted & (groups[p] < mine)
-                place = live_before(groups[p], members)
-            elif p in EARLY:
-                wanted = wanted & active(0) if middle else wanted
-                place = live_before(groups[p], EARLY)
-            else:
-                place = 4 + live_before(groups[p], LATER)
-
-            @pl.when(wanted)
-            def _():
-                place_copy(j, place).start()
+
+            @pl.when((live[groups[p]] == 1) & (groups[p] < bound))
+            def _():
+                place_copy(j, live_before(groups[p])).start()
 
         for i in range(many):
 
@@ -158,30 +149,17 @@
                     copy.wait()
 
     def source(i):
-        if early:
-            count, split, base = n_early, n_early, 4
-        elif middle:
-            count = jnp.where(i == 0, n_early + n_later, n_later)
-            split, base = jnp.where(i == 0, n_early, 0), 4
-        else:
-            count = n_own + 1
-            split, base = count, 4
-        chunks = (count + 1) // 2
-
-        waits = (i == 0) | jnp.logical_not(active(0))
-
-        def place_of(k):
-            return jnp.where(k < split, k, base + k - split)
+        waits = i == 0
 
         def arrive(t):
             for k in (2 * t, 2 * t + 1):
 
                 @pl.when(waits & (k < count))
                 def _():
-                    place_copy(0, place_of(k)).wait()
+                    place_copy(0, k).wait()
 
         def at(k):
-            place = place_of(jnp.maximum(jnp.minimum(k, count - 1), 0))
+            place = jnp.maximum(jnp.minimum(k, count - 1), 0)
             return pl.ds(pl.multiple_of(place * ROWS, 64), ROWS)
 
         for head in range(HEADS_HERE):
@@ -194,9 +172,7 @@
             top[i] = jnp.full(top.shape[1:], LOWEST, jnp.float32)
             acc[i] = jnp.zeros(acc.shape[1:], jnp.float32)
 
-        if middle:
-            pl.when(i == 0)(fresh)
-        else:
+        if not middle:
             fresh()
 
         def scores_of(t, head):
@@ -280,10 +256,7 @@
         pad = jnp.zeros((16, 2 * WIDTH - ROWS), jnp.bfloat16)
         done[i, ROWS + 16 : ROWS + 32, :] = jnp.concatenate([flat[:, WIDTH:], pad], axis=1)
 
-    if late:
-        run()
-    else:
-        pl.when(active(steps.index(1)))(run)
+    pl.when(active(0))(run)
 
 
 def attend(call, ids, live, level, queries, pairs, states=()):
@@ -292,7 +265,7 @@
     bf16, f32 = jnp.bfloat16, jnp.float32
     many = len(CALLS[call])
     early = call == "early"
-    members = EARLY if early else tuple(range(8))
+    members = MEMBERS[call]
     state = [(HEADS_HERE, ROWS, 2 * HD), (HEADS_HERE, ROWS, HD)]
     if early:
         out_shape = [jax.ShapeDtypeStruct(shape, f32) for shape in state * many]
@@ -319,7 +292,7 @@
         ],
         compiler_params=pltpu.CompilerParams(vmem_limit_bytes=ATTEND_VMEM),
         cost_estimate=pl.CostEstimate(
-            flops=12 * HEADS_HERE * ROWS * ROWS * HD * 12, bytes_accessed=8000000, transcendentals=0
+            flops=COSTS[call], bytes_accessed=10**6, transcendentals=0
         ),
         name="attend_" + call,
     )(ids, live, level, *operands)
@@ -591,19 +564,19 @@
         [next_one, next_three],
         [pair, below, above, None, pair_there],
     )
-    next_two, across, piece_three, below_there, above_there, piece_one, piece_two, *states = together(
+    next_two, across, piece_one, piece_three, below_there, piece_two, above, *states = together(
         to_level(queries, 2),
         around(pair, "y", 2),
+        around(pieces[0], "x", 1),
         around(pieces[2], "x", 3),
         around(below, "c", 1),
-        around(above, "c", 1),
-        pieces[0],
         pieces[1],
+        above,
         *states,
     )
-    across_there = around(across, "c", 1)
+    above_there, across_there = around(above, "c", 1), around(across, "c", 1)
     pairs = [pair, below, above, across, pair_there, below_there, above_there, across_there]
-    piece_one, piece_two = around(piece_one, "x", 1), around(piece_two, "x", 2)
+    piece_two = around(piece_two, "x", 2)
 
     def back(share, d):
         pairs_back = [
@@ -611,13 +584,17 @@
         ]
         return lax.ppermute(share, SLOT, pairs_back)
 
-    two, one, three = attend(
-        "middle", ids, group_live, noise_level, [next_two, next_one, next_three], pairs, states
-    )
-    values_later, sides_later = combine_later(ids, back(one, 1), back(two, 2), back(three, 3))
-    live_later, one = together(group_live, one)
-    (zero,) = attend("late", ids, live_later, noise_level, [queries], pairs)
-    zero, piece_one, piece_two = together(zero, piece_one, piece_two)
+    one, three = attend(
+        "middle", ids, group_live, noise_level, [next_one, next_three], pairs, states
+    )
+    back_one, back_three = back(one, 1), back(three, 3)
+    live_third, one = together(group_live, one)
+    (two,) = attend("third", ids, live_third, noise_level, [next_two], pairs)
+    back_two = back(two, 2)
+    live_late, two = together(group_live, two)
+    (zero,) = attend("late", ids, live_late, noise_level, [queries], pairs)
+    zero, back_one, back_three, piece_two = together(zero, back_one, back_three, piece_two)
+    values_later, sides_later = combine_later(ids, back_one, back_two, back_three)
     (fetched,) = copied(
         "stack",
         ids,

time: 151 us -> 149 us (0.987)
  the two profiles are of different devices: /device:TPU:25 before, /device:TPU:1 now
where the time goes in v6:
time: 149 us; the launch traced here: 146 us
  waiting for transfers between devices  63.3 us (42%)
  Pallas kernels  49.4 us (33%)
  starting transfers between devices  29.9 us (20%)
  local copies, waits for them, and re-layouts  2.45 us (2%)
    ppermute x16, waiting for transfers between devices, around(): lax.ppermute(value, axis, [(i, (i + steps) % count) for i in range(count)])  37.9 us
    pallas_call x4, Pallas kernels, attend(): pl.pallas_call(functools.partial(attend_kernel, call), out_shape=out_shap...  35.3 us
    ppermute x16, starting transfers between devices, around(): lax.ppermute(value, axis, [(i, (i + steps) % count) for i in range(count)])  17.8 us
    ppermute x3, waiting for transfers between devices, to_level(): return lax.ppermute(value, 'z', [(i, i - d) for i in range(d, 4)])  13.2 us
    ppermute x4, waiting for transfers between devices, back(): return lax.ppermute(share, SLOT, pairs_back)  12.2 us
    ppermute x4, starting transfers between devices, back(): return lax.ppermute(share, SLOT, pairs_back)  8.22 us
    pallas_call x2, Pallas kernels, project(): pl.pallas_call(functools.partial(project_kernel, far), out_shape=jax.Shap...  5.63 us
    ppermute x3, starting transfers between devices, to_level(): return lax.ppermute(value, 'z', [(i, i - d) for i in range(d, 4)])  3.86 us
  transfers between devices with their start and end apart: 23, of which 11 were waited for; matrix products, arithmetic and copies ran while one was open for 0% of the time, Pallas kernels for 31%

profile of v6, /device:TPU:1, one launch (start us, length us, event | category | flops | bytes accessed | tf_op | source)
XLA Modules:
  0.0 146.0 jit_solution(6775681327760665086)
XLA Ops:
  0.0 2.0 %pack.1.refs_2_.refs_1_ = bf16[448,768]{1,0:T(8,128)(2,1)} custom-call(bf16[448,384]{1,0:T(8,128)(2,1)} %keys.1, bf16[448,384]{1,0:T(8,128)(2,1)} %values.1), custom_call_target="tpu_custom_call" | custom-call | tf_op jit(solution)/shard_map/pack/pallas_call | solution.py:432
  2.0 3.2 %collective-permute-start.4 = (bf16[448,768]{1,0:T(8,128)(2,1)}, bf16[448,768]{1,0:T(8,128)(2,1)S(1)}, u32[]{:S(2)}, u32[]{:S(2)}) collective-permute-start(bf16[448,768]{1,0:T(8,128)(2,1)} %pack.1.refs_2_.refs_1_), channel_id=1, source_target_pairs={{0,8},{8,0},{1,9},{9,1},{2,10},{10,2},{3,11},{11,3},{4,12},{12,4},... | collective-permute-start | bytes 2064392 | tf_op jit(solution)/shard_map/ppermute | solution.py:520
  5.2 1.0 collective-permute-start.3
  6.2 0.5 collective-permute-start.2
  6.7 1.3 collective-permute-start
  8.0 1.3 collective-permute-start.1
  10.0 0.1 stack.40.ids
  10.1 2.3 %copy-done = bf16[384,6144]{1,0:T(8,128)(2,1)S(1)} copy-done((bf16[384,6144]{1,0:T(8,128)(2,1)S(1)}, bf16[384,6144]{1,0:T(8,128)(2,1)}, u32[]{:S(2)}) %copy-start) | copy-done | bytes 4718616
  12.4 0.9 columns.1
  13.3 13.2 %collective-permute-done.refs_0_ = bf16[448,384]{1,0:T(8,128)(2,1)S(1)} collective-permute-done((bf16[448,384]{1,0:T(8,128)(2,1)}, bf16[448,384]{1,0:T(8,128)(2,1)S(1)}, u32[]{:S(2)}, u32[]{:S(2)}) %collective-permute-start) | collective-permute-done | bytes 344096 | tf_op jit(solution)/shard_map/ppermute | solution.py:538
  26.5 1.3 collective-permute-start.5
  27.8 1.7 %collective-permute-start.7 = (bf16[384,768]{1,0:T(8,128)(2,1)S(1)}, bf16[384,768]{1,0:T(8,128)(2,1)S(1)}, u32[]{:S(2)}, u32[]{:S(2)}) collective-permute-start(bf16[384,768]{1,0:T(8,128)(2,1)S(1)} %get-tuple-element.57), channel_id=1, source_target_pairs={{0,1},{1,2},{2,3},{3,0},{4,5},{5,6},{6,7},{7,4},{8,9},{9,10},{10,1... | collective-permute-start | bytes 1769480 | tf_op jit(solution)/shard_map/ppermute | solution.py:520
  29.6 1.4 collective-permute-start.8
  30.9 1.4 collective-permute-start.6
  32.3 1.9 %collective-permute-start.9 = (bf16[448,768]{1,0:T(8,128)(2,1)S(1)}, bf16[448,768]{1,0:T(8,128)(2,1)S(1)}, u32[]{:S(2)}, u32[]{:S(2)}) collective-permute-start(bf16[448,768]{1,0:T(8,128)(2,1)S(1)} %collective-permute-done.2.refs_3_.refs_2_), channel_id=1, source_target_pairs={{0,8},{8,0},{1,9},{9,1},{2,10},{10,2},{3,11},{11,3},{4,12},{12,4},... | collective-permute-start | bytes 2064392 | tf_op jit(solution)/shard_map/ppermute | solution.py:520
  34.3 7.9 %attend_early.1 = (f32[3,448,256]{2,1,0:T(8,128)S(1)}, f32[3,448,128]{2,1,0:T(8,128)S(1)}, f32[3,448,256]{2,1,0:T(8,128)S(1)}, f32[3,448,128]{2,1,0:T(8,128)S(1)}) custom-call(s32[9]{0:T(128)S(1)} %stack.40.ids, s32[32]{0:T(128)S(1)} %copy-done.4, s32[1]{0:T(128)S(6)} %copy.9.level, bf16[448,384]{1,0:T(8,128)(2,1)S(1)} %collective-permute-done.refs_0_, ...), custom_call_target="tpu_custom_call" | custom-call | flops 10000000000 | bytes 1000000 | tf_op jit(solution)/shard_map/attend_early/pallas_call | solution.py:275
  42.3 1.0 collective-permute-done.7.refs_0_
  43.2 0.1 collective-permute-done.8.refs_2_
  43.3 4.6 %collective-permute-done.6.refs_2_.refs_4_ = bf16[448,768]{1,0:T(8,128)(2,1)S(1)} collective-permute-done((bf16[448,768]{1,0:T(8,128)(2,1)S(1)}, bf16[448,768]{1,0:T(8,128)(2,1)S(1)}, u32[]{:S(2)}, u32[]{:S(2)}) %collective-permute-start.6) | collective-permute-done | bytes 688160 | tf_op jit(solution)/shard_map/ppermute | solution.py:520
  47.9 2.4 %collective-permute-start.10 = (bf16[448,768]{1,0:T(8,128)(2,1)S(1)}, bf16[448,768]{1,0:T(8,128)(2,1)S(1)}, u32[]{:S(2)}, u32[]{:S(2)}) collective-permute-start(bf16[448,768]{1,0:T(8,128)(2,1)S(1)} %collective-permute-done.3.refs_4_.refs_3_), channel_id=1, source_target_pairs={{0,8},{8,0},{1,9},{9,1},{2,10},{10,2},{3,11},{11,3},{4,12},{12,4},... | collective-permute-start | bytes 2064392 | tf_op jit(solution)/shard_map/ppermute | solution.py:520
  50.3 1.6 %collective-permute-start.14 = (bf16[384,768]{1,0:T(8,128)(2,1)S(1)}, bf16[384,768]{1,0:T(8,128)(2,1)S(1)}, u32[]{:S(2)}, u32[]{:S(2)}) collective-permute-start(bf16[384,768]{1,0:T(8,128)(2,1)S(1)} %get-tuple-element.79), channel_id=1, source_target_pairs={{0,2},{1,3},{2,0},{3,1},{4,6},{5,7},{6,4},{7,5},{8,10},{9,11},{10,... | collective-permute-start | bytes 1769480 | tf_op jit(solution)/shard_map/ppermute | solution.py:520
  51.9 0.1 collective-permute-done.10.refs_4_.refs_7_
  52.0 1.0 collective-permute-done.11.refs_5_.refs_8_
  53.0 13.2 %attend_middle.1 = (bf16[480,384]{1,0:T(8,128)(2,1)S(1)}, bf16[480,384]{1,0:T(8,128)(2,1)S(1)}) custom-call(s32[9]{0:T(128)S(1)} %stack.40.ids, s32[32]{0:T(128)S(1)} %copy-done.4, s32[1]{0:T(128)S(6)} %copy.9.level, bf16[448,384]{1,0:T(8,128)(2,1)S(1)} %collective-permute-done.refs_0_, bf16[448,384]{1,0:T(8,128)(2,1)S(1)} %collective-permute-done.1.refs_1_, ...), custom_call_target="tpu_custom_call" | custom-call | flops 10000000000 | bytes 1000000 | tf_op jit(solution)/shard_map/attend_middle/pallas_call | solution.py:275
  66.2 1.3 collective-permute-start.12
  67.6 1.3 collective-permute-start.13
  68.9 9.5 %attend_third.1 = bf16[480,384]{1,0:T(8,128)(2,1)S(1)} custom-call(s32[9]{0:T(128)S(1)} %stack.40.ids, s32[32]{0:T(128)S(1)} %copy-done.4, s32[1]{0:T(128)S(6)} %copy.9.level, bf16[448,384]{1,0:T(8,128)(2,1)S(1)} %collective-permute-done.5.refs_0_, bf16[448,768]{1,0:T(8,128)(2,1)S(1)} %copy-done.1, ...), custom_call_target="tpu_custom_call" | custom-call | flops 49999998976 | bytes 1000000 | tf_op jit(solution)/shard_map/attend_third/pallas_call | solution.py:275
  78.4 1.3 collective-permute-start.16
  79.7 4.7 %attend_late.1 = bf16[480,384]{1,0:T(8,128)(2,1)S(1)} custom-call(s32[9]{0:T(128)S(1)} %stack.40.ids, s32[32]{0:T(128)S(1)} %copy-done.4, s32[1]{0:T(128)S(6)} %copy.9.level, bf16[448,384]{1,0:T(8,128)(2,1)S(1)} %copy-done.2, bf16[448,768]{1,0:T(8,128)(2,1)S(1)} %copy-done.1, bf16[448,768]{1,0:T(8,128)(2,1)S(1)} %collective-permute-done.2.refs_3_.refs_2_, ...), custom_call_target="tpu_custom_call" | custom-call | flops 1000000 | bytes 1000000 | tf_op jit(solution)/shard_map/attend_late/pallas_call | solution.py:275
  84.4 4.3 %collective-permute-start.15 = (bf16[480,384]{1,0:T(8,128)(2,1)S(1)}, bf16[480,384]{1,0:T(8,128)(2,1)S(1)}, u32[]{:S(2)}, u32[]{:S(2)}) collective-permute-start(bf16[480,384]{1,0:T(8,128)(2,1)S(1)} %attend_late.1), channel_id=1, source_target_pairs={{0,248},{8,0},{16,8},{24,16},{32,24},{40,32},{48,40},{56,48},{64,5... | collective-permute-start | bytes 1105928 | tf_op jit(solution)/shard_map/ppermute | solution.py:585
  88.7 0.9 stack.41.refs_5_
  89.7 0.0 copy-start.3
  89.7 0.0 copy-start.5
  89.7 0.1 collective-permute-start.21
  89.8 1.9 %combine_later.1 = (f32[448,384]{1,0:T(8,128)S(1)}, f32[448,128]{1,0:T(8,128)S(1)}) custom-call(s32[9]{0:T(128)S(1)} %stack.40.ids, bf16[480,384]{1,0:T(8,128)(2,1)S(1)} %collective-permute-done.12.one, bf16[480,384]{1,0:T(8,128)(2,1)S(1)} %collective-permute-done.16.two, bf16[480,384]{1,0:T(8,128)(2,1)S(1)} %collective-permute-done.13.three), custom_call_target="tpu_custom_call" | custom-call | flops 99999997952 | bytes 200000000 | tf_op jit(solution)/shard_map/combine_later/pallas_call | solution.py:356
  91.7 12.2 %collective-permute-done.15.zero = bf16[480,384]{1,0:T(8,128)(2,1)S(1)} collective-permute-done((bf16[480,384]{1,0:T(8,128)(2,1)S(1)}, bf16[480,384]{1,0:T(8,128)(2,1)S(1)}, u32[]{:S(2)}, u32[]{:S(2)}) %collective-permute-start.15) | collective-permute-done | bytes 368672 | tf_op jit(solution)/shard_map/ppermute | solution.py:585
  103.9 1.2 combine.1
  105.1 1.3 collective-permute-start.20
  106.4 0.5 collective-permute-start.19
  106.9 0.6 collective-permute-start.18
  107.5 7.8 %collective-permute-done.20.refs_3_ = bf16[448,384]{1,0:T(8,128)(2,1)S(1)} collective-permute-done((bf16[448,384]{1,0:T(8,128)(2,1)S(1)}, bf16[448,384]{1,0:T(8,128)(2,1)S(1)}, u32[]{:S(2)}, u32[]{:S(2)}) %collective-permute-start.20) | collective-permute-done | bytes 344096 | tf_op jit(solution)/shard_map/ppermute | solution.py:520
  115.3 2.5 %collective-permute-done.19.refs_2_ = bf16[448,384]{1,0:T(8,128)(2,1)S(1)} collective-permute-done((bf16[448,384]{1,0:T(8,128)(2,1)S(1)}, bf16[448,384]{1,0:T(8,128)(2,1)S(1)}, u32[]{:S(2)}, u32[]{:S(2)}) %collective-permute-start.19) | collective-permute-done | bytes 344096 | tf_op jit(solution)/shard_map/ppermute | solution.py:520
  117.8 4.3 %collective-permute-done.18.refs_1_ = bf16[448,384]{1,0:T(8,128)(2,1)S(1)} collective-permute-done((bf16[448,384]{1,0:T(8,128)(2,1)S(1)}, bf16[448,384]{1,0:T(8,128)(2,1)S(1)}, u32[]{:S(2)}, u32[]{:S(2)}) %collective-permute-start.18) | collective-permute-done | bytes 344096 | tf_op jit(solution)/shard_map/ppermute | solution.py:520
  122.1 2.8 %project.3 = bf16[448,768]{1,0:T(8,128)(2,1)S(1)} custom-call(s32[9]{0:T(128)S(1)} %stack.40.ids, bf16[448,384]{1,0:T(8,128)(2,1)S(1)} %get-tuple-element.88.refs_0_, bf16[448,384]{1,0:T(8,128)(2,1)S(1)} %collective-permute-done.18.refs_1_, bf16[448,384]{1,0:T(8,128)(2,1)S(1)} %collective-permute-done.19.refs_2_, ...), custom_call_target="tpu_custom_call" | custom-call | flops 1056964608 | bytes 5000000 | tf_op jit(solution)/shard_map/project/pallas_call | solution.py:504
  124.9 0.1 collective-permute-start.22
  125.0 2.8 %project.2.near = f32[448,768]{1,0:T(8,128)S(1)} custom-call(s32[9]{0:T(128)S(1)} %stack.40.ids, bf16[448,384]{1,0:T(8,128)(2,1)S(1)} %get-tuple-element.88.refs_0_, bf16[448,384]{1,0:T(8,128)(2,1)S(1)} %collective-permute-done.18.refs_1_, bf16[448,384]{1,0:T(8,128)(2,1)S(1)} %collective-permute-done.19.refs_2_, ...), custom_call_target="tpu_custom_call" | custom-call | flops 1056964608 | bytes 5000000 | tf_op jit(solution)/shard_map/project/pallas_call | solution.py:504
  127.9 16.6 %collective-permute-done.22.arrived = bf16[448,768]{1,0:T(8,128)(2,1)S(1)} collective-permute-done((bf16[448,768]{1,0:T(8,128)(2,1)S(1)}, bf16[448,768]{1,0:T(8,128)(2,1)S(1)}, u32[]{:S(2)}, u32[]{:S(2)}) %collective-permute-start.22) | collective-permute-done | bytes 688160 | tf_op jit(solution)/shard_map/ppermute | solution.py:520
  144.4 1.6 %finish.1 = bf16[448,768]{1,0:T(8,128)(2,1)} custom-call(bf16[448,768]{1,0:T(8,128)(2,1)S(1)} %collective-permute-done.17.hidden, f32[448,768]{1,0:T(8,128)S(1)} %project.2.near, bf16[448,768]{1,0:T(8,128)(2,1)S(1)} %collective-permute-done.22.arrived, f32[1,768]{1,0:T(1,128)S(1)} %get-tuple-element.94.gate), custom_call_target="tpu_custom_call" | custom-call | tf_op jit(solution)/shard_map/finish/pallas_call | solution.py:414
  (23 shorter events, 0.1 us)
Async XLA Ops:
  2.0 24.5 %collective-permute-start.4 = (bf16[448,768]{1,0:T(8,128)(2,1)}, bf16[448,768]{1,0:T(8,128)(2,1)S(1)}, u32[]{:S(2)}, u32[]{:S(2)}) collective-permute-start(bf16[448,768]{1,0:T(8,128)(2,1)} %pack.1.refs_2_.refs_1_), channel_id=1, source_target_pairs={{0,8},{8,0},{1,9},{9,1},{2,10},{10,2},{3,11},{11,3},{4,12},{12,4},... | collective-permute-start | bytes 2064392 | tf_op jit(solution)/shard_map/ppermute | solution.py:520
  5.2 21.3 %collective-permute-start.3 = (bf16[448,768]{1,0:T(8,128)(2,1)}, bf16[448,768]{1,0:T(8,128)(2,1)S(1)}, u32[]{:S(2)}, u32[]{:S(2)}) collective-permute-start(bf16[448,768]{1,0:T(8,128)(2,1)} %pack.1.refs_2_.refs_1_), channel_id=1, source_target_pairs={{0,48},{16,0},{32,16},{48,32},{1,49},{17,1},{33,17},{49,33},{2,50}... | collective-permute-start | bytes 2064392 | tf_op jit(solution)/shard_map/ppermute | solution.py:520
  6.2 20.3 %collective-permute-start.2 = (bf16[448,768]{1,0:T(8,128)(2,1)}, bf16[448,768]{1,0:T(8,128)(2,1)S(1)}, u32[]{:S(2)}, u32[]{:S(2)}) collective-permute-start(bf16[448,768]{1,0:T(8,128)(2,1)} %pack.1.refs_2_.refs_1_), channel_id=1, source_target_pairs={{0,16},{16,32},{32,48},{48,0},{1,17},{17,33},{33,49},{49,1},{2,18}... | collective-permute-start | bytes 2064392 | tf_op jit(solution)/shard_map/ppermute | solution.py:520
  6.7 19.8 %collective-permute-start = (bf16[448,384]{1,0:T(8,128)(2,1)}, bf16[448,384]{1,0:T(8,128)(2,1)S(1)}, u32[]{:S(2)}, u32[]{:S(2)}) collective-permute-start(bf16[448,384]{1,0:T(8,128)(2,1)} %refs_0_.2), channel_id=1, source_target_pairs={{64,0},{128,64},{192,128},{65,1},{129,65},{193,129},{66,2},{130,66... | collective-permute-start | bytes 1032200 | tf_op jit(solution)/shard_map/ppermute | solution.py:538
  8.0 18.5 %collective-permute-start.1 = (bf16[448,384]{1,0:T(8,128)(2,1)}, bf16[448,384]{1,0:T(8,128)(2,1)S(1)}, u32[]{:S(2)}, u32[]{:S(2)}) collective-permute-start(bf16[448,384]{1,0:T(8,128)(2,1)} %refs_0_.2), channel_id=1, source_target_pairs={{192,0},{193,1},{194,2},{195,3},{196,4},{197,5},{198,6},{199,7},{2... | collective-permute-start | bytes 1032200 | tf_op jit(solution)/shard_map/ppermute | solution.py:538
  10.1 2.3 %copy-start = (bf16[384,6144]{1,0:T(8,128)(2,1)S(1)}, bf16[384,6144]{1,0:T(8,128)(2,1)}, u32[]{:S(2)}) copy-start(bf16[384,6144]{1,0:T(8,128)(2,1)} %refs_0_.1) | copy-start | bytes 14155780
  12.4 14.1 %copy-start.2 = (bf16[448,384]{1,0:T(8,128)(2,1)S(1)}, bf16[448,384]{1,0:T(8,128)(2,1)}, u32[]{:S(2)}) copy-start(bf16[448,384]{1,0:T(8,128)(2,1)} %refs_0_.2) | copy-start | bytes 1032196
  12.4 18.5 %copy-start.1 = (bf16[448,768]{1,0:T(8,128)(2,1)S(1)}, bf16[448,768]{1,0:T(8,128)(2,1)}, u32[]{:S(2)}) copy-start(bf16[448,768]{1,0:T(8,128)(2,1)} %pack.1.refs_2_.refs_1_) | copy-start | bytes 2064388
  12.4 21.9 %copy-start.4 = (s32[32]{0:T(128)S(1)}, s32[32]{0:T(128)}, u32[]{:S(2)}) copy-start(s32[32]{0:T(128)} %live.5) | copy-start | bytes 388
  26.5 15.7 %collective-permute-start.5 = (bf16[448,384]{1,0:T(8,128)(2,1)S(1)}, bf16[448,384]{1,0:T(8,128)(2,1)S(1)}, u32[]{:S(2)}, u32[]{:S(2)}) collective-permute-start(bf16[448,384]{1,0:T(8,128)(2,1)S(1)} %copy-done.2), channel_id=1, source_target_pairs={{128,0},{192,64},{129,1},{193,65},{130,2},{194,66},{131,3},{195,67... | collective-permute-start | bytes 1032200 | tf_op jit(solution)/shard_map/ppermute | solution.py:538
  27.8 15.4 %collective-permute-start.7 = (bf16[384,768]{1,0:T(8,128)(2,1)S(1)}, bf16[384,768]{1,0:T(8,128)(2,1)S(1)}, u32[]{:S(2)}, u32[]{:S(2)}) collective-permute-start(bf16[384,768]{1,0:T(8,128)(2,1)S(1)} %get-tuple-element.57), channel_id=1, source_target_pairs={{0,1},{1,2},{2,3},{3,0},{4,5},{5,6},{6,7},{7,4},{8,9},{9,10},{10,1... | collective-permute-start | bytes 1769480 | tf_op jit(solution)/shard_map/ppermute | solution.py:520
  29.6 13.8 %collective-permute-start.8 = (bf16[384,768]{1,0:T(8,128)(2,1)S(1)}, bf16[384,768]{1,0:T(8,128)(2,1)S(1)}, u32[]{:S(2)}, u32[]{:S(2)}) collective-permute-start(bf16[384,768]{1,0:T(8,128)(2,1)S(1)} %get-tuple-element.58), channel_id=1, source_target_pairs={{0,3},{1,0},{2,1},{3,2},{4,7},{5,4},{6,5},{7,6},{8,11},{9,8},{10,9... | collective-permute-start | bytes 1769480 | tf_op jit(solution)/shard_map/ppermute | solution.py:520
  30.9 17.0 %collective-permute-start.6 = (bf16[448,768]{1,0:T(8,128)(2,1)S(1)}, bf16[448,768]{1,0:T(8,128)(2,1)S(1)}, u32[]{:S(2)}, u32[]{:S(2)}) collective-permute-start(bf16[448,768]{1,0:T(8,128)(2,1)S(1)} %copy-done.1), channel_id=1, source_target_pairs={{0,32},{16,48},{32,0},{48,16},{1,33},{17,49},{33,1},{49,17},{2,34}... | collective-permute-start | bytes 2064392 | tf_op jit(solution)/shard_map/ppermute | solution.py:520
  32.3 15.6 %collective-permute-start.9 = (bf16[448,768]{1,0:T(8,128)(2,1)S(1)}, bf16[448,768]{1,0:T(8,128)(2,1)S(1)}, u32[]{:S(2)}, u32[]{:S(2)}) collective-permute-start(bf16[448,768]{1,0:T(8,128)(2,1)S(1)} %collective-permute-done.2.refs_3_.refs_2_), channel_id=1, source_target_pairs={{0,8},{8,0},{1,9},{9,1},{2,10},{10,2},{3,11},{11,3},{4,12},{12,4},... | collective-permute-start | bytes 2064392 | tf_op jit(solution)/shard_map/ppermute | solution.py:520
  47.9 4.1 %collective-permute-start.10 = (bf16[448,768]{1,0:T(8,128)(2,1)S(1)}, bf16[448,768]{1,0:T(8,128)(2,1)S(1)}, u32[]{:S(2)}, u32[]{:S(2)}) collective-permute-start(bf16[448,768]{1,0:T(8,128)(2,1)S(1)} %collective-permute-done.3.refs_4_.refs_3_), channel_id=1, source_target_pairs={{0,8},{8,0},{1,9},{9,1},{2,10},{10,2},{3,11},{11,3},{4,12},{12,4},... | collective-permute-start | bytes 2064392 | tf_op jit(solution)/shard_map/ppermute | solution.py:520
  50.3 2.8 %collective-permute-start.11 = (bf16[448,768]{1,0:T(8,128)(2,1)S(1)}, bf16[448,768]{1,0:T(8,128)(2,1)S(1)}, u32[]{:S(2)}, u32[]{:S(2)}) collective-permute-start(bf16[448,768]{1,0:T(8,128)(2,1)S(1)} %collective-permute-done.6.refs_2_.refs_4_), channel_id=1, source_target_pairs={{0,8},{8,0},{1,9},{9,1},{2,10},{10,2},{3,11},{11,3},{4,12},{12,4},... | collective-permute-start | bytes 2064392 | tf_op jit(solution)/shard_map/ppermute | solution.py:520
  50.3 34.1 %collective-permute-start.14 = (bf16[384,768]{1,0:T(8,128)(2,1)S(1)}, bf16[384,768]{1,0:T(8,128)(2,1)S(1)}, u32[]{:S(2)}, u32[]{:S(2)}) collective-permute-start(bf16[384,768]{1,0:T(8,128)(2,1)S(1)} %get-tuple-element.79), channel_id=1, source_target_pairs={{0,2},{1,3},{2,0},{3,1},{4,6},{5,7},{6,4},{7,5},{8,10},{9,11},{10,... | collective-permute-start | bytes 1769480 | tf_op jit(solution)/shard_map/ppermute | solution.py:520
  66.2 18.2 %collective-permute-start.12 = (bf16[480,384]{1,0:T(8,128)(2,1)S(1)}, bf16[480,384]{1,0:T(8,128)(2,1)S(1)}, u32[]{:S(2)}, u32[]{:S(2)}) collective-permute-start(bf16[480,384]{1,0:T(8,128)(2,1)S(1)} %get-tuple-element.74), channel_id=1, source_target_pairs={{0,56},{8,64},{16,72},{24,80},{32,88},{40,96},{48,104},{56,112},{6... | collective-permute-start | bytes 1105928 | tf_op jit(solution)/shard_map/ppermute | solution.py:585
  67.6 16.9 %collective-permute-start.13 = (bf16[480,384]{1,0:T(8,128)(2,1)S(1)}, bf16[480,384]{1,0:T(8,128)(2,1)S(1)}, u32[]{:S(2)}, u32[]{:S(2)}) collective-permute-start(bf16[480,384]{1,0:T(8,128)(2,1)S(1)} %get-tuple-element.78), channel_id=1, source_target_pairs={{0,184},{8,192},{16,200},{24,208},{32,216},{40,224},{48,232},{56,2... | collective-permute-start | bytes 1105928 | tf_op jit(solution)/shard_map/ppermute | solution.py:585
  78.4 11.4 %collective-permute-start.16 = (bf16[480,384]{1,0:T(8,128)(2,1)S(1)}, bf16[480,384]{1,0:T(8,128)(2,1)S(1)}, u32[]{:S(2)}, u32[]{:S(2)}) collective-permute-start(bf16[480,384]{1,0:T(8,128)(2,1)S(1)} %attend_third.1), channel_id=1, source_target_pairs={{0,120},{8,128},{16,136},{24,144},{32,152},{40,160},{48,168},{56,1... | collective-permute-start | bytes 1105928 | tf_op jit(solution)/shard_map/ppermute | solution.py:585
  84.4 19.4 %collective-permute-start.15 = (bf16[480,384]{1,0:T(8,128)(2,1)S(1)}, bf16[480,384]{1,0:T(8,128)(2,1)S(1)}, u32[]{:S(2)}, u32[]{:S(2)}) collective-permute-start(bf16[480,384]{1,0:T(8,128)(2,1)S(1)} %attend_late.1), channel_id=1, source_target_pairs={{0,248},{8,0},{16,8},{24,16},{32,24},{40,32},{48,40},{56,48},{64,5... | collective-permute-start | bytes 1105928 | tf_op jit(solution)/shard_map/ppermute | solution.py:585
  89.7 14.2 %copy-start.3 = (f32[64,768]{1,0:T(8,128)S(1)}, f32[64,768]{1,0:T(8,128)}, u32[]{:S(2)}) copy-start(f32[64,768]{1,0:T(8,128)} %table.1) | copy-start | bytes 589828
  89.7 17.8 %copy-start.5 = (bf16[448,768]{1,0:T(8,128)(2,1)S(1)}, bf16[448,768]{1,0:T(8,128)(2,1)}, u32[]{:S(2)}) copy-start(bf16[448,768]{1,0:T(8,128)(2,1)} %param.8) | copy-start | bytes 2064388
  89.7 32.4 %collective-permute-start.21 = (bf16[3,384,768]{2,1,0:T(8,128)(2,1)S(1)}, bf16[3,384,768]{2,1,0:T(8,128)(2,1)S(1)}, u32[]{:S(2)}, u32[]{:S(2)}) collective-permute-start(bf16[3,384,768]{2,1,0:T(8,128)(2,1)S(1)} %stack.41.refs_5_), channel_id=1, source_target_pairs={{0,8},{8,0},{1,9},{9,1},{2,10},{10,2},{3,11},{11,3},{4,12},{12,4},... | collective-permute-start | bytes 5308424 | tf_op jit(solution)/shard_map/ppermute | solution.py:520
  105.1 10.2 %collective-permute-start.20 = (bf16[448,384]{1,0:T(8,128)(2,1)S(1)}, bf16[448,384]{1,0:T(8,128)(2,1)S(1)}, u32[]{:S(2)}, u32[]{:S(2)}) collective-permute-start(bf16[448,384]{1,0:T(8,128)(2,1)S(1)} %get-tuple-element.88.refs_0_), channel_id=1, source_target_pairs={{0,3},{1,0},{2,1},{3,2},{4,7},{5,4},{6,5},{7,6},{8,11},{9,8},{10,9... | collective-permute-start | bytes 1032200 | tf_op jit(solution)/shard_map/ppermute | solution.py:520
  106.4 11.4 %collective-permute-start.19 = (bf16[448,384]{1,0:T(8,128)(2,1)S(1)}, bf16[448,384]{1,0:T(8,128)(2,1)S(1)}, u32[]{:S(2)}, u32[]{:S(2)}) collective-permute-start(bf16[448,384]{1,0:T(8,128)(2,1)S(1)} %get-tuple-element.88.refs_0_), channel_id=1, source_target_pairs={{0,2},{1,3},{2,0},{3,1},{4,6},{5,7},{6,4},{7,5},{8,10},{9,11},{10,... | collective-permute-start | bytes 1032200 | tf_op jit(solution)/shard_map/ppermute | solution.py:520
  106.9 15.2 %collective-permute-start.18 = (bf16[448,384]{1,0:T(8,128)(2,1)S(1)}, bf16[448,384]{1,0:T(8,128)(2,1)S(1)}, u32[]{:S(2)}, u32[]{:S(2)}) collective-permute-start(bf16[448,384]{1,0:T(8,128)(2,1)S(1)} %get-tuple-element.88.refs_0_), channel_id=1, source_target_pairs={{0,1},{1,2},{2,3},{3,0},{4,5},{5,6},{6,7},{7,4},{8,9},{9,10},{10,1... | collective-permute-start | bytes 1032200 | tf_op jit(solution)/shard_map/ppermute | solution.py:520
  107.5 20.3 %collective-permute-start.17 = (bf16[448,768]{1,0:T(8,128)(2,1)S(1)}, bf16[448,768]{1,0:T(8,128)(2,1)S(1)}, u32[]{:S(2)}, u32[]{:S(2)}) collective-permute-start(bf16[448,768]{1,0:T(8,128)(2,1)S(1)} %copy-done.5), channel_id=1, source_target_pairs={{0,248},{8,0},{16,8},{24,16},{32,24},{40,32},{48,40},{56,48},{64,5... | collective-permute-start | bytes 2064392 | tf_op jit(solution)/shard_map/ppermute | solution.py:520
  124.9 19.5 %collective-permute-start.22 = (bf16[448,768]{1,0:T(8,128)(2,1)S(1)}, bf16[448,768]{1,0:T(8,128)(2,1)S(1)}, u32[]{:S(2)}, u32[]{:S(2)}) collective-permute-start(bf16[448,768]{1,0:T(8,128)(2,1)S(1)} %project.3), channel_id=1, source_target_pairs={{0,4},{4,0},{1,5},{5,1},{2,6},{6,2},{3,7},{7,3},{8,12},{12,8},{9,1... | collective-permute-start | bytes 2064392 | tf_op jit(solution)/shard_map/ppermute | solution.py:520

commit v7 on v6

--- a/solution.py
+++ b/solution.py
@@ -19,7 +19,7 @@
 EXP2_SCALE = HD**-0.5 * math.log2(math.e)
 Y_STEPS = (0, -1, 1, 2)
 SLOT = ("z", "y", "c")
-ATTEND_VMEM = 22 * 1024 * 1024
+ATTEND_VMEM = 30 * 1024 * 1024
 SMALL_VMEM = 8 * 1024 * 1024
 WHOLE_VMEM = 60 * 1024 * 1024
 
@@ -30,19 +30,17 @@
     )
 
 
-CALLS = {"early": (1, 3), "middle": (1, 3), "third": (2,), "late": (0,)}
+CALLS = {"early": (1, 3, 0), "third": (2,), "middle": (1, 3), "late": (0,)}
 EARLY, LATER, ALL = (0, 1, 2, 4), (3, 5, 6, 7), tuple(range(8))
-COSTS = {"early": 10**10, "middle": 10**10, "third": 5 * 10**10, "late": 10**6}
-MEMBERS = {"early": EARLY, "middle": LATER, "third": ALL, "late": ALL}
+MEMBERS = {"early": EARLY, "third": ALL, "middle": LATER, "late": LATER}
+COSTS = {"early": 10**10, "third": 10**10, "middle": 5 * 10**10, "late": 10**6}
 
 
 def attend_kernel(call, ids, live, level, *refs):
     steps = CALLS[call]
     many = len(steps)
-    early, middle, late = call == "early", call == "middle", call == "late"
+    early, resumed = call == "early", call in ("middle", "late")
     members = MEMBERS[call]
-    resumed = (0, 1) if middle else ()
-    kept = many if early else len(resumed)
     refs = list(refs)
 
     def take(count):
@@ -51,8 +49,8 @@
         return taken
 
     query_in, pair_in = take(many), take(len(members))
-    state_in = [] if early else take(2 * kept)
-    out = take(2 * many if early else many)
+    state_in = take(2) if resumed else []
+    out = take(4 if early else many)
     raw, scaled, pairs, held, acc, top, done, raw_sem, pair_sem, state_sem, out_sem = refs
     here, y, core = ids[0], ids[1], ids[2]
     first = here * 8
@@ -68,10 +66,12 @@
             count = count + jnp.where(groups[p] < group, live[groups[p]], 0)
         return count
 
-    bound = mine if late else first + 8
-    n_live = live_before(bound)
-    count = n_live + 1 if late else n_live
-    chunks = (count + 1) // 2
+    bound = mine if call == "late" else first + 8
+    n_live, n_before = live_before(bound), live_before(mine)
+    own_place = jnp.where(live[mine] == 1, n_before, n_live)
+
+    def active(i):
+        return here + steps[i] <= 3
 
     def raw_copy(i):
         return pltpu.make_async_copy(query_in[i], raw.at[i], raw_sem.at[i])
@@ -80,111 +80,62 @@
         at = pl.ds(pl.multiple_of(place * ROWS, 64), ROWS)
         return pltpu.make_async_copy(pair_in[j], pairs.at[at], pair_sem.at[place])
 
-    def state_copies(k):
-        i = resumed[k]
+    def state_copies():
         return (
-            pltpu.make_async_copy(state_in[2 * k], acc.at[i], state_sem.at[2 * k]),
-            pltpu.make_async_copy(state_in[2 * k + 1], top.at[i], state_sem.at[2 * k + 1]),
+            pltpu.make_async_copy(state_in[0], acc, state_sem.at[0]),
+            pltpu.make_async_copy(state_in[1], top, state_sem.at[1]),
         )
 
-    def out_copies(i):
-        if early:
-            return (
-                pltpu.make_async_copy(acc.at[i], out[2 * i], out_sem.at[2 * i]),
-                pltpu.make_async_copy(top.at[i], out[2 * i + 1], out_sem.at[2 * i + 1]),
-            )
-        return (pltpu.make_async_copy(done.at[i], out[i], out_sem.at[i]),)
-
-    def active(i):
-        return here + steps[i] <= 3
-
-    def step_of(i):
-        step = jnp.int32(steps[-1])
-        for k in range(many - 1):
-            step = jnp.where(i == k, steps[k], step)
-        return step
-
-    def run():
-        for j, p in enumerate(members):
-            if late and p == 0:
-                place_copy(j, n_live).start()
-                continue
-
-            @pl.when((live[groups[p]] == 1) & (groups[p] < bound))
-            def _():
-                place_copy(j, live_before(groups[p])).start()
-
-        for i in range(many):
-
-            @pl.when(active(i))
-            def _():
-                raw_copy(i).start()
-
-        for k in range(len(resumed)):
-
-            @pl.when(active(resumed[k]))
-            def _():
-                for copy in state_copies(k):
-                    copy.start()
-
-        for i in range(many):
-
-            @pl.when(active(i))
-            def _():
-                raw_copy(i).wait()
-
-        def one(i, unused):
-            @pl.when(here + step_of(i) <= 3)
-            def _():
-                source(i)
-
-            return 0
-
-        lax.fori_loop(0, many, one, 0)
-        for i in range(many):
-
-            @pl.when(active(i))
-            def _():
-                for copy in out_copies(i):
-                    copy.wait()
-
-    def source(i):
-        waits = i == 0
-
-        def arrive(t):
-            for k in (2 * t, 2 * t + 1):
-
-                @pl.when(waits & (k < count))
-                def _():
-                    place_copy(0, k).wait()
-
-        def at(k):
-            place = jnp.maximum(jnp.minimum(k, count - 1), 0)
-            return pl.ds(pl.multiple_of(place * ROWS, 64), ROWS)
-
+    def out_copies(part):
+        at = pl.ds(0, 2 * ROWS) if part == 0 else pl.ds(2 * ROWS, ROWS)
+        return (
+            pltpu.make_async_copy(acc.at[:, at], out[2 * part], out_sem.at[2 * part]),
+            pltpu.make_async_copy(top.at[:, at], out[2 * part + 1], out_sem.at[2 * part + 1]),
+        )
+
+    def share_copy(i):
+        return pltpu.make_async_copy(done.at[i], out[i], out_sem.at[i])
+
+    def prepare(i):
+        raw_copy(i).wait()
+        at = slice(i * ROWS, (i + 1) * ROWS)
         for head in range(HEADS_HERE):
             exact = raw[i, :, head * HD : (head + 1) * HD].astype(jnp.float32) * EXP2_SCALE
             high = exact.astype(jnp.bfloat16)
-            scaled[head, :, :HD] = high
-            scaled[head, :, HD:] = (exact - high.astype(jnp.float32)).astype(jnp.bfloat16)
-
-        def fresh():
-            top[i] = jnp.full(top.shape[1:], LOWEST, jnp.float32)
-            acc[i] = jnp.zeros(acc.shape[1:], jnp.float32)
-
-        if not middle:
-            fresh()
+            scaled[head, at, :HD] = high
+            scaled[head, at, HD:] = (exact - high.astype(jnp.float32)).astype(jnp.bfloat16)
+
+    def sweep(start, rows, count, place_of, waits):
+        span = slice(start, start + rows)
+        chunks = (count + 1) // 2
+
+        def arrive(t):
+            if waits:
+                for k in (2 * t, 2 * t + 1):
+
+                    @pl.when(k < count)
+                    def _():
+                        place_copy(0, k).wait()
+
+        def at(k):
+            place = place_of(jnp.maximum(jnp.minimum(k, count - 1), 0))
+            return pl.ds(pl.multiple_of(place * ROWS, 64), ROWS)
+
+        def columns(base, head):
+            if isinstance(head, int):
+                return slice(base + head * HD, base + (head + 1) * HD)
+            return pl.ds(pl.multiple_of(base + head * HD, HD), HD)
 
         def scores_of(t, head):
-            cols = slice(head * HD, (head + 1) * HD)
+            cols = columns(0, head)
             key = jnp.concatenate([pairs[at(2 * t), cols], pairs[at(2 * t + 1), cols]], axis=0)
-            return score(scaled[head], jnp.concatenate([key, key], axis=1))
+            return score(scaled[head, span], jnp.concatenate([key, key], axis=1))
 
         def absorb(t, head, scores):
-            old = top[i, head]
+            old = top[head, span]
             new = jnp.maximum(old, jnp.max(scores, axis=1, keepdims=True))
             weights = jnp.exp2(scores - jnp.concatenate([new] * (2 * ROWS // HD), axis=1))
-            cols = slice(WIDTH + head * HD, WIDTH + (head + 1) * HD)
+            cols = columns(WIDTH, head)
             there = jnp.where(2 * t + 1 < count, 1.0, 0.0).astype(jnp.bfloat16)
             ones = jnp.ones((ROWS, HD), jnp.bfloat16)
             value = jnp.concatenate(
@@ -198,55 +149,62 @@
                 weights.astype(jnp.bfloat16), value, preferred_element_type=jnp.float32
             )
             shrink = jnp.exp2(old - new)
-            acc[i, head] = acc[i, head] * jnp.concatenate([shrink, shrink], axis=1) + weighted
-            top[i, head] = new
+            acc[head, span] = (
+                acc[head, span] * jnp.concatenate([shrink, shrink], axis=1) + weighted
+            )
+            top[head, span] = new
 
         arrive(0)
 
         @pl.when(chunks > 0)
         def _():
-            held[...] = scores_of(0, 0)
-
-        for k in range(len(resumed)):
-
-            @pl.when(i == resumed[k])
-            def _():
-                for copy in state_copies(k):
-                    copy.wait()
+            held[0:rows] = scores_of(0, 0)
+
+        if rows > ROWS:
+
+            def unit(u, unused):
+                head, t = lax.rem(u, HEADS_HERE), u // HEADS_HERE
+                scores = held[0:rows]
+
+                @pl.when(head == 1)
+                def _():
+                    arrive(t + 1)
+
+                following = jnp.minimum(u + 1, HEADS_HERE * chunks - 1)
+                upcoming = scores_of(following // HEADS_HERE, lax.rem(following, HEADS_HERE))
+                absorb(t, head, scores)
+                held[0:rows] = upcoming
+                return 0
+
+            lax.fori_loop(0, HEADS_HERE * chunks, unit, 0)
+            return
 
         def chunk(t, unused):
-            scores = held[...]
+            scores = held[0:rows]
             following = scores_of(t, 1)
             absorb(t, 0, scores)
             scores = scores_of(t, 2)
             absorb(t, 1, following)
             arrive(t + 1)
-            held[...] = scores_of(t + 1, 0)
+            held[0:rows] = scores_of(t + 1, 0)
             absorb(t, 2, scores)
             return 0
 
         lax.fori_loop(0, chunks, chunk, 0)
-        if not early:
-            finish(i)
-        for k in range(many):
-
-            @pl.when(i == k)
-            def _():
-                for copy in out_copies(k):
-                    copy.start()
-
-    def finish(i):
+
+    def finish(i, unused):
+        span = pl.ds(pl.multiple_of(i * ROWS, 64), ROWS)
         lane = lax.broadcasted_iota(jnp.int32, (ROWS, HD), 1)
         stats = jnp.where(lane == 3 * HEADS_HERE, level[0].astype(jnp.float32), 0.0)
         for head in range(HEADS_HERE):
-            exact = top[i, head]
+            exact = top[head, span]
             sent = exact.astype(jnp.bfloat16).astype(jnp.float32)
             factor = jnp.exp2(exact - sent)
-            both = acc[i, head]
-            done[i, 0:ROWS, head * HD : (head + 1) * HD] = (both[:, :HD] * factor).astype(
+            weighted = acc[head, span]
+            done[i, 0:ROWS, head * HD : (head + 1) * HD] = (weighted[:, :HD] * factor).astype(
                 jnp.bfloat16
             )
-            total = both[:, HD:] * factor
+            total = weighted[:, HD:] * factor
             high = total.astype(jnp.bfloat16).astype(jnp.float32)
             stats = jnp.where(lane == head, sent, stats)
             stats = jnp.where(lane == HEADS_HERE + head, high, stats)
@@ -255,8 +213,81 @@
         done[i, ROWS : ROWS + 16, :] = flat[:, :WIDTH]
         pad = jnp.zeros((16, 2 * WIDTH - ROWS), jnp.bfloat16)
         done[i, ROWS + 16 : ROWS + 32, :] = jnp.concatenate([flat[:, WIDTH:], pad], axis=1)
-
-    pl.when(active(0))(run)
+        for k in range(many):
+
+            @pl.when(i == k)
+            def _():
+                share_copy(k).start()
+
+        return 0
+
+    def run():
+        if resumed:
+            for copy in state_copies():
+                copy.start()
+        for j, p in enumerate(members):
+            if early and p == 0:
+                place_copy(j, own_place).start()
+                continue
+
+            @pl.when((live[groups[p]] == 1) & (groups[p] < bound))
+            def _():
+                place_copy(j, live_before(groups[p])).start()
+
+        for i in range(many):
+            raw_copy(i).start()
+        if early:
+            place_copy(0, own_place).wait()
+            for k in range(len(EARLY)):
+
+                @pl.when((k < n_live) & (k != own_place))
+                def _():
+                    place_copy(0, k).wait()
+
+        for i in range(many):
+            prepare(i)
+        if resumed:
+            for copy in state_copies():
+                copy.wait()
+        else:
+            top[...] = jnp.full(top.shape, LOWEST, jnp.float32)
+            acc[...] = jnp.zeros(acc.shape, jnp.float32)
+        if early:
+
+            @pl.when(active(0))
+            def _():
+                sweep(0, 2 * ROWS, n_live, lambda k: k, False)
+                for copy in out_copies(0):
+                    copy.start()
+
+            sweep(
+                2 * ROWS,
+                ROWS,
+                n_before + 1,
+                lambda k: jnp.where(k < n_before, k, own_place),
+                False,
+            )
+            for copy in out_copies(1):
+                copy.start()
+            for copy in out_copies(1):
+                copy.wait()
+
+            @pl.when(active(0))
+            def _():
+                for copy in out_copies(0):
+                    copy.wait()
+
+            return
+
+        sweep(0, many * ROWS, n_live, lambda k: k, True)
+        lax.fori_loop(0, many, finish, 0)
+        for i in range(many):
+            share_copy(i).wait()
+
+    if early:
+        run()
+    else:
+        pl.when(active(0))(run)
 
 
 def attend(call, ids, live, level, queries, pairs, states=()):
@@ -264,14 +295,18 @@
     anywhere = pl.BlockSpec(memory_space=pl.ANY)
     bf16, f32 = jnp.bfloat16, jnp.float32
     many = len(CALLS[call])
-    early = call == "early"
     members = MEMBERS[call]
-    state = [(HEADS_HERE, ROWS, 2 * HD), (HEADS_HERE, ROWS, HD)]
-    if early:
-        out_shape = [jax.ShapeDtypeStruct(shape, f32) for shape in state * many]
+    together_rows = 2 * ROWS if call in ("early", "middle") else ROWS
+
+    def state(rows):
+        return [(HEADS_HERE, rows, 2 * HD), (HEADS_HERE, rows, HD)]
+
+    if call == "early":
+        out_shape = [jax.ShapeDtypeStruct(shape, f32) for shape in state(2 * ROWS) + state(ROWS)]
     else:
         out_shape = [jax.ShapeDtypeStruct((ROWS + STAT, WIDTH), bf16)] * many
     operands = [*queries, *[pairs[p] for p in members], *states]
+    rows = many * ROWS
     return pl.pallas_call(
         functools.partial(attend_kernel, call),
         out_shape=out_shape,
@@ -279,16 +314,16 @@
         out_specs=[anywhere] * len(out_shape),
         scratch_shapes=[
             pltpu.VMEM((many, ROWS, WIDTH), bf16),
-            pltpu.VMEM((HEADS_HERE, ROWS, 2 * HD), bf16),
+            pltpu.VMEM((HEADS_HERE, rows, 2 * HD), bf16),
             pltpu.VMEM((8 * ROWS, 2 * WIDTH), bf16),
-            pltpu.VMEM((ROWS, 2 * ROWS), f32),
-            pltpu.VMEM((many, *state[0]), f32),
-            pltpu.VMEM((many, *state[1]), f32),
+            pltpu.VMEM((together_rows, 2 * ROWS), f32),
+            pltpu.VMEM(state(rows)[0], f32),
+            pltpu.VMEM(state(rows)[1], f32),
             pltpu.VMEM((many, ROWS + STAT, WIDTH), bf16),
             pltpu.SemaphoreType.DMA((many,)),
             pltpu.SemaphoreType.DMA((8,)),
+            pltpu.SemaphoreType.DMA((2,)),
             pltpu.SemaphoreType.DMA((4,)),
-            pltpu.SemaphoreType.DMA((2 * many,)),
         ],
         compiler_params=pltpu.CompilerParams(vmem_limit_bytes=ATTEND_VMEM),
         cost_estimate=pl.CostEstimate(
@@ -561,7 +596,7 @@
         ids,
         group_live,
         noise_level,
-        [next_one, next_three],
+        [next_one, next_three, queries],
         [pair, below, above, None, pair_there],
     )
     next_two, across, piece_one, piece_three, below_there, piece_two, above, *states = together(
@@ -584,17 +619,16 @@
         ]
         return lax.ppermute(share, SLOT, pairs_back)
 
+    (two,) = attend("third", ids, group_live, noise_level, [next_two], pairs)
+    back_two = back(two, 2)
+    live_middle, two = together(group_live, two)
     one, three = attend(
-        "middle", ids, group_live, noise_level, [next_one, next_three], pairs, states
+        "middle", ids, live_middle, noise_level, [next_one, next_three], pairs, states[0:2]
     )
     back_one, back_three = back(one, 1), back(three, 3)
-    live_third, one = together(group_live, one)
-    (two,) = attend("third", ids, live_third, noise_level, [next_two], pairs)
-    back_two = back(two, 2)
-    live_late, two = together(group_live, two)
-    (zero,) = attend("late", ids, live_late, noise_level, [queries], pairs)
-    zero, back_one, back_three, piece_two = together(zero, back_one, back_three, piece_two)
-    values_later, sides_later = combine_later(ids, back_one, back_two, back_three)
+    live_late, one = together(group_live, one)
+    (zero,) = attend("late", ids, live_late, noise_level, [queries], pairs, states[2:4])
+    zero, back_two, piece_two = together(zero, back_two, piece_two)
     (fetched,) = copied(
         "stack",
         ids,
@@ -603,6 +637,7 @@
         tuple(("stack", k, 0, k) for k in range(3)),
     )
     swapped = around(fetched, "c", 1)
+    values_later, sides_later = combine_later(ids, back_one, back_two, back_three)
     attended, gate_row = combine(level_table, back(zero, 0), values_later, sides_later)
 
     attended, hidden = together(attended, hidden)

time: 149 us -> 146 us (0.980)
  the two profiles are of different devices: /device:TPU:1 before, /device:TPU:64 now
where the time goes in v7:
time: 146 us; the launch traced here: 144 us
  waiting for transfers between devices  50.1 us (34%)
  Pallas kernels  48.8 us (33%)
  starting transfers between devices  41.8 us (29%)
  local copies, waits for them, and re-layouts  2.45 us (2%)
    pallas_call x4, Pallas kernels, attend(): pl.pallas_call(functools.partial(attend_kernel, call), out_shape=out_shap...  34.7 us
    ppermute x16, waiting for transfers between devices, around(): lax.ppermute(value, axis, [(i, (i + steps) % count) for i in range(count)])  28.3 us
    ppermute x16, starting transfers between devices, around(): lax.ppermute(value, axis, [(i, (i + steps) % count) for i in range(count)])  24 us
    ppermute x3, waiting for transfers between devices, to_level(): return lax.ppermute(value, 'z', [(i, i - d) for i in range(d, 4)])  19.9 us
    ppermute x4, starting transfers between devices, back(): return lax.ppermute(share, SLOT, pairs_back)  13.5 us
    pallas_call x2, Pallas kernels, project(): pl.pallas_call(functools.partial(project_kernel, far), out_shape=jax.Shap...  5.61 us
    ppermute x3, starting transfers between devices, to_level(): return lax.ppermute(value, 'z', [(i, i - d) for i in range(d, 4)])  4.27 us
  transfers between devices with their start and end apart: 23, of which 9 were waited for; matrix products, arithmetic and copies ran while one was open for 0% of the time, Pallas kernels for 31%

profile of v7, /device:TPU:64, one launch (start us, length us, event | category | flops | bytes accessed | tf_op | source)
XLA Modules:
  0.0 144.0 jit_solution(15830734924280776105)
XLA Ops:
  0.0 2.0 %pack.1.refs_3_.refs_1_ = bf16[448,768]{1,0:T(8,128)(2,1)} custom-call(bf16[448,384]{1,0:T(8,128)(2,1)} %keys.1, bf16[448,384]{1,0:T(8,128)(2,1)} %values.1), custom_call_target="tpu_custom_call" | custom-call | tf_op jit(solution)/shard_map/pack/pallas_call | solution.py:467
  2.0 0.0 collective-permute-start.4
  2.0 3.0 %collective-permute-start.3 = (bf16[448,768]{1,0:T(8,128)(2,1)}, bf16[448,768]{1,0:T(8,128)(2,1)S(1)}, u32[]{:S(2)}, u32[]{:S(2)}) collective-permute-start(bf16[448,768]{1,0:T(8,128)(2,1)} %pack.1.refs_3_.refs_1_), channel_id=1, source_target_pairs={{0,48},{16,0},{32,16},{48,32},{1,49},{17,1},{33,17},{49,33},{2,50}... | collective-permute-start | bytes 2064392 | tf_op jit(solution)/shard_map/ppermute | solution.py:555
  5.0 0.0 collective-permute-start.2
  5.0 2.3 %collective-permute-start = (bf16[448,384]{1,0:T(8,128)(2,1)}, bf16[448,384]{1,0:T(8,128)(2,1)S(1)}, u32[]{:S(2)}, u32[]{:S(2)}) collective-permute-start(bf16[448,384]{1,0:T(8,128)(2,1)} %refs_0_.2), channel_id=1, source_target_pairs={{64,0},{128,64},{192,128},{65,1},{129,65},{193,129},{66,2},{130,66... | collective-permute-start | bytes 1032200 | tf_op jit(solution)/shard_map/ppermute | solution.py:573
  7.3 0.7 collective-permute-start.1
  8.7 0.1 stack.40.ids
  8.8 2.3 %copy-done = bf16[384,6144]{1,0:T(8,128)(2,1)S(1)} copy-done((bf16[384,6144]{1,0:T(8,128)(2,1)S(1)}, bf16[384,6144]{1,0:T(8,128)(2,1)}, u32[]{:S(2)}) %copy-start) | copy-done | bytes 4718616
  11.1 0.9 columns.1
  12.0 15.4 %collective-permute-done.refs_0_ = bf16[448,384]{1,0:T(8,128)(2,1)S(1)} collective-permute-done((bf16[448,384]{1,0:T(8,128)(2,1)}, bf16[448,384]{1,0:T(8,128)(2,1)S(1)}, u32[]{:S(2)}, u32[]{:S(2)}) %collective-permute-start) | collective-permute-done | bytes 344096 | tf_op jit(solution)/shard_map/ppermute | solution.py:573
  27.4 0.0 collective-permute-done.1.refs_1_
  27.4 0.0 collective-permute-done.4.refs_6_.refs_5_
  27.5 1.3 collective-permute-start.5
  28.8 1.6 %collective-permute-start.7 = (bf16[384,768]{1,0:T(8,128)(2,1)S(1)}, bf16[384,768]{1,0:T(8,128)(2,1)S(1)}, u32[]{:S(2)}, u32[]{:S(2)}) collective-permute-start(bf16[384,768]{1,0:T(8,128)(2,1)S(1)} %get-tuple-element.54), channel_id=1, source_target_pairs={{0,1},{1,2},{2,3},{3,0},{4,5},{5,6},{6,7},{7,4},{8,9},{9,10},{10,1... | collective-permute-start | bytes 1769480 | tf_op jit(solution)/shard_map/ppermute | solution.py:555
  30.3 1.7 %collective-permute-start.8 = (bf16[384,768]{1,0:T(8,128)(2,1)S(1)}, bf16[384,768]{1,0:T(8,128)(2,1)S(1)}, u32[]{:S(2)}, u32[]{:S(2)}) collective-permute-start(bf16[384,768]{1,0:T(8,128)(2,1)S(1)} %get-tuple-element.55), channel_id=1, source_target_pairs={{0,3},{1,0},{2,1},{3,2},{4,7},{5,4},{6,5},{7,6},{8,11},{9,8},{10,9... | collective-permute-start | bytes 1769480 | tf_op jit(solution)/shard_map/ppermute | solution.py:555
  32.1 1.9 %collective-permute-start.6 = (bf16[448,768]{1,0:T(8,128)(2,1)S(1)}, bf16[448,768]{1,0:T(8,128)(2,1)S(1)}, u32[]{:S(2)}, u32[]{:S(2)}) collective-permute-start(bf16[448,768]{1,0:T(8,128)(2,1)S(1)} %copy-done.1), channel_id=1, source_target_pairs={{0,32},{16,48},{32,0},{48,16},{1,33},{17,49},{33,1},{49,17},{2,34}... | collective-permute-start | bytes 2064392 | tf_op jit(solution)/shard_map/ppermute | solution.py:555
  34.0 9.8 %attend_early.1 = (f32[3,896,256]{2,1,0:T(8,128)S(1)}, f32[3,896,128]{2,1,0:T(8,128)S(1)}, f32[3,448,256]{2,1,0:T(8,128)S(1)}, f32[3,448,128]{2,1,0:T(8,128)S(1)}) custom-call(s32[9]{0:T(128)S(1)} %stack.40.ids, s32[32]{0:T(128)S(1)} %copy-done.4, s32[1]{0:T(128)S(6)} %copy.9.level, bf16[448,384]{1,0:T(8,128)(2,1)S(1)} %collective-permute-done.refs_0_, ...), custom_call_target="tpu_custom_call" | custom-call | flops 10000000000 | bytes 1000000 | tf_op jit(solution)/shard_map/attend_early/pallas_call | solution.py:310
  43.8 4.5 %collective-permute-done.5.refs_0_ = bf16[448,384]{1,0:T(8,128)(2,1)S(1)} collective-permute-done((bf16[448,384]{1,0:T(8,128)(2,1)S(1)}, bf16[448,384]{1,0:T(8,128)(2,1)S(1)}, u32[]{:S(2)}, u32[]{:S(2)}) %collective-permute-start.5) | collective-permute-done | bytes 344096 | tf_op jit(solution)/shard_map/ppermute | solution.py:573
  48.4 1.7 %collective-permute-done.6.refs_4_.refs_2_.refs_1_ = bf16[448,768]{1,0:T(8,128)(2,1)S(1)} collective-permute-done((bf16[448,768]{1,0:T(8,128)(2,1)S(1)}, bf16[448,768]{1,0:T(8,128)(2,1)S(1)}, u32[]{:S(2)}, u32[]{:S(2)}) %collective-permute-start.6) | collective-permute-done | bytes 688160 | tf_op jit(solution)/shard_map/ppermute | solution.py:555
  50.1 0.5 collective-permute-start.11
  50.6 1.8 %collective-permute-start.13 = (bf16[384,768]{1,0:T(8,128)(2,1)S(1)}, bf16[384,768]{1,0:T(8,128)(2,1)S(1)}, u32[]{:S(2)}, u32[]{:S(2)}) collective-permute-start(bf16[384,768]{1,0:T(8,128)(2,1)S(1)} %get-tuple-element.77), channel_id=1, source_target_pairs={{0,2},{1,3},{2,0},{3,1},{4,6},{5,7},{6,4},{7,5},{8,10},{9,11},{10,... | collective-permute-start | bytes 1769480 | tf_op jit(solution)/shard_map/ppermute | solution.py:555
  52.4 0.8 collective-permute-done.11.refs_8_.refs_5_.refs_4_
  53.2 9.8 %attend_third.1 = bf16[480,384]{1,0:T(8,128)(2,1)S(1)} custom-call(s32[9]{0:T(128)S(1)} %stack.40.ids, s32[32]{0:T(128)S(1)} %copy-done.4, s32[1]{0:T(128)S(6)} %copy.9.level, bf16[448,384]{1,0:T(8,128)(2,1)S(1)} %collective-permute-done.5.refs_0_, bf16[448,768]{1,0:T(8,128)(2,1)S(1)} %copy-done.1, ...), custom_call_target="tpu_custom_call" | custom-call | flops 10000000000 | bytes 1000000 | tf_op jit(solution)/shard_map/attend_third/pallas_call | solution.py:310
  63.0 1.3 collective-permute-start.12
  64.3 13.1 %attend_middle.1 = (bf16[480,384]{1,0:T(8,128)(2,1)S(1)}, bf16[480,384]{1,0:T(8,128)(2,1)S(1)}) custom-call(s32[9]{0:T(128)S(1)} %stack.40.ids, s32[32]{0:T(128)S(1)} %copy-done.4, s32[1]{0:T(128)S(6)} %copy.9.level, bf16[448,384]{1,0:T(8,128)(2,1)S(1)} %collective-permute-done.refs_0_, bf16[448,384]{1,0:T(8,128)(2,1)S(1)} %collective-permute-done.1.refs_1_, ...), custom_call_target="tpu_custom_call" | custom-call | flops 49999998976 | bytes 1000000 | tf_op jit(solution)/shard_map/attend_middle/pallas_call | solution.py:310
  77.4 0.7 collective-permute-start.16
  78.1 4.6 %collective-permute-start.15 = (bf16[480,384]{1,0:T(8,128)(2,1)S(1)}, bf16[480,384]{1,0:T(8,128)(2,1)S(1)}, u32[]{:S(2)}, u32[]{:S(2)}) collective-permute-start(bf16[480,384]{1,0:T(8,128)(2,1)S(1)} %get-tuple-element.73), channel_id=1, source_target_pairs={{0,56},{8,64},{16,72},{24,80},{32,88},{40,96},{48,104},{56,112},{6... | collective-permute-start | bytes 1105928 | tf_op jit(solution)/shard_map/ppermute | solution.py:620
  82.7 2.0 %attend_late.1 = bf16[480,384]{1,0:T(8,128)(2,1)S(1)} custom-call(s32[9]{0:T(128)S(1)} %stack.40.ids, s32[32]{0:T(128)S(1)} %copy-done.4, s32[1]{0:T(128)S(6)} %copy.9.level, bf16[448,384]{1,0:T(8,128)(2,1)S(1)} %copy-done.2, bf16[448,768]{1,0:T(8,128)(2,1)S(1)} %collective-permute-done.6.refs_4_.refs_2_.refs_1_, ...), custom_call_target="tpu_custom_call" | custom-call | flops 1000000 | bytes 1000000 | tf_op jit(solution)/shard_map/attend_late/pallas_call | solution.py:310
  84.7 7.0 %collective-permute-start.14 = (bf16[480,384]{1,0:T(8,128)(2,1)S(1)}, bf16[480,384]{1,0:T(8,128)(2,1)S(1)}, u32[]{:S(2)}, u32[]{:S(2)}) collective-permute-start(bf16[480,384]{1,0:T(8,128)(2,1)S(1)} %attend_late.1), channel_id=1, source_target_pairs={{0,248},{8,0},{16,8},{24,16},{32,24},{40,32},{48,40},{56,48},{64,5... | collective-permute-start | bytes 1105928 | tf_op jit(solution)/shard_map/ppermute | solution.py:620
  91.7 0.9 stack.41.refs_5_
  92.6 0.0 copy-start.3
  92.6 0.0 copy-start.5
  92.7 0.3 collective-permute-start.21
  93.0 1.9 %combine_later.1 = (f32[448,384]{1,0:T(8,128)S(1)}, f32[448,128]{1,0:T(8,128)S(1)}) custom-call(s32[9]{0:T(128)S(1)} %stack.40.ids, bf16[480,384]{1,0:T(8,128)(2,1)S(1)} %collective-permute-done.15.one, bf16[480,384]{1,0:T(8,128)(2,1)S(1)} %collective-permute-done.12.two, bf16[480,384]{1,0:T(8,128)(2,1)S(1)} %collective-permute-done.16.three), custom_call_target="tpu_custom_call" | custom-call | flops 99999997952 | bytes 200000000 | tf_op jit(solution)/shard_map/combine_later/pallas_call | solution.py:391
  94.9 1.9 %collective-permute-done.14.zero = bf16[480,384]{1,0:T(8,128)(2,1)S(1)} collective-permute-done((bf16[480,384]{1,0:T(8,128)(2,1)S(1)}, bf16[480,384]{1,0:T(8,128)(2,1)S(1)}, u32[]{:S(2)}, u32[]{:S(2)}) %collective-permute-start.14) | collective-permute-done | bytes 368672 | tf_op jit(solution)/shard_map/ppermute | solution.py:620
  96.8 1.2 combine.1
  98.0 1.6 %collective-permute-start.20 = (bf16[448,384]{1,0:T(8,128)(2,1)S(1)}, bf16[448,384]{1,0:T(8,128)(2,1)S(1)}, u32[]{:S(2)}, u32[]{:S(2)}) collective-permute-start(bf16[448,384]{1,0:T(8,128)(2,1)S(1)} %get-tuple-element.86.refs_0_), channel_id=1, source_target_pairs={{0,3},{1,0},{2,1},{3,2},{4,7},{5,4},{6,5},{7,6},{8,11},{9,8},{10,9... | collective-permute-start | bytes 1032200 | tf_op jit(solution)/shard_map/ppermute | solution.py:555
  99.6 0.8 collective-permute-start.19
  100.4 0.9 collective-permute-start.18
  101.3 4.1 %collective-permute-start.17 = (bf16[448,768]{1,0:T(8,128)(2,1)S(1)}, bf16[448,768]{1,0:T(8,128)(2,1)S(1)}, u32[]{:S(2)}, u32[]{:S(2)}) collective-permute-start(bf16[448,768]{1,0:T(8,128)(2,1)S(1)} %copy-done.5), channel_id=1, source_target_pairs={{0,248},{8,0},{16,8},{24,16},{32,24},{40,32},{48,40},{56,48},{64,5... | collective-permute-start | bytes 2064392 | tf_op jit(solution)/shard_map/ppermute | solution.py:555
  105.4 3.6 %collective-permute-done.20.refs_3_ = bf16[448,384]{1,0:T(8,128)(2,1)S(1)} collective-permute-done((bf16[448,384]{1,0:T(8,128)(2,1)S(1)}, bf16[448,384]{1,0:T(8,128)(2,1)S(1)}, u32[]{:S(2)}, u32[]{:S(2)}) %collective-permute-start.20) | collective-permute-done | bytes 344096 | tf_op jit(solution)/shard_map/ppermute | solution.py:555
  109.1 3.1 %collective-permute-done.19.refs_2_ = bf16[448,384]{1,0:T(8,128)(2,1)S(1)} collective-permute-done((bf16[448,384]{1,0:T(8,128)(2,1)S(1)}, bf16[448,384]{1,0:T(8,128)(2,1)S(1)}, u32[]{:S(2)}, u32[]{:S(2)}) %collective-permute-start.19) | collective-permute-done | bytes 344096 | tf_op jit(solution)/shard_map/ppermute | solution.py:555
  112.1 4.7 %collective-permute-done.18.refs_1_ = bf16[448,384]{1,0:T(8,128)(2,1)S(1)} collective-permute-done((bf16[448,384]{1,0:T(8,128)(2,1)S(1)}, bf16[448,384]{1,0:T(8,128)(2,1)S(1)}, u32[]{:S(2)}, u32[]{:S(2)}) %collective-permute-start.18) | collective-permute-done | bytes 344096 | tf_op jit(solution)/shard_map/ppermute | solution.py:555
  116.8 2.8 %project.3 = bf16[448,768]{1,0:T(8,128)(2,1)S(1)} custom-call(s32[9]{0:T(128)S(1)} %stack.40.ids, bf16[448,384]{1,0:T(8,128)(2,1)S(1)} %get-tuple-element.86.refs_0_, bf16[448,384]{1,0:T(8,128)(2,1)S(1)} %collective-permute-done.18.refs_1_, bf16[448,384]{1,0:T(8,128)(2,1)S(1)} %collective-permute-done.19.refs_2_, ...), custom_call_target="tpu_custom_call" | custom-call | flops 1056964608 | bytes 5000000 | tf_op jit(solution)/shard_map/project/pallas_call | solution.py:539
  119.6 5.6 %collective-permute-start.22 = (bf16[448,768]{1,0:T(8,128)(2,1)S(1)}, bf16[448,768]{1,0:T(8,128)(2,1)S(1)}, u32[]{:S(2)}, u32[]{:S(2)}) collective-permute-start(bf16[448,768]{1,0:T(8,128)(2,1)S(1)} %project.3), channel_id=1, source_target_pairs={{0,4},{4,0},{1,5},{5,1},{2,6},{6,2},{3,7},{7,3},{8,12},{12,8},{9,1... | collective-permute-start | bytes 2064392 | tf_op jit(solution)/shard_map/ppermute | solution.py:555
  125.2 2.8 %project.2.near = f32[448,768]{1,0:T(8,128)S(1)} custom-call(s32[9]{0:T(128)S(1)} %stack.40.ids, bf16[448,384]{1,0:T(8,128)(2,1)S(1)} %get-tuple-element.86.refs_0_, bf16[448,384]{1,0:T(8,128)(2,1)S(1)} %collective-permute-done.18.refs_1_, bf16[448,384]{1,0:T(8,128)(2,1)S(1)} %collective-permute-done.19.refs_2_, ...), custom_call_target="tpu_custom_call" | custom-call | flops 1056964608 | bytes 5000000 | tf_op jit(solution)/shard_map/project/pallas_call | solution.py:539
  128.0 14.4 %collective-permute-done.22.arrived = bf16[448,768]{1,0:T(8,128)(2,1)S(1)} collective-permute-done((bf16[448,768]{1,0:T(8,128)(2,1)S(1)}, bf16[448,768]{1,0:T(8,128)(2,1)S(1)}, u32[]{:S(2)}, u32[]{:S(2)}) %collective-permute-start.22) | collective-permute-done | bytes 688160 | tf_op jit(solution)/shard_map/ppermute | solution.py:555
  142.4 1.6 %finish.1 = bf16[448,768]{1,0:T(8,128)(2,1)} custom-call(bf16[448,768]{1,0:T(8,128)(2,1)S(1)} %collective-permute-done.17.hidden, f32[448,768]{1,0:T(8,128)S(1)} %project.2.near, bf16[448,768]{1,0:T(8,128)(2,1)S(1)} %collective-permute-done.22.arrived, f32[1,768]{1,0:T(1,128)S(1)} %get-tuple-element.92.gate), custom_call_target="tpu_custom_call" | custom-call | tf_op jit(solution)/shard_map/finish/pallas_call | solution.py:449
  (23 shorter events, 0.1 us)
Async XLA Ops:
  2.0 25.4 %collective-permute-start.4 = (bf16[448,768]{1,0:T(8,128)(2,1)}, bf16[448,768]{1,0:T(8,128)(2,1)S(1)}, u32[]{:S(2)}, u32[]{:S(2)}) collective-permute-start(bf16[448,768]{1,0:T(8,128)(2,1)} %pack.1.refs_3_.refs_1_), channel_id=1, source_target_pairs={{0,8},{8,0},{1,9},{9,1},{2,10},{10,2},{3,11},{11,3},{4,12},{12,4},... | collective-permute-start | bytes 2064392 | tf_op jit(solution)/shard_map/ppermute | solution.py:555
  2.0 25.4 %collective-permute-start.3 = (bf16[448,768]{1,0:T(8,128)(2,1)}, bf16[448,768]{1,0:T(8,128)(2,1)S(1)}, u32[]{:S(2)}, u32[]{:S(2)}) collective-permute-start(bf16[448,768]{1,0:T(8,128)(2,1)} %pack.1.refs_3_.refs_1_), channel_id=1, source_target_pairs={{0,48},{16,0},{32,16},{48,32},{1,49},{17,1},{33,17},{49,33},{2,50}... | collective-permute-start | bytes 2064392 | tf_op jit(solution)/shard_map/ppermute | solution.py:555
  5.0 22.4 %collective-permute-start.2 = (bf16[448,768]{1,0:T(8,128)(2,1)}, bf16[448,768]{1,0:T(8,128)(2,1)S(1)}, u32[]{:S(2)}, u32[]{:S(2)}) collective-permute-start(bf16[448,768]{1,0:T(8,128)(2,1)} %pack.1.refs_3_.refs_1_), channel_id=1, source_target_pairs={{0,16},{16,32},{32,48},{48,0},{1,17},{17,33},{33,49},{49,1},{2,18}... | collective-permute-start | bytes 2064392 | tf_op jit(solution)/shard_map/ppermute | solution.py:555
  5.0 22.4 %collective-permute-start = (bf16[448,384]{1,0:T(8,128)(2,1)}, bf16[448,384]{1,0:T(8,128)(2,1)S(1)}, u32[]{:S(2)}, u32[]{:S(2)}) collective-permute-start(bf16[448,384]{1,0:T(8,128)(2,1)} %refs_0_.2), channel_id=1, source_target_pairs={{64,0},{128,64},{192,128},{65,1},{129,65},{193,129},{66,2},{130,66... | collective-permute-start | bytes 1032200 | tf_op jit(solution)/shard_map/ppermute | solution.py:573
  7.3 20.1 %collective-permute-start.1 = (bf16[448,384]{1,0:T(8,128)(2,1)}, bf16[448,384]{1,0:T(8,128)(2,1)S(1)}, u32[]{:S(2)}, u32[]{:S(2)}) collective-permute-start(bf16[448,384]{1,0:T(8,128)(2,1)} %refs_0_.2), channel_id=1, source_target_pairs={{192,0},{193,1},{194,2},{195,3},{196,4},{197,5},{198,6},{199,7},{2... | collective-permute-start | bytes 1032200 | tf_op jit(solution)/shard_map/ppermute | solution.py:573
  8.8 2.3 %copy-start = (bf16[384,6144]{1,0:T(8,128)(2,1)S(1)}, bf16[384,6144]{1,0:T(8,128)(2,1)}, u32[]{:S(2)}) copy-start(bf16[384,6144]{1,0:T(8,128)(2,1)} %refs_0_.1) | copy-start | bytes 14155780
  11.1 16.3 %copy-start.2 = (bf16[448,384]{1,0:T(8,128)(2,1)S(1)}, bf16[448,384]{1,0:T(8,128)(2,1)}, u32[]{:S(2)}) copy-start(bf16[448,384]{1,0:T(8,128)(2,1)} %refs_0_.2) | copy-start | bytes 1032196
  11.1 20.9 %copy-start.1 = (bf16[448,768]{1,0:T(8,128)(2,1)S(1)}, bf16[448,768]{1,0:T(8,128)(2,1)}, u32[]{:S(2)}) copy-start(bf16[448,768]{1,0:T(8,128)(2,1)} %pack.1.refs_3_.refs_1_) | copy-start | bytes 2064388
  11.1 22.9 %copy-start.4 = (s32[32]{0:T(128)S(1)}, s32[32]{0:T(128)}, u32[]{:S(2)}) copy-start(s32[32]{0:T(128)} %live.5) | copy-start | bytes 388
  27.5 20.9 %collective-permute-start.5 = (bf16[448,384]{1,0:T(8,128)(2,1)S(1)}, bf16[448,384]{1,0:T(8,128)(2,1)S(1)}, u32[]{:S(2)}, u32[]{:S(2)}) collective-permute-start(bf16[448,384]{1,0:T(8,128)(2,1)S(1)} %copy-done.2), channel_id=1, source_target_pairs={{128,0},{192,64},{129,1},{193,65},{130,2},{194,66},{131,3},{195,67... | collective-permute-start | bytes 1032200 | tf_op jit(solution)/shard_map/ppermute | solution.py:573
  28.8 19.6 %collective-permute-start.7 = (bf16[384,768]{1,0:T(8,128)(2,1)S(1)}, bf16[384,768]{1,0:T(8,128)(2,1)S(1)}, u32[]{:S(2)}, u32[]{:S(2)}) collective-permute-start(bf16[384,768]{1,0:T(8,128)(2,1)S(1)} %get-tuple-element.54), channel_id=1, source_target_pairs={{0,1},{1,2},{2,3},{3,0},{4,5},{5,6},{6,7},{7,4},{8,9},{9,10},{10,1... | collective-permute-start | bytes 1769480 | tf_op jit(solution)/shard_map/ppermute | solution.py:555
  30.3 18.0 %collective-permute-start.8 = (bf16[384,768]{1,0:T(8,128)(2,1)S(1)}, bf16[384,768]{1,0:T(8,128)(2,1)S(1)}, u32[]{:S(2)}, u32[]{:S(2)}) collective-permute-start(bf16[384,768]{1,0:T(8,128)(2,1)S(1)} %get-tuple-element.55), channel_id=1, source_target_pairs={{0,3},{1,0},{2,1},{3,2},{4,7},{5,4},{6,5},{7,6},{8,11},{9,8},{10,9... | collective-permute-start | bytes 1769480 | tf_op jit(solution)/shard_map/ppermute | solution.py:555
  32.1 18.0 %collective-permute-start.6 = (bf16[448,768]{1,0:T(8,128)(2,1)S(1)}, bf16[448,768]{1,0:T(8,128)(2,1)S(1)}, u32[]{:S(2)}, u32[]{:S(2)}) collective-permute-start(bf16[448,768]{1,0:T(8,128)(2,1)S(1)} %copy-done.1), channel_id=1, source_target_pairs={{0,32},{16,48},{32,0},{48,16},{1,33},{17,49},{33,1},{49,17},{2,34}... | collective-permute-start | bytes 2064392 | tf_op jit(solution)/shard_map/ppermute | solution.py:555
  34.0 16.1 %collective-permute-start.9 = (bf16[448,768]{1,0:T(8,128)(2,1)S(1)}, bf16[448,768]{1,0:T(8,128)(2,1)S(1)}, u32[]{:S(2)}, u32[]{:S(2)}) collective-permute-start(bf16[448,768]{1,0:T(8,128)(2,1)S(1)} %collective-permute-done.2.refs_4_.refs_2_), channel_id=1, source_target_pairs={{0,8},{8,0},{1,9},{9,1},{2,10},{10,2},{3,11},{11,3},{4,12},{12,4},... | collective-permute-start | bytes 2064392 | tf_op jit(solution)/shard_map/ppermute | solution.py:555
  50.1 2.3 %collective-permute-start.10 = (bf16[448,768]{1,0:T(8,128)(2,1)S(1)}, bf16[448,768]{1,0:T(8,128)(2,1)S(1)}, u32[]{:S(2)}, u32[]{:S(2)}) collective-permute-start(bf16[448,768]{1,0:T(8,128)(2,1)S(1)} %collective-permute-done.3.refs_5_.refs_3_), channel_id=1, source_target_pairs={{0,8},{8,0},{1,9},{9,1},{2,10},{10,2},{3,11},{11,3},{4,12},{12,4},... | collective-permute-start | bytes 2064392 | tf_op jit(solution)/shard_map/ppermute | solution.py:555
  50.1 3.1 %collective-permute-start.11 = (bf16[448,768]{1,0:T(8,128)(2,1)S(1)}, bf16[448,768]{1,0:T(8,128)(2,1)S(1)}, u32[]{:S(2)}, u32[]{:S(2)}) collective-permute-start(bf16[448,768]{1,0:T(8,128)(2,1)S(1)} %collective-permute-done.6.refs_4_.refs_2_.refs_1_), channel_id=1, source_target_pairs={{0,8},{8,0},{1,9},{9,1},{2,10},{10,2},{3,11},{11,3},{4,12},{12,4},... | collective-permute-start | bytes 2064392 | tf_op jit(solution)/shard_map/ppermute | solution.py:555
  50.6 34.1 %collective-permute-start.13 = (bf16[384,768]{1,0:T(8,128)(2,1)S(1)}, bf16[384,768]{1,0:T(8,128)(2,1)S(1)}, u32[]{:S(2)}, u32[]{:S(2)}) collective-permute-start(bf16[384,768]{1,0:T(8,128)(2,1)S(1)} %get-tuple-element.77), channel_id=1, source_target_pairs={{0,2},{1,3},{2,0},{3,1},{4,6},{5,7},{6,4},{7,5},{8,10},{9,11},{10,... | collective-permute-start | bytes 1769480 | tf_op jit(solution)/shard_map/ppermute | solution.py:555
  63.0 21.7 %collective-permute-start.12 = (bf16[480,384]{1,0:T(8,128)(2,1)S(1)}, bf16[480,384]{1,0:T(8,128)(2,1)S(1)}, u32[]{:S(2)}, u32[]{:S(2)}) collective-permute-start(bf16[480,384]{1,0:T(8,128)(2,1)S(1)} %attend_third.1), channel_id=1, source_target_pairs={{0,120},{8,128},{16,136},{24,144},{32,152},{40,160},{48,168},{56,1... | collective-permute-start | bytes 1105928 | tf_op jit(solution)/shard_map/ppermute | solution.py:620
  77.4 15.5 %collective-permute-start.16 = (bf16[480,384]{1,0:T(8,128)(2,1)S(1)}, bf16[480,384]{1,0:T(8,128)(2,1)S(1)}, u32[]{:S(2)}, u32[]{:S(2)}) collective-permute-start(bf16[480,384]{1,0:T(8,128)(2,1)S(1)} %get-tuple-element.80), channel_id=1, source_target_pairs={{0,184},{8,192},{16,200},{24,208},{32,216},{40,224},{48,232},{56,2... | collective-permute-start | bytes 1105928 | tf_op jit(solution)/shard_map/ppermute | solution.py:620
  78.1 14.9 %collective-permute-start.15 = (bf16[480,384]{1,0:T(8,128)(2,1)S(1)}, bf16[480,384]{1,0:T(8,128)(2,1)S(1)}, u32[]{:S(2)}, u32[]{:S(2)}) collective-permute-start(bf16[480,384]{1,0:T(8,128)(2,1)S(1)} %get-tuple-element.73), channel_id=1, source_target_pairs={{0,56},{8,64},{16,72},{24,80},{32,88},{40,96},{48,104},{56,112},{6... | collective-permute-start | bytes 1105928 | tf_op jit(solution)/shard_map/ppermute | solution.py:620
  84.7 12.1 %collective-permute-start.14 = (bf16[480,384]{1,0:T(8,128)(2,1)S(1)}, bf16[480,384]{1,0:T(8,128)(2,1)S(1)}, u32[]{:S(2)}, u32[]{:S(2)}) collective-permute-start(bf16[480,384]{1,0:T(8,128)(2,1)S(1)} %attend_late.1), channel_id=1, source_target_pairs={{0,248},{8,0},{16,8},{24,16},{32,24},{40,32},{48,40},{56,48},{64,5... | collective-permute-start | bytes 1105928 | tf_op jit(solution)/shard_map/ppermute | solution.py:620
  92.6 4.1 %copy-start.3 = (f32[64,768]{1,0:T(8,128)S(1)}, f32[64,768]{1,0:T(8,128)}, u32[]{:S(2)}) copy-start(f32[64,768]{1,0:T(8,128)} %table.1) | copy-start | bytes 589828
  92.6 8.7 %copy-start.5 = (bf16[448,768]{1,0:T(8,128)(2,1)S(1)}, bf16[448,768]{1,0:T(8,128)(2,1)}, u32[]{:S(2)}) copy-start(bf16[448,768]{1,0:T(8,128)(2,1)} %param.8) | copy-start | bytes 2064388
  92.7 24.1 %collective-permute-start.21 = (bf16[3,384,768]{2,1,0:T(8,128)(2,1)S(1)}, bf16[3,384,768]{2,1,0:T(8,128)(2,1)S(1)}, u32[]{:S(2)}, u32[]{:S(2)}) collective-permute-start(bf16[3,384,768]{2,1,0:T(8,128)(2,1)S(1)} %stack.41.refs_5_), channel_id=1, source_target_pairs={{0,8},{8,0},{1,9},{9,1},{2,10},{10,2},{3,11},{11,3},{4,12},{12,4},... | collective-permute-start | bytes 5308424 | tf_op jit(solution)/shard_map/ppermute | solution.py:555
  98.0 11.1 %collective-permute-start.20 = (bf16[448,384]{1,0:T(8,128)(2,1)S(1)}, bf16[448,384]{1,0:T(8,128)(2,1)S(1)}, u32[]{:S(2)}, u32[]{:S(2)}) collective-permute-start(bf16[448,384]{1,0:T(8,128)(2,1)S(1)} %get-tuple-element.86.refs_0_), channel_id=1, source_target_pairs={{0,3},{1,0},{2,1},{3,2},{4,7},{5,4},{6,5},{7,6},{8,11},{9,8},{10,9... | collective-permute-start | bytes 1032200 | tf_op jit(solution)/shard_map/ppermute | solution.py:555
  99.6 12.5 %collective-permute-start.19 = (bf16[448,384]{1,0:T(8,128)(2,1)S(1)}, bf16[448,384]{1,0:T(8,128)(2,1)S(1)}, u32[]{:S(2)}, u32[]{:S(2)}) collective-permute-start(bf16[448,384]{1,0:T(8,128)(2,1)S(1)} %get-tuple-element.86.refs_0_), channel_id=1, source_target_pairs={{0,2},{1,3},{2,0},{3,1},{4,6},{5,7},{6,4},{7,5},{8,10},{9,11},{10,... | collective-permute-start | bytes 1032200 | tf_op jit(solution)/shard_map/ppermute | solution.py:555
  100.4 16.4 %collective-permute-start.18 = (bf16[448,384]{1,0:T(8,128)(2,1)S(1)}, bf16[448,384]{1,0:T(8,128)(2,1)S(1)}, u32[]{:S(2)}, u32[]{:S(2)}) collective-permute-start(bf16[448,384]{1,0:T(8,128)(2,1)S(1)} %get-tuple-element.86.refs_0_), channel_id=1, source_target_pairs={{0,1},{1,2},{2,3},{3,0},{4,5},{5,6},{6,7},{7,4},{8,9},{9,10},{10,1... | collective-permute-start | bytes 1032200 | tf_op jit(solution)/shard_map/ppermute | solution.py:555
  101.3 26.7 %collective-permute-start.17 = (bf16[448,768]{1,0:T(8,128)(2,1)S(1)}, bf16[448,768]{1,0:T(8,128)(2,1)S(1)}, u32[]{:S(2)}, u32[]{:S(2)}) collective-permute-start(bf16[448,768]{1,0:T(8,128)(2,1)S(1)} %copy-done.5), channel_id=1, source_target_pairs={{0,248},{8,0},{16,8},{24,16},{32,24},{40,32},{48,40},{56,48},{64,5... | collective-permute-start | bytes 2064392 | tf_op jit(solution)/shard_map/ppermute | solution.py:555
  119.6 22.8 %collective-permute-start.22 = (bf16[448,768]{1,0:T(8,128)(2,1)S(1)}, bf16[448,768]{1,0:T(8,128)(2,1)S(1)}, u32[]{:S(2)}, u32[]{:S(2)}) collective-permute-start(bf16[448,768]{1,0:T(8,128)(2,1)S(1)} %project.3), channel_id=1, source_target_pairs={{0,4},{4,0},{1,5},{5,1},{2,6},{6,2},{3,7},{7,3},{8,12},{12,8},{9,1... | collective-permute-start | bytes 2064392 | tf_op jit(solution)/shard_map/ppermute | solution.py:555

commit v8 on v7

--- a/solution.py
+++ b/solution.py
@@ -105,7 +105,7 @@
             scaled[head, at, :HD] = high
             scaled[head, at, HD:] = (exact - high.astype(jnp.float32)).astype(jnp.bfloat16)
 
-    def sweep(start, rows, count, place_of, waits):
+    def sweep(start, rows, count, place_of, waits, loop_heads):
         span = slice(start, start + rows)
         chunks = (count + 1) // 2
 
@@ -160,7 +160,7 @@
         def _():
             held[0:rows] = scores_of(0, 0)
 
-        if rows > ROWS:
+        if loop_heads:
 
             def unit(u, unused):
                 head, t = lax.rem(u, HEADS_HERE), u // HEADS_HERE
@@ -221,6 +221,15 @@
 
         return 0
 
+    def first_sources(waits):
+        @pl.when(active(1))
+        def _():
+            sweep(0, 2 * ROWS, n_live, lambda k: k, waits, True)
+
+        @pl.when(active(0) & jnp.logical_not(active(1)))
+        def _():
+            sweep(0, ROWS, n_live, lambda k: k, waits, True)
+
     def run():
         if resumed:
             for copy in state_copies():
@@ -235,7 +244,7 @@
                 place_copy(j, live_before(groups[p])).start()
 
         for i in range(many):
-            raw_copy(i).start()
+            pl.when(active(i))(raw_copy(i).start)
         if early:
             place_copy(0, own_place).wait()
             for k in range(len(EARLY)):
@@ -245,7 +254,7 @@
                     place_copy(0, k).wait()
 
         for i in range(many):
-            prepare(i)
+            pl.when(active(i))(functools.partial(prepare, i))
         if resumed:
             for copy in state_copies():
                 copy.wait()
@@ -254,9 +263,10 @@
             acc[...] = jnp.zeros(acc.shape, jnp.float32)
         if early:
 
+            first_sources(False)
+
             @pl.when(active(0))
             def _():
-                sweep(0, 2 * ROWS, n_live, lambda k: k, False)
                 for copy in out_copies(0):
                     copy.start()
 
@@ -266,6 +276,7 @@
                 n_before + 1,
                 lambda k: jnp.where(k < n_before, k, own_place),
                 False,
+                False,
             )
             for copy in out_copies(1):
                 copy.start()
@@ -279,10 +290,13 @@
 
             return
 
-        sweep(0, many * ROWS, n_live, lambda k: k, True)
-        lax.fori_loop(0, many, finish, 0)
+        if many == 2:
+            first_sources(True)
+        else:
+            sweep(0, ROWS, n_live, lambda k: k, True, False)
+        lax.fori_loop(0, jnp.where(active(many - 1), many, 1), finish, 0)
         for i in range(many):
-            share_copy(i).wait()
+            pl.when(active(i))(share_copy(i).wait)
 
     if early:
         run()

time: 146 us -> 143 us (0.979)
  the two profiles are of different devices: /device:TPU:64 before, /device:TPU:25 now
where the time goes in v8:
time: 143 us; the launch traced here: 141 us
  Pallas kernels  59.7 us (42%)
  waiting for transfers between devices  52.2 us (37%)
  starting transfers between devices  25.7 us (18%)
  local copies, waits for them, and re-layouts  2.45 us (2%)
    pallas_call x4, Pallas kernels, attend(): pl.pallas_call(functools.partial(attend_kernel, call), out_shape=out_shap...  45.6 us
    ppermute x16, waiting for transfers between devices, around(): lax.ppermute(value, axis, [(i, (i + steps) % count) for i in range(count)])  31.6 us
    ppermute x16, starting transfers between devices, around(): lax.ppermute(value, axis, [(i, (i + steps) % count) for i in range(count)])  17 us
    ppermute x3, waiting for transfers between devices, to_level(): return lax.ppermute(value, 'z', [(i, i - d) for i in range(d, 4)])  13.8 us
    ppermute x4, waiting for transfers between devices, back(): return lax.ppermute(share, SLOT, pairs_back)  6.83 us
    pallas_call x2, Pallas kernels, project(): pl.pallas_call(functools.partial(project_kernel, far), out_shape=jax.Shap...  5.61 us
    ppermute x4, starting transfers between devices, back(): return lax.ppermute(share, SLOT, pairs_back)  4.9 us
    ppermute x3, starting transfers between devices, to_level(): return lax.ppermute(value, 'z', [(i, i - d) for i in range(d, 4)])  3.86 us
  transfers between devices with their start and end apart: 23, of which 9 were waited for; matrix products, arithmetic and copies ran while one was open for 0% of the time, Pallas kernels for 40%

profile of v8, /device:TPU:25, one launch (start us, length us, event | category | flops | bytes accessed | tf_op | source)
XLA Modules:
  0.0 141.0 jit_solution(11584732327126145209)
XLA Ops:
  0.0 2.0 %pack.1.refs_3_.refs_1_ = bf16[448,768]{1,0:T(8,128)(2,1)} custom-call(bf16[448,384]{1,0:T(8,128)(2,1)} %keys.1, bf16[448,384]{1,0:T(8,128)(2,1)} %values.1), custom_call_target="tpu_custom_call" | custom-call | tf_op jit(solution)/shard_map/pack/pallas_call | solution.py:481
  2.0 0.7 collective-permute-start.4
  2.7 0.5 collective-permute-start.3
  3.1 2.2 %collective-permute-start.2 = (bf16[448,768]{1,0:T(8,128)(2,1)}, bf16[448,768]{1,0:T(8,128)(2,1)S(1)}, u32[]{:S(2)}, u32[]{:S(2)}) collective-permute-start(bf16[448,768]{1,0:T(8,128)(2,1)} %pack.1.refs_3_.refs_1_), channel_id=1, source_target_pairs={{0,16},{16,32},{32,48},{48,0},{1,17},{17,33},{33,49},{49,1},{2,18}... | collective-permute-start | bytes 2064392 | tf_op jit(solution)/shard_map/ppermute | solution.py:569
  5.3 1.3 collective-permute-start
  6.6 1.3 collective-permute-start.1
  8.6 0.1 stack.40.ids
  8.7 2.3 %copy-done = bf16[384,6144]{1,0:T(8,128)(2,1)S(1)} copy-done((bf16[384,6144]{1,0:T(8,128)(2,1)S(1)}, bf16[384,6144]{1,0:T(8,128)(2,1)}, u32[]{:S(2)}) %copy-start) | copy-done | bytes 4718616
  11.1 0.9 columns.1
  12.0 13.8 %collective-permute-done.refs_0_ = bf16[448,384]{1,0:T(8,128)(2,1)S(1)} collective-permute-done((bf16[448,384]{1,0:T(8,128)(2,1)}, bf16[448,384]{1,0:T(8,128)(2,1)S(1)}, u32[]{:S(2)}, u32[]{:S(2)}) %collective-permute-start) | collective-permute-done | bytes 344096 | tf_op jit(solution)/shard_map/ppermute | solution.py:587
  25.7 0.0 collective-permute-done.1.refs_1_
  25.8 1.3 collective-permute-start.5
  27.1 1.3 collective-permute-start.7
  28.3 1.5 %collective-permute-start.8 = (bf16[384,768]{1,0:T(8,128)(2,1)S(1)}, bf16[384,768]{1,0:T(8,128)(2,1)S(1)}, u32[]{:S(2)}, u32[]{:S(2)}) collective-permute-start(bf16[384,768]{1,0:T(8,128)(2,1)S(1)} %get-tuple-element.55), channel_id=1, source_target_pairs={{0,3},{1,0},{2,1},{3,2},{4,7},{5,4},{6,5},{7,6},{8,11},{9,8},{10,9... | collective-permute-start | bytes 1769480 | tf_op jit(solution)/shard_map/ppermute | solution.py:569
  29.8 1.7 %collective-permute-start.9 = (bf16[448,768]{1,0:T(8,128)(2,1)S(1)}, bf16[448,768]{1,0:T(8,128)(2,1)S(1)}, u32[]{:S(2)}, u32[]{:S(2)}) collective-permute-start(bf16[448,768]{1,0:T(8,128)(2,1)S(1)} %collective-permute-done.2.refs_4_.refs_2_), channel_id=1, source_target_pairs={{0,8},{8,0},{1,9},{9,1},{2,10},{10,2},{3,11},{11,3},{4,12},{12,4},... | collective-permute-start | bytes 2064392 | tf_op jit(solution)/shard_map/ppermute | solution.py:569
  31.5 15.7 %attend_early.1 = (f32[3,896,256]{2,1,0:T(8,128)S(1)}, f32[3,896,128]{2,1,0:T(8,128)S(1)}, f32[3,448,256]{2,1,0:T(8,128)S(1)}, f32[3,448,128]{2,1,0:T(8,128)S(1)}) custom-call(s32[9]{0:T(128)S(1)} %stack.40.ids, s32[32]{0:T(128)S(1)} %copy-done.4, s32[1]{0:T(128)S(6)} %copy.9.level, bf16[448,384]{1,0:T(8,128)(2,1)S(1)} %collective-permute-done.refs_0_, ...), custom_call_target="tpu_custom_call" | custom-call | flops 10000000000 | bytes 1000000 | tf_op jit(solution)/shard_map/attend_early/pallas_call | solution.py:324
  47.3 1.9 %collective-permute-start.10 = (bf16[448,768]{1,0:T(8,128)(2,1)S(1)}, bf16[448,768]{1,0:T(8,128)(2,1)S(1)}, u32[]{:S(2)}, u32[]{:S(2)}) collective-permute-start(bf16[448,768]{1,0:T(8,128)(2,1)S(1)} %collective-permute-done.3.refs_5_.refs_3_), channel_id=1, source_target_pairs={{0,8},{8,0},{1,9},{9,1},{2,10},{10,2},{3,11},{11,3},{4,12},{12,4},... | collective-permute-start | bytes 2064392 | tf_op jit(solution)/shard_map/ppermute | solution.py:569
  49.2 0.0 collective-permute-start.11
  49.2 1.5 %collective-permute-start.13 = (bf16[384,768]{1,0:T(8,128)(2,1)S(1)}, bf16[384,768]{1,0:T(8,128)(2,1)S(1)}, u32[]{:S(2)}, u32[]{:S(2)}) collective-permute-start(bf16[384,768]{1,0:T(8,128)(2,1)S(1)} %get-tuple-element.77), channel_id=1, source_target_pairs={{0,2},{1,3},{2,0},{3,1},{4,6},{5,7},{6,4},{7,5},{8,10},{9,11},{10,... | collective-permute-start | bytes 1769480 | tf_op jit(solution)/shard_map/ppermute | solution.py:569
  50.7 0.2 collective-permute-done.10.refs_7_.refs_4_.refs_3_
  50.9 1.0 collective-permute-done.11.refs_8_.refs_5_.refs_4_
  51.9 9.7 %attend_third.1 = bf16[480,384]{1,0:T(8,128)(2,1)S(1)} custom-call(s32[9]{0:T(128)S(1)} %stack.40.ids, s32[32]{0:T(128)S(1)} %copy-done.4, s32[1]{0:T(128)S(6)} %copy.9.level, bf16[448,384]{1,0:T(8,128)(2,1)S(1)} %collective-permute-done.5.refs_0_, bf16[448,768]{1,0:T(8,128)(2,1)S(1)} %copy-done.1, ...), custom_call_target="tpu_custom_call" | custom-call | flops 10000000000 | bytes 1000000 | tf_op jit(solution)/shard_map/attend_third/pallas_call | solution.py:324
  61.7 1.3 collective-permute-start.12
  63.0 12.9 %attend_middle.1 = (bf16[480,384]{1,0:T(8,128)(2,1)S(1)}, bf16[480,384]{1,0:T(8,128)(2,1)S(1)}) custom-call(s32[9]{0:T(128)S(1)} %stack.40.ids, s32[32]{0:T(128)S(1)} %copy-done.4, s32[1]{0:T(128)S(6)} %copy.9.level, bf16[448,384]{1,0:T(8,128)(2,1)S(1)} %collective-permute-done.refs_0_, bf16[448,384]{1,0:T(8,128)(2,1)S(1)} %collective-permute-done.1.refs_1_, ...), custom_call_target="tpu_custom_call" | custom-call | flops 49999998976 | bytes 1000000 | tf_op jit(solution)/shard_map/attend_middle/pallas_call | solution.py:324
  75.9 1.3 collective-permute-start.16
  77.2 1.9 %collective-permute-start.15 = (bf16[480,384]{1,0:T(8,128)(2,1)S(1)}, bf16[480,384]{1,0:T(8,128)(2,1)S(1)}, u32[]{:S(2)}, u32[]{:S(2)}) collective-permute-start(bf16[480,384]{1,0:T(8,128)(2,1)S(1)} %get-tuple-element.73), channel_id=1, source_target_pairs={{0,56},{8,64},{16,72},{24,80},{32,88},{40,96},{48,104},{56,112},{6... | collective-permute-start | bytes 1105928 | tf_op jit(solution)/shard_map/ppermute | solution.py:634
  79.1 7.3 %attend_late.1 = bf16[480,384]{1,0:T(8,128)(2,1)S(1)} custom-call(s32[9]{0:T(128)S(1)} %stack.40.ids, s32[32]{0:T(128)S(1)} %copy-done.4, s32[1]{0:T(128)S(6)} %copy.9.level, bf16[448,384]{1,0:T(8,128)(2,1)S(1)} %copy-done.2, bf16[448,768]{1,0:T(8,128)(2,1)S(1)} %collective-permute-done.6.refs_4_.refs_2_.refs_1_, ...), custom_call_target="tpu_custom_call" | custom-call | flops 1000000 | bytes 1000000 | tf_op jit(solution)/shard_map/attend_late/pallas_call | solution.py:324
  86.4 0.4 collective-permute-start.14
  86.8 0.9 stack.41.refs_5_
  87.7 0.0 copy-start.3
  87.7 0.0 copy-start.5
  87.8 0.1 collective-permute-start.21
  87.9 4.7 %collective-permute-done.16.three = bf16[480,384]{1,0:T(8,128)(2,1)S(1)} collective-permute-done((bf16[480,384]{1,0:T(8,128)(2,1)S(1)}, bf16[480,384]{1,0:T(8,128)(2,1)S(1)}, u32[]{:S(2)}, u32[]{:S(2)}) %collective-permute-start.16) | collective-permute-done | bytes 368672 | tf_op jit(solution)/shard_map/ppermute | solution.py:634
  92.6 1.9 %combine_later.1 = (f32[448,384]{1,0:T(8,128)S(1)}, f32[448,128]{1,0:T(8,128)S(1)}) custom-call(s32[9]{0:T(128)S(1)} %stack.40.ids, bf16[480,384]{1,0:T(8,128)(2,1)S(1)} %collective-permute-done.15.one, bf16[480,384]{1,0:T(8,128)(2,1)S(1)} %collective-permute-done.12.two, bf16[480,384]{1,0:T(8,128)(2,1)S(1)} %collective-permute-done.16.three), custom_call_target="tpu_custom_call" | custom-call | flops 99999997952 | bytes 200000000 | tf_op jit(solution)/shard_map/combine_later/pallas_call | solution.py:405
  94.5 2.1 %collective-permute-done.14.zero = bf16[480,384]{1,0:T(8,128)(2,1)S(1)} collective-permute-done((bf16[480,384]{1,0:T(8,128)(2,1)S(1)}, bf16[480,384]{1,0:T(8,128)(2,1)S(1)}, u32[]{:S(2)}, u32[]{:S(2)}) %collective-permute-start.14) | collective-permute-done | bytes 368672 | tf_op jit(solution)/shard_map/ppermute | solution.py:634
  96.6 1.2 combine.1
  97.8 1.3 collective-permute-start.20
  99.1 0.5 collective-permute-start.19
  99.6 0.6 collective-permute-start.18
  100.2 0.1 collective-permute-start.17
  100.3 7.6 %collective-permute-done.20.refs_3_ = bf16[448,384]{1,0:T(8,128)(2,1)S(1)} collective-permute-done((bf16[448,384]{1,0:T(8,128)(2,1)S(1)}, bf16[448,384]{1,0:T(8,128)(2,1)S(1)}, u32[]{:S(2)}, u32[]{:S(2)}) %collective-permute-start.20) | collective-permute-done | bytes 344096 | tf_op jit(solution)/shard_map/ppermute | solution.py:569
  107.9 2.7 %collective-permute-done.19.refs_2_ = bf16[448,384]{1,0:T(8,128)(2,1)S(1)} collective-permute-done((bf16[448,384]{1,0:T(8,128)(2,1)S(1)}, bf16[448,384]{1,0:T(8,128)(2,1)S(1)}, u32[]{:S(2)}, u32[]{:S(2)}) %collective-permute-start.19) | collective-permute-done | bytes 344096 | tf_op jit(solution)/shard_map/ppermute | solution.py:569
  110.7 7.4 %collective-permute-done.18.refs_1_ = bf16[448,384]{1,0:T(8,128)(2,1)S(1)} collective-permute-done((bf16[448,384]{1,0:T(8,128)(2,1)S(1)}, bf16[448,384]{1,0:T(8,128)(2,1)S(1)}, u32[]{:S(2)}, u32[]{:S(2)}) %collective-permute-start.18) | collective-permute-done | bytes 344096 | tf_op jit(solution)/shard_map/ppermute | solution.py:569
  118.0 2.8 %project.3 = bf16[448,768]{1,0:T(8,128)(2,1)S(1)} custom-call(s32[9]{0:T(128)S(1)} %stack.40.ids, bf16[448,384]{1,0:T(8,128)(2,1)S(1)} %get-tuple-element.86.refs_0_, bf16[448,384]{1,0:T(8,128)(2,1)S(1)} %collective-permute-done.18.refs_1_, bf16[448,384]{1,0:T(8,128)(2,1)S(1)} %collective-permute-done.19.refs_2_, ...), custom_call_target="tpu_custom_call" | custom-call | flops 1056964608 | bytes 5000000 | tf_op jit(solution)/shard_map/project/pallas_call | solution.py:553
  120.8 3.1 %collective-permute-start.22 = (bf16[448,768]{1,0:T(8,128)(2,1)S(1)}, bf16[448,768]{1,0:T(8,128)(2,1)S(1)}, u32[]{:S(2)}, u32[]{:S(2)}) collective-permute-start(bf16[448,768]{1,0:T(8,128)(2,1)S(1)} %project.3), channel_id=1, source_target_pairs={{0,4},{4,0},{1,5},{5,1},{2,6},{6,2},{3,7},{7,3},{8,12},{12,8},{9,1... | collective-permute-start | bytes 2064392 | tf_op jit(solution)/shard_map/ppermute | solution.py:569
  123.9 2.8 %project.2.near = f32[448,768]{1,0:T(8,128)S(1)} custom-call(s32[9]{0:T(128)S(1)} %stack.40.ids, bf16[448,384]{1,0:T(8,128)(2,1)S(1)} %get-tuple-element.86.refs_0_, bf16[448,384]{1,0:T(8,128)(2,1)S(1)} %collective-permute-done.18.refs_1_, bf16[448,384]{1,0:T(8,128)(2,1)S(1)} %collective-permute-done.19.refs_2_, ...), custom_call_target="tpu_custom_call" | custom-call | flops 1056964608 | bytes 5000000 | tf_op jit(solution)/shard_map/project/pallas_call | solution.py:553
  126.8 12.7 %collective-permute-done.22.arrived = bf16[448,768]{1,0:T(8,128)(2,1)S(1)} collective-permute-done((bf16[448,768]{1,0:T(8,128)(2,1)S(1)}, bf16[448,768]{1,0:T(8,128)(2,1)S(1)}, u32[]{:S(2)}, u32[]{:S(2)}) %collective-permute-start.22) | collective-permute-done | bytes 688160 | tf_op jit(solution)/shard_map/ppermute | solution.py:569
  139.4 1.6 %finish.1 = bf16[448,768]{1,0:T(8,128)(2,1)} custom-call(bf16[448,768]{1,0:T(8,128)(2,1)S(1)} %collective-permute-done.17.hidden, f32[448,768]{1,0:T(8,128)S(1)} %project.2.near, bf16[448,768]{1,0:T(8,128)(2,1)S(1)} %collective-permute-done.22.arrived, f32[1,768]{1,0:T(1,128)S(1)} %get-tuple-element.92.gate), custom_call_target="tpu_custom_call" | custom-call | tf_op jit(solution)/shard_map/finish/pallas_call | solution.py:463
  (23 shorter events, 0.1 us)
Async XLA Ops:
  2.0 23.7 %collective-permute-start.4 = (bf16[448,768]{1,0:T(8,128)(2,1)}, bf16[448,768]{1,0:T(8,128)(2,1)S(1)}, u32[]{:S(2)}, u32[]{:S(2)}) collective-permute-start(bf16[448,768]{1,0:T(8,128)(2,1)} %pack.1.refs_3_.refs_1_), channel_id=1, source_target_pairs={{0,8},{8,0},{1,9},{9,1},{2,10},{10,2},{3,11},{11,3},{4,12},{12,4},... | collective-permute-start | bytes 2064392 | tf_op jit(solution)/shard_map/ppermute | solution.py:569
  2.7 23.1 %collective-permute-start.3 = (bf16[448,768]{1,0:T(8,128)(2,1)}, bf16[448,768]{1,0:T(8,128)(2,1)S(1)}, u32[]{:S(2)}, u32[]{:S(2)}) collective-permute-start(bf16[448,768]{1,0:T(8,128)(2,1)} %pack.1.refs_3_.refs_1_), channel_id=1, source_target_pairs={{0,48},{16,0},{32,16},{48,32},{1,49},{17,1},{33,17},{49,33},{2,50}... | collective-permute-start | bytes 2064392 | tf_op jit(solution)/shard_map/ppermute | solution.py:569
  3.1 22.6 %collective-permute-start.2 = (bf16[448,768]{1,0:T(8,128)(2,1)}, bf16[448,768]{1,0:T(8,128)(2,1)S(1)}, u32[]{:S(2)}, u32[]{:S(2)}) collective-permute-start(bf16[448,768]{1,0:T(8,128)(2,1)} %pack.1.refs_3_.refs_1_), channel_id=1, source_target_pairs={{0,16},{16,32},{32,48},{48,0},{1,17},{17,33},{33,49},{49,1},{2,18}... | collective-permute-start | bytes 2064392 | tf_op jit(solution)/shard_map/ppermute | solution.py:569
  5.3 20.4 %collective-permute-start = (bf16[448,384]{1,0:T(8,128)(2,1)}, bf16[448,384]{1,0:T(8,128)(2,1)S(1)}, u32[]{:S(2)}, u32[]{:S(2)}) collective-permute-start(bf16[448,384]{1,0:T(8,128)(2,1)} %refs_0_.2), channel_id=1, source_target_pairs={{64,0},{128,64},{192,128},{65,1},{129,65},{193,129},{66,2},{130,66... | collective-permute-start | bytes 1032200 | tf_op jit(solution)/shard_map/ppermute | solution.py:587
  6.6 19.1 %collective-permute-start.1 = (bf16[448,384]{1,0:T(8,128)(2,1)}, bf16[448,384]{1,0:T(8,128)(2,1)S(1)}, u32[]{:S(2)}, u32[]{:S(2)}) collective-permute-start(bf16[448,384]{1,0:T(8,128)(2,1)} %refs_0_.2), channel_id=1, source_target_pairs={{192,0},{193,1},{194,2},{195,3},{196,4},{197,5},{198,6},{199,7},{2... | collective-permute-start | bytes 1032200 | tf_op jit(solution)/shard_map/ppermute | solution.py:587
  8.7 2.3 %copy-start = (bf16[384,6144]{1,0:T(8,128)(2,1)S(1)}, bf16[384,6144]{1,0:T(8,128)(2,1)}, u32[]{:S(2)}) copy-start(bf16[384,6144]{1,0:T(8,128)(2,1)} %refs_0_.1) | copy-start | bytes 14155780
  11.0 14.7 %copy-start.2 = (bf16[448,384]{1,0:T(8,128)(2,1)S(1)}, bf16[448,384]{1,0:T(8,128)(2,1)}, u32[]{:S(2)}) copy-start(bf16[448,384]{1,0:T(8,128)(2,1)} %refs_0_.2) | copy-start | bytes 1032196
  11.1 18.8 %copy-start.1 = (bf16[448,768]{1,0:T(8,128)(2,1)S(1)}, bf16[448,768]{1,0:T(8,128)(2,1)}, u32[]{:S(2)}) copy-start(bf16[448,768]{1,0:T(8,128)(2,1)} %pack.1.refs_3_.refs_1_) | copy-start | bytes 2064388
  11.1 20.4 %copy-start.4 = (s32[32]{0:T(128)S(1)}, s32[32]{0:T(128)}, u32[]{:S(2)}) copy-start(s32[32]{0:T(128)} %live.5) | copy-start | bytes 388
  25.8 21.5 %collective-permute-start.5 = (bf16[448,384]{1,0:T(8,128)(2,1)S(1)}, bf16[448,384]{1,0:T(8,128)(2,1)S(1)}, u32[]{:S(2)}, u32[]{:S(2)}) collective-permute-start(bf16[448,384]{1,0:T(8,128)(2,1)S(1)} %copy-done.2), channel_id=1, source_target_pairs={{128,0},{192,64},{129,1},{193,65},{130,2},{194,66},{131,3},{195,67... | collective-permute-start | bytes 1032200 | tf_op jit(solution)/shard_map/ppermute | solution.py:587
  27.1 20.2 %collective-permute-start.7 = (bf16[384,768]{1,0:T(8,128)(2,1)S(1)}, bf16[384,768]{1,0:T(8,128)(2,1)S(1)}, u32[]{:S(2)}, u32[]{:S(2)}) collective-permute-start(bf16[384,768]{1,0:T(8,128)(2,1)S(1)} %get-tuple-element.54), channel_id=1, source_target_pairs={{0,1},{1,2},{2,3},{3,0},{4,5},{5,6},{6,7},{7,4},{8,9},{9,10},{10,1... | collective-permute-start | bytes 1769480 | tf_op jit(solution)/shard_map/ppermute | solution.py:569
  28.3 18.9 %collective-permute-start.8 = (bf16[384,768]{1,0:T(8,128)(2,1)S(1)}, bf16[384,768]{1,0:T(8,128)(2,1)S(1)}, u32[]{:S(2)}, u32[]{:S(2)}) collective-permute-start(bf16[384,768]{1,0:T(8,128)(2,1)S(1)} %get-tuple-element.55), channel_id=1, source_target_pairs={{0,3},{1,0},{2,1},{3,2},{4,7},{5,4},{6,5},{7,6},{8,11},{9,8},{10,9... | collective-permute-start | bytes 1769480 | tf_op jit(solution)/shard_map/ppermute | solution.py:569
  29.8 17.5 %collective-permute-start.6 = (bf16[448,768]{1,0:T(8,128)(2,1)S(1)}, bf16[448,768]{1,0:T(8,128)(2,1)S(1)}, u32[]{:S(2)}, u32[]{:S(2)}) collective-permute-start(bf16[448,768]{1,0:T(8,128)(2,1)S(1)} %copy-done.1), channel_id=1, source_target_pairs={{0,32},{16,48},{32,0},{48,16},{1,33},{17,49},{33,1},{49,17},{2,34}... | collective-permute-start | bytes 2064392 | tf_op jit(solution)/shard_map/ppermute | solution.py:569
  29.8 17.5 %collective-permute-start.9 = (bf16[448,768]{1,0:T(8,128)(2,1)S(1)}, bf16[448,768]{1,0:T(8,128)(2,1)S(1)}, u32[]{:S(2)}, u32[]{:S(2)}) collective-permute-start(bf16[448,768]{1,0:T(8,128)(2,1)S(1)} %collective-permute-done.2.refs_4_.refs_2_), channel_id=1, source_target_pairs={{0,8},{8,0},{1,9},{9,1},{2,10},{10,2},{3,11},{11,3},{4,12},{12,4},... | collective-permute-start | bytes 2064392 | tf_op jit(solution)/shard_map/ppermute | solution.py:569
  47.3 3.7 %collective-permute-start.10 = (bf16[448,768]{1,0:T(8,128)(2,1)S(1)}, bf16[448,768]{1,0:T(8,128)(2,1)S(1)}, u32[]{:S(2)}, u32[]{:S(2)}) collective-permute-start(bf16[448,768]{1,0:T(8,128)(2,1)S(1)} %collective-permute-done.3.refs_5_.refs_3_), channel_id=1, source_target_pairs={{0,8},{8,0},{1,9},{9,1},{2,10},{10,2},{3,11},{11,3},{4,12},{12,4},... | collective-permute-start | bytes 2064392 | tf_op jit(solution)/shard_map/ppermute | solution.py:569
  49.2 2.8 %collective-permute-start.11 = (bf16[448,768]{1,0:T(8,128)(2,1)S(1)}, bf16[448,768]{1,0:T(8,128)(2,1)S(1)}, u32[]{:S(2)}, u32[]{:S(2)}) collective-permute-start(bf16[448,768]{1,0:T(8,128)(2,1)S(1)} %collective-permute-done.6.refs_4_.refs_2_.refs_1_), channel_id=1, source_target_pairs={{0,8},{8,0},{1,9},{9,1},{2,10},{10,2},{3,11},{11,3},{4,12},{12,4},... | collective-permute-start | bytes 2064392 | tf_op jit(solution)/shard_map/ppermute | solution.py:569
  49.2 37.2 %collective-permute-start.13 = (bf16[384,768]{1,0:T(8,128)(2,1)S(1)}, bf16[384,768]{1,0:T(8,128)(2,1)S(1)}, u32[]{:S(2)}, u32[]{:S(2)}) collective-permute-start(bf16[384,768]{1,0:T(8,128)(2,1)S(1)} %get-tuple-element.77), channel_id=1, source_target_pairs={{0,2},{1,3},{2,0},{3,1},{4,6},{5,7},{6,4},{7,5},{8,10},{9,11},{10,... | collective-permute-start | bytes 1769480 | tf_op jit(solution)/shard_map/ppermute | solution.py:569
  61.7 24.8 %collective-permute-start.12 = (bf16[480,384]{1,0:T(8,128)(2,1)S(1)}, bf16[480,384]{1,0:T(8,128)(2,1)S(1)}, u32[]{:S(2)}, u32[]{:S(2)}) collective-permute-start(bf16[480,384]{1,0:T(8,128)(2,1)S(1)} %attend_third.1), channel_id=1, source_target_pairs={{0,120},{8,128},{16,136},{24,144},{32,152},{40,160},{48,168},{56,1... | collective-permute-start | bytes 1105928 | tf_op jit(solution)/shard_map/ppermute | solution.py:634
  75.9 16.7 %collective-permute-start.16 = (bf16[480,384]{1,0:T(8,128)(2,1)S(1)}, bf16[480,384]{1,0:T(8,128)(2,1)S(1)}, u32[]{:S(2)}, u32[]{:S(2)}) collective-permute-start(bf16[480,384]{1,0:T(8,128)(2,1)S(1)} %get-tuple-element.80), channel_id=1, source_target_pairs={{0,184},{8,192},{16,200},{24,208},{32,216},{40,224},{48,232},{56,2... | collective-permute-start | bytes 1105928 | tf_op jit(solution)/shard_map/ppermute | solution.py:634
  77.2 15.4 %collective-permute-start.15 = (bf16[480,384]{1,0:T(8,128)(2,1)S(1)}, bf16[480,384]{1,0:T(8,128)(2,1)S(1)}, u32[]{:S(2)}, u32[]{:S(2)}) collective-permute-start(bf16[480,384]{1,0:T(8,128)(2,1)S(1)} %get-tuple-element.73), channel_id=1, source_target_pairs={{0,56},{8,64},{16,72},{24,80},{32,88},{40,96},{48,104},{56,112},{6... | collective-permute-start | bytes 1105928 | tf_op jit(solution)/shard_map/ppermute | solution.py:634
  86.4 10.1 %collective-permute-start.14 = (bf16[480,384]{1,0:T(8,128)(2,1)S(1)}, bf16[480,384]{1,0:T(8,128)(2,1)S(1)}, u32[]{:S(2)}, u32[]{:S(2)}) collective-permute-start(bf16[480,384]{1,0:T(8,128)(2,1)S(1)} %attend_late.1), channel_id=1, source_target_pairs={{0,248},{8,0},{16,8},{24,16},{32,24},{40,32},{48,40},{56,48},{64,5... | collective-permute-start | bytes 1105928 | tf_op jit(solution)/shard_map/ppermute | solution.py:634
  87.7 8.8 %copy-start.3 = (f32[64,768]{1,0:T(8,128)S(1)}, f32[64,768]{1,0:T(8,128)}, u32[]{:S(2)}) copy-start(f32[64,768]{1,0:T(8,128)} %table.1) | copy-start | bytes 589828
  87.7 12.5 %copy-start.5 = (bf16[448,768]{1,0:T(8,128)(2,1)S(1)}, bf16[448,768]{1,0:T(8,128)(2,1)}, u32[]{:S(2)}) copy-start(bf16[448,768]{1,0:T(8,128)(2,1)} %param.8) | copy-start | bytes 2064388
  87.8 30.3 %collective-permute-start.21 = (bf16[3,384,768]{2,1,0:T(8,128)(2,1)S(1)}, bf16[3,384,768]{2,1,0:T(8,128)(2,1)S(1)}, u32[]{:S(2)}, u32[]{:S(2)}) collective-permute-start(bf16[3,384,768]{2,1,0:T(8,128)(2,1)S(1)} %stack.41.refs_5_), channel_id=1, source_target_pairs={{0,8},{8,0},{1,9},{9,1},{2,10},{10,2},{3,11},{11,3},{4,12},{12,4},... | collective-permute-start | bytes 5308424 | tf_op jit(solution)/shard_map/ppermute | solution.py:569
  97.8 10.2 %collective-permute-start.20 = (bf16[448,384]{1,0:T(8,128)(2,1)S(1)}, bf16[448,384]{1,0:T(8,128)(2,1)S(1)}, u32[]{:S(2)}, u32[]{:S(2)}) collective-permute-start(bf16[448,384]{1,0:T(8,128)(2,1)S(1)} %get-tuple-element.86.refs_0_), channel_id=1, source_target_pairs={{0,3},{1,0},{2,1},{3,2},{4,7},{5,4},{6,5},{7,6},{8,11},{9,8},{10,9... | collective-permute-start | bytes 1032200 | tf_op jit(solution)/shard_map/ppermute | solution.py:569
  99.1 11.5 %collective-permute-start.19 = (bf16[448,384]{1,0:T(8,128)(2,1)S(1)}, bf16[448,384]{1,0:T(8,128)(2,1)S(1)}, u32[]{:S(2)}, u32[]{:S(2)}) collective-permute-start(bf16[448,384]{1,0:T(8,128)(2,1)S(1)} %get-tuple-element.86.refs_0_), channel_id=1, source_target_pairs={{0,2},{1,3},{2,0},{3,1},{4,6},{5,7},{6,4},{7,5},{8,10},{9,11},{10,... | collective-permute-start | bytes 1032200 | tf_op jit(solution)/shard_map/ppermute | solution.py:569
  99.6 18.4 %collective-permute-start.18 = (bf16[448,384]{1,0:T(8,128)(2,1)S(1)}, bf16[448,384]{1,0:T(8,128)(2,1)S(1)}, u32[]{:S(2)}, u32[]{:S(2)}) collective-permute-start(bf16[448,384]{1,0:T(8,128)(2,1)S(1)} %get-tuple-element.86.refs_0_), channel_id=1, source_target_pairs={{0,1},{1,2},{2,3},{3,0},{4,5},{5,6},{6,7},{7,4},{8,9},{9,10},{10,1... | collective-permute-start | bytes 1032200 | tf_op jit(solution)/shard_map/ppermute | solution.py:569
  100.2 26.5 %collective-permute-start.17 = (bf16[448,768]{1,0:T(8,128)(2,1)S(1)}, bf16[448,768]{1,0:T(8,128)(2,1)S(1)}, u32[]{:S(2)}, u32[]{:S(2)}) collective-permute-start(bf16[448,768]{1,0:T(8,128)(2,1)S(1)} %copy-done.5), channel_id=1, source_target_pairs={{0,248},{8,0},{16,8},{24,16},{32,24},{40,32},{48,40},{56,48},{64,5... | collective-permute-start | bytes 2064392 | tf_op jit(solution)/shard_map/ppermute | solution.py:569
  120.8 18.6 %collective-permute-start.22 = (bf16[448,768]{1,0:T(8,128)(2,1)S(1)}, bf16[448,768]{1,0:T(8,128)(2,1)S(1)}, u32[]{:S(2)}, u32[]{:S(2)}) collective-permute-start(bf16[448,768]{1,0:T(8,128)(2,1)S(1)} %project.3), channel_id=1, source_target_pairs={{0,4},{4,0},{1,5},{5,1},{2,6},{6,2},{3,7},{7,3},{8,12},{12,8},{9,1... | collective-permute-start | bytes 2064392 | tf_op jit(solution)/shard_map/ppermute | solution.py:569

commit v9 on v8

--- a/solution.py
+++ b/solution.py
@@ -530,12 +530,16 @@
     def _():
         pltpu.make_async_copy(swapped, held, sem).start()
 
-    pltpu.make_async_copy(fetched, held, sem).wait()
     block = out.shape[1] // 3
 
     def columns(n, unused):
         at = pl.ds(pl.multiple_of(n * block, block), block)
         total = jnp.dot(rows[0][...], own[:, at], preferred_element_type=jnp.float32)
+
+        @pl.when(n == 0)
+        def _():
+            pltpu.make_async_copy(fetched, held, sem).wait()
+
         for k in range(3):
             total = total + jnp.dot(
                 rows[k + 1][...], held[k, :, at], preferred_element_type=jnp.float32
@@ -613,19 +617,19 @@
         [next_one, next_three, queries],
         [pair, below, above, None, pair_there],
     )
-    next_two, across, piece_one, piece_three, below_there, piece_two, above, *states = together(
+    next_two, across, piece_three, below_there, above_there, piece_one, piece_two, *states = together(
         to_level(queries, 2),
         around(pair, "y", 2),
-        around(pieces[0], "x", 1),
         around(pieces[2], "x", 3),
         around(below, "c", 1),
+        around(above, "c", 1),
+        pieces[0],
         pieces[1],
-        above,
         *states,
     )
-    above_there, across_there = around(above, "c", 1), around(across, "c", 1)
+    across_there = around(across, "c", 1)
     pairs = [pair, below, above, across, pair_there, below_there, above_there, across_there]
-    piece_two = around(piece_two, "x", 2)
+    piece_one, piece_two = around(piece_one, "x", 1), around(piece_two, "x", 2)
 
     def back(share, d):
         pairs_back = [
@@ -642,7 +646,7 @@
     back_one, back_three = back(one, 1), back(three, 3)
     live_late, one = together(group_live, one)
     (zero,) = attend("late", ids, live_late, noise_level, [queries], pairs, states[2:4])
-    zero, back_two, piece_two = together(zero, back_two, piece_two)
+    zero, back_two, piece_one, piece_two = together(zero, back_two, piece_one, piece_two)
     (fetched,) = copied(
         "stack",
         ids,

time: 143 us -> 141 us (0.986)
  Pallas kernels: 59.7 us -> 53.1 us
  starting transfers between devices: 25.7 us -> 29.7 us
    pallas_call x4, Pallas kernels: 45.6 us -> 38.9 us  [attend(): pl.pallas_call(functools.partial(attend_kernel, call), out_shape=out_shap...]
    ppermute x4, starting transfers between devices: 4.9 us -> 11.4 us  [back(): return lax.ppermute(share, SLOT, pairs_back)]
    ppermute x16, starting transfers between devices: 17 us -> 14.4 us  [around(): lax.ppermute(value, axis, [(i, (i + steps) % count) for i in range(count)])]
    ppermute x4, waiting for transfers between devices: 6.83 us -> 9.15 us  [back(): return lax.ppermute(share, SLOT, pairs_back)]
    ppermute x16, waiting for transfers between devices: 31.6 us -> 30.1 us  [around(): lax.ppermute(value, axis, [(i, (i + steps) % count) for i in range(count)])]
  transfers between devices with their start and end apart: 23 -> 23, of which waited for: 9 -> 7; matrix products, arithmetic and copies ran while one was open for 0% -> 0% of each run, Pallas kernels for 40% -> 36%
where the time goes in v9:
time: 141 us; the launch traced here: 139 us
  Pallas kernels  53.1 us (38%)
  waiting for transfers between devices  53 us (38%)
  starting transfers between devices  29.7 us (21%)
  local copies, waits for them, and re-layouts  2.45 us (2%)
    pallas_call x4, Pallas kernels, attend(): pl.pallas_call(functools.partial(attend_kernel, call), out_shape=out_shap...  38.9 us
    ppermute x16, waiting for transfers between devices, around(): lax.ppermute(value, axis, [(i, (i + steps) % count) for i in range(count)])  30.1 us
    ppermute x16, starting transfers between devices, around(): lax.ppermute(value, axis, [(i, (i + steps) % count) for i in range(count)])  14.4 us
    ppermute x3, waiting for transfers between devices, to_level(): return lax.ppermute(value, 'z', [(i, i - d) for i in range(d, 4)])  13.8 us
    ppermute x4, starting transfers between devices, back(): return lax.ppermute(share, SLOT, pairs_back)  11.4 us
    ppermute x4, waiting for transfers between devices, back(): return lax.ppermute(share, SLOT, pairs_back)  9.15 us
    pallas_call x2, Pallas kernels, project(): pl.pallas_call(functools.partial(project_kernel, far), out_shape=jax.Shap...  5.82 us
    ppermute x3, starting transfers between devices, to_level(): return lax.ppermute(value, 'z', [(i, i - d) for i in range(d, 4)])  3.86 us
  transfers between devices with their start and end apart: 23, of which 7 were waited for; matrix products, arithmetic and copies ran while one was open for 0% of the time, Pallas kernels for 36%

profile of v9, /device:TPU:25, one launch (start us, length us, event | category | flops | bytes accessed | tf_op | source)
XLA Modules:
  0.0 139.2 jit_solution(16512448299631303717)
XLA Ops:
  0.0 2.0 %pack.1.refs_3_.refs_1_ = bf16[448,768]{1,0:T(8,128)(2,1)} custom-call(bf16[448,384]{1,0:T(8,128)(2,1)} %keys.1, bf16[448,384]{1,0:T(8,128)(2,1)} %values.1), custom_call_target="tpu_custom_call" | custom-call | tf_op jit(solution)/shard_map/pack/pallas_call | solution.py:481
  2.0 0.7 collective-permute-start.4
  2.7 0.5 collective-permute-start.3
  3.1 2.2 %collective-permute-start.2 = (bf16[448,768]{1,0:T(8,128)(2,1)}, bf16[448,768]{1,0:T(8,128)(2,1)S(1)}, u32[]{:S(2)}, u32[]{:S(2)}) collective-permute-start(bf16[448,768]{1,0:T(8,128)(2,1)} %pack.1.refs_3_.refs_1_), channel_id=1, source_target_pairs={{0,16},{16,32},{32,48},{48,0},{1,17},{17,33},{33,49},{49,1},{2,18}... | collective-permute-start | bytes 2064392 | tf_op jit(solution)/shard_map/ppermute | solution.py:573
  5.3 1.3 collective-permute-start
  6.6 1.3 collective-permute-start.1
  8.6 0.1 stack.40.ids
  8.7 2.3 %copy-done = bf16[384,6144]{1,0:T(8,128)(2,1)S(1)} copy-done((bf16[384,6144]{1,0:T(8,128)(2,1)S(1)}, bf16[384,6144]{1,0:T(8,128)(2,1)}, u32[]{:S(2)}) %copy-start) | copy-done | bytes 4718616
  11.1 0.9 columns.1
  12.0 13.8 %collective-permute-done.refs_0_ = bf16[448,384]{1,0:T(8,128)(2,1)S(1)} collective-permute-done((bf16[448,384]{1,0:T(8,128)(2,1)}, bf16[448,384]{1,0:T(8,128)(2,1)S(1)}, u32[]{:S(2)}, u32[]{:S(2)}) %collective-permute-start) | collective-permute-done | bytes 344096 | tf_op jit(solution)/shard_map/ppermute | solution.py:591
  25.7 0.0 collective-permute-done.2.refs_4_.refs_2_
  25.8 1.3 collective-permute-start.5
  27.1 2.6 %collective-permute-start.7 = (bf16[384,768]{1,0:T(8,128)(2,1)S(1)}, bf16[384,768]{1,0:T(8,128)(2,1)S(1)}, u32[]{:S(2)}, u32[]{:S(2)}) collective-permute-start(bf16[384,768]{1,0:T(8,128)(2,1)S(1)} %get-tuple-element.55), channel_id=1, source_target_pairs={{0,3},{1,0},{2,1},{3,2},{4,7},{5,4},{6,5},{7,6},{8,11},{9,8},{10,9... | collective-permute-start | bytes 1769480 | tf_op jit(solution)/shard_map/ppermute | solution.py:573
  29.6 0.0 collective-permute-start.6
  29.6 1.4 %collective-permute-start.8 = (bf16[448,768]{1,0:T(8,128)(2,1)S(1)}, bf16[448,768]{1,0:T(8,128)(2,1)S(1)}, u32[]{:S(2)}, u32[]{:S(2)}) collective-permute-start(bf16[448,768]{1,0:T(8,128)(2,1)S(1)} %collective-permute-done.2.refs_4_.refs_2_), channel_id=1, source_target_pairs={{0,8},{8,0},{1,9},{9,1},{2,10},{10,2},{3,11},{11,3},{4,12},{12,4},... | collective-permute-start | bytes 2064392 | tf_op jit(solution)/shard_map/ppermute | solution.py:573
  31.0 0.1 collective-permute-start.9
  31.1 15.7 %attend_early.1 = (f32[3,896,256]{2,1,0:T(8,128)S(1)}, f32[3,896,128]{2,1,0:T(8,128)S(1)}, f32[3,448,256]{2,1,0:T(8,128)S(1)}, f32[3,448,128]{2,1,0:T(8,128)S(1)}) custom-call(s32[9]{0:T(128)S(1)} %stack.40.ids, s32[32]{0:T(128)S(1)} %copy-done.4, s32[1]{0:T(128)S(6)} %copy.9.level, bf16[448,384]{1,0:T(8,128)(2,1)S(1)} %collective-permute-done.refs_0_, ...), custom_call_target="tpu_custom_call" | custom-call | flops 10000000000 | bytes 1000000 | tf_op jit(solution)/shard_map/attend_early/pallas_call | solution.py:324
  46.8 0.0 collective-permute-done.7.refs_2_
  46.9 0.0 collective-permute-done.6.refs_4_.refs_2_.refs_1_
  46.9 2.1 %collective-permute-start.10 = (bf16[448,768]{1,0:T(8,128)(2,1)S(1)}, bf16[448,768]{1,0:T(8,128)(2,1)S(1)}, u32[]{:S(2)}, u32[]{:S(2)}) collective-permute-start(bf16[448,768]{1,0:T(8,128)(2,1)S(1)} %collective-permute-done.6.refs_4_.refs_2_.refs_1_), channel_id=1, source_target_pairs={{0,8},{8,0},{1,9},{9,1},{2,10},{10,2},{3,11},{11,3},{4,12},{12,4},... | collective-permute-start | bytes 2064392 | tf_op jit(solution)/shard_map/ppermute | solution.py:573
  49.0 1.7 %collective-permute-start.13 = (bf16[384,768]{1,0:T(8,128)(2,1)S(1)}, bf16[384,768]{1,0:T(8,128)(2,1)S(1)}, u32[]{:S(2)}, u32[]{:S(2)}) collective-permute-start(bf16[384,768]{1,0:T(8,128)(2,1)S(1)} %get-tuple-element.79), channel_id=1, source_target_pairs={{0,2},{1,3},{2,0},{3,1},{4,6},{5,7},{6,4},{7,5},{8,10},{9,11},{10,... | collective-permute-start | bytes 1769480 | tf_op jit(solution)/shard_map/ppermute | solution.py:573
  50.7 0.0 collective-permute-done.10.refs_8_.refs_5_.refs_4_
  50.8 9.7 %attend_third.1 = bf16[480,384]{1,0:T(8,128)(2,1)S(1)} custom-call(s32[9]{0:T(128)S(1)} %stack.40.ids, s32[32]{0:T(128)S(1)} %copy-done.4, s32[1]{0:T(128)S(6)} %copy.9.level, bf16[448,384]{1,0:T(8,128)(2,1)S(1)} %collective-permute-done.5.refs_0_, bf16[448,768]{1,0:T(8,128)(2,1)S(1)} %copy-done.1, ...), custom_call_target="tpu_custom_call" | custom-call | flops 10000000000 | bytes 1000000 | tf_op jit(solution)/shard_map/attend_third/pallas_call | solution.py:324
  60.4 1.3 collective-permute-start.11
  61.8 8.4 %attend_middle.1 = (bf16[480,384]{1,0:T(8,128)(2,1)S(1)}, bf16[480,384]{1,0:T(8,128)(2,1)S(1)}) custom-call(s32[9]{0:T(128)S(1)} %stack.40.ids, s32[32]{0:T(128)S(1)} %copy-done.4, s32[1]{0:T(128)S(6)} %copy.9.level, bf16[448,384]{1,0:T(8,128)(2,1)S(1)} %collective-permute-done.refs_0_, bf16[448,384]{1,0:T(8,128)(2,1)S(1)} %collective-permute-done.1.refs_1_, ...), custom_call_target="tpu_custom_call" | custom-call | flops 49999998976 | bytes 1000000 | tf_op jit(solution)/shard_map/attend_middle/pallas_call | solution.py:324
  70.2 1.3 collective-permute-start.16
  71.5 6.8 %collective-permute-start.15 = (bf16[480,384]{1,0:T(8,128)(2,1)S(1)}, bf16[480,384]{1,0:T(8,128)(2,1)S(1)}, u32[]{:S(2)}, u32[]{:S(2)}) collective-permute-start(bf16[480,384]{1,0:T(8,128)(2,1)S(1)} %get-tuple-element.74), channel_id=1, source_target_pairs={{0,56},{8,64},{16,72},{24,80},{32,88},{40,96},{48,104},{56,112},{6... | collective-permute-start | bytes 1105928 | tf_op jit(solution)/shard_map/ppermute | solution.py:638
  78.3 5.1 %attend_late.1 = bf16[480,384]{1,0:T(8,128)(2,1)S(1)} custom-call(s32[9]{0:T(128)S(1)} %stack.40.ids, s32[32]{0:T(128)S(1)} %copy-done.4, s32[1]{0:T(128)S(6)} %copy.9.level, bf16[448,384]{1,0:T(8,128)(2,1)S(1)} %copy-done.2, bf16[448,768]{1,0:T(8,128)(2,1)S(1)} %collective-permute-done.6.refs_4_.refs_2_.refs_1_, ...), custom_call_target="tpu_custom_call" | custom-call | flops 1000000 | bytes 1000000 | tf_op jit(solution)/shard_map/attend_late/pallas_call | solution.py:324
  83.4 1.9 %collective-permute-start.14 = (bf16[480,384]{1,0:T(8,128)(2,1)S(1)}, bf16[480,384]{1,0:T(8,128)(2,1)S(1)}, u32[]{:S(2)}, u32[]{:S(2)}) collective-permute-start(bf16[480,384]{1,0:T(8,128)(2,1)S(1)} %attend_late.1), channel_id=1, source_target_pairs={{0,248},{8,0},{16,8},{24,16},{32,24},{40,32},{48,40},{56,48},{64,5... | collective-permute-start | bytes 1105928 | tf_op jit(solution)/shard_map/ppermute | solution.py:638
  85.4 0.9 stack.41.refs_5_
  86.3 0.0 copy-start.3
  86.3 0.0 copy-start.5
  86.3 0.1 collective-permute-start.21
  86.4 7.4 %collective-permute-done.16.three = bf16[480,384]{1,0:T(8,128)(2,1)S(1)} collective-permute-done((bf16[480,384]{1,0:T(8,128)(2,1)S(1)}, bf16[480,384]{1,0:T(8,128)(2,1)S(1)}, u32[]{:S(2)}, u32[]{:S(2)}) %collective-permute-start.16) | collective-permute-done | bytes 368672 | tf_op jit(solution)/shard_map/ppermute | solution.py:638
  93.9 1.9 %combine_later.1 = (f32[448,384]{1,0:T(8,128)S(1)}, f32[448,128]{1,0:T(8,128)S(1)}) custom-call(s32[9]{0:T(128)S(1)} %stack.40.ids, bf16[480,384]{1,0:T(8,128)(2,1)S(1)} %collective-permute-done.15.one, bf16[480,384]{1,0:T(8,128)(2,1)S(1)} %collective-permute-done.11.two, bf16[480,384]{1,0:T(8,128)(2,1)S(1)} %collective-permute-done.16.three), custom_call_target="tpu_custom_call" | custom-call | flops 99999997952 | bytes 200000000 | tf_op jit(solution)/shard_map/combine_later/pallas_call | solution.py:405
  95.8 1.7 %collective-permute-done.14.zero = bf16[480,384]{1,0:T(8,128)(2,1)S(1)} collective-permute-done((bf16[480,384]{1,0:T(8,128)(2,1)S(1)}, bf16[480,384]{1,0:T(8,128)(2,1)S(1)}, u32[]{:S(2)}, u32[]{:S(2)}) %collective-permute-start.14) | collective-permute-done | bytes 368672 | tf_op jit(solution)/shard_map/ppermute | solution.py:638
  97.5 1.2 combine.1
  98.7 1.2 collective-permute-start.20
  99.9 1.2 collective-permute-start.19
  101.1 0.3 collective-permute-start.17
  101.4 7.4 %collective-permute-done.20.refs_3_ = bf16[448,384]{1,0:T(8,128)(2,1)S(1)} collective-permute-done((bf16[448,384]{1,0:T(8,128)(2,1)S(1)}, bf16[448,384]{1,0:T(8,128)(2,1)S(1)}, u32[]{:S(2)}, u32[]{:S(2)}) %collective-permute-start.20) | collective-permute-done | bytes 344096 | tf_op jit(solution)/shard_map/ppermute | solution.py:573
  108.8 2.3 %collective-permute-done.19.refs_2_ = bf16[448,384]{1,0:T(8,128)(2,1)S(1)} collective-permute-done((bf16[448,384]{1,0:T(8,128)(2,1)S(1)}, bf16[448,384]{1,0:T(8,128)(2,1)S(1)}, u32[]{:S(2)}, u32[]{:S(2)}) %collective-permute-start.19) | collective-permute-done | bytes 344096 | tf_op jit(solution)/shard_map/ppermute | solution.py:573
  111.1 7.0 %collective-permute-done.18.refs_1_ = bf16[448,384]{1,0:T(8,128)(2,1)S(1)} collective-permute-done((bf16[448,384]{1,0:T(8,128)(2,1)S(1)}, bf16[448,384]{1,0:T(8,128)(2,1)S(1)}, u32[]{:S(2)}, u32[]{:S(2)}) %collective-permute-start.18) | collective-permute-done | bytes 344096 | tf_op jit(solution)/shard_map/ppermute | solution.py:573
  118.1 2.9 %project.3 = bf16[448,768]{1,0:T(8,128)(2,1)S(1)} custom-call(s32[9]{0:T(128)S(1)} %stack.40.ids, bf16[448,384]{1,0:T(8,128)(2,1)S(1)} %get-tuple-element.88.refs_0_, bf16[448,384]{1,0:T(8,128)(2,1)S(1)} %collective-permute-done.18.refs_1_, bf16[448,384]{1,0:T(8,128)(2,1)S(1)} %collective-permute-done.19.refs_2_, ...), custom_call_target="tpu_custom_call" | custom-call | flops 1056964608 | bytes 5000000 | tf_op jit(solution)/shard_map/project/pallas_call | solution.py:557
  121.0 0.4 collective-permute-start.22
  121.4 2.9 %project.2.near = f32[448,768]{1,0:T(8,128)S(1)} custom-call(s32[9]{0:T(128)S(1)} %stack.40.ids, bf16[448,384]{1,0:T(8,128)(2,1)S(1)} %get-tuple-element.88.refs_0_, bf16[448,384]{1,0:T(8,128)(2,1)S(1)} %collective-permute-done.18.refs_1_, bf16[448,384]{1,0:T(8,128)(2,1)S(1)} %collective-permute-done.19.refs_2_, ...), custom_call_target="tpu_custom_call" | custom-call | flops 1056964608 | bytes 5000000 | tf_op jit(solution)/shard_map/project/pallas_call | solution.py:557
  124.3 13.3 %collective-permute-done.22.arrived = bf16[448,768]{1,0:T(8,128)(2,1)S(1)} collective-permute-done((bf16[448,768]{1,0:T(8,128)(2,1)S(1)}, bf16[448,768]{1,0:T(8,128)(2,1)S(1)}, u32[]{:S(2)}, u32[]{:S(2)}) %collective-permute-start.22) | collective-permute-done | bytes 688160 | tf_op jit(solution)/shard_map/ppermute | solution.py:573
  137.7 1.6 %finish.1 = bf16[448,768]{1,0:T(8,128)(2,1)} custom-call(bf16[448,768]{1,0:T(8,128)(2,1)S(1)} %collective-permute-done.17.hidden, f32[448,768]{1,0:T(8,128)S(1)} %project.2.near, bf16[448,768]{1,0:T(8,128)(2,1)S(1)} %collective-permute-done.22.arrived, f32[1,768]{1,0:T(1,128)S(1)} %get-tuple-element.94.gate), custom_call_target="tpu_custom_call" | custom-call | tf_op jit(solution)/shard_map/finish/pallas_call | solution.py:463
  (23 shorter events, 0.1 us)
Async XLA Ops:
  2.0 23.7 %collective-permute-start.4 = (bf16[448,768]{1,0:T(8,128)(2,1)}, bf16[448,768]{1,0:T(8,128)(2,1)S(1)}, u32[]{:S(2)}, u32[]{:S(2)}) collective-permute-start(bf16[448,768]{1,0:T(8,128)(2,1)} %pack.1.refs_3_.refs_1_), channel_id=1, source_target_pairs={{0,8},{8,0},{1,9},{9,1},{2,10},{10,2},{3,11},{11,3},{4,12},{12,4},... | collective-permute-start | bytes 2064392 | tf_op jit(solution)/shard_map/ppermute | solution.py:573
  2.7 23.1 %collective-permute-start.3 = (bf16[448,768]{1,0:T(8,128)(2,1)}, bf16[448,768]{1,0:T(8,128)(2,1)S(1)}, u32[]{:S(2)}, u32[]{:S(2)}) collective-permute-start(bf16[448,768]{1,0:T(8,128)(2,1)} %pack.1.refs_3_.refs_1_), channel_id=1, source_target_pairs={{0,48},{16,0},{32,16},{48,32},{1,49},{17,1},{33,17},{49,33},{2,50}... | collective-permute-start | bytes 2064392 | tf_op jit(solution)/shard_map/ppermute | solution.py:573
  3.1 22.6 %collective-permute-start.2 = (bf16[448,768]{1,0:T(8,128)(2,1)}, bf16[448,768]{1,0:T(8,128)(2,1)S(1)}, u32[]{:S(2)}, u32[]{:S(2)}) collective-permute-start(bf16[448,768]{1,0:T(8,128)(2,1)} %pack.1.refs_3_.refs_1_), channel_id=1, source_target_pairs={{0,16},{16,32},{32,48},{48,0},{1,17},{17,33},{33,49},{49,1},{2,18}... | collective-permute-start | bytes 2064392 | tf_op jit(solution)/shard_map/ppermute | solution.py:573
  5.3 20.4 %collective-permute-start = (bf16[448,384]{1,0:T(8,128)(2,1)}, bf16[448,384]{1,0:T(8,128)(2,1)S(1)}, u32[]{:S(2)}, u32[]{:S(2)}) collective-permute-start(bf16[448,384]{1,0:T(8,128)(2,1)} %refs_0_.2), channel_id=1, source_target_pairs={{64,0},{128,64},{192,128},{65,1},{129,65},{193,129},{66,2},{130,66... | collective-permute-start | bytes 1032200 | tf_op jit(solution)/shard_map/ppermute | solution.py:591
  6.6 19.1 %collective-permute-start.1 = (bf16[448,384]{1,0:T(8,128)(2,1)}, bf16[448,384]{1,0:T(8,128)(2,1)S(1)}, u32[]{:S(2)}, u32[]{:S(2)}) collective-permute-start(bf16[448,384]{1,0:T(8,128)(2,1)} %refs_0_.2), channel_id=1, source_target_pairs={{192,0},{193,1},{194,2},{195,3},{196,4},{197,5},{198,6},{199,7},{2... | collective-permute-start | bytes 1032200 | tf_op jit(solution)/shard_map/ppermute | solution.py:591
  8.7 2.3 %copy-start = (bf16[384,6144]{1,0:T(8,128)(2,1)S(1)}, bf16[384,6144]{1,0:T(8,128)(2,1)}, u32[]{:S(2)}) copy-start(bf16[384,6144]{1,0:T(8,128)(2,1)} %refs_0_.1) | copy-start | bytes 14155780
  11.0 14.7 %copy-start.2 = (bf16[448,384]{1,0:T(8,128)(2,1)S(1)}, bf16[448,384]{1,0:T(8,128)(2,1)}, u32[]{:S(2)}) copy-start(bf16[448,384]{1,0:T(8,128)(2,1)} %refs_0_.2) | copy-start | bytes 1032196
  11.1 18.6 %copy-start.1 = (bf16[448,768]{1,0:T(8,128)(2,1)S(1)}, bf16[448,768]{1,0:T(8,128)(2,1)}, u32[]{:S(2)}) copy-start(bf16[448,768]{1,0:T(8,128)(2,1)} %pack.1.refs_3_.refs_1_) | copy-start | bytes 2064388
  11.1 20.0 %copy-start.4 = (s32[32]{0:T(128)S(1)}, s32[32]{0:T(128)}, u32[]{:S(2)}) copy-start(s32[32]{0:T(128)} %live.5) | copy-start | bytes 388
  25.8 21.1 %collective-permute-start.5 = (bf16[448,384]{1,0:T(8,128)(2,1)S(1)}, bf16[448,384]{1,0:T(8,128)(2,1)S(1)}, u32[]{:S(2)}, u32[]{:S(2)}) collective-permute-start(bf16[448,384]{1,0:T(8,128)(2,1)S(1)} %copy-done.2), channel_id=1, source_target_pairs={{128,0},{192,64},{129,1},{193,65},{130,2},{194,66},{131,3},{195,67... | collective-permute-start | bytes 1032200 | tf_op jit(solution)/shard_map/ppermute | solution.py:591
  27.1 19.8 %collective-permute-start.7 = (bf16[384,768]{1,0:T(8,128)(2,1)S(1)}, bf16[384,768]{1,0:T(8,128)(2,1)S(1)}, u32[]{:S(2)}, u32[]{:S(2)}) collective-permute-start(bf16[384,768]{1,0:T(8,128)(2,1)S(1)} %get-tuple-element.55), channel_id=1, source_target_pairs={{0,3},{1,0},{2,1},{3,2},{4,7},{5,4},{6,5},{7,6},{8,11},{9,8},{10,9... | collective-permute-start | bytes 1769480 | tf_op jit(solution)/shard_map/ppermute | solution.py:573
  29.6 17.2 %collective-permute-start.6 = (bf16[448,768]{1,0:T(8,128)(2,1)S(1)}, bf16[448,768]{1,0:T(8,128)(2,1)S(1)}, u32[]{:S(2)}, u32[]{:S(2)}) collective-permute-start(bf16[448,768]{1,0:T(8,128)(2,1)S(1)} %copy-done.1), channel_id=1, source_target_pairs={{0,32},{16,48},{32,0},{48,16},{1,33},{17,49},{33,1},{49,17},{2,34}... | collective-permute-start | bytes 2064392 | tf_op jit(solution)/shard_map/ppermute | solution.py:573
  29.6 17.3 %collective-permute-start.8 = (bf16[448,768]{1,0:T(8,128)(2,1)S(1)}, bf16[448,768]{1,0:T(8,128)(2,1)S(1)}, u32[]{:S(2)}, u32[]{:S(2)}) collective-permute-start(bf16[448,768]{1,0:T(8,128)(2,1)S(1)} %collective-permute-done.2.refs_4_.refs_2_), channel_id=1, source_target_pairs={{0,8},{8,0},{1,9},{9,1},{2,10},{10,2},{3,11},{11,3},{4,12},{12,4},... | collective-permute-start | bytes 2064392 | tf_op jit(solution)/shard_map/ppermute | solution.py:573
  31.0 15.9 %collective-permute-start.9 = (bf16[448,768]{1,0:T(8,128)(2,1)S(1)}, bf16[448,768]{1,0:T(8,128)(2,1)S(1)}, u32[]{:S(2)}, u32[]{:S(2)}) collective-permute-start(bf16[448,768]{1,0:T(8,128)(2,1)S(1)} %collective-permute-done.3.refs_5_.refs_3_), channel_id=1, source_target_pairs={{0,8},{8,0},{1,9},{9,1},{2,10},{10,2},{3,11},{11,3},{4,12},{12,4},... | collective-permute-start | bytes 2064392 | tf_op jit(solution)/shard_map/ppermute | solution.py:573
  46.9 3.9 %collective-permute-start.10 = (bf16[448,768]{1,0:T(8,128)(2,1)S(1)}, bf16[448,768]{1,0:T(8,128)(2,1)S(1)}, u32[]{:S(2)}, u32[]{:S(2)}) collective-permute-start(bf16[448,768]{1,0:T(8,128)(2,1)S(1)} %collective-permute-done.6.refs_4_.refs_2_.refs_1_), channel_id=1, source_target_pairs={{0,8},{8,0},{1,9},{9,1},{2,10},{10,2},{3,11},{11,3},{4,12},{12,4},... | collective-permute-start | bytes 2064392 | tf_op jit(solution)/shard_map/ppermute | solution.py:573
  49.0 34.4 %collective-permute-start.12 = (bf16[384,768]{1,0:T(8,128)(2,1)S(1)}, bf16[384,768]{1,0:T(8,128)(2,1)S(1)}, u32[]{:S(2)}, u32[]{:S(2)}) collective-permute-start(bf16[384,768]{1,0:T(8,128)(2,1)S(1)} %get-tuple-element.78), channel_id=1, source_target_pairs={{0,1},{1,2},{2,3},{3,0},{4,5},{5,6},{6,7},{7,4},{8,9},{9,10},{10,1... | collective-permute-start | bytes 1769480 | tf_op jit(solution)/shard_map/ppermute | solution.py:573
  49.0 34.4 %collective-permute-start.13 = (bf16[384,768]{1,0:T(8,128)(2,1)S(1)}, bf16[384,768]{1,0:T(8,128)(2,1)S(1)}, u32[]{:S(2)}, u32[]{:S(2)}) collective-permute-start(bf16[384,768]{1,0:T(8,128)(2,1)S(1)} %get-tuple-element.79), channel_id=1, source_target_pairs={{0,2},{1,3},{2,0},{3,1},{4,6},{5,7},{6,4},{7,5},{8,10},{9,11},{10,... | collective-permute-start | bytes 1769480 | tf_op jit(solution)/shard_map/ppermute | solution.py:573
  60.4 23.0 %collective-permute-start.11 = (bf16[480,384]{1,0:T(8,128)(2,1)S(1)}, bf16[480,384]{1,0:T(8,128)(2,1)S(1)}, u32[]{:S(2)}, u32[]{:S(2)}) collective-permute-start(bf16[480,384]{1,0:T(8,128)(2,1)S(1)} %attend_third.1), channel_id=1, source_target_pairs={{0,120},{8,128},{16,136},{24,144},{32,152},{40,160},{48,168},{56,1... | collective-permute-start | bytes 1105928 | tf_op jit(solution)/shard_map/ppermute | solution.py:638
  70.2 23.7 %collective-permute-start.16 = (bf16[480,384]{1,0:T(8,128)(2,1)S(1)}, bf16[480,384]{1,0:T(8,128)(2,1)S(1)}, u32[]{:S(2)}, u32[]{:S(2)}) collective-permute-start(bf16[480,384]{1,0:T(8,128)(2,1)S(1)} %get-tuple-element.82), channel_id=1, source_target_pairs={{0,184},{8,192},{16,200},{24,208},{32,216},{40,224},{48,232},{56,2... | collective-permute-start | bytes 1105928 | tf_op jit(solution)/shard_map/ppermute | solution.py:638
  71.5 22.4 %collective-permute-start.15 = (bf16[480,384]{1,0:T(8,128)(2,1)S(1)}, bf16[480,384]{1,0:T(8,128)(2,1)S(1)}, u32[]{:S(2)}, u32[]{:S(2)}) collective-permute-start(bf16[480,384]{1,0:T(8,128)(2,1)S(1)} %get-tuple-element.74), channel_id=1, source_target_pairs={{0,56},{8,64},{16,72},{24,80},{32,88},{40,96},{48,104},{56,112},{6... | collective-permute-start | bytes 1105928 | tf_op jit(solution)/shard_map/ppermute | solution.py:638
  83.4 14.0 %collective-permute-start.14 = (bf16[480,384]{1,0:T(8,128)(2,1)S(1)}, bf16[480,384]{1,0:T(8,128)(2,1)S(1)}, u32[]{:S(2)}, u32[]{:S(2)}) collective-permute-start(bf16[480,384]{1,0:T(8,128)(2,1)S(1)} %attend_late.1), channel_id=1, source_target_pairs={{0,248},{8,0},{16,8},{24,16},{32,24},{40,32},{48,40},{56,48},{64,5... | collective-permute-start | bytes 1105928 | tf_op jit(solution)/shard_map/ppermute | solution.py:638
  86.3 11.1 %copy-start.3 = (f32[64,768]{1,0:T(8,128)S(1)}, f32[64,768]{1,0:T(8,128)}, u32[]{:S(2)}) copy-start(f32[64,768]{1,0:T(8,128)} %table.1) | copy-start | bytes 589828
  86.3 14.8 %copy-start.5 = (bf16[448,768]{1,0:T(8,128)(2,1)S(1)}, bf16[448,768]{1,0:T(8,128)(2,1)}, u32[]{:S(2)}) copy-start(bf16[448,768]{1,0:T(8,128)(2,1)} %param.8) | copy-start | bytes 2064388
  86.3 31.8 %collective-permute-start.21 = (bf16[3,384,768]{2,1,0:T(8,128)(2,1)S(1)}, bf16[3,384,768]{2,1,0:T(8,128)(2,1)S(1)}, u32[]{:S(2)}, u32[]{:S(2)}) collective-permute-start(bf16[3,384,768]{2,1,0:T(8,128)(2,1)S(1)} %stack.41.refs_5_), channel_id=1, source_target_pairs={{0,8},{8,0},{1,9},{9,1},{2,10},{10,2},{3,11},{11,3},{4,12},{12,4},... | collective-permute-start | bytes 5308424 | tf_op jit(solution)/shard_map/ppermute | solution.py:573
  98.7 10.1 %collective-permute-start.20 = (bf16[448,384]{1,0:T(8,128)(2,1)S(1)}, bf16[448,384]{1,0:T(8,128)(2,1)S(1)}, u32[]{:S(2)}, u32[]{:S(2)}) collective-permute-start(bf16[448,384]{1,0:T(8,128)(2,1)S(1)} %get-tuple-element.88.refs_0_), channel_id=1, source_target_pairs={{0,3},{1,0},{2,1},{3,2},{4,7},{5,4},{6,5},{7,6},{8,11},{9,8},{10,9... | collective-permute-start | bytes 1032200 | tf_op jit(solution)/shard_map/ppermute | solution.py:573
  99.9 11.3 %collective-permute-start.19 = (bf16[448,384]{1,0:T(8,128)(2,1)S(1)}, bf16[448,384]{1,0:T(8,128)(2,1)S(1)}, u32[]{:S(2)}, u32[]{:S(2)}) collective-permute-start(bf16[448,384]{1,0:T(8,128)(2,1)S(1)} %get-tuple-element.88.refs_0_), channel_id=1, source_target_pairs={{0,2},{1,3},{2,0},{3,1},{4,6},{5,7},{6,4},{7,5},{8,10},{9,11},{10,... | collective-permute-start | bytes 1032200 | tf_op jit(solution)/shard_map/ppermute | solution.py:573
  101.1 17.0 %collective-permute-start.18 = (bf16[448,384]{1,0:T(8,128)(2,1)S(1)}, bf16[448,384]{1,0:T(8,128)(2,1)S(1)}, u32[]{:S(2)}, u32[]{:S(2)}) collective-permute-start(bf16[448,384]{1,0:T(8,128)(2,1)S(1)} %get-tuple-element.88.refs_0_), channel_id=1, source_target_pairs={{0,1},{1,2},{2,3},{3,0},{4,5},{5,6},{6,7},{7,4},{8,9},{9,10},{10,1... | collective-permute-start | bytes 1032200 | tf_op jit(solution)/shard_map/ppermute | solution.py:573
  101.1 23.2 %collective-permute-start.17 = (bf16[448,768]{1,0:T(8,128)(2,1)S(1)}, bf16[448,768]{1,0:T(8,128)(2,1)S(1)}, u32[]{:S(2)}, u32[]{:S(2)}) collective-permute-start(bf16[448,768]{1,0:T(8,128)(2,1)S(1)} %copy-done.5), channel_id=1, source_target_pairs={{0,248},{8,0},{16,8},{24,16},{32,24},{40,32},{48,40},{56,48},{64,5... | collective-permute-start | bytes 2064392 | tf_op jit(solution)/shard_map/ppermute | solution.py:573
  121.0 16.6 %collective-permute-start.22 = (bf16[448,768]{1,0:T(8,128)(2,1)S(1)}, bf16[448,768]{1,0:T(8,128)(2,1)S(1)}, u32[]{:S(2)}, u32[]{:S(2)}) collective-permute-start(bf16[448,768]{1,0:T(8,128)(2,1)S(1)} %project.3), channel_id=1, source_target_pairs={{0,4},{4,0},{1,5},{5,1},{2,6},{6,2},{3,7},{7,3},{8,12},{12,8},{9,1... | collective-permute-start | bytes 2064392 | tf_op jit(solution)/shard_map/ppermute | solution.py:573

commit v10 on v8

--- a/solution.py
+++ b/solution.py
@@ -231,9 +231,8 @@
             sweep(0, ROWS, n_live, lambda k: k, waits, True)
 
     def run():
-        if resumed:
-            for copy in state_copies():
-                copy.start()
+        for i in range(many):
+            pl.when(active(i))(raw_copy(i).start)
         for j, p in enumerate(members):
             if early and p == 0:
                 place_copy(j, own_place).start()
@@ -243,8 +242,11 @@
             def _():
                 place_copy(j, live_before(groups[p])).start()
 
+        if resumed:
+            for copy in state_copies():
+                copy.start()
         for i in range(many):
-            pl.when(active(i))(raw_copy(i).start)
+            pl.when(active(i))(functools.partial(prepare, i))
         if early:
             place_copy(0, own_place).wait()
             for k in range(len(EARLY)):
@@ -253,8 +255,6 @@
                 def _():
                     place_copy(0, k).wait()
 
-        for i in range(many):
-            pl.when(active(i))(functools.partial(prepare, i))
         if resumed:
             for copy in state_copies():
                 copy.wait()

time: 143 us -> 142 us (level); the launches traced: 141 us -> 143 us
  Pallas kernels: 59.7 us -> 62.2 us
    pallas_call x4, Pallas kernels: 45.6 us -> 48.1 us  [attend(): pl.pallas_call(functools.partial(attend_kernel, call), out_shape=out_shap...]
  transfers between devices with their start and end apart: 23 -> 23, of which waited for: 9 -> 9; matrix products, arithmetic and copies ran while one was open for 0% -> 0% of each run, Pallas kernels for 40% -> 41%
where the time goes in v10:
time: 142 us; the launch traced here: 143 us
  Pallas kernels  62.2 us (44%)
  waiting for transfers between devices  52.4 us (37%)
  starting transfers between devices  25.1 us (18%)
  local copies, waits for them, and re-layouts  2.45 us (2%)
    pallas_call x4, Pallas kernels, attend(): pl.pallas_call(functools.partial(attend_kernel, call), out_shape=out_shap...  48.1 us
    ppermute x16, waiting for transfers between devices, around(): lax.ppermute(value, axis, [(i, (i + steps) % count) for i in range(count)])  31.5 us
    ppermute x16, starting transfers between devices, around(): lax.ppermute(value, axis, [(i, (i + steps) % count) for i in range(count)])  16.6 us
    ppermute x3, waiting for transfers between devices, to_level(): return lax.ppermute(value, 'z', [(i, i - d) for i in range(d, 4)])  13.8 us
    ppermute x4, waiting for transfers between devices, back(): return lax.ppermute(share, SLOT, pairs_back)  7.1 us
    pallas_call x2, Pallas kernels, project(): pl.pallas_call(functools.partial(project_kernel, far), out_shape=jax.Shap...  5.61 us
    ppermute x4, starting transfers between devices, back(): return lax.ppermute(share, SLOT, pairs_back)  4.63 us
    ppermute x3, starting transfers between devices, to_level(): return lax.ppermute(value, 'z', [(i, i - d) for i in range(d, 4)])  3.86 us
  transfers between devices with their start and end apart: 23, of which 9 were waited for; matrix products, arithmetic and copies ran while one was open for 0% of the time, Pallas kernels for 41%

profile of v10, /device:TPU:25, one launch (start us, length us, event | category | flops | bytes accessed | tf_op | source)
XLA Modules:
  0.0 143.0 jit_solution(8631270984903596578)
XLA Ops:
  0.0 2.0 %pack.1.refs_3_.refs_1_ = bf16[448,768]{1,0:T(8,128)(2,1)} custom-call(bf16[448,384]{1,0:T(8,128)(2,1)} %keys.1, bf16[448,384]{1,0:T(8,128)(2,1)} %values.1), custom_call_target="tpu_custom_call" | custom-call | tf_op jit(solution)/shard_map/pack/pallas_call | solution.py:481
  2.0 0.7 collective-permute-start.4
  2.7 0.5 collective-permute-start.3
  3.1 2.2 %collective-permute-start.2 = (bf16[448,768]{1,0:T(8,128)(2,1)}, bf16[448,768]{1,0:T(8,128)(2,1)S(1)}, u32[]{:S(2)}, u32[]{:S(2)}) collective-permute-start(bf16[448,768]{1,0:T(8,128)(2,1)} %pack.1.refs_3_.refs_1_), channel_id=1, source_target_pairs={{0,16},{16,32},{32,48},{48,0},{1,17},{17,33},{33,49},{49,1},{2,18}... | collective-permute-start | bytes 2064392 | tf_op jit(solution)/shard_map/ppermute | solution.py:569
  5.3 1.3 collective-permute-start
  6.6 1.3 collective-permute-start.1
  8.6 0.1 stack.40.ids
  8.7 2.3 %copy-done = bf16[384,6144]{1,0:T(8,128)(2,1)S(1)} copy-done((bf16[384,6144]{1,0:T(8,128)(2,1)S(1)}, bf16[384,6144]{1,0:T(8,128)(2,1)}, u32[]{:S(2)}) %copy-start) | copy-done | bytes 4718616
  11.1 0.9 columns.1
  12.0 13.8 %collective-permute-done.refs_0_ = bf16[448,384]{1,0:T(8,128)(2,1)S(1)} collective-permute-done((bf16[448,384]{1,0:T(8,128)(2,1)}, bf16[448,384]{1,0:T(8,128)(2,1)S(1)}, u32[]{:S(2)}, u32[]{:S(2)}) %collective-permute-start) | collective-permute-done | bytes 344096 | tf_op jit(solution)/shard_map/ppermute | solution.py:587
  25.7 0.0 collective-permute-done.1.refs_1_
  25.8 1.3 collective-permute-start.5
  27.1 1.3 collective-permute-start.7
  28.3 1.5 %collective-permute-start.8 = (bf16[384,768]{1,0:T(8,128)(2,1)S(1)}, bf16[384,768]{1,0:T(8,128)(2,1)S(1)}, u32[]{:S(2)}, u32[]{:S(2)}) collective-permute-start(bf16[384,768]{1,0:T(8,128)(2,1)S(1)} %get-tuple-element.55), channel_id=1, source_target_pairs={{0,3},{1,0},{2,1},{3,2},{4,7},{5,4},{6,5},{7,6},{8,11},{9,8},{10,9... | collective-permute-start | bytes 1769480 | tf_op jit(solution)/shard_map/ppermute | solution.py:569
  29.8 0.0 collective-permute-start.6
  29.8 1.7 %collective-permute-start.9 = (bf16[448,768]{1,0:T(8,128)(2,1)S(1)}, bf16[448,768]{1,0:T(8,128)(2,1)S(1)}, u32[]{:S(2)}, u32[]{:S(2)}) collective-permute-start(bf16[448,768]{1,0:T(8,128)(2,1)S(1)} %collective-permute-done.2.refs_4_.refs_2_), channel_id=1, source_target_pairs={{0,8},{8,0},{1,9},{9,1},{2,10},{10,2},{3,11},{11,3},{4,12},{12,4},... | collective-permute-start | bytes 2064392 | tf_op jit(solution)/shard_map/ppermute | solution.py:569
  31.5 15.5 %attend_early.1 = (f32[3,896,256]{2,1,0:T(8,128)S(1)}, f32[3,896,128]{2,1,0:T(8,128)S(1)}, f32[3,448,256]{2,1,0:T(8,128)S(1)}, f32[3,448,128]{2,1,0:T(8,128)S(1)}) custom-call(s32[9]{0:T(128)S(1)} %stack.40.ids, s32[32]{0:T(128)S(1)} %copy-done.4, s32[1]{0:T(128)S(6)} %copy.9.level, bf16[448,384]{1,0:T(8,128)(2,1)S(1)} %collective-permute-done.refs_0_, ...), custom_call_target="tpu_custom_call" | custom-call | flops 10000000000 | bytes 1000000 | tf_op jit(solution)/shard_map/attend_early/pallas_call | solution.py:324
  47.0 2.2 %collective-permute-start.10 = (bf16[448,768]{1,0:T(8,128)(2,1)S(1)}, bf16[448,768]{1,0:T(8,128)(2,1)S(1)}, u32[]{:S(2)}, u32[]{:S(2)}) collective-permute-start(bf16[448,768]{1,0:T(8,128)(2,1)S(1)} %collective-permute-done.3.refs_5_.refs_3_), channel_id=1, source_target_pairs={{0,8},{8,0},{1,9},{9,1},{2,10},{10,2},{3,11},{11,3},{4,12},{12,4},... | collective-permute-start | bytes 2064392 | tf_op jit(solution)/shard_map/ppermute | solution.py:569
  49.2 0.0 collective-permute-start.11
  49.2 1.5 %collective-permute-start.13 = (bf16[384,768]{1,0:T(8,128)(2,1)S(1)}, bf16[384,768]{1,0:T(8,128)(2,1)S(1)}, u32[]{:S(2)}, u32[]{:S(2)}) collective-permute-start(bf16[384,768]{1,0:T(8,128)(2,1)S(1)} %get-tuple-element.77), channel_id=1, source_target_pairs={{0,2},{1,3},{2,0},{3,1},{4,6},{5,7},{6,4},{7,5},{8,10},{9,11},{10,... | collective-permute-start | bytes 1769480 | tf_op jit(solution)/shard_map/ppermute | solution.py:569
  50.7 0.2 collective-permute-done.10.refs_7_.refs_4_.refs_3_
  50.9 1.0 collective-permute-done.11.refs_8_.refs_5_.refs_4_
  51.9 12.0 %attend_third.1 = bf16[480,384]{1,0:T(8,128)(2,1)S(1)} custom-call(s32[9]{0:T(128)S(1)} %stack.40.ids, s32[32]{0:T(128)S(1)} %copy-done.4, s32[1]{0:T(128)S(6)} %copy.9.level, bf16[448,384]{1,0:T(8,128)(2,1)S(1)} %collective-permute-done.5.refs_0_, bf16[448,768]{1,0:T(8,128)(2,1)S(1)} %copy-done.1, ...), custom_call_target="tpu_custom_call" | custom-call | flops 10000000000 | bytes 1000000 | tf_op jit(solution)/shard_map/attend_third/pallas_call | solution.py:324
  63.9 1.3 collective-permute-start.12
  65.2 13.1 %attend_middle.1 = (bf16[480,384]{1,0:T(8,128)(2,1)S(1)}, bf16[480,384]{1,0:T(8,128)(2,1)S(1)}) custom-call(s32[9]{0:T(128)S(1)} %stack.40.ids, s32[32]{0:T(128)S(1)} %copy-done.4, s32[1]{0:T(128)S(6)} %copy.9.level, bf16[448,384]{1,0:T(8,128)(2,1)S(1)} %collective-permute-done.refs_0_, bf16[448,384]{1,0:T(8,128)(2,1)S(1)} %collective-permute-done.1.refs_1_, ...), custom_call_target="tpu_custom_call" | custom-call | flops 49999998976 | bytes 1000000 | tf_op jit(solution)/shard_map/attend_middle/pallas_call | solution.py:324
  78.4 1.3 collective-permute-start.16
  79.7 1.9 %collective-permute-start.15 = (bf16[480,384]{1,0:T(8,128)(2,1)S(1)}, bf16[480,384]{1,0:T(8,128)(2,1)S(1)}, u32[]{:S(2)}, u32[]{:S(2)}) collective-permute-start(bf16[480,384]{1,0:T(8,128)(2,1)S(1)} %get-tuple-element.73), channel_id=1, source_target_pairs={{0,56},{8,64},{16,72},{24,80},{32,88},{40,96},{48,104},{56,112},{6... | collective-permute-start | bytes 1105928 | tf_op jit(solution)/shard_map/ppermute | solution.py:634
  81.6 7.5 %attend_late.1 = bf16[480,384]{1,0:T(8,128)(2,1)S(1)} custom-call(s32[9]{0:T(128)S(1)} %stack.40.ids, s32[32]{0:T(128)S(1)} %copy-done.4, s32[1]{0:T(128)S(6)} %copy.9.level, bf16[448,384]{1,0:T(8,128)(2,1)S(1)} %copy-done.2, bf16[448,768]{1,0:T(8,128)(2,1)S(1)} %collective-permute-done.6.refs_4_.refs_2_.refs_1_, ...), custom_call_target="tpu_custom_call" | custom-call | flops 1000000 | bytes 1000000 | tf_op jit(solution)/shard_map/attend_late/pallas_call | solution.py:324
  89.2 0.1 collective-permute-start.14
  89.3 0.9 stack.41.refs_5_
  90.2 0.0 copy-start.3
  90.2 0.0 copy-start.5
  90.2 0.1 collective-permute-start.21
  90.3 5.3 %collective-permute-done.16.three = bf16[480,384]{1,0:T(8,128)(2,1)S(1)} collective-permute-done((bf16[480,384]{1,0:T(8,128)(2,1)S(1)}, bf16[480,384]{1,0:T(8,128)(2,1)S(1)}, u32[]{:S(2)}, u32[]{:S(2)}) %collective-permute-start.16) | collective-permute-done | bytes 368672 | tf_op jit(solution)/shard_map/ppermute | solution.py:634
  95.7 1.9 %combine_later.1 = (f32[448,384]{1,0:T(8,128)S(1)}, f32[448,128]{1,0:T(8,128)S(1)}) custom-call(s32[9]{0:T(128)S(1)} %stack.40.ids, bf16[480,384]{1,0:T(8,128)(2,1)S(1)} %collective-permute-done.15.one, bf16[480,384]{1,0:T(8,128)(2,1)S(1)} %collective-permute-done.12.two, bf16[480,384]{1,0:T(8,128)(2,1)S(1)} %collective-permute-done.16.three), custom_call_target="tpu_custom_call" | custom-call | flops 99999997952 | bytes 200000000 | tf_op jit(solution)/shard_map/combine_later/pallas_call | solution.py:405
  97.6 1.7 %collective-permute-done.14.zero = bf16[480,384]{1,0:T(8,128)(2,1)S(1)} collective-permute-done((bf16[480,384]{1,0:T(8,128)(2,1)S(1)}, bf16[480,384]{1,0:T(8,128)(2,1)S(1)}, u32[]{:S(2)}, u32[]{:S(2)}) %collective-permute-start.14) | collective-permute-done | bytes 368672 | tf_op jit(solution)/shard_map/ppermute | solution.py:634
  99.3 1.2 combine.1
  100.5 1.3 collective-permute-start.20
  101.9 0.5 collective-permute-start.19
  102.4 0.6 collective-permute-start.18
  103.0 7.6 %collective-permute-done.20.refs_3_ = bf16[448,384]{1,0:T(8,128)(2,1)S(1)} collective-permute-done((bf16[448,384]{1,0:T(8,128)(2,1)S(1)}, bf16[448,384]{1,0:T(8,128)(2,1)S(1)}, u32[]{:S(2)}, u32[]{:S(2)}) %collective-permute-start.20) | collective-permute-done | bytes 344096 | tf_op jit(solution)/shard_map/ppermute | solution.py:569
  110.6 2.6 %collective-permute-done.19.refs_2_ = bf16[448,384]{1,0:T(8,128)(2,1)S(1)} collective-permute-done((bf16[448,384]{1,0:T(8,128)(2,1)S(1)}, bf16[448,384]{1,0:T(8,128)(2,1)S(1)}, u32[]{:S(2)}, u32[]{:S(2)}) %collective-permute-start.19) | collective-permute-done | bytes 344096 | tf_op jit(solution)/shard_map/ppermute | solution.py:569
  113.2 7.3 %collective-permute-done.18.refs_1_ = bf16[448,384]{1,0:T(8,128)(2,1)S(1)} collective-permute-done((bf16[448,384]{1,0:T(8,128)(2,1)S(1)}, bf16[448,384]{1,0:T(8,128)(2,1)S(1)}, u32[]{:S(2)}, u32[]{:S(2)}) %collective-permute-start.18) | collective-permute-done | bytes 344096 | tf_op jit(solution)/shard_map/ppermute | solution.py:569
  120.5 2.8 %project.3 = bf16[448,768]{1,0:T(8,128)(2,1)S(1)} custom-call(s32[9]{0:T(128)S(1)} %stack.40.ids, bf16[448,384]{1,0:T(8,128)(2,1)S(1)} %get-tuple-element.86.refs_0_, bf16[448,384]{1,0:T(8,128)(2,1)S(1)} %collective-permute-done.18.refs_1_, bf16[448,384]{1,0:T(8,128)(2,1)S(1)} %collective-permute-done.19.refs_2_, ...), custom_call_target="tpu_custom_call" | custom-call | flops 1056964608 | bytes 5000000 | tf_op jit(solution)/shard_map/project/pallas_call | solution.py:553
  123.3 2.5 %collective-permute-start.22 = (bf16[448,768]{1,0:T(8,128)(2,1)S(1)}, bf16[448,768]{1,0:T(8,128)(2,1)S(1)}, u32[]{:S(2)}, u32[]{:S(2)}) collective-permute-start(bf16[448,768]{1,0:T(8,128)(2,1)S(1)} %project.3), channel_id=1, source_target_pairs={{0,4},{4,0},{1,5},{5,1},{2,6},{6,2},{3,7},{7,3},{8,12},{12,8},{9,1... | collective-permute-start | bytes 2064392 | tf_op jit(solution)/shard_map/ppermute | solution.py:569
  125.9 2.8 %project.2.near = f32[448,768]{1,0:T(8,128)S(1)} custom-call(s32[9]{0:T(128)S(1)} %stack.40.ids, bf16[448,384]{1,0:T(8,128)(2,1)S(1)} %get-tuple-element.86.refs_0_, bf16[448,384]{1,0:T(8,128)(2,1)S(1)} %collective-permute-done.18.refs_1_, bf16[448,384]{1,0:T(8,128)(2,1)S(1)} %collective-permute-done.19.refs_2_, ...), custom_call_target="tpu_custom_call" | custom-call | flops 1056964608 | bytes 5000000 | tf_op jit(solution)/shard_map/project/pallas_call | solution.py:553
  128.7 12.8 %collective-permute-done.22.arrived = bf16[448,768]{1,0:T(8,128)(2,1)S(1)} collective-permute-done((bf16[448,768]{1,0:T(8,128)(2,1)S(1)}, bf16[448,768]{1,0:T(8,128)(2,1)S(1)}, u32[]{:S(2)}, u32[]{:S(2)}) %collective-permute-start.22) | collective-permute-done | bytes 688160 | tf_op jit(solution)/shard_map/ppermute | solution.py:569
  141.5 1.6 %finish.1 = bf16[448,768]{1,0:T(8,128)(2,1)} custom-call(bf16[448,768]{1,0:T(8,128)(2,1)S(1)} %collective-permute-done.17.hidden, f32[448,768]{1,0:T(8,128)S(1)} %project.2.near, bf16[448,768]{1,0:T(8,128)(2,1)S(1)} %collective-permute-done.22.arrived, f32[1,768]{1,0:T(1,128)S(1)} %get-tuple-element.92.gate), custom_call_target="tpu_custom_call" | custom-call | tf_op jit(solution)/shard_map/finish/pallas_call | solution.py:463
  (23 shorter events, 0.1 us)
Async XLA Ops:
  2.0 23.7 %collective-permute-start.4 = (bf16[448,768]{1,0:T(8,128)(2,1)}, bf16[448,768]{1,0:T(8,128)(2,1)S(1)}, u32[]{:S(2)}, u32[]{:S(2)}) collective-permute-start(bf16[448,768]{1,0:T(8,128)(2,1)} %pack.1.refs_3_.refs_1_), channel_id=1, source_target_pairs={{0,8},{8,0},{1,9},{9,1},{2,10},{10,2},{3,11},{11,3},{4,12},{12,4},... | collective-permute-start | bytes 2064392 | tf_op jit(solution)/shard_map/ppermute | solution.py:569
  2.7 23.1 %collective-permute-start.3 = (bf16[448,768]{1,0:T(8,128)(2,1)}, bf16[448,768]{1,0:T(8,128)(2,1)S(1)}, u32[]{:S(2)}, u32[]{:S(2)}) collective-permute-start(bf16[448,768]{1,0:T(8,128)(2,1)} %pack.1.refs_3_.refs_1_), channel_id=1, source_target_pairs={{0,48},{16,0},{32,16},{48,32},{1,49},{17,1},{33,17},{49,33},{2,50}... | collective-permute-start | bytes 2064392 | tf_op jit(solution)/shard_map/ppermute | solution.py:569
  3.1 22.6 %collective-permute-start.2 = (bf16[448,768]{1,0:T(8,128)(2,1)}, bf16[448,768]{1,0:T(8,128)(2,1)S(1)}, u32[]{:S(2)}, u32[]{:S(2)}) collective-permute-start(bf16[448,768]{1,0:T(8,128)(2,1)} %pack.1.refs_3_.refs_1_), channel_id=1, source_target_pairs={{0,16},{16,32},{32,48},{48,0},{1,17},{17,33},{33,49},{49,1},{2,18}... | collective-permute-start | bytes 2064392 | tf_op jit(solution)/shard_map/ppermute | solution.py:569
  5.3 20.4 %collective-permute-start = (bf16[448,384]{1,0:T(8,128)(2,1)}, bf16[448,384]{1,0:T(8,128)(2,1)S(1)}, u32[]{:S(2)}, u32[]{:S(2)}) collective-permute-start(bf16[448,384]{1,0:T(8,128)(2,1)} %refs_0_.2), channel_id=1, source_target_pairs={{64,0},{128,64},{192,128},{65,1},{129,65},{193,129},{66,2},{130,66... | collective-permute-start | bytes 1032200 | tf_op jit(solution)/shard_map/ppermute | solution.py:587
  6.6 19.1 %collective-permute-start.1 = (bf16[448,384]{1,0:T(8,128)(2,1)}, bf16[448,384]{1,0:T(8,128)(2,1)S(1)}, u32[]{:S(2)}, u32[]{:S(2)}) collective-permute-start(bf16[448,384]{1,0:T(8,128)(2,1)} %refs_0_.2), channel_id=1, source_target_pairs={{192,0},{193,1},{194,2},{195,3},{196,4},{197,5},{198,6},{199,7},{2... | collective-permute-start | bytes 1032200 | tf_op jit(solution)/shard_map/ppermute | solution.py:587
  8.7 2.3 %copy-start = (bf16[384,6144]{1,0:T(8,128)(2,1)S(1)}, bf16[384,6144]{1,0:T(8,128)(2,1)}, u32[]{:S(2)}) copy-start(bf16[384,6144]{1,0:T(8,128)(2,1)} %refs_0_.1) | copy-start | bytes 14155780
  11.0 14.7 %copy-start.2 = (bf16[448,384]{1,0:T(8,128)(2,1)S(1)}, bf16[448,384]{1,0:T(8,128)(2,1)}, u32[]{:S(2)}) copy-start(bf16[448,384]{1,0:T(8,128)(2,1)} %refs_0_.2) | copy-start | bytes 1032196
  11.1 18.8 %copy-start.1 = (bf16[448,768]{1,0:T(8,128)(2,1)S(1)}, bf16[448,768]{1,0:T(8,128)(2,1)}, u32[]{:S(2)}) copy-start(bf16[448,768]{1,0:T(8,128)(2,1)} %pack.1.refs_3_.refs_1_) | copy-start | bytes 2064388
  11.1 20.4 %copy-start.4 = (s32[32]{0:T(128)S(1)}, s32[32]{0:T(128)}, u32[]{:S(2)}) copy-start(s32[32]{0:T(128)} %live.5) | copy-start | bytes 388
  25.8 21.2 %collective-permute-start.5 = (bf16[448,384]{1,0:T(8,128)(2,1)S(1)}, bf16[448,384]{1,0:T(8,128)(2,1)S(1)}, u32[]{:S(2)}, u32[]{:S(2)}) collective-permute-start(bf16[448,384]{1,0:T(8,128)(2,1)S(1)} %copy-done.2), channel_id=1, source_target_pairs={{128,0},{192,64},{129,1},{193,65},{130,2},{194,66},{131,3},{195,67... | collective-permute-start | bytes 1032200 | tf_op jit(solution)/shard_map/ppermute | solution.py:587
  27.1 19.9 %collective-permute-start.7 = (bf16[384,768]{1,0:T(8,128)(2,1)S(1)}, bf16[384,768]{1,0:T(8,128)(2,1)S(1)}, u32[]{:S(2)}, u32[]{:S(2)}) collective-permute-start(bf16[384,768]{1,0:T(8,128)(2,1)S(1)} %get-tuple-element.54), channel_id=1, source_target_pairs={{0,1},{1,2},{2,3},{3,0},{4,5},{5,6},{6,7},{7,4},{8,9},{9,10},{10,1... | collective-permute-start | bytes 1769480 | tf_op jit(solution)/shard_map/ppermute | solution.py:569
  28.3 18.6 %collective-permute-start.8 = (bf16[384,768]{1,0:T(8,128)(2,1)S(1)}, bf16[384,768]{1,0:T(8,128)(2,1)S(1)}, u32[]{:S(2)}, u32[]{:S(2)}) collective-permute-start(bf16[384,768]{1,0:T(8,128)(2,1)S(1)} %get-tuple-element.55), channel_id=1, source_target_pairs={{0,3},{1,0},{2,1},{3,2},{4,7},{5,4},{6,5},{7,6},{8,11},{9,8},{10,9... | collective-permute-start | bytes 1769480 | tf_op jit(solution)/shard_map/ppermute | solution.py:569
  29.8 17.2 %collective-permute-start.6 = (bf16[448,768]{1,0:T(8,128)(2,1)S(1)}, bf16[448,768]{1,0:T(8,128)(2,1)S(1)}, u32[]{:S(2)}, u32[]{:S(2)}) collective-permute-start(bf16[448,768]{1,0:T(8,128)(2,1)S(1)} %copy-done.1), channel_id=1, source_target_pairs={{0,32},{16,48},{32,0},{48,16},{1,33},{17,49},{33,1},{49,17},{2,34}... | collective-permute-start | bytes 2064392 | tf_op jit(solution)/shard_map/ppermute | solution.py:569
  29.8 17.2 %collective-permute-start.9 = (bf16[448,768]{1,0:T(8,128)(2,1)S(1)}, bf16[448,768]{1,0:T(8,128)(2,1)S(1)}, u32[]{:S(2)}, u32[]{:S(2)}) collective-permute-start(bf16[448,768]{1,0:T(8,128)(2,1)S(1)} %collective-permute-done.2.refs_4_.refs_2_), channel_id=1, source_target_pairs={{0,8},{8,0},{1,9},{9,1},{2,10},{10,2},{3,11},{11,3},{4,12},{12,4},... | collective-permute-start | bytes 2064392 | tf_op jit(solution)/shard_map/ppermute | solution.py:569
  47.0 3.9 %collective-permute-start.10 = (bf16[448,768]{1,0:T(8,128)(2,1)S(1)}, bf16[448,768]{1,0:T(8,128)(2,1)S(1)}, u32[]{:S(2)}, u32[]{:S(2)}) collective-permute-start(bf16[448,768]{1,0:T(8,128)(2,1)S(1)} %collective-permute-done.3.refs_5_.refs_3_), channel_id=1, source_target_pairs={{0,8},{8,0},{1,9},{9,1},{2,10},{10,2},{3,11},{11,3},{4,12},{12,4},... | collective-permute-start | bytes 2064392 | tf_op jit(solution)/shard_map/ppermute | solution.py:569
  49.2 2.8 %collective-permute-start.11 = (bf16[448,768]{1,0:T(8,128)(2,1)S(1)}, bf16[448,768]{1,0:T(8,128)(2,1)S(1)}, u32[]{:S(2)}, u32[]{:S(2)}) collective-permute-start(bf16[448,768]{1,0:T(8,128)(2,1)S(1)} %collective-permute-done.6.refs_4_.refs_2_.refs_1_), channel_id=1, source_target_pairs={{0,8},{8,0},{1,9},{9,1},{2,10},{10,2},{3,11},{11,3},{4,12},{12,4},... | collective-permute-start | bytes 2064392 | tf_op jit(solution)/shard_map/ppermute | solution.py:569
  49.2 40.0 %collective-permute-start.13 = (bf16[384,768]{1,0:T(8,128)(2,1)S(1)}, bf16[384,768]{1,0:T(8,128)(2,1)S(1)}, u32[]{:S(2)}, u32[]{:S(2)}) collective-permute-start(bf16[384,768]{1,0:T(8,128)(2,1)S(1)} %get-tuple-element.77), channel_id=1, source_target_pairs={{0,2},{1,3},{2,0},{3,1},{4,6},{5,7},{6,4},{7,5},{8,10},{9,11},{10,... | collective-permute-start | bytes 1769480 | tf_op jit(solution)/shard_map/ppermute | solution.py:569
  63.9 25.3 %collective-permute-start.12 = (bf16[480,384]{1,0:T(8,128)(2,1)S(1)}, bf16[480,384]{1,0:T(8,128)(2,1)S(1)}, u32[]{:S(2)}, u32[]{:S(2)}) collective-permute-start(bf16[480,384]{1,0:T(8,128)(2,1)S(1)} %attend_third.1), channel_id=1, source_target_pairs={{0,120},{8,128},{16,136},{24,144},{32,152},{40,160},{48,168},{56,1... | collective-permute-start | bytes 1105928 | tf_op jit(solution)/shard_map/ppermute | solution.py:634
  78.4 17.3 %collective-permute-start.16 = (bf16[480,384]{1,0:T(8,128)(2,1)S(1)}, bf16[480,384]{1,0:T(8,128)(2,1)S(1)}, u32[]{:S(2)}, u32[]{:S(2)}) collective-permute-start(bf16[480,384]{1,0:T(8,128)(2,1)S(1)} %get-tuple-element.80), channel_id=1, source_target_pairs={{0,184},{8,192},{16,200},{24,208},{32,216},{40,224},{48,232},{56,2... | collective-permute-start | bytes 1105928 | tf_op jit(solution)/shard_map/ppermute | solution.py:634
  79.7 16.0 %collective-permute-start.15 = (bf16[480,384]{1,0:T(8,128)(2,1)S(1)}, bf16[480,384]{1,0:T(8,128)(2,1)S(1)}, u32[]{:S(2)}, u32[]{:S(2)}) collective-permute-start(bf16[480,384]{1,0:T(8,128)(2,1)S(1)} %get-tuple-element.73), channel_id=1, source_target_pairs={{0,56},{8,64},{16,72},{24,80},{32,88},{40,96},{48,104},{56,112},{6... | collective-permute-start | bytes 1105928 | tf_op jit(solution)/shard_map/ppermute | solution.py:634
  89.2 10.1 %collective-permute-start.14 = (bf16[480,384]{1,0:T(8,128)(2,1)S(1)}, bf16[480,384]{1,0:T(8,128)(2,1)S(1)}, u32[]{:S(2)}, u32[]{:S(2)}) collective-permute-start(bf16[480,384]{1,0:T(8,128)(2,1)S(1)} %attend_late.1), channel_id=1, source_target_pairs={{0,248},{8,0},{16,8},{24,16},{32,24},{40,32},{48,40},{56,48},{64,5... | collective-permute-start | bytes 1105928 | tf_op jit(solution)/shard_map/ppermute | solution.py:634
  90.2 9.1 %copy-start.3 = (f32[64,768]{1,0:T(8,128)S(1)}, f32[64,768]{1,0:T(8,128)}, u32[]{:S(2)}) copy-start(f32[64,768]{1,0:T(8,128)} %table.1) | copy-start | bytes 589828
  90.2 12.8 %copy-start.5 = (bf16[448,768]{1,0:T(8,128)(2,1)S(1)}, bf16[448,768]{1,0:T(8,128)(2,1)}, u32[]{:S(2)}) copy-start(bf16[448,768]{1,0:T(8,128)(2,1)} %param.8) | copy-start | bytes 2064388
  90.2 30.3 %collective-permute-start.21 = (bf16[3,384,768]{2,1,0:T(8,128)(2,1)S(1)}, bf16[3,384,768]{2,1,0:T(8,128)(2,1)S(1)}, u32[]{:S(2)}, u32[]{:S(2)}) collective-permute-start(bf16[3,384,768]{2,1,0:T(8,128)(2,1)S(1)} %stack.41.refs_5_), channel_id=1, source_target_pairs={{0,8},{8,0},{1,9},{9,1},{2,10},{10,2},{3,11},{11,3},{4,12},{12,4},... | collective-permute-start | bytes 5308424 | tf_op jit(solution)/shard_map/ppermute | solution.py:569
  100.5 10.1 %collective-permute-start.20 = (bf16[448,384]{1,0:T(8,128)(2,1)S(1)}, bf16[448,384]{1,0:T(8,128)(2,1)S(1)}, u32[]{:S(2)}, u32[]{:S(2)}) collective-permute-start(bf16[448,384]{1,0:T(8,128)(2,1)S(1)} %get-tuple-element.86.refs_0_), channel_id=1, source_target_pairs={{0,3},{1,0},{2,1},{3,2},{4,7},{5,4},{6,5},{7,6},{8,11},{9,8},{10,9... | collective-permute-start | bytes 1032200 | tf_op jit(solution)/shard_map/ppermute | solution.py:569
  101.9 11.3 %collective-permute-start.19 = (bf16[448,384]{1,0:T(8,128)(2,1)S(1)}, bf16[448,384]{1,0:T(8,128)(2,1)S(1)}, u32[]{:S(2)}, u32[]{:S(2)}) collective-permute-start(bf16[448,384]{1,0:T(8,128)(2,1)S(1)} %get-tuple-element.86.refs_0_), channel_id=1, source_target_pairs={{0,2},{1,3},{2,0},{3,1},{4,6},{5,7},{6,4},{7,5},{8,10},{9,11},{10,... | collective-permute-start | bytes 1032200 | tf_op jit(solution)/shard_map/ppermute | solution.py:569
  102.4 18.1 %collective-permute-start.18 = (bf16[448,384]{1,0:T(8,128)(2,1)S(1)}, bf16[448,384]{1,0:T(8,128)(2,1)S(1)}, u32[]{:S(2)}, u32[]{:S(2)}) collective-permute-start(bf16[448,384]{1,0:T(8,128)(2,1)S(1)} %get-tuple-element.86.refs_0_), channel_id=1, source_target_pairs={{0,1},{1,2},{2,3},{3,0},{4,5},{5,6},{6,7},{7,4},{8,9},{9,10},{10,1... | collective-permute-start | bytes 1032200 | tf_op jit(solution)/shard_map/ppermute | solution.py:569
  103.0 25.7 %collective-permute-start.17 = (bf16[448,768]{1,0:T(8,128)(2,1)S(1)}, bf16[448,768]{1,0:T(8,128)(2,1)S(1)}, u32[]{:S(2)}, u32[]{:S(2)}) collective-permute-start(bf16[448,768]{1,0:T(8,128)(2,1)S(1)} %copy-done.5), channel_id=1, source_target_pairs={{0,248},{8,0},{16,8},{24,16},{32,24},{40,32},{48,40},{56,48},{64,5... | collective-permute-start | bytes 2064392 | tf_op jit(solution)/shard_map/ppermute | solution.py:569
  123.3 18.2 %collective-permute-start.22 = (bf16[448,768]{1,0:T(8,128)(2,1)S(1)}, bf16[448,768]{1,0:T(8,128)(2,1)S(1)}, u32[]{:S(2)}, u32[]{:S(2)}) collective-permute-start(bf16[448,768]{1,0:T(8,128)(2,1)S(1)} %project.3), channel_id=1, source_target_pairs={{0,4},{4,0},{1,5},{5,1},{2,6},{6,2},{3,7},{7,3},{8,12},{12,8},{9,1... | collective-permute-start | bytes 2064392 | tf_op jit(solution)/shard_map/ppermute | solution.py:569

commit v11 on v10

--- a/solution.py
+++ b/solution.py
@@ -459,10 +459,10 @@
 
 def finish(hidden, near, arrived, gate):
     part = hidden.shape[1]
-    rows = pl.BlockSpec((ROWS // 4, part), lambda i: (i, 0))
+    rows = pl.BlockSpec((ROWS // 2, part), lambda i: (i, 0))
     return pl.pallas_call(
         finish_kernel,
-        grid=(4,),
+        grid=(2,),
         out_shape=jax.ShapeDtypeStruct(hidden.shape, jnp.bfloat16),
         in_specs=[rows, rows, rows, pl.BlockSpec((1, part), lambda i: (0, 0))],
         out_specs=rows,
@@ -477,12 +477,12 @@
 
 
 def pack(keys, values):
-    vmem = pl.BlockSpec(memory_space=pltpu.VMEM)
     return pl.pallas_call(
         pack_kernel,
+        grid=(2,),
         out_shape=jax.ShapeDtypeStruct((ROWS, 2 * WIDTH), jnp.bfloat16),
-        in_specs=[vmem] * 2,
-        out_specs=vmem,
+        in_specs=[pl.BlockSpec((ROWS // 2, WIDTH), lambda i: (i, 0))] * 2,
+        out_specs=pl.BlockSpec((ROWS // 2, 2 * WIDTH), lambda i: (i, 0)),
         compiler_params=pltpu.CompilerParams(vmem_limit_bytes=WHOLE_VMEM),
         name="pack",
     )(keys, values)

time: 142 us -> 141 us (level); the launches traced: 143 us -> 140 us
  Pallas kernels: 62.2 us -> 58.8 us
  starting transfers between devices: 25.1 us -> 26.6 us
    pallas_call x4, Pallas kernels: 48.1 us -> 45.4 us  [attend(): pl.pallas_call(functools.partial(attend_kernel, call), out_shape=out_shap...]
    ppermute x16, starting transfers between devices: 16.6 us -> 18.1 us  [around(): lax.ppermute(value, axis, [(i, (i + steps) % count) for i in range(count)])]
  transfers between devices with their start and end apart: 23 -> 23, of which waited for: 9 -> 8; matrix products, arithmetic and copies ran while one was open for 0% -> 0% of each run, Pallas kernels for 41% -> 40%
where the time goes in v11:
time: 141 us; the launch traced here: 140 us
  Pallas kernels  58.8 us (42%)
  waiting for transfers between devices  51.4 us (36%)
  starting transfers between devices  26.6 us (19%)
  local copies, waits for them, and re-layouts  2.45 us (2%)
    pallas_call x4, Pallas kernels, attend(): pl.pallas_call(functools.partial(attend_kernel, call), out_shape=out_shap...  45.4 us
    ppermute x16, waiting for transfers between devices, around(): lax.ppermute(value, axis, [(i, (i + steps) % count) for i in range(count)])  30.3 us
    ppermute x16, starting transfers between devices, around(): lax.ppermute(value, axis, [(i, (i + steps) % count) for i in range(count)])  18.1 us
    ppermute x3, waiting for transfers between devices, to_level(): return lax.ppermute(value, 'z', [(i, i - d) for i in range(d, 4)])  13.8 us
    ppermute x4, waiting for transfers between devices, back(): return lax.ppermute(share, SLOT, pairs_back)  7.36 us
    pallas_call x2, Pallas kernels, project(): pl.pallas_call(functools.partial(project_kernel, far), out_shape=jax.Shap...  5.61 us
    ppermute x4, starting transfers between devices, back(): return lax.ppermute(share, SLOT, pairs_back)  4.63 us
    ppermute x3, starting transfers between devices, to_level(): return lax.ppermute(value, 'z', [(i, i - d) for i in range(d, 4)])  3.86 us
  transfers between devices with their start and end apart: 23, of which 8 were waited for; matrix products, arithmetic and copies ran while one was open for 0% of the time, Pallas kernels for 40%

profile of v11, /device:TPU:25, one launch (start us, length us, event | category | flops | bytes accessed | tf_op | source)
XLA Modules:
  0.0 140.3 jit_solution(9057804733388610665)
XLA Ops:
  0.0 1.9 %pack.1.refs_3_.refs_1_ = bf16[448,768]{1,0:T(8,128)(2,1)} custom-call(bf16[448,384]{1,0:T(8,128)(2,1)} %keys.1, bf16[448,384]{1,0:T(8,128)(2,1)} %values.1), custom_call_target="tpu_custom_call" | custom-call | tf_op jit(solution)/shard_map/pack/pallas_call | solution.py:480
  1.9 0.7 collective-permute-start.4
  2.6 0.5 collective-permute-start.3
  3.1 2.2 %collective-permute-start.2 = (bf16[448,768]{1,0:T(8,128)(2,1)}, bf16[448,768]{1,0:T(8,128)(2,1)S(1)}, u32[]{:S(2)}, u32[]{:S(2)}) collective-permute-start(bf16[448,768]{1,0:T(8,128)(2,1)} %pack.1.refs_3_.refs_1_), channel_id=1, source_target_pairs={{0,16},{16,32},{32,48},{48,0},{1,17},{17,33},{33,49},{49,1},{2,18}... | collective-permute-start | bytes 2064392 | tf_op jit(solution)/shard_map/ppermute | solution.py:569
  5.3 1.3 collective-permute-start
  6.6 1.3 collective-permute-start.1
  8.6 0.1 stack.40.ids
  8.7 2.3 %copy-done = bf16[384,6144]{1,0:T(8,128)(2,1)S(1)} copy-done((bf16[384,6144]{1,0:T(8,128)(2,1)S(1)}, bf16[384,6144]{1,0:T(8,128)(2,1)}, u32[]{:S(2)}) %copy-start) | copy-done | bytes 4718616
  11.0 0.9 columns.1
  11.9 13.8 %collective-permute-done.refs_0_ = bf16[448,384]{1,0:T(8,128)(2,1)S(1)} collective-permute-done((bf16[448,384]{1,0:T(8,128)(2,1)}, bf16[448,384]{1,0:T(8,128)(2,1)S(1)}, u32[]{:S(2)}, u32[]{:S(2)}) %collective-permute-start) | collective-permute-done | bytes 344096 | tf_op jit(solution)/shard_map/ppermute | solution.py:587
  25.7 0.0 collective-permute-done.1.refs_1_
  25.7 0.0 collective-permute-done.4.refs_6_.refs_5_
  25.7 1.3 collective-permute-start.5
  27.0 1.3 collective-permute-start.7
  28.3 1.5 %collective-permute-start.8 = (bf16[384,768]{1,0:T(8,128)(2,1)S(1)}, bf16[384,768]{1,0:T(8,128)(2,1)S(1)}, u32[]{:S(2)}, u32[]{:S(2)}) collective-permute-start(bf16[384,768]{1,0:T(8,128)(2,1)S(1)} %get-tuple-element.55), channel_id=1, source_target_pairs={{0,3},{1,0},{2,1},{3,2},{4,7},{5,4},{6,5},{7,6},{8,11},{9,8},{10,9... | collective-permute-start | bytes 1769480 | tf_op jit(solution)/shard_map/ppermute | solution.py:569
  29.8 1.7 %collective-permute-start.9 = (bf16[448,768]{1,0:T(8,128)(2,1)S(1)}, bf16[448,768]{1,0:T(8,128)(2,1)S(1)}, u32[]{:S(2)}, u32[]{:S(2)}) collective-permute-start(bf16[448,768]{1,0:T(8,128)(2,1)S(1)} %collective-permute-done.2.refs_4_.refs_2_), channel_id=1, source_target_pairs={{0,8},{8,0},{1,9},{9,1},{2,10},{10,2},{3,11},{11,3},{4,12},{12,4},... | collective-permute-start | bytes 2064392 | tf_op jit(solution)/shard_map/ppermute | solution.py:569
  31.4 15.5 %attend_early.1 = (f32[3,896,256]{2,1,0:T(8,128)S(1)}, f32[3,896,128]{2,1,0:T(8,128)S(1)}, f32[3,448,256]{2,1,0:T(8,128)S(1)}, f32[3,448,128]{2,1,0:T(8,128)S(1)}) custom-call(s32[9]{0:T(128)S(1)} %stack.40.ids, s32[32]{0:T(128)S(1)} %copy-done.4, s32[1]{0:T(128)S(6)} %copy.9.level, bf16[448,384]{1,0:T(8,128)(2,1)S(1)} %collective-permute-done.refs_0_, ...), custom_call_target="tpu_custom_call" | custom-call | flops 10000000000 | bytes 1000000 | tf_op jit(solution)/shard_map/attend_early/pallas_call | solution.py:324
  47.0 2.1 %collective-permute-start.10 = (bf16[448,768]{1,0:T(8,128)(2,1)S(1)}, bf16[448,768]{1,0:T(8,128)(2,1)S(1)}, u32[]{:S(2)}, u32[]{:S(2)}) collective-permute-start(bf16[448,768]{1,0:T(8,128)(2,1)S(1)} %collective-permute-done.3.refs_5_.refs_3_), channel_id=1, source_target_pairs={{0,8},{8,0},{1,9},{9,1},{2,10},{10,2},{3,11},{11,3},{4,12},{12,4},... | collective-permute-start | bytes 2064392 | tf_op jit(solution)/shard_map/ppermute | solution.py:569
  49.1 0.0 collective-permute-start.11
  49.1 1.5 %collective-permute-start.13 = (bf16[384,768]{1,0:T(8,128)(2,1)S(1)}, bf16[384,768]{1,0:T(8,128)(2,1)S(1)}, u32[]{:S(2)}, u32[]{:S(2)}) collective-permute-start(bf16[384,768]{1,0:T(8,128)(2,1)S(1)} %get-tuple-element.77), channel_id=1, source_target_pairs={{0,2},{1,3},{2,0},{3,1},{4,6},{5,7},{6,4},{7,5},{8,10},{9,11},{10,... | collective-permute-start | bytes 1769480 | tf_op jit(solution)/shard_map/ppermute | solution.py:569
  50.6 0.2 collective-permute-done.10.refs_7_.refs_4_.refs_3_
  50.9 1.0 collective-permute-done.11.refs_8_.refs_5_.refs_4_
  51.9 9.7 %attend_third.1 = bf16[480,384]{1,0:T(8,128)(2,1)S(1)} custom-call(s32[9]{0:T(128)S(1)} %stack.40.ids, s32[32]{0:T(128)S(1)} %copy-done.4, s32[1]{0:T(128)S(6)} %copy.9.level, bf16[448,384]{1,0:T(8,128)(2,1)S(1)} %collective-permute-done.5.refs_0_, bf16[448,768]{1,0:T(8,128)(2,1)S(1)} %copy-done.1, ...), custom_call_target="tpu_custom_call" | custom-call | flops 10000000000 | bytes 1000000 | tf_op jit(solution)/shard_map/attend_third/pallas_call | solution.py:324
  61.6 1.3 collective-permute-start.12
  62.9 12.9 %attend_middle.1 = (bf16[480,384]{1,0:T(8,128)(2,1)S(1)}, bf16[480,384]{1,0:T(8,128)(2,1)S(1)}) custom-call(s32[9]{0:T(128)S(1)} %stack.40.ids, s32[32]{0:T(128)S(1)} %copy-done.4, s32[1]{0:T(128)S(6)} %copy.9.level, bf16[448,384]{1,0:T(8,128)(2,1)S(1)} %collective-permute-done.refs_0_, bf16[448,384]{1,0:T(8,128)(2,1)S(1)} %collective-permute-done.1.refs_1_, ...), custom_call_target="tpu_custom_call" | custom-call | flops 49999998976 | bytes 1000000 | tf_op jit(solution)/shard_map/attend_middle/pallas_call | solution.py:324
  75.8 1.3 collective-permute-start.16
  77.1 1.9 %collective-permute-start.15 = (bf16[480,384]{1,0:T(8,128)(2,1)S(1)}, bf16[480,384]{1,0:T(8,128)(2,1)S(1)}, u32[]{:S(2)}, u32[]{:S(2)}) collective-permute-start(bf16[480,384]{1,0:T(8,128)(2,1)S(1)} %get-tuple-element.73), channel_id=1, source_target_pairs={{0,56},{8,64},{16,72},{24,80},{32,88},{40,96},{48,104},{56,112},{6... | collective-permute-start | bytes 1105928 | tf_op jit(solution)/shard_map/ppermute | solution.py:634
  79.1 7.3 %attend_late.1 = bf16[480,384]{1,0:T(8,128)(2,1)S(1)} custom-call(s32[9]{0:T(128)S(1)} %stack.40.ids, s32[32]{0:T(128)S(1)} %copy-done.4, s32[1]{0:T(128)S(6)} %copy.9.level, bf16[448,384]{1,0:T(8,128)(2,1)S(1)} %copy-done.2, bf16[448,768]{1,0:T(8,128)(2,1)S(1)} %collective-permute-done.6.refs_4_.refs_2_.refs_1_, ...), custom_call_target="tpu_custom_call" | custom-call | flops 1000000 | bytes 1000000 | tf_op jit(solution)/shard_map/attend_late/pallas_call | solution.py:324
  86.4 0.1 collective-permute-start.14
  86.5 0.9 stack.41.refs_5_
  87.4 0.0 copy-start.3
  87.4 0.0 copy-start.5
  87.4 0.1 collective-permute-start.21
  87.5 7.3 %collective-permute-done.16.three = bf16[480,384]{1,0:T(8,128)(2,1)S(1)} collective-permute-done((bf16[480,384]{1,0:T(8,128)(2,1)S(1)}, bf16[480,384]{1,0:T(8,128)(2,1)S(1)}, u32[]{:S(2)}, u32[]{:S(2)}) %collective-permute-start.16) | collective-permute-done | bytes 368672 | tf_op jit(solution)/shard_map/ppermute | solution.py:634
  94.9 1.9 %combine_later.1 = (f32[448,384]{1,0:T(8,128)S(1)}, f32[448,128]{1,0:T(8,128)S(1)}) custom-call(s32[9]{0:T(128)S(1)} %stack.40.ids, bf16[480,384]{1,0:T(8,128)(2,1)S(1)} %collective-permute-done.15.one, bf16[480,384]{1,0:T(8,128)(2,1)S(1)} %collective-permute-done.12.two, bf16[480,384]{1,0:T(8,128)(2,1)S(1)} %collective-permute-done.16.three), custom_call_target="tpu_custom_call" | custom-call | flops 99999997952 | bytes 200000000 | tf_op jit(solution)/shard_map/combine_later/pallas_call | solution.py:405
  96.8 1.2 combine.1
  98.0 1.3 collective-permute-start.20
  99.3 0.5 collective-permute-start.19
  99.9 0.6 collective-permute-start.18
  100.5 1.3 collective-permute-start.17
  101.8 5.4 %collective-permute-done.20.refs_3_ = bf16[448,384]{1,0:T(8,128)(2,1)S(1)} collective-permute-done((bf16[448,384]{1,0:T(8,128)(2,1)S(1)}, bf16[448,384]{1,0:T(8,128)(2,1)S(1)}, u32[]{:S(2)}, u32[]{:S(2)}) %collective-permute-start.20) | collective-permute-done | bytes 344096 | tf_op jit(solution)/shard_map/ppermute | solution.py:569
  107.2 2.5 %collective-permute-done.19.refs_2_ = bf16[448,384]{1,0:T(8,128)(2,1)S(1)} collective-permute-done((bf16[448,384]{1,0:T(8,128)(2,1)S(1)}, bf16[448,384]{1,0:T(8,128)(2,1)S(1)}, u32[]{:S(2)}, u32[]{:S(2)}) %collective-permute-start.19) | collective-permute-done | bytes 344096 | tf_op jit(solution)/shard_map/ppermute | solution.py:569
  109.7 8.5 %collective-permute-done.18.refs_1_ = bf16[448,384]{1,0:T(8,128)(2,1)S(1)} collective-permute-done((bf16[448,384]{1,0:T(8,128)(2,1)S(1)}, bf16[448,384]{1,0:T(8,128)(2,1)S(1)}, u32[]{:S(2)}, u32[]{:S(2)}) %collective-permute-start.18) | collective-permute-done | bytes 344096 | tf_op jit(solution)/shard_map/ppermute | solution.py:569
  118.2 2.8 %project.3 = bf16[448,768]{1,0:T(8,128)(2,1)S(1)} custom-call(s32[9]{0:T(128)S(1)} %stack.40.ids, bf16[448,384]{1,0:T(8,128)(2,1)S(1)} %get-tuple-element.86.refs_0_, bf16[448,384]{1,0:T(8,128)(2,1)S(1)} %collective-permute-done.18.refs_1_, bf16[448,384]{1,0:T(8,128)(2,1)S(1)} %collective-permute-done.19.refs_2_, ...), custom_call_target="tpu_custom_call" | custom-call | flops 1056964608 | bytes 5000000 | tf_op jit(solution)/shard_map/project/pallas_call | solution.py:553
  121.0 2.8 %collective-permute-start.22 = (bf16[448,768]{1,0:T(8,128)(2,1)S(1)}, bf16[448,768]{1,0:T(8,128)(2,1)S(1)}, u32[]{:S(2)}, u32[]{:S(2)}) collective-permute-start(bf16[448,768]{1,0:T(8,128)(2,1)S(1)} %project.3), channel_id=1, source_target_pairs={{0,4},{4,0},{1,5},{5,1},{2,6},{6,2},{3,7},{7,3},{8,12},{12,8},{9,1... | collective-permute-start | bytes 2064392 | tf_op jit(solution)/shard_map/ppermute | solution.py:569
  123.8 2.8 %project.2.near = f32[448,768]{1,0:T(8,128)S(1)} custom-call(s32[9]{0:T(128)S(1)} %stack.40.ids, bf16[448,384]{1,0:T(8,128)(2,1)S(1)} %get-tuple-element.86.refs_0_, bf16[448,384]{1,0:T(8,128)(2,1)S(1)} %collective-permute-done.18.refs_1_, bf16[448,384]{1,0:T(8,128)(2,1)S(1)} %collective-permute-done.19.refs_2_, ...), custom_call_target="tpu_custom_call" | custom-call | flops 1056964608 | bytes 5000000 | tf_op jit(solution)/shard_map/project/pallas_call | solution.py:553
  126.6 12.7 %collective-permute-done.22.arrived = bf16[448,768]{1,0:T(8,128)(2,1)S(1)} collective-permute-done((bf16[448,768]{1,0:T(8,128)(2,1)S(1)}, bf16[448,768]{1,0:T(8,128)(2,1)S(1)}, u32[]{:S(2)}, u32[]{:S(2)}) %collective-permute-start.22) | collective-permute-done | bytes 688160 | tf_op jit(solution)/shard_map/ppermute | solution.py:569
  139.3 1.0 finish.1
  (23 shorter events, 0.1 us)
Async XLA Ops:
  1.9 23.7 %collective-permute-start.4 = (bf16[448,768]{1,0:T(8,128)(2,1)}, bf16[448,768]{1,0:T(8,128)(2,1)S(1)}, u32[]{:S(2)}, u32[]{:S(2)}) collective-permute-start(bf16[448,768]{1,0:T(8,128)(2,1)} %pack.1.refs_3_.refs_1_), channel_id=1, source_target_pairs={{0,8},{8,0},{1,9},{9,1},{2,10},{10,2},{3,11},{11,3},{4,12},{12,4},... | collective-permute-start | bytes 2064392 | tf_op jit(solution)/shard_map/ppermute | solution.py:569
  2.6 23.1 %collective-permute-start.3 = (bf16[448,768]{1,0:T(8,128)(2,1)}, bf16[448,768]{1,0:T(8,128)(2,1)S(1)}, u32[]{:S(2)}, u32[]{:S(2)}) collective-permute-start(bf16[448,768]{1,0:T(8,128)(2,1)} %pack.1.refs_3_.refs_1_), channel_id=1, source_target_pairs={{0,48},{16,0},{32,16},{48,32},{1,49},{17,1},{33,17},{49,33},{2,50}... | collective-permute-start | bytes 2064392 | tf_op jit(solution)/shard_map/ppermute | solution.py:569
  3.1 22.6 %collective-permute-start.2 = (bf16[448,768]{1,0:T(8,128)(2,1)}, bf16[448,768]{1,0:T(8,128)(2,1)S(1)}, u32[]{:S(2)}, u32[]{:S(2)}) collective-permute-start(bf16[448,768]{1,0:T(8,128)(2,1)} %pack.1.refs_3_.refs_1_), channel_id=1, source_target_pairs={{0,16},{16,32},{32,48},{48,0},{1,17},{17,33},{33,49},{49,1},{2,18}... | collective-permute-start | bytes 2064392 | tf_op jit(solution)/shard_map/ppermute | solution.py:569
  5.3 20.4 %collective-permute-start = (bf16[448,384]{1,0:T(8,128)(2,1)}, bf16[448,384]{1,0:T(8,128)(2,1)S(1)}, u32[]{:S(2)}, u32[]{:S(2)}) collective-permute-start(bf16[448,384]{1,0:T(8,128)(2,1)} %refs_0_.2), channel_id=1, source_target_pairs={{64,0},{128,64},{192,128},{65,1},{129,65},{193,129},{66,2},{130,66... | collective-permute-start | bytes 1032200 | tf_op jit(solution)/shard_map/ppermute | solution.py:587
  6.6 19.1 %collective-permute-start.1 = (bf16[448,384]{1,0:T(8,128)(2,1)}, bf16[448,384]{1,0:T(8,128)(2,1)S(1)}, u32[]{:S(2)}, u32[]{:S(2)}) collective-permute-start(bf16[448,384]{1,0:T(8,128)(2,1)} %refs_0_.2), channel_id=1, source_target_pairs={{192,0},{193,1},{194,2},{195,3},{196,4},{197,5},{198,6},{199,7},{2... | collective-permute-start | bytes 1032200 | tf_op jit(solution)/shard_map/ppermute | solution.py:587
  8.6 2.3 %copy-start = (bf16[384,6144]{1,0:T(8,128)(2,1)S(1)}, bf16[384,6144]{1,0:T(8,128)(2,1)}, u32[]{:S(2)}) copy-start(bf16[384,6144]{1,0:T(8,128)(2,1)} %refs_0_.1) | copy-start | bytes 14155780
  11.0 14.7 %copy-start.2 = (bf16[448,384]{1,0:T(8,128)(2,1)S(1)}, bf16[448,384]{1,0:T(8,128)(2,1)}, u32[]{:S(2)}) copy-start(bf16[448,384]{1,0:T(8,128)(2,1)} %refs_0_.2) | copy-start | bytes 1032196
  11.0 18.8 %copy-start.1 = (bf16[448,768]{1,0:T(8,128)(2,1)S(1)}, bf16[448,768]{1,0:T(8,128)(2,1)}, u32[]{:S(2)}) copy-start(bf16[448,768]{1,0:T(8,128)(2,1)} %pack.1.refs_3_.refs_1_) | copy-start | bytes 2064388
  11.0 20.4 %copy-start.4 = (s32[32]{0:T(128)S(1)}, s32[32]{0:T(128)}, u32[]{:S(2)}) copy-start(s32[32]{0:T(128)} %live.5) | copy-start | bytes 388
  25.7 21.2 %collective-permute-start.5 = (bf16[448,384]{1,0:T(8,128)(2,1)S(1)}, bf16[448,384]{1,0:T(8,128)(2,1)S(1)}, u32[]{:S(2)}, u32[]{:S(2)}) collective-permute-start(bf16[448,384]{1,0:T(8,128)(2,1)S(1)} %copy-done.2), channel_id=1, source_target_pairs={{128,0},{192,64},{129,1},{193,65},{130,2},{194,66},{131,3},{195,67... | collective-permute-start | bytes 1032200 | tf_op jit(solution)/shard_map/ppermute | solution.py:587
  27.0 19.9 %collective-permute-start.7 = (bf16[384,768]{1,0:T(8,128)(2,1)S(1)}, bf16[384,768]{1,0:T(8,128)(2,1)S(1)}, u32[]{:S(2)}, u32[]{:S(2)}) collective-permute-start(bf16[384,768]{1,0:T(8,128)(2,1)S(1)} %get-tuple-element.54), channel_id=1, source_target_pairs={{0,1},{1,2},{2,3},{3,0},{4,5},{5,6},{6,7},{7,4},{8,9},{9,10},{10,1... | collective-permute-start | bytes 1769480 | tf_op jit(solution)/shard_map/ppermute | solution.py:569
  28.3 18.7 %collective-permute-start.8 = (bf16[384,768]{1,0:T(8,128)(2,1)S(1)}, bf16[384,768]{1,0:T(8,128)(2,1)S(1)}, u32[]{:S(2)}, u32[]{:S(2)}) collective-permute-start(bf16[384,768]{1,0:T(8,128)(2,1)S(1)} %get-tuple-element.55), channel_id=1, source_target_pairs={{0,3},{1,0},{2,1},{3,2},{4,7},{5,4},{6,5},{7,6},{8,11},{9,8},{10,9... | collective-permute-start | bytes 1769480 | tf_op jit(solution)/shard_map/ppermute | solution.py:569
  29.8 17.2 %collective-permute-start.6 = (bf16[448,768]{1,0:T(8,128)(2,1)S(1)}, bf16[448,768]{1,0:T(8,128)(2,1)S(1)}, u32[]{:S(2)}, u32[]{:S(2)}) collective-permute-start(bf16[448,768]{1,0:T(8,128)(2,1)S(1)} %copy-done.1), channel_id=1, source_target_pairs={{0,32},{16,48},{32,0},{48,16},{1,33},{17,49},{33,1},{49,17},{2,34}... | collective-permute-start | bytes 2064392 | tf_op jit(solution)/shard_map/ppermute | solution.py:569
  29.8 17.2 %collective-permute-start.9 = (bf16[448,768]{1,0:T(8,128)(2,1)S(1)}, bf16[448,768]{1,0:T(8,128)(2,1)S(1)}, u32[]{:S(2)}, u32[]{:S(2)}) collective-permute-start(bf16[448,768]{1,0:T(8,128)(2,1)S(1)} %collective-permute-done.2.refs_4_.refs_2_), channel_id=1, source_target_pairs={{0,8},{8,0},{1,9},{9,1},{2,10},{10,2},{3,11},{11,3},{4,12},{12,4},... | collective-permute-start | bytes 2064392 | tf_op jit(solution)/shard_map/ppermute | solution.py:569
  47.0 3.9 %collective-permute-start.10 = (bf16[448,768]{1,0:T(8,128)(2,1)S(1)}, bf16[448,768]{1,0:T(8,128)(2,1)S(1)}, u32[]{:S(2)}, u32[]{:S(2)}) collective-permute-start(bf16[448,768]{1,0:T(8,128)(2,1)S(1)} %collective-permute-done.3.refs_5_.refs_3_), channel_id=1, source_target_pairs={{0,8},{8,0},{1,9},{9,1},{2,10},{10,2},{3,11},{11,3},{4,12},{12,4},... | collective-permute-start | bytes 2064392 | tf_op jit(solution)/shard_map/ppermute | solution.py:569
  49.1 2.8 %collective-permute-start.11 = (bf16[448,768]{1,0:T(8,128)(2,1)S(1)}, bf16[448,768]{1,0:T(8,128)(2,1)S(1)}, u32[]{:S(2)}, u32[]{:S(2)}) collective-permute-start(bf16[448,768]{1,0:T(8,128)(2,1)S(1)} %collective-permute-done.6.refs_4_.refs_2_.refs_1_), channel_id=1, source_target_pairs={{0,8},{8,0},{1,9},{9,1},{2,10},{10,2},{3,11},{11,3},{4,12},{12,4},... | collective-permute-start | bytes 2064392 | tf_op jit(solution)/shard_map/ppermute | solution.py:569
  49.1 37.2 %collective-permute-start.13 = (bf16[384,768]{1,0:T(8,128)(2,1)S(1)}, bf16[384,768]{1,0:T(8,128)(2,1)S(1)}, u32[]{:S(2)}, u32[]{:S(2)}) collective-permute-start(bf16[384,768]{1,0:T(8,128)(2,1)S(1)} %get-tuple-element.77), channel_id=1, source_target_pairs={{0,2},{1,3},{2,0},{3,1},{4,6},{5,7},{6,4},{7,5},{8,10},{9,11},{10,... | collective-permute-start | bytes 1769480 | tf_op jit(solution)/shard_map/ppermute | solution.py:569
  61.6 24.8 %collective-permute-start.12 = (bf16[480,384]{1,0:T(8,128)(2,1)S(1)}, bf16[480,384]{1,0:T(8,128)(2,1)S(1)}, u32[]{:S(2)}, u32[]{:S(2)}) collective-permute-start(bf16[480,384]{1,0:T(8,128)(2,1)S(1)} %attend_third.1), channel_id=1, source_target_pairs={{0,120},{8,128},{16,136},{24,144},{32,152},{40,160},{48,168},{56,1... | collective-permute-start | bytes 1105928 | tf_op jit(solution)/shard_map/ppermute | solution.py:634
  75.8 19.1 %collective-permute-start.16 = (bf16[480,384]{1,0:T(8,128)(2,1)S(1)}, bf16[480,384]{1,0:T(8,128)(2,1)S(1)}, u32[]{:S(2)}, u32[]{:S(2)}) collective-permute-start(bf16[480,384]{1,0:T(8,128)(2,1)S(1)} %get-tuple-element.80), channel_id=1, source_target_pairs={{0,184},{8,192},{16,200},{24,208},{32,216},{40,224},{48,232},{56,2... | collective-permute-start | bytes 1105928 | tf_op jit(solution)/shard_map/ppermute | solution.py:634
  77.1 17.8 %collective-permute-start.15 = (bf16[480,384]{1,0:T(8,128)(2,1)S(1)}, bf16[480,384]{1,0:T(8,128)(2,1)S(1)}, u32[]{:S(2)}, u32[]{:S(2)}) collective-permute-start(bf16[480,384]{1,0:T(8,128)(2,1)S(1)} %get-tuple-element.73), channel_id=1, source_target_pairs={{0,56},{8,64},{16,72},{24,80},{32,88},{40,96},{48,104},{56,112},{6... | collective-permute-start | bytes 1105928 | tf_op jit(solution)/shard_map/ppermute | solution.py:634
  86.4 10.4 %collective-permute-start.14 = (bf16[480,384]{1,0:T(8,128)(2,1)S(1)}, bf16[480,384]{1,0:T(8,128)(2,1)S(1)}, u32[]{:S(2)}, u32[]{:S(2)}) collective-permute-start(bf16[480,384]{1,0:T(8,128)(2,1)S(1)} %attend_late.1), channel_id=1, source_target_pairs={{0,248},{8,0},{16,8},{24,16},{32,24},{40,32},{48,40},{56,48},{64,5... | collective-permute-start | bytes 1105928 | tf_op jit(solution)/shard_map/ppermute | solution.py:634
  87.4 9.4 %copy-start.3 = (f32[64,768]{1,0:T(8,128)S(1)}, f32[64,768]{1,0:T(8,128)}, u32[]{:S(2)}) copy-start(f32[64,768]{1,0:T(8,128)} %table.1) | copy-start | bytes 589828
  87.4 13.0 %copy-start.5 = (bf16[448,768]{1,0:T(8,128)(2,1)S(1)}, bf16[448,768]{1,0:T(8,128)(2,1)}, u32[]{:S(2)}) copy-start(bf16[448,768]{1,0:T(8,128)(2,1)} %param.8) | copy-start | bytes 2064388
  87.4 30.8 %collective-permute-start.21 = (bf16[3,384,768]{2,1,0:T(8,128)(2,1)S(1)}, bf16[3,384,768]{2,1,0:T(8,128)(2,1)S(1)}, u32[]{:S(2)}, u32[]{:S(2)}) collective-permute-start(bf16[3,384,768]{2,1,0:T(8,128)(2,1)S(1)} %stack.41.refs_5_), channel_id=1, source_target_pairs={{0,8},{8,0},{1,9},{9,1},{2,10},{10,2},{3,11},{11,3},{4,12},{12,4},... | collective-permute-start | bytes 5308424 | tf_op jit(solution)/shard_map/ppermute | solution.py:569
  98.0 9.2 %collective-permute-start.20 = (bf16[448,384]{1,0:T(8,128)(2,1)S(1)}, bf16[448,384]{1,0:T(8,128)(2,1)S(1)}, u32[]{:S(2)}, u32[]{:S(2)}) collective-permute-start(bf16[448,384]{1,0:T(8,128)(2,1)S(1)} %get-tuple-element.86.refs_0_), channel_id=1, source_target_pairs={{0,3},{1,0},{2,1},{3,2},{4,7},{5,4},{6,5},{7,6},{8,11},{9,8},{10,9... | collective-permute-start | bytes 1032200 | tf_op jit(solution)/shard_map/ppermute | solution.py:569
  99.3 10.4 %collective-permute-start.19 = (bf16[448,384]{1,0:T(8,128)(2,1)S(1)}, bf16[448,384]{1,0:T(8,128)(2,1)S(1)}, u32[]{:S(2)}, u32[]{:S(2)}) collective-permute-start(bf16[448,384]{1,0:T(8,128)(2,1)S(1)} %get-tuple-element.86.refs_0_), channel_id=1, source_target_pairs={{0,2},{1,3},{2,0},{3,1},{4,6},{5,7},{6,4},{7,5},{8,10},{9,11},{10,... | collective-permute-start | bytes 1032200 | tf_op jit(solution)/shard_map/ppermute | solution.py:569
  99.9 18.3 %collective-permute-start.18 = (bf16[448,384]{1,0:T(8,128)(2,1)S(1)}, bf16[448,384]{1,0:T(8,128)(2,1)S(1)}, u32[]{:S(2)}, u32[]{:S(2)}) collective-permute-start(bf16[448,384]{1,0:T(8,128)(2,1)S(1)} %get-tuple-element.86.refs_0_), channel_id=1, source_target_pairs={{0,1},{1,2},{2,3},{3,0},{4,5},{5,6},{6,7},{7,4},{8,9},{9,10},{10,1... | collective-permute-start | bytes 1032200 | tf_op jit(solution)/shard_map/ppermute | solution.py:569
  100.5 26.1 %collective-permute-start.17 = (bf16[448,768]{1,0:T(8,128)(2,1)S(1)}, bf16[448,768]{1,0:T(8,128)(2,1)S(1)}, u32[]{:S(2)}, u32[]{:S(2)}) collective-permute-start(bf16[448,768]{1,0:T(8,128)(2,1)S(1)} %copy-done.5), channel_id=1, source_target_pairs={{0,248},{8,0},{16,8},{24,16},{32,24},{40,32},{48,40},{56,48},{64,5... | collective-permute-start | bytes 2064392 | tf_op jit(solution)/shard_map/ppermute | solution.py:569
  121.0 18.3 %collective-permute-start.22 = (bf16[448,768]{1,0:T(8,128)(2,1)S(1)}, bf16[448,768]{1,0:T(8,128)(2,1)S(1)}, u32[]{:S(2)}, u32[]{:S(2)}) collective-permute-start(bf16[448,768]{1,0:T(8,128)(2,1)S(1)} %project.3), channel_id=1, source_target_pairs={{0,4},{4,0},{1,5},{5,1},{2,6},{6,2},{3,7},{7,3},{8,12},{12,8},{9,1... | collective-permute-start | bytes 2064392 | tf_op jit(solution)/shard_map/ppermute | solution.py:569
